TPU v7x, 512 devices: a whole 4x4x16 slice. The times are simulated.
512 devices in a mesh: section: 8 (over z_lo), node: 2 (over core), local: 32 (over z_hi, x, y).
Axes of the slice: x: 4, y: 4, z: 16 (z_hi: 2, z_lo: 8; z = z_hi * 8 + z_lo), core: 2. Of those that a mesh axis runs over, the one named last changes fastest.
Arguments:
- act_forward: bfloat16 [32768, 2048], P(('section', 'local'), 'node'), may hold values from -6 to 6
- routes_forward: int32 [32768, 6], P(('section', 'local')), may hold values from 0 to 31, all different within a row; in each aligned block of 128 rows (0 to 127, 128 to 255, ...) at most 25 rows name the same one
- gates_forward: bfloat16 [32768, 6], P(('section', 'local')), may hold values from 0.049804688 to 1
- act_backward: bfloat16 [32768, 2048], P(('section', 'local'), 'node'), may hold values from -6 to 6
- grad_backward: bfloat16 [32768, 2048], P(('section', 'local'), 'node'), may hold values from -6 to 6
- routes_backward: int32 [32768, 6], P(('section', 'local')), may hold values from 0 to 31, all different within a row; in each aligned block of 128 rows (0 to 127, 128 to 255, ...) at most 25 rows name the same one
- gates_backward: bfloat16 [32768, 6], P(('section', 'local')), may hold values from 0.049804688 to 1
- w_in: bfloat16 [8, 32, 2048, 768], P('section', 'local', 'node'), may hold values from -0.125 to 0.125
- w_out: bfloat16 [8, 32, 768, 2048], P('section', 'local', None, 'node'), may hold values from -0.21875 to 0.21875
Outputs:
- sent_forward: bfloat16 [32768, 2048], P(('section', 'local'), 'node')
- sent_backward: bfloat16 [32768, 2048], P(('section', 'local'), 'node')
Inputs may be any that keep to these rules, and one draw needn't show every extreme that they name: `routes_forward`: each token names 6 different experts. In each aligned block of 128 rows no expert is named by more than 25 rows, a bound that some block reaches. `routes_backward`: as for routes_forward.
All inputs are finite; a program needn't handle non-finite values.
Results may differ from a plain program's by a relative error of at most 0.019.
Values may be sent and summed in bfloat16 or wider, within the bound.
No kernel may reach another device: no remote copies, remote signals or barrier semaphores. Data moves between devices by JAX's collectives and lax.ppermute only.
A program may use at most 64 MiB of HBM per device.

v0:
```python
import jax
import jax.numpy as jnp
from jax import lax
from jax.sharding import PartitionSpec as P


def passed_along(x, axis, by):
    devices = lax.axis_size(axis)
    return lax.ppermute(x, axis, [(i, (i + by) % devices) for i in range(devices)])


def slot_tables(route_ids, gates, experts, capacity):
    tok_count, top_count = route_ids.shape
    flat_ids = route_ids.reshape(tok_count * top_count)
    labels = jnp.arange(experts, dtype=jnp.int32)
    onehot = (flat_ids[:, None] == labels[None, :]).astype(jnp.int32)
    before = jnp.cumsum(onehot, axis=0) - onehot
    ranking = jnp.sum(before * onehot, axis=1)
    target = (flat_ids * capacity + ranking).reshape(tok_count, top_count)
    slot_ids = jnp.arange(experts * capacity, dtype=jnp.int32)
    matches = target[:, :, None] == slot_ids[None, None, :]
    dispatch = jnp.sum(matches.astype(jnp.float32), axis=1).astype(jnp.bfloat16).T
    gathering = jnp.sum(
        jnp.where(matches, gates.astype(jnp.float32)[:, :, None], 0.0), axis=1
    ).astype(jnp.bfloat16)
    return (dispatch, gathering)


def hidden_act(rows, weight_in):
    part_sum = (
        jnp.dot(rows, weight_in, preferred_element_type=jnp.float32)
        .astype(jnp.bfloat16)
        .astype(jnp.float32)
    )
    summed = lax.psum(part_sum.astype(jnp.bfloat16), "node").astype(jnp.float32)
    hidden = jax.nn.silu(summed).astype(jnp.bfloat16)
    return hidden


def hidden_slope(preact, back_h):
    sigma = jax.nn.sigmoid(preact)
    return (back_h * sigma * (1.0 + preact * (1.0 - sigma))).astype(jnp.bfloat16)


def expert_forward(received, weight_in, weight_out):
    rows = received.reshape(-1, received.shape[2])
    hidden = hidden_act(rows, weight_in)
    return (
        jnp.dot(hidden, weight_out, preferred_element_type=jnp.float32)
        .astype(jnp.bfloat16)
        .reshape(received.shape)
    )


def expert_backward(received_act, received_grad, weight_in, weight_out):
    rows_act = received_act.reshape(-1, received_act.shape[2])
    rows_grad = received_grad.reshape(-1, received_grad.shape[2])
    contract = (((1,), (1,)), ((), ()))
    part_pre = (
        jnp.dot(rows_act, weight_in, preferred_element_type=jnp.float32)
        .astype(jnp.bfloat16)
        .astype(jnp.float32)
    )
    part_back = (
        lax.dot_general(rows_grad, weight_out, contract, preferred_element_type=jnp.float32)
        .astype(jnp.bfloat16)
        .astype(jnp.float32)
    )
    preact, back_h = (
        lax.psum(part_pre.astype(jnp.bfloat16), "node").astype(jnp.float32),
        lax.psum(part_back.astype(jnp.bfloat16), "node").astype(jnp.float32),
    )
    grad_hidden = hidden_slope(preact, back_h)
    result = lax.dot_general(grad_hidden, weight_in, contract, preferred_element_type=jnp.float32)
    return result.astype(jnp.bfloat16).reshape(received_act.shape)


def local(
    act_forward,
    routes_forward,
    gates_forward,
    act_backward,
    grad_backward,
    routes_backward,
    gates_backward,
    w_in,
    w_out,
):
    weight_in = w_in[0, 0]
    weight_out = w_out[0, 0]
    feature_cols = act_forward.shape[1]
    experts = lax.axis_size("local") * w_in.shape[1]
    tok_count, top_count = routes_forward.shape
    capacity = (25 * top_count * tok_count + 24 * experts - 1) // (24 * experts)
    send_fwd, mix_fwd = slot_tables(routes_forward, gates_forward, experts, capacity)
    send_bwd, mix_bwd = slot_tables(routes_backward, gates_backward, experts, capacity)
    block_shape = (experts, capacity, feature_cols)
    packed_fwd = (
        jnp.dot(send_fwd, act_forward, preferred_element_type=jnp.float32)
        .astype(jnp.bfloat16)
        .reshape(block_shape)
    )
    joined = jnp.concatenate([act_backward, grad_backward], axis=1)
    packed_both = jnp.dot(send_bwd, joined, preferred_element_type=jnp.float32).astype(jnp.bfloat16)
    packed_act = packed_both[:, :feature_cols].reshape(block_shape)
    packed_grad = packed_both[:, feature_cols:].reshape(block_shape)
    results = expert_forward(
        lax.all_to_all(packed_fwd, "local", split_axis=0, concat_axis=0, tiled=True),
        weight_in,
        weight_out,
    )
    back_fwd = lax.all_to_all(results, "local", split_axis=0, concat_axis=0, tiled=True)
    results = expert_backward(
        lax.all_to_all(packed_act, "local", split_axis=0, concat_axis=0, tiled=True),
        lax.all_to_all(packed_grad, "local", split_axis=0, concat_axis=0, tiled=True),
        weight_in,
        weight_out,
    )
    back_bwd = lax.all_to_all(results, "local", split_axis=0, concat_axis=0, tiled=True)
    layer_out = jnp.dot(
        mix_fwd, back_fwd.reshape(-1, feature_cols), preferred_element_type=jnp.float32
    ).astype(jnp.bfloat16)
    input_grad = jnp.dot(
        mix_bwd, back_bwd.reshape(-1, feature_cols), preferred_element_type=jnp.float32
    ).astype(jnp.bfloat16)
    sent_forward = passed_along(layer_out, "section", 1)
    sent_backward = passed_along(input_grad, "section", -1)
    return (sent_forward, sent_backward)


def solution(mesh):
    in_specs = (
        P(("section", "local"), "node"),
        P(("section", "local"), None),
        P(("section", "local"), None),
        P(("section", "local"), "node"),
        P(("section", "local"), "node"),
        P(("section", "local"), None),
        P(("section", "local"), None),
        P("section", "local", "node", None),
        P("section", "local", None, "node"),
    )
    out_specs = (P(("section", "local"), "node"), P(("section", "local"), "node"))
    return jax.shard_map(local, mesh=mesh, in_specs=in_specs, out_specs=out_specs, check_vma=False)
```

profile of v0, /device:TPU:102, one launch (start us, length us, event | category | flops | bytes accessed | tf_op | source)
XLA Modules:
  0.0 635.7 jit_solution(5495356983200089866)
XLA Ops:
  12.7 2.0 convolution_convert_fusion
  16.3 2.7 reshape.92
  19.0 18.3 %all-to-all-start.3 = ((bf16[32,25,1024]{2,1,0:T(8,128)(2,1)}), bf16[32,25,1024]{2,1,0:T(8,128)(2,1)}, u32[]{:S(2)}, u32[]{:S(2)}) async-start(bf16[32,25,1024]{2,1,0:T(8,128)(2,1)} %reshape.92), calls=%async_computation.3 | async-start | bytes 4194304 | tf_op jit(solution)/shard_map/all_to_all | solution.py:114
  38.4 3.3 reduce-window.14
  43.5 2.7 convolution_convert_fusion.3
  46.2 2.7 reshape.85
  48.9 95.1 %all-to-all-done.3 = bf16[32,25,1024]{2,1,0:T(8,128)(2,1)} async-done(((bf16[32,25,1024]{2,1,0:T(8,128)(2,1)}), bf16[32,25,1024]{2,1,0:T(8,128)(2,1)}, u32[]{:S(2)}, u32[]{:S(2)}) %all-to-all-start.3) | async-done | bytes 1638432 | tf_op jit(solution)/shard_map/all_to_all | solution.py:114
  144.1 25.6 %all-to-all-start = ((bf16[32,25,1024]{2,1,0:T(8,128)(2,1)}), bf16[32,25,1024]{2,1,0:T(8,128)(2,1)}, u32[]{:S(2)}, u32[]{:S(2)}) async-start(bf16[32,25,1024]{2,1,0:T(8,128)(2,1)} %reshape.85), calls=%async_computation | async-start | bytes 4194304 | tf_op jit(solution)/shard_map/all_to_all | solution.py:108
  171.2 73.8 %all-to-all-done = bf16[32,25,1024]{2,1,0:T(8,128)(2,1)} async-done(((bf16[32,25,1024]{2,1,0:T(8,128)(2,1)}), bf16[32,25,1024]{2,1,0:T(8,128)(2,1)}, u32[]{:S(2)}, u32[]{:S(2)}) %all-to-all-start) | async-done | bytes 1638432 | tf_op jit(solution)/shard_map/all_to_all | solution.py:108
  245.0 32.3 %all-to-all-start.2 = ((bf16[32,25,1024]{2,1,0:T(8,128)(2,1)}), bf16[32,25,1024]{2,1,0:T(8,128)(2,1)}, u32[]{:S(2)}, u32[]{:S(2)}) async-start(bf16[32,25,1024]{2,1,0:T(8,128)(2,1)} %reshape.90), calls=%async_computation.2 | async-start | bytes 4194304 | tf_op jit(solution)/shard_map/all_to_all | solution.py:115
  279.3 2.7 reshape.86
  282.1 2.5 fusion.21
  284.6 2.5 fusion.18
  287.0 47.4 %all-to-all-done.2 = bf16[32,25,1024]{2,1,0:T(8,128)(2,1)} async-done(((bf16[32,25,1024]{2,1,0:T(8,128)(2,1)}), bf16[32,25,1024]{2,1,0:T(8,128)(2,1)}, u32[]{:S(2)}, u32[]{:S(2)}) %all-to-all-start.2) | async-done | bytes 1638432 | tf_op jit(solution)/shard_map/all_to_all | solution.py:115
  336.3 4.0 fusion.24
  340.3 44.0 %all-reduce.3.cloned.1.call-done = (bf16[800,768]{1,0:T(8,128)(2,1)}, bf16[800,768]{1,0:T(8,128)(2,1)}, bf16[800,768]{1,0:T(8,128)(2,1)}) async-done(((bf16[800,768]{1,0:T(8,128)(2,1)}, bf16[800,768]{1,0:T(8,128)(2,1)}, bf16[800,768]{1,0:T(8,128)(2,1)}), (bf16[800,768]{1,0:T(8,128)(2,1)}, bf16[800,768]{1,0:T(8,128)(2,1)}, bf16[800,768]{1,0:T(8,128)(2,1)})) %all-reduce.3.cloned.1.call-update) | async-done | bytes 3686416 | tf_op jit(solution)/shard_map/psum | solution.py:35
  384.3 3.7 convolution_convert_fusion.1
  389.7 15.1 %all-to-all-start.4 = ((bf16[32,25,1024]{2,1,0:T(8,128)(2,1)}), bf16[32,25,1024]{2,1,0:T(8,128)(2,1)}, u32[]{:S(2)}, u32[]{:S(2)}) async-start(bf16[32,25,1024]{2,1,0:T(8,128)(2,1)} %reshape.94), calls=%async_computation.4 | async-start | bytes 4194304 | tf_op jit(solution)/shard_map/all_to_all | solution.py:119
  404.8 3.3 convolution_convert_fusion.2
  409.6 121.5 %all-to-all-done.4 = bf16[32,25,1024]{2,1,0:T(8,128)(2,1)} async-done(((bf16[32,25,1024]{2,1,0:T(8,128)(2,1)}), bf16[32,25,1024]{2,1,0:T(8,128)(2,1)}, u32[]{:S(2)}, u32[]{:S(2)}) %all-to-all-start.4) | async-done | bytes 1638432 | tf_op jit(solution)/shard_map/all_to_all | solution.py:119
  531.1 7.8 %all-to-all-start.1 = ((bf16[32,25,1024]{2,1,0:T(8,128)(2,1)}), bf16[32,25,1024]{2,1,0:T(8,128)(2,1)}, u32[]{:S(2)}, u32[]{:S(2)}) async-start(bf16[32,25,1024]{2,1,0:T(8,128)(2,1)} %reshape.87), calls=%async_computation.1 | async-start | bytes 4194304 | tf_op jit(solution)/shard_map/all_to_all | solution.py:112
  541.9 2.0 collective-permute-start.1
  543.9 70.5 %all-to-all-done.1 = bf16[32,25,1024]{2,1,0:T(8,128)(2,1)} async-done(((bf16[32,25,1024]{2,1,0:T(8,128)(2,1)}), bf16[32,25,1024]{2,1,0:T(8,128)(2,1)}, u32[]{:S(2)}, u32[]{:S(2)}) %all-to-all-start.1) | async-done | bytes 1638432 | tf_op jit(solution)/shard_map/all_to_all | solution.py:112
  618.7 7.8 %collective-permute-done = bf16[128,1024]{1,0:T(8,128)(2,1)S(1)} collective-permute-done((bf16[128,1024]{1,0:T(8,128)(2,1)S(1)}, bf16[128,1024]{1,0:T(8,128)(2,1)S(1)}, u32[]{:S(2)}, u32[]{:S(2)}) %collective-permute-start) | collective-permute-done | bytes 262176 | tf_op jit(solution)/shard_map/ppermute | solution.py:9
  (51 shorter events, 28.2 us)
Async XLA Ops:
  7.2 274.9 %copy-start = (bf16[1,1,1024,768]{3,2,1,0:T(8,128)(2,1)S(1)}, bf16[1,1,1024,768]{3,2,1,0:T(8,128)(2,1)}, u32[]{:S(2)}) copy-start(bf16[1,1,1024,768]{3,2,1,0:T(8,128)(2,1)} %param.16) | copy-start | bytes 4718596
  19.0 18.3 %copy-start.3 = (s32[128,6]{0,1:T(8,128)S(1)}, s32[128,6]{0,1:T(8,128)}, u32[]{:S(2)}) copy-start(s32[128,6]{0,1:T(8,128)} %param.10) | copy-start | bytes 9220
  19.0 23.3 %copy-start.4 = (bf16[128,6]{0,1:T(8,128)(2,1)S(1)}, bf16[128,6]{0,1:T(8,128)(2,1)}, u32[]{:S(2)}) copy-start(bf16[128,6]{0,1:T(8,128)(2,1)} %param.11) | copy-start | bytes 4612
  19.0 125.0 %all-to-all-start.3 = ((bf16[32,25,1024]{2,1,0:T(8,128)(2,1)}), bf16[32,25,1024]{2,1,0:T(8,128)(2,1)}, u32[]{:S(2)}, u32[]{:S(2)}) async-start(bf16[32,25,1024]{2,1,0:T(8,128)(2,1)} %reshape.92), calls=%async_computation.3 | async-start | bytes 4194304 | tf_op jit(solution)/shard_map/all_to_all | solution.py:114
  144.1 100.9 %all-to-all-start = ((bf16[32,25,1024]{2,1,0:T(8,128)(2,1)}), bf16[32,25,1024]{2,1,0:T(8,128)(2,1)}, u32[]{:S(2)}, u32[]{:S(2)}) async-start(bf16[32,25,1024]{2,1,0:T(8,128)(2,1)} %reshape.85), calls=%async_computation | async-start | bytes 4194304 | tf_op jit(solution)/shard_map/all_to_all | solution.py:108
  245.0 89.4 %all-to-all-start.2 = ((bf16[32,25,1024]{2,1,0:T(8,128)(2,1)}), bf16[32,25,1024]{2,1,0:T(8,128)(2,1)}, u32[]{:S(2)}, u32[]{:S(2)}) async-start(bf16[32,25,1024]{2,1,0:T(8,128)(2,1)} %reshape.90), calls=%async_computation.2 | async-start | bytes 4194304 | tf_op jit(solution)/shard_map/all_to_all | solution.py:115
  277.2 107.1 %all-reduce.3.cloned.1.call-start = ((), (), s32[]{:S(2)}) async-start(), calls=%async_computation.5 | async-start | bytes 7372800 | tf_op jit(solution)/shard_map/psum | solution.py:35
  282.1 2.5 copy-start.1
  389.7 141.4 %all-to-all-start.4 = ((bf16[32,25,1024]{2,1,0:T(8,128)(2,1)}), bf16[32,25,1024]{2,1,0:T(8,128)(2,1)}, u32[]{:S(2)}, u32[]{:S(2)}) async-start(bf16[32,25,1024]{2,1,0:T(8,128)(2,1)} %reshape.94), calls=%async_computation.4 | async-start | bytes 4194304 | tf_op jit(solution)/shard_map/all_to_all | solution.py:119
  531.1 83.3 %all-to-all-start.1 = ((bf16[32,25,1024]{2,1,0:T(8,128)(2,1)}), bf16[32,25,1024]{2,1,0:T(8,128)(2,1)}, u32[]{:S(2)}, u32[]{:S(2)}) async-start(bf16[32,25,1024]{2,1,0:T(8,128)(2,1)} %reshape.87), calls=%async_computation.1 | async-start | bytes 4194304 | tf_op jit(solution)/shard_map/all_to_all | solution.py:112
  541.9 74.4 %copy-start.2 = (bf16[128,800]{0,1:T(8,128)(2,1)S(1)}, bf16[128,800]{0,1:T(8,128)(2,1)}, u32[]{:S(2)}) copy-start(bf16[128,800]{0,1:T(8,128)(2,1)} %get-tuple-element.4) | copy-start | bytes 614404
  541.9 76.8 %collective-permute-start.1 = (bf16[128,1024]{1,0:T(8,128)(2,1)}, bf16[128,1024]{1,0:T(8,128)(2,1)}, u32[]{:S(2)}, u32[]{:S(2)}) collective-permute-start(bf16[128,1024]{1,0:T(8,128)(2,1)} %convolution_convert_fusion.4), channel_id=1, source_target_pairs={{0,448},{64,0},{128,64},{192,128},{256,192},{320,256},{384,320},{4... | collective-permute-start | bytes 786440 | tf_op jit(solution)/shard_map/ppermute | solution.py:9
  616.7 9.7 %collective-permute-start = (bf16[128,1024]{1,0:T(8,128)(2,1)S(1)}, bf16[128,1024]{1,0:T(8,128)(2,1)S(1)}, u32[]{:S(2)}, u32[]{:S(2)}) collective-permute-start(bf16[128,1024]{1,0:T(8,128)(2,1)S(1)} %convolution_convert_fusion.5), channel_id=1, source_target_pairs={{0,64},{64,128},{128,192},{192,256},{256,320},{320,384},{384,448},... | collective-permute-start | bytes 786440 | tf_op jit(solution)/shard_map/ppermute | solution.py:9
Sparse Core Ops, SparseCore 0:
  340.4 43.8 all-reduce.2
where the time goes:
time: 637 us; the launch traced here: 636 us
  waiting for transfers between devices  460 us (72%)
  starting transfers between devices  103 us (16%)
  local copies, waits for them, and re-layouts  26.8 us (4%)
  matrix products  22.3 us (4%)
  between operations  14.3 us (2%)
  other arithmetic  9.09 us (1%)
    all_to_all x2, waiting for transfers between devices, local(): lax.all_to_all(results, 'local', split_axis=0, concat_axis=0, tiled=True)  192 us
    all_to_all x1, waiting for transfers between devices, local(): lax.all_to_all(packed_act, 'local', split_axis=0, concat_axis=0, tiled=True)  95.1 us
    all_to_all x1, waiting for transfers between devices, local(): lax.all_to_all(packed_fwd, 'local', split_axis=0, concat_axis=0, tiled=True)  73.8 us
    all_to_all x1, waiting for transfers between devices, local(): lax.all_to_all(packed_grad, 'local', split_axis=0, concat_axis=0, tiled=T...  47.4 us
    psum x1, waiting for transfers between devices, hidden_act(): summed = lax.psum(part_sum.astype(jnp.bfloat16), 'node').astype(jnp.float32)  44 us
    all_to_all x1, starting transfers between devices, local(): lax.all_to_all(packed_grad, 'local', split_axis=0, concat_axis=0, tiled=T...  32.3 us
    all_to_all x1, starting transfers between devices, local(): lax.all_to_all(packed_fwd, 'local', split_axis=0, concat_axis=0, tiled=True)  25.6 us
    all_to_all x2, starting transfers between devices, local(): lax.all_to_all(results, 'local', split_axis=0, concat_axis=0, tiled=True)  22.9 us
  transfers between devices with their start and end apart: 8, of which 7 were waited for; matrix products, arithmetic and copies ran while one was open for 5% of the time, Pallas kernels for 0%

commit v1 on v0

v1 whole, which is shorter than its diff:
```python
import jax
import jax.numpy as jnp
from jax import lax
from jax.sharding import Mesh, PartitionSpec as P

CAP = 25
NODE = "node"
PLANE = ("x", "y")
RING = ("section", "zhi", "x", "y")


def pairs_of(shape, move):
    sections, halves, xs, ys = shape
    pairs = []
    for s in range(sections):
        for h in range(halves):
            for x in range(xs):
                for y in range(ys):
                    s2, h2 = move(s, h)
                    src = ((s * halves + h) * xs + x) * ys + y
                    dst = ((s2 * halves + h2) * xs + x) * ys + y
                    pairs.append((src, dst))
    return pairs


def moved(v, by, cross):
    shape = tuple(lax.axis_size(a) for a in RING)
    sections = shape[0]
    return lax.ppermute(
        v, RING, pairs_of(shape, lambda s, h: ((s + by) % sections, 1 - h if cross else h))
    )


def other_core(v):
    return lax.ppermute(v, NODE, [(0, 1), (1, 0)])


def exchange(v):
    return lax.all_to_all(v, PLANE, split_axis=0, concat_axis=0, tiled=True)


def note_of(routes, gates, width):
    note = jnp.concatenate([routes.astype(jnp.bfloat16).T, gates.T], axis=0)
    return jnp.pad(note, ((0, 16 - note.shape[0]), (0, width - note.shape[1])))


def tables(routes, gates, first, experts, rows):
    top, tokens = routes.shape
    half = tokens // 2
    labels = first + jnp.arange(experts, dtype=jnp.int32)
    match = routes[:, None, :] == labels[None, :, None]
    chosen = jnp.sum(match.astype(jnp.float32), axis=0)
    weight = jnp.sum(jnp.where(match, gates.astype(jnp.float32)[:, None, :], 0.0), axis=0)
    at = jnp.arange(tokens, dtype=jnp.int32)
    earlier = (at[:, None] < at[None, :]) & ((at[:, None] // half) == (at[None, :] // half))
    rank = jnp.dot(
        chosen.astype(jnp.bfloat16), earlier.astype(jnp.bfloat16), preferred_element_type=jnp.float32
    )
    place = jnp.where(chosen > 0, rank.astype(jnp.int32) + CAP * (at // half)[None, :], -1)
    hit = place[:, None, :] == jnp.arange(rows, dtype=jnp.int32)[None, :, None]
    send = hit.astype(jnp.bfloat16).reshape(experts * rows, tokens)
    mix = jnp.where(hit, weight[:, None, :], 0.0).astype(jnp.bfloat16).reshape(experts * rows, tokens)
    return send, mix


def dot32(a, b, dims=(((1,), (0,)), ((), ()))):
    return lax.dot_general(a, b, dims, preferred_element_type=jnp.float32)


def local(
    act_forward,
    routes_forward,
    gates_forward,
    act_backward,
    grad_backward,
    routes_backward,
    gates_backward,
    w_in,
    w_out,
):
    weight_in = w_in[0, 0]
    weight_out = w_out[0, 0]
    tok, cols = act_forward.shape
    top = routes_forward.shape[1]
    experts = lax.axis_size("x") * lax.axis_size("y")
    rows = (2 * CAP + 7) // 8 * 8
    first = lax.axis_index("zhi") * experts
    bf = jnp.bfloat16

    note_f = note_of(routes_forward, gates_forward, cols)
    note_b = note_of(routes_backward, gates_backward, cols)
    far_f = moved(jnp.concatenate([act_forward, note_f], axis=0), 0, True)
    far_a = moved(jnp.concatenate([act_backward, note_b], axis=0), 0, True)
    far_g = moved(grad_backward, 0, True)

    def both_tables(note, far):
        far_note = far[tok:]
        joined = jnp.concatenate([note[: 2 * top, :tok], far_note[: 2 * top, :tok]], axis=1)
        return tables(
            joined[:top].astype(jnp.int32), joined[top:], first, experts, rows
        )

    send_f, mix_f = both_tables(note_f, far_f)
    send_b, mix_b = both_tables(note_b, far_a)

    def pack(send, near, far):
        return dot32(send, jnp.concatenate([near, far[:tok]], axis=0)).astype(bf).reshape(
            experts, rows, cols
        )

    got_f = exchange(pack(send_f, act_forward, far_f)).reshape(-1, cols)
    got_a = exchange(pack(send_b, act_backward, far_a)).reshape(-1, cols)
    got_g = exchange(pack(send_b, grad_backward, far_g)).reshape(-1, cols)

    part = dot32(got_f, weight_in).astype(bf)
    pre = part.astype(jnp.float32) + other_core(part).astype(jnp.float32)
    hidden = jax.nn.silu(pre).astype(bf)
    out_f = dot32(hidden, weight_out).astype(bf).reshape(experts, rows, cols)
    back_f = exchange(out_f).reshape(-1, cols)

    contract = (((1,), (1,)), ((), ()))
    part_pre = dot32(got_a, weight_in).astype(bf)
    part_back = dot32(got_g, weight_out, contract).astype(bf)
    pre_b = part_pre.astype(jnp.float32) + other_core(part_pre).astype(jnp.float32)
    back_h = part_back.astype(jnp.float32) + other_core(part_back).astype(jnp.float32)
    sigma = jax.nn.sigmoid(pre_b)
    grad_hidden = (back_h * sigma * (1.0 + pre_b * (1.0 - sigma))).astype(bf)
    out_b = dot32(grad_hidden, weight_in, contract).astype(bf).reshape(experts, rows, cols)
    back_b = exchange(out_b).reshape(-1, cols)

    over_rows = (((0,), (0,)), ((), ()))
    sum_f = dot32(mix_f, back_f, over_rows).astype(bf)
    sum_b = dot32(mix_b, back_b, over_rows).astype(bf)

    def settle(total, by):
        near = moved(total[:tok], by, False)
        far = moved(total[tok:], by, True)
        return (near.astype(jnp.float32) + far.astype(jnp.float32)).astype(bf)

    return settle(sum_f, 1), settle(sum_b, -1)


def solution(mesh):
    devices = mesh.devices
    sections, nodes, locals_ = devices.shape
    fine = Mesh(devices.reshape(sections, nodes, 2, 4, locals_ // 8), ("section", "node", "zhi", "x", "y"))
    where = ("zhi", "x", "y")
    tokens = P(("section",) + where, "node")
    picks = P(("section",) + where, None)
    in_specs = (
        tokens,
        picks,
        picks,
        tokens,
        tokens,
        picks,
        picks,
        P("section", where, "node", None),
        P("section", where, None, "node"),
    )
    return jax.shard_map(
        local, mesh=fine, in_specs=in_specs, out_specs=(tokens, tokens), check_vma=False
    )
```

time: 637 us -> 292 us (0.46)
  the two profiles are of different devices: /device:TPU:102 before, /device:TPU:33 now
where the time goes in v1:
time: 292 us; the launch traced here: 291 us
  waiting for transfers between devices  166 us (57%)
  starting transfers between devices  81.5 us (28%)
  matrix products  31.3 us (11%)
  other arithmetic  9.24 us (3%)
    ppermute x7, waiting for transfers between devices, moved(): lax.ppermute(v, RING, pairs_of(shape, lambda s, h: ((s + by) % sections,...  101 us
    all_to_all x5, waiting for transfers between devices, exchange(): return lax.all_to_all(v, PLANE, split_axis=0, concat_axis=0, tiled=True)  64.8 us
    ppermute x7, starting transfers between devices, moved(): lax.ppermute(v, RING, pairs_of(shape, lambda s, h: ((s + by) % sections,...  40.6 us
    dot_general x10, matrix products, dot32(): return lax.dot_general(a, b, dims, preferred_element_type=jnp.float32)  30.8 us
    all_to_all x5, starting transfers between devices, exchange(): return lax.all_to_all(v, PLANE, split_axis=0, concat_axis=0, tiled=True)  27.4 us
    ppermute x3, starting transfers between devices, other_core(): return lax.ppermute(v, NODE, [(0, 1), (1, 0)])  13.5 us
  transfers between devices with their start and end apart: 15, of which 9 were waited for; matrix products, arithmetic and copies ran while one was open for 12% of the time, Pallas kernels for 0%

profile of v1, /device:TPU:33, one launch (start us, length us, event | category | flops | bytes accessed | tf_op | source)
XLA Modules:
  0.0 290.9 jit_solution(13354235434830706536)
XLA Ops:
  3.1 14.5 %collective-permute-start.4 = (bf16[144,1024]{1,0:T(8,128)(2,1)S(1)}, bf16[144,1024]{1,0:T(8,128)(2,1)S(1)}, u32[]{:S(2)}, u32[]{:S(2)}) collective-permute-start(bf16[144,1024]{1,0:T(8,128)(2,1)S(1)} %pad_maximum_fusion.1), channel_id=1, source_target_pairs={{0,16},{1,17},{2,18},{3,19},{4,20},{5,21},{6,22},{7,23},{8,24},{9,... | collective-permute-start | bytes 884744 | tf_op jit(solution)/shard_map/ppermute | solution.py:29
  22.1 39.0 %collective-permute-done.4 = bf16[144,1024]{1,0:T(8,128)(2,1)S(1)} collective-permute-done((bf16[144,1024]{1,0:T(8,128)(2,1)S(1)}, bf16[144,1024]{1,0:T(8,128)(2,1)S(1)}, u32[]{:S(2)}, u32[]{:S(2)}) %collective-permute-start.4) | collective-permute-done | bytes 294944 | tf_op jit(solution)/shard_map/ppermute | solution.py:29
  61.8 7.0 %collective-permute-done = bf16[144,1024]{1,0:T(8,128)(2,1)S(1)} collective-permute-done((bf16[144,1024]{1,0:T(8,128)(2,1)S(1)}, bf16[144,1024]{1,0:T(8,128)(2,1)S(1)}, u32[]{:S(2)}, u32[]{:S(2)}) %collective-permute-start) | collective-permute-done | bytes 294944 | tf_op jit(solution)/shard_map/ppermute | solution.py:29
  72.3 6.9 %all-to-all-start = ((bf16[16,56,1024]{2,1,0:T(8,128)(2,1)}), bf16[16,56,1024]{2,1,0:T(8,128)(2,1)}, u32[]{:S(2)}, u32[]{:S(2)}) async-start(bf16[16,56,1024]{2,1,0:T(8,128)(2,1)} %bitcast.3), calls=%async_computation | async-start | bytes 3670016 | tf_op jit(solution)/shard_map/all_to_all | solution.py:39
  79.3 11.7 %collective-permute-start.5 = (bf16[128,1024]{1,0:T(8,128)(2,1)S(1)}, bf16[128,1024]{1,0:T(8,128)(2,1)S(1)}, u32[]{:S(2)}, u32[]{:S(2)}) collective-permute-start(bf16[128,1024]{1,0:T(8,128)(2,1)S(1)} %copy-done.4), channel_id=1, source_target_pairs={{0,16},{1,17},{2,18},{3,19},{4,20},{5,21},{6,22},{7,23},{8,24},{9,... | collective-permute-start | bytes 786440 | tf_op jit(solution)/shard_map/ppermute | solution.py:29
  91.0 15.8 %collective-permute-done.5 = bf16[128,1024]{1,0:T(8,128)(2,1)S(1)} collective-permute-done((bf16[128,1024]{1,0:T(8,128)(2,1)S(1)}, bf16[128,1024]{1,0:T(8,128)(2,1)S(1)}, u32[]{:S(2)}, u32[]{:S(2)}) %collective-permute-start.5) | collective-permute-done | bytes 262176 | tf_op jit(solution)/shard_map/ppermute | solution.py:29
  108.6 6.8 %all-to-all-start.2 = ((bf16[16,56,1024]{2,1,0:T(8,128)(2,1)}), bf16[16,56,1024]{2,1,0:T(8,128)(2,1)}, u32[]{:S(2)}, u32[]{:S(2)}) async-start(bf16[16,56,1024]{2,1,0:T(8,128)(2,1)} %bitcast.12), calls=%async_computation.2 | async-start | bytes 3670016 | tf_op jit(solution)/shard_map/all_to_all | solution.py:39
  117.3 22.2 %all-to-all-done.2 = bf16[16,56,1024]{2,1,0:T(8,128)(2,1)} async-done(((bf16[16,56,1024]{2,1,0:T(8,128)(2,1)}), bf16[16,56,1024]{2,1,0:T(8,128)(2,1)}, u32[]{:S(2)}, u32[]{:S(2)}) %all-to-all-start.2) | async-done | bytes 1835040 | tf_op jit(solution)/shard_map/all_to_all | solution.py:39
  139.6 4.9 %all-to-all-start.3 = ((bf16[16,56,1024]{2,1,0:T(8,128)(2,1)}), bf16[16,56,1024]{2,1,0:T(8,128)(2,1)S(1)}, u32[]{:S(2)}, u32[]{:S(2)}) async-start(bf16[16,56,1024]{2,1,0:T(8,128)(2,1)} %bitcast.14), calls=%async_computation.3 | async-start | bytes 3670016 | tf_op jit(solution)/shard_map/all_to_all | solution.py:39
  144.5 4.3 %convolution_convert_fusion.7 = bf16[896,768]{1,0:T(8,128)(2,1)} fusion(bf16[896,1024]{1,0:T(8,128)(2,1)} %bitcast.4, bf16[1,1,1024,768]{3,2,1,0:T(8,128)(2,1)S(1)} %copy-done), kind=kOutput, calls=%fused_computation.9 | convolution fusion | flops 1409974272 | bytes 4784128 | tf_op jit(solution)/shard_map/dot_general | solution.py:67
  148.8 4.7 %collective-permute-start.1 = (bf16[896,768]{1,0:T(8,128)(2,1)}, bf16[896,768]{1,0:T(8,128)(2,1)}, u32[]{:S(2)}, u32[]{:S(2)}) collective-permute-start(bf16[896,768]{1,0:T(8,128)(2,1)} %convolution_convert_fusion.7), channel_id=1, source_target_pairs={{0,32},{32,0},{1,33},{33,1},{2,34},{34,2},{3,35},{35,3},{4,36},{36... | collective-permute-start | bytes 4128776 | tf_op jit(solution)/shard_map/ppermute | solution.py:35
  153.5 4.2 %convolution_convert_fusion.6 = bf16[896,768]{1,0:T(8,128)(2,1)} fusion(bf16[896,1024]{1,0:T(8,128)(2,1)} %bitcast.13, bf16[1,1,768,1024]{3,2,1,0:T(8,128)(2,1)S(1)} %copy-done.5), kind=kOutput, calls=%fused_computation.8 | convolution fusion | flops 1409974272 | bytes 4784128 | tf_op jit(solution)/shard_map/dot_general | solution.py:67
  159.7 7.5 %all-to-all-done.3 = bf16[16,56,1024]{2,1,0:T(8,128)(2,1)S(1)} async-done(((bf16[16,56,1024]{2,1,0:T(8,128)(2,1)}), bf16[16,56,1024]{2,1,0:T(8,128)(2,1)S(1)}, u32[]{:S(2)}, u32[]{:S(2)}) %all-to-all-start.3) | async-done | bytes 1835040 | tf_op jit(solution)/shard_map/all_to_all | solution.py:39
  169.9 6.9 %collective-permute-start.7 = (bf16[896,768]{1,0:T(8,128)(2,1)}, bf16[896,768]{1,0:T(8,128)(2,1)}, u32[]{:S(2)}, u32[]{:S(2)}) collective-permute-start(bf16[896,768]{1,0:T(8,128)(2,1)} %convolution_convert_fusion.5), channel_id=1, source_target_pairs={{0,32},{32,0},{1,33},{33,1},{2,34},{34,2},{3,35},{35,3},{4,36},{36... | collective-permute-start | bytes 4128776 | tf_op jit(solution)/shard_map/ppermute | solution.py:35
  176.8 4.7 %convolution_convert_fusion.3 = bf16[896,1024]{1,0:T(8,128)(2,1)} fusion(bf16[1,1,768,1024]{3,2,1,0:T(8,128)(2,1)S(1)} %copy-done.6, bf16[896,768]{1,0:T(8,128)(2,1)} %collective-permute-done.1, bf16[896,768]{1,0:T(8,128)(2,1)} %convolution_convert_fusion.7), kind=kOutput, calls=%fused_computation.5 | convolution fusion | flops 1415708672 | bytes 6160384 | tf_op jit(solution)/shard_map/dot_general | solution.py:67
  181.5 3.7 %all-to-all-start.1 = ((bf16[16,56,1024]{2,1,0:T(8,128)(2,1)}), bf16[16,56,1024]{2,1,0:T(8,128)(2,1)S(1)}, u32[]{:S(2)}, u32[]{:S(2)}) async-start(bf16[16,56,1024]{2,1,0:T(8,128)(2,1)} %bitcast.48), calls=%async_computation.1 | async-start | bytes 3670016 | tf_op jit(solution)/shard_map/all_to_all | solution.py:39
  185.3 6.2 %convolution_convert_fusion = bf16[896,1024]{1,0:T(8,128)(2,1)} fusion(bf16[1,1,1024,768]{3,2,1,0:T(8,128)(2,1)S(1)} %copy-done, bf16[896,768]{1,0:T(8,128)(2,1)} %collective-permute-done.7, bf16[896,768]{1,0:T(8,128)(2,1)} %convolution_convert_fusion.5, bf16[896,768]{1,0:T(8,128)(2,1)} %collective-permute-done.6, bf16[896,768]{1,0:T(8,128)(2,1)} %convolution_convert_fusion.6), kind=kOutput, calls=%fused_computation.2 | convolution fusion | flops 1420525568 | bytes 8912896 | tf_op jit(solution)/shard_map/dot_general | solution.py:67
  191.4 20.1 %all-to-all-done.1 = bf16[16,56,1024]{2,1,0:T(8,128)(2,1)S(1)} async-done(((bf16[16,56,1024]{2,1,0:T(8,128)(2,1)}), bf16[16,56,1024]{2,1,0:T(8,128)(2,1)S(1)}, u32[]{:S(2)}, u32[]{:S(2)}) %all-to-all-start.1) | async-done | bytes 1835040 | tf_op jit(solution)/shard_map/all_to_all | solution.py:39
  212.8 5.1 %all-to-all-start.4 = ((bf16[16,56,1024]{2,1,0:T(8,128)(2,1)}), bf16[16,56,1024]{2,1,0:T(8,128)(2,1)S(1)}, u32[]{:S(2)}, u32[]{:S(2)}) async-start(bf16[16,56,1024]{2,1,0:T(8,128)(2,1)} %bitcast.46), calls=%async_computation.4 | async-start | bytes 3670016 | tf_op jit(solution)/shard_map/all_to_all | solution.py:39
  222.8 3.1 %collective-permute-start.3 = (bf16[128,1024]{1,0:T(8,128)(2,1)}, bf16[128,1024]{1,0:T(8,128)(2,1)}, u32[]{:S(2)}, u32[]{:S(2)}) collective-permute-start(bf16[128,1024]{1,0:T(8,128)(2,1)} %get-tuple-element.11), channel_id=1, source_target_pairs={{0,80},{1,81},{2,82},{3,83},{4,84},{5,85},{6,86},{7,87},{8,88},{9,... | collective-permute-start | bytes 786440 | tf_op jit(solution)/shard_map/ppermute | solution.py:29
  225.9 15.0 %all-to-all-done.4 = bf16[16,56,1024]{2,1,0:T(8,128)(2,1)S(1)} async-done(((bf16[16,56,1024]{2,1,0:T(8,128)(2,1)}), bf16[16,56,1024]{2,1,0:T(8,128)(2,1)S(1)}, u32[]{:S(2)}, u32[]{:S(2)}) %all-to-all-start.4) | async-done | bytes 1835040 | tf_op jit(solution)/shard_map/all_to_all | solution.py:39
  243.7 5.6 %collective-permute-start.9 = (bf16[128,1024]{1,0:T(8,128)(2,1)S(1)}, bf16[128,1024]{1,0:T(8,128)(2,1)S(1)}, u32[]{:S(2)}, u32[]{:S(2)}) collective-permute-start(bf16[128,1024]{1,0:T(8,128)(2,1)S(1)} %get-tuple-element.9), channel_id=1, source_target_pairs={{0,464},{1,465},{2,466},{3,467},{4,468},{5,469},{6,470},{7,471},{8... | collective-permute-start | bytes 786440 | tf_op jit(solution)/shard_map/ppermute | solution.py:29
  249.3 21.8 %collective-permute-done.3 = bf16[128,1024]{1,0:T(8,128)(2,1)} collective-permute-done((bf16[128,1024]{1,0:T(8,128)(2,1)}, bf16[128,1024]{1,0:T(8,128)(2,1)}, u32[]{:S(2)}, u32[]{:S(2)}) %collective-permute-start.3) | collective-permute-done | bytes 262176 | tf_op jit(solution)/shard_map/ppermute | solution.py:29
  272.9 17.3 %collective-permute-done.9 = bf16[128,1024]{1,0:T(8,128)(2,1)S(1)} collective-permute-done((bf16[128,1024]{1,0:T(8,128)(2,1)S(1)}, bf16[128,1024]{1,0:T(8,128)(2,1)S(1)}, u32[]{:S(2)}, u32[]{:S(2)}) %collective-permute-start.9) | collective-permute-done | bytes 262176 | tf_op jit(solution)/shard_map/ppermute | solution.py:29
  (55 shorter events, 31.0 us)
Async XLA Ops:
  0.6 143.9 %copy-start = (bf16[1,1,1024,768]{3,2,1,0:T(8,128)(2,1)S(1)}, bf16[1,1,1024,768]{3,2,1,0:T(8,128)(2,1)}, u32[]{:S(2)}) copy-start(bf16[1,1,1024,768]{3,2,1,0:T(8,128)(2,1)} %param.16) | copy-start | bytes 4718596
  0.6 69.8 %copy-start.2 = (bf16[128,1024]{1,0:T(8,128)(2,1)S(1)}, bf16[128,1024]{1,0:T(8,128)(2,1)}, u32[]{:S(2)}) copy-start(bf16[128,1024]{1,0:T(8,128)(2,1)} %param.9) | copy-start | bytes 786436
  3.1 58.0 %collective-permute-start.4 = (bf16[144,1024]{1,0:T(8,128)(2,1)S(1)}, bf16[144,1024]{1,0:T(8,128)(2,1)S(1)}, u32[]{:S(2)}, u32[]{:S(2)}) collective-permute-start(bf16[144,1024]{1,0:T(8,128)(2,1)S(1)} %pad_maximum_fusion.1), channel_id=1, source_target_pairs={{0,16},{1,17},{2,18},{3,19},{4,20},{5,21},{6,22},{7,23},{8,24},{9,... | collective-permute-start | bytes 884744 | tf_op jit(solution)/shard_map/ppermute | solution.py:29
  20.1 48.7 %collective-permute-start = (bf16[144,1024]{1,0:T(8,128)(2,1)S(1)}, bf16[144,1024]{1,0:T(8,128)(2,1)S(1)}, u32[]{:S(2)}, u32[]{:S(2)}) collective-permute-start(bf16[144,1024]{1,0:T(8,128)(2,1)S(1)} %pad_maximum_fusion), channel_id=1, source_target_pairs={{0,16},{1,17},{2,18},{3,19},{4,20},{5,21},{6,22},{7,23},{8,24},{9,... | collective-permute-start | bytes 884744 | tf_op jit(solution)/shard_map/ppermute | solution.py:29
  72.3 6.9 %copy-start.4 = (bf16[128,1024]{1,0:T(8,128)(2,1)S(1)}, bf16[128,1024]{1,0:T(8,128)(2,1)}, u32[]{:S(2)}) copy-start(bf16[128,1024]{1,0:T(8,128)(2,1)} %param.13) | copy-start | bytes 786436
  72.3 36.3 %all-to-all-start = ((bf16[16,56,1024]{2,1,0:T(8,128)(2,1)}), bf16[16,56,1024]{2,1,0:T(8,128)(2,1)}, u32[]{:S(2)}, u32[]{:S(2)}) async-start(bf16[16,56,1024]{2,1,0:T(8,128)(2,1)} %bitcast.3), calls=%async_computation | async-start | bytes 3670016 | tf_op jit(solution)/shard_map/all_to_all | solution.py:39
  79.3 27.4 %collective-permute-start.5 = (bf16[128,1024]{1,0:T(8,128)(2,1)S(1)}, bf16[128,1024]{1,0:T(8,128)(2,1)S(1)}, u32[]{:S(2)}, u32[]{:S(2)}) collective-permute-start(bf16[128,1024]{1,0:T(8,128)(2,1)S(1)} %copy-done.4), channel_id=1, source_target_pairs={{0,16},{1,17},{2,18},{3,19},{4,20},{5,21},{6,22},{7,23},{8,24},{9,... | collective-permute-start | bytes 786440 | tf_op jit(solution)/shard_map/ppermute | solution.py:29
  108.6 6.8 %copy-start.3 = (bf16[128,1024]{1,0:T(8,128)(2,1)S(1)}, bf16[128,1024]{1,0:T(8,128)(2,1)}, u32[]{:S(2)}) copy-start(bf16[128,1024]{1,0:T(8,128)(2,1)} %param.12) | copy-start | bytes 786436
  108.6 30.9 %all-to-all-start.2 = ((bf16[16,56,1024]{2,1,0:T(8,128)(2,1)}), bf16[16,56,1024]{2,1,0:T(8,128)(2,1)}, u32[]{:S(2)}, u32[]{:S(2)}) async-start(bf16[16,56,1024]{2,1,0:T(8,128)(2,1)} %bitcast.12), calls=%async_computation.2 | async-start | bytes 3670016 | tf_op jit(solution)/shard_map/all_to_all | solution.py:39
  139.6 27.6 %all-to-all-start.3 = ((bf16[16,56,1024]{2,1,0:T(8,128)(2,1)}), bf16[16,56,1024]{2,1,0:T(8,128)(2,1)S(1)}, u32[]{:S(2)}, u32[]{:S(2)}) async-start(bf16[16,56,1024]{2,1,0:T(8,128)(2,1)} %bitcast.14), calls=%async_computation.3 | async-start | bytes 3670016 | tf_op jit(solution)/shard_map/all_to_all | solution.py:39
  144.5 9.0 %copy-start.5 = (bf16[1,1,768,1024]{3,2,1,0:T(8,128)(2,1)S(1)}, bf16[1,1,768,1024]{3,2,1,0:T(8,128)(2,1)}, u32[]{:S(2)}) copy-start(bf16[1,1,768,1024]{3,2,1,0:T(8,128)(2,1)} %param.17) | copy-start | bytes 4718596
  148.8 28.0 %collective-permute-start.1 = (bf16[896,768]{1,0:T(8,128)(2,1)}, bf16[896,768]{1,0:T(8,128)(2,1)}, u32[]{:S(2)}, u32[]{:S(2)}) collective-permute-start(bf16[896,768]{1,0:T(8,128)(2,1)} %convolution_convert_fusion.7), channel_id=1, source_target_pairs={{0,32},{32,0},{1,33},{33,1},{2,34},{34,2},{3,35},{35,3},{4,36},{36... | collective-permute-start | bytes 4128776 | tf_op jit(solution)/shard_map/ppermute | solution.py:35
  157.7 27.5 %collective-permute-start.6 = (bf16[896,768]{1,0:T(8,128)(2,1)}, bf16[896,768]{1,0:T(8,128)(2,1)}, u32[]{:S(2)}, u32[]{:S(2)}) collective-permute-start(bf16[896,768]{1,0:T(8,128)(2,1)} %convolution_convert_fusion.6), channel_id=1, source_target_pairs={{0,32},{32,0},{1,33},{33,1},{2,34},{34,2},{3,35},{35,3},{4,36},{36... | collective-permute-start | bytes 4128776 | tf_op jit(solution)/shard_map/ppermute | solution.py:35
  167.1 9.7 %copy-start.6 = (bf16[1,1,768,1024]{3,2,1,0:T(8,128)(2,1)S(1)}, bf16[1,1,768,1024]{3,2,1,0:T(8,128)(2,1)}, u32[]{:S(2)}) copy-start(bf16[1,1,768,1024]{3,2,1,0:T(8,128)(2,1)} %param.17) | copy-start | bytes 4718596
  169.9 15.4 %collective-permute-start.7 = (bf16[896,768]{1,0:T(8,128)(2,1)}, bf16[896,768]{1,0:T(8,128)(2,1)}, u32[]{:S(2)}, u32[]{:S(2)}) collective-permute-start(bf16[896,768]{1,0:T(8,128)(2,1)} %convolution_convert_fusion.5), channel_id=1, source_target_pairs={{0,32},{32,0},{1,33},{33,1},{2,34},{34,2},{3,35},{35,3},{4,36},{36... | collective-permute-start | bytes 4128776 | tf_op jit(solution)/shard_map/ppermute | solution.py:35
  181.5 30.0 %all-to-all-start.1 = ((bf16[16,56,1024]{2,1,0:T(8,128)(2,1)}), bf16[16,56,1024]{2,1,0:T(8,128)(2,1)S(1)}, u32[]{:S(2)}, u32[]{:S(2)}) async-start(bf16[16,56,1024]{2,1,0:T(8,128)(2,1)} %bitcast.48), calls=%async_computation.1 | async-start | bytes 3670016 | tf_op jit(solution)/shard_map/all_to_all | solution.py:39
  211.5 1.2 copy-start.1
  212.8 28.2 %all-to-all-start.4 = ((bf16[16,56,1024]{2,1,0:T(8,128)(2,1)}), bf16[16,56,1024]{2,1,0:T(8,128)(2,1)S(1)}, u32[]{:S(2)}, u32[]{:S(2)}) async-start(bf16[16,56,1024]{2,1,0:T(8,128)(2,1)} %bitcast.46), calls=%async_computation.4 | async-start | bytes 3670016 | tf_op jit(solution)/shard_map/all_to_all | solution.py:39
  220.9 28.4 %collective-permute-start.2 = (bf16[128,1024]{1,0:T(8,128)(2,1)}, bf16[128,1024]{1,0:T(8,128)(2,1)}, u32[]{:S(2)}, u32[]{:S(2)}) collective-permute-start(bf16[128,1024]{1,0:T(8,128)(2,1)} %get-tuple-element.10), channel_id=1, source_target_pairs={{0,64},{1,65},{2,66},{3,67},{4,68},{5,69},{6,70},{7,71},{8,72},{9,... | collective-permute-start | bytes 786440 | tf_op jit(solution)/shard_map/ppermute | solution.py:29
  222.8 48.2 %collective-permute-start.3 = (bf16[128,1024]{1,0:T(8,128)(2,1)}, bf16[128,1024]{1,0:T(8,128)(2,1)}, u32[]{:S(2)}, u32[]{:S(2)}) collective-permute-start(bf16[128,1024]{1,0:T(8,128)(2,1)} %get-tuple-element.11), channel_id=1, source_target_pairs={{0,80},{1,81},{2,82},{3,83},{4,84},{5,85},{6,86},{7,87},{8,88},{9,... | collective-permute-start | bytes 786440 | tf_op jit(solution)/shard_map/ppermute | solution.py:29
  241.7 31.1 %collective-permute-start.8 = (bf16[128,1024]{1,0:T(8,128)(2,1)S(1)}, bf16[128,1024]{1,0:T(8,128)(2,1)S(1)}, u32[]{:S(2)}, u32[]{:S(2)}) collective-permute-start(bf16[128,1024]{1,0:T(8,128)(2,1)S(1)} %get-tuple-element.8), channel_id=1, source_target_pairs={{0,448},{1,449},{2,450},{3,451},{4,452},{5,453},{6,454},{7,455},{8... | collective-permute-start | bytes 786440 | tf_op jit(solution)/shard_map/ppermute | solution.py:29
  243.7 46.5 %collective-permute-start.9 = (bf16[128,1024]{1,0:T(8,128)(2,1)S(1)}, bf16[128,1024]{1,0:T(8,128)(2,1)S(1)}, u32[]{:S(2)}, u32[]{:S(2)}) collective-permute-start(bf16[128,1024]{1,0:T(8,128)(2,1)S(1)} %get-tuple-element.9), channel_id=1, source_target_pairs={{0,464},{1,465},{2,466},{3,467},{4,468},{5,469},{6,470},{7,471},{8... | collective-permute-start | bytes 786440 | tf_op jit(solution)/shard_map/ppermute | solution.py:29

commit v2 on v1

v2 whole, which is shorter than its diff:
```python
import jax
import jax.numpy as jnp
from jax import lax
from jax.sharding import Mesh, PartitionSpec as P

CAP = 25
NODE = "node"
PLANE = ("x", "y")
RING = ("section", "zhi", "x", "y")


def pairs_of(shape, move):
    sections, halves, xs, ys = shape
    pairs = []
    for s in range(sections):
        for h in range(halves):
            for x in range(xs):
                for y in range(ys):
                    s2, h2 = move(s, h)
                    src = ((s * halves + h) * xs + x) * ys + y
                    dst = ((s2 * halves + h2) * xs + x) * ys + y
                    pairs.append((src, dst))
    return pairs


def moved(v, by, cross):
    shape = tuple(lax.axis_size(a) for a in RING)
    sections = shape[0]
    return lax.ppermute(
        v, RING, pairs_of(shape, lambda s, h: ((s + by) % sections, 1 - h if cross else h))
    )


def other_core(v):
    return lax.ppermute(v, NODE, [(0, 1), (1, 0)])


def exchange(v):
    return lax.all_to_all(v, PLANE, split_axis=0, concat_axis=0, tiled=True)


def note_of(routes, gates):
    note = jnp.concatenate([routes.astype(jnp.bfloat16).T, gates.T], axis=0)
    return jnp.pad(note, ((0, 16 - note.shape[0]), (0, 0)))


def places(note, top, first, experts):
    tokens = note.shape[1]
    routes = note[:top].astype(jnp.int32)
    gates = note[top : 2 * top].astype(jnp.float32)
    labels = first + jnp.arange(experts, dtype=jnp.int32)
    match = routes[:, None, :] == labels[None, :, None]
    chosen = jnp.sum(match.astype(jnp.float32), axis=0)
    weight = jnp.sum(jnp.where(match, gates[:, None, :], 0.0), axis=0)
    at = jnp.arange(tokens, dtype=jnp.int32)
    earlier = (at[:, None] < at[None, :]).astype(jnp.bfloat16)
    rank = jnp.dot(chosen.astype(jnp.bfloat16), earlier, preferred_element_type=jnp.float32)
    return jnp.where(chosen > 0, rank.astype(jnp.int32), -1), weight


def offset(place, by):
    return jnp.where(place >= 0, place + by, -1)


def hits(place, rows):
    return place[:, None, :] == jnp.arange(rows, dtype=jnp.int32)[None, :, None]


def pack(place, rows, tokens):
    experts = place.shape[0]
    send = hits(place, rows).astype(jnp.bfloat16).reshape(experts * rows, -1)
    return dot32(send, tokens).astype(jnp.bfloat16).reshape(experts, rows, -1)


def combine(place, weight, got):
    experts, rows, cols = got.shape
    mix = jnp.where(hits(place, rows), weight[:, None, :], 0.0).astype(jnp.bfloat16)
    over_rows = (((0,), (0,)), ((), ()))
    return dot32(mix.reshape(experts * rows, -1), got.reshape(-1, cols), over_rows).astype(
        jnp.bfloat16
    )


def after(value, *done):
    return lax.optimization_barrier((value,) + done)[0]


def dot32(a, b, dims=(((1,), (0,)), ((), ()))):
    return lax.dot_general(a, b, dims, preferred_element_type=jnp.float32)


def local(
    act_forward,
    routes_forward,
    gates_forward,
    act_backward,
    grad_backward,
    routes_backward,
    gates_backward,
    w_in,
    w_out,
):
    weight_in = w_in[0, 0]
    weight_out = w_out[0, 0]
    tok, cols = act_forward.shape
    top = routes_forward.shape[1]
    experts = lax.axis_size("x") * lax.axis_size("y")
    first = lax.axis_index("zhi") * experts
    bf = jnp.bfloat16
    contract = (((1,), (1,)), ((), ()))

    note_f = note_of(routes_forward, gates_forward)
    note_b = note_of(routes_backward, gates_backward)
    notes = jnp.concatenate([note_b, note_f], axis=1)
    both = jnp.concatenate([act_backward, grad_backward], axis=1)
    notes_wide = jnp.pad(notes, ((0, 0), (0, 2 * cols - notes.shape[1])))
    far_b = moved(jnp.concatenate([both, notes_wide], axis=0), 0, True)
    far_f = moved(after(act_forward, far_b), 0, True)

    place_f, weight_f = places(note_f, top, first, experts)
    place_b, weight_b = places(note_b, top, first, experts)
    own_rows = jnp.concatenate([act_forward, act_backward, grad_backward], axis=0)
    own_places = jnp.concatenate(
        [place_f, offset(place_b, CAP), offset(place_b, 2 * CAP)], axis=1
    )
    got_own = exchange(pack(own_places, (3 * CAP + 7) // 8 * 8, own_rows))

    far_place_b, far_weight_b = places(far_b[tok:, :tok], top, first, experts)
    far_place_f, far_weight_f = places(far_b[tok:, tok : 2 * tok], top, first, experts)
    padded = (CAP + 7) // 8 * 8
    got_far_b = exchange(after(pack(far_place_b, padded, far_b[:tok]), got_own))
    got_far_f = exchange(after(pack(far_place_f, padded, far_f), got_far_b))

    def added(part):
        part = part.astype(bf)
        return part.astype(jnp.float32) + other_core(part).astype(jnp.float32)

    def forward(pre):
        return dot32(jax.nn.silu(pre).astype(bf), weight_out).astype(bf)

    def backward(pre, back_h):
        sigma = jax.nn.sigmoid(pre)
        slope = (back_h * sigma * (1.0 + pre * (1.0 - sigma))).astype(bf)
        return dot32(slope, weight_in, contract).astype(bf)

    cut = experts * CAP
    own_fa = jnp.concatenate([got_own[:, :CAP], got_own[:, CAP : 2 * CAP]], axis=0)
    own_pre = added(dot32(own_fa.reshape(-1, cols), weight_in))
    own_back = added(
        dot32(got_own[:, 2 * CAP : 3 * CAP].reshape(-1, cols), weight_out, contract)
    )
    own_out_f = forward(own_pre[:cut]).reshape(experts, CAP, cols)
    own_out_b = backward(own_pre[cut:], own_back).reshape(experts, CAP, cols)

    rows_b = got_far_b.reshape(-1, 2 * cols)
    far_pre = added(dot32(rows_b[:, :cols], weight_in))
    far_back = added(dot32(rows_b[:, cols:], weight_out, contract))
    far_out_b = backward(far_pre, far_back).reshape(experts, padded, cols)
    far_out_f = forward(added(dot32(got_far_f.reshape(-1, cols), weight_in))).reshape(
        experts, padded, cols
    )

    def returned(far, own, *done):
        joined = jnp.concatenate([far[:, :CAP], own], axis=1)
        joined = jnp.pad(joined, ((0, 0), (0, (2 * CAP + 7) // 8 * 8 - 2 * CAP), (0, 0)))
        return exchange(after(joined, *done))

    back_b = returned(far_out_b, own_out_b, got_far_f)
    back_f = returned(far_out_f, own_out_f, back_b)

    def settle(back, far_place, far_weight, place, weight, by):
        both_places = jnp.concatenate([far_place, offset(place, CAP)], axis=1)
        total = combine(both_places, jnp.concatenate([far_weight, weight], axis=1), back)
        far = moved(total[:tok], by, True)
        near = moved(total[tok:], by, False)
        return (near.astype(jnp.float32) + far.astype(jnp.float32)).astype(bf)

    return (
        settle(back_f, far_place_f, far_weight_f, place_f, weight_f, 1),
        settle(back_b, far_place_b, far_weight_b, place_b, weight_b, -1),
    )


def solution(mesh):
    devices = mesh.devices
    sections, nodes, locals_ = devices.shape
    fine = Mesh(devices.reshape(sections, nodes, 2, 4, locals_ // 8), ("section", "node", "zhi", "x", "y"))
    where = ("zhi", "x", "y")
    tokens = P(("section",) + where, "node")
    picks = P(("section",) + where, None)
    in_specs = (
        tokens,
        picks,
        picks,
        tokens,
        tokens,
        picks,
        picks,
        P("section", where, "node", None),
        P("section", where, None, "node"),
    )
    return jax.shard_map(
        local, mesh=fine, in_specs=in_specs, out_specs=(tokens, tokens), check_vma=False
    )
```

time: 292 us -> 301 us (1.031)
  the two profiles are of different devices: /device:TPU:33 before, /device:TPU:32 now
where the time goes in v2:
time: 301 us; the launch traced here: 300 us
  waiting for transfers between devices  152 us (50%)
  starting transfers between devices  86 us (29%)
  matrix products  37.7 us (13%)
  other arithmetic  14.6 us (5%)
  local copies, waits for them, and re-layouts  8.91 us (3%)
    ppermute x6, waiting for transfers between devices, moved(): lax.ppermute(v, RING, pairs_of(shape, lambda s, h: ((s + by) % sections,...  88.4 us
    all_to_all x5, waiting for transfers between devices, exchange(): return lax.all_to_all(v, PLANE, split_axis=0, concat_axis=0, tiled=True)  63.1 us
    ppermute x6, starting transfers between devices, moved(): lax.ppermute(v, RING, pairs_of(shape, lambda s, h: ((s + by) % sections,...  48.5 us
    dot_general x14, matrix products, dot32(): return lax.dot_general(a, b, dims, preferred_element_type=jnp.float32)  37.1 us
    all_to_all x5, starting transfers between devices, exchange(): return lax.all_to_all(v, PLANE, split_axis=0, concat_axis=0, tiled=True)  26.9 us
    ppermute x5, starting transfers between devices, other_core(): return lax.ppermute(v, NODE, [(0, 1), (1, 0)])  10.5 us
  transfers between devices with their start and end apart: 16, of which 7 were waited for; matrix products, arithmetic and copies ran while one was open for 17% of the time, Pallas kernels for 0%

profile of v2, /device:TPU:32, one launch (start us, length us, event | category | flops | bytes accessed | tf_op | source)
XLA Modules:
  0.0 299.8 jit_solution(7735790538337300704)
XLA Ops:
  4.0 14.8 %collective-permute-start = (bf16[144,2048]{1,0:T(8,128)(2,1)S(1)}, bf16[144,2048]{1,0:T(8,128)(2,1)S(1)}, u32[]{:S(2)}, u32[]{:S(2)}) collective-permute-start(bf16[144,2048]{1,0:T(8,128)(2,1)S(1)} %pad_maximum_fusion.1), channel_id=1, source_target_pairs={{0,16},{1,17},{2,18},{3,19},{4,20},{5,21},{6,22},{7,23},{8,24},{9,... | collective-permute-start | bytes 1769480 | tf_op jit(solution)/shard_map/ppermute | solution.py:29
  19.6 50.7 %collective-permute-done = bf16[144,2048]{1,0:T(8,128)(2,1)S(1)} collective-permute-done((bf16[144,2048]{1,0:T(8,128)(2,1)S(1)}, bf16[144,2048]{1,0:T(8,128)(2,1)S(1)}, u32[]{:S(2)}, u32[]{:S(2)}) %collective-permute-start) | collective-permute-done | bytes 589856 | tf_op jit(solution)/shard_map/ppermute | solution.py:29
  71.1 4.0 %convolution_convert_fusion = bf16[1280,1024]{1,0:T(8,128)(2,1)} fusion(pred[1280,384]{1,0:T(32,128)(4,1)S(1)} %bitcast_compare_fusion, bf16[128,1024]{1,0:T(8,128)(2,1)S(1)} %copy-done.3, bf16[128,1024]{1,0:T(8,128)(2,1)S(1)} %copy-done.4, bf16[128,1024]{1,0:T(8,128)(2,1)} %param.9), kind=kOutput, calls=%fused_computation | convolution fusion | flops 1010302976 | bytes 3899392 | tf_op jit(solution)/shard_map/dot_general | solution.py:89
  75.1 7.1 %all-to-all-start = ((bf16[16,80,1024]{2,1,0:T(8,128)(2,1)}), bf16[16,80,1024]{2,1,0:T(8,128)(2,1)}, u32[]{:S(2)}, u32[]{:S(2)}) async-start(bf16[16,80,1024]{2,1,0:T(8,128)(2,1)} %bitcast.81), calls=%async_computation | async-start | bytes 5242880 | tf_op jit(solution)/shard_map/all_to_all | solution.py:39
  84.7 33.2 %all-to-all-done = bf16[16,80,1024]{2,1,0:T(8,128)(2,1)} async-done(((bf16[16,80,1024]{2,1,0:T(8,128)(2,1)}), bf16[16,80,1024]{2,1,0:T(8,128)(2,1)}, u32[]{:S(2)}, u32[]{:S(2)}) %all-to-all-start) | async-done | bytes 2621472 | tf_op jit(solution)/shard_map/all_to_all | solution.py:39
  117.9 4.6 %all-to-all-start.1 = ((bf16[16,32,2048]{2,1,0:T(8,128)(2,1)}), bf16[16,32,2048]{2,1,0:T(8,128)(2,1)}, u32[]{:S(2)}, u32[]{:S(2)}) async-start(bf16[16,32,2048]{2,1,0:T(8,128)(2,1)} %bitcast.80), calls=%async_computation.1 | async-start | bytes 4194304 | tf_op jit(solution)/shard_map/all_to_all | solution.py:39
  122.5 11.9 %collective-permute-start.1 = (bf16[128,1024]{1,0:T(8,128)(2,1)S(1)}, bf16[128,1024]{1,0:T(8,128)(2,1)S(1)}, u32[]{:S(2)}, u32[]{:S(2)}) collective-permute-start(bf16[128,1024]{1,0:T(8,128)(2,1)S(1)} %copy-done.6), channel_id=1, source_target_pairs={{0,16},{1,17},{2,18},{3,19},{4,20},{5,21},{6,22},{7,23},{8,24},{9,... | collective-permute-start | bytes 786440 | tf_op jit(solution)/shard_map/ppermute | solution.py:29
  141.6 3.9 %fusion.24 = bf16[800,768]{1,0:T(8,128)(2,1)} fusion(bf16[800,1024]{1,0:T(8,128)(2,1)} %reshape.74, bf16[1,1,1024,768]{3,2,1,0:T(8,128)(2,1)S(1)} %copy-done), kind=kOutput, calls=%fused_computation.32 | convolution fusion | flops 1258905600 | bytes 4440064 | tf_op jit(solution)/shard_map/dot_general | solution.py:89
  153.8 3.6 %fusion.45 = bf16[512,768]{1,0:T(8,128)(2,1)} fusion(bf16[1,1,768,1024]{3,2,1,0:T(8,128)(2,1)} %param.17, bf16[512,2048]{1,0:T(8,128)(2,1)} %bitcast.14), kind=kOutput, calls=%fused_computation.40 | convolution fusion | flops 805699584 | bytes 3407872 | tf_op jit(solution)/shard_map/dot_general | solution.py:89
  159.4 3.1 %fusion.42 = bf16[512,768]{1,0:T(8,128)(2,1)} fusion(bf16[1,1,1024,768]{3,2,1,0:T(8,128)(2,1)S(1)} %copy-done, bf16[512,2048]{1,0:T(8,128)(2,1)} %bitcast.14), kind=kOutput, calls=%fused_computation.39 | convolution fusion | flops 805699584 | bytes 3407872 | tf_op jit(solution)/shard_map/dot_general | solution.py:89
  164.9 3.3 %convert_add_fusion = f32[800,768]{1,0:T(8,128)} fusion(bf16[800,768]{1,0:T(8,128)(2,1)} %collective-permute-done.3, bf16[800,768]{1,0:T(8,128)(2,1)} %fusion.24), kind=kLoop, calls=%fused_computation.7 | loop fusion | flops 1843200 | bytes 4915200 | tf_op jit(solution)/shard_map/add | solution.py:136
  168.2 7.1 %all-to-all-start.2 = ((bf16[16,32,1024]{2,1,0:T(8,128)(2,1)}), bf16[16,32,1024]{2,1,0:T(8,128)(2,1)}, u32[]{:S(2)}, u32[]{:S(2)}) async-start(bf16[16,32,1024]{2,1,0:T(8,128)(2,1)} %bitcast.5), calls=%async_computation.2 | async-start | bytes 2097152 | tf_op jit(solution)/shard_map/all_to_all | solution.py:39
  178.2 3.3 %fusion.27 = bf16[512,1024]{1,0:T(8,128)(2,1)S(1)} fusion(bf16[1,1,1024,768]{3,2,1,0:T(8,128)(2,1)S(1)} %copy-done, bf16[512,768]{1,0:T(8,128)(2,1)} %collective-permute-done.5, bf16[512,768]{1,0:T(8,128)(2,1)} %fusion.42, bf16[512,768]{1,0:T(8,128)(2,1)} %collective-permute-done.4, bf16[512,768]{1,0:T(8,128)(2,1)} %fusion.45), kind=kOutput, calls=%fused_computation.33 | convolution fusion | flops 811728896 | bytes 5767168 | tf_op jit(solution)/shard_map/dot_general | solution.py:89
  183.2 10.2 %all-to-all-done.2 = bf16[16,32,1024]{2,1,0:T(8,128)(2,1)} async-done(((bf16[16,32,1024]{2,1,0:T(8,128)(2,1)}), bf16[16,32,1024]{2,1,0:T(8,128)(2,1)}, u32[]{:S(2)}, u32[]{:S(2)}) %all-to-all-start.2) | async-done | bytes 1048608 | tf_op jit(solution)/shard_map/all_to_all | solution.py:39
  193.4 3.7 %all-to-all-start.3 = ((bf16[16,56,1024]{2,1,0:T(8,128)(2,1)}), bf16[16,56,1024]{2,1,0:T(8,128)(2,1)S(1)}, u32[]{:S(2)}, u32[]{:S(2)}) async-start(bf16[16,56,1024]{2,1,0:T(8,128)(2,1)} %fusion.5), calls=%async_computation.3 | async-start | bytes 3670016 | tf_op jit(solution)/shard_map/all_to_all | solution.py:39
  197.2 3.3 %fusion.39 = bf16[512,768]{1,0:T(8,128)(2,1)} fusion(bf16[512,1024]{1,0:T(8,128)(2,1)} %bitcast.10, bf16[1,1,1024,768]{3,2,1,0:T(8,128)(2,1)S(1)} %copy-done), kind=kOutput, calls=%fused_computation.38 | convolution fusion | flops 805699584 | bytes 3407872 | tf_op jit(solution)/shard_map/dot_general | solution.py:89
  206.5 3.0 %fusion.30 = bf16[512,1024]{1,0:T(8,128)(2,1)S(1)} fusion(bf16[1,1,768,1024]{3,2,1,0:T(8,128)(2,1)} %param.17, bf16[512,768]{1,0:T(8,128)(2,1)} %collective-permute-done.2, bf16[512,768]{1,0:T(8,128)(2,1)} %fusion.39), kind=kOutput, calls=%fused_computation.34 | convolution fusion | flops 808976384 | bytes 4194304 | tf_op jit(solution)/shard_map/dot_general | solution.py:89
  211.3 10.8 %all-to-all-done.3 = bf16[16,56,1024]{2,1,0:T(8,128)(2,1)S(1)} async-done(((bf16[16,56,1024]{2,1,0:T(8,128)(2,1)}), bf16[16,56,1024]{2,1,0:T(8,128)(2,1)S(1)}, u32[]{:S(2)}, u32[]{:S(2)}) %all-to-all-start.3) | async-done | bytes 1835040 | tf_op jit(solution)/shard_map/all_to_all | solution.py:39
  222.2 4.4 %all-to-all-start.4 = ((bf16[16,56,1024]{2,1,0:T(8,128)(2,1)}), bf16[16,56,1024]{2,1,0:T(8,128)(2,1)}, u32[]{:S(2)}, u32[]{:S(2)}) async-start(bf16[16,56,1024]{2,1,0:T(8,128)(2,1)} %fusion.4), calls=%async_computation.4 | async-start | bytes 3670016 | tf_op jit(solution)/shard_map/all_to_all | solution.py:39
  229.4 12.3 %collective-permute-start.10 = (bf16[128,1024]{1,0:T(8,128)(2,1)S(1)}, bf16[128,1024]{1,0:T(8,128)(2,1)S(1)}, u32[]{:S(2)}, u32[]{:S(2)}) collective-permute-start(bf16[128,1024]{1,0:T(8,128)(2,1)S(1)} %get-tuple-element.38), channel_id=1, source_target_pairs={{0,464},{1,465},{2,466},{3,467},{4,468},{5,469},{6,470},{7,471},{8... | collective-permute-start | bytes 786440 | tf_op jit(solution)/shard_map/ppermute | solution.py:29
  241.7 8.9 %all-to-all-done.4 = bf16[16,56,1024]{2,1,0:T(8,128)(2,1)} async-done(((bf16[16,56,1024]{2,1,0:T(8,128)(2,1)}), bf16[16,56,1024]{2,1,0:T(8,128)(2,1)}, u32[]{:S(2)}, u32[]{:S(2)}) %all-to-all-start.4) | async-done | bytes 1835040 | tf_op jit(solution)/shard_map/all_to_all | solution.py:39
  254.7 5.7 %collective-permute-start.8 = (bf16[128,1024]{1,0:T(8,128)(2,1)S(1)}, bf16[128,1024]{1,0:T(8,128)(2,1)S(1)}, u32[]{:S(2)}, u32[]{:S(2)}) collective-permute-start(bf16[128,1024]{1,0:T(8,128)(2,1)S(1)} %get-tuple-element.40), channel_id=1, source_target_pairs={{0,80},{1,81},{2,82},{3,83},{4,84},{5,85},{6,86},{7,87},{8,88},{9,... | collective-permute-start | bytes 786440 | tf_op jit(solution)/shard_map/ppermute | solution.py:29
  260.5 15.6 %collective-permute-done.10 = bf16[128,1024]{1,0:T(8,128)(2,1)S(1)} collective-permute-done((bf16[128,1024]{1,0:T(8,128)(2,1)S(1)}, bf16[128,1024]{1,0:T(8,128)(2,1)S(1)}, u32[]{:S(2)}, u32[]{:S(2)}) %collective-permute-start.10) | collective-permute-done | bytes 262176 | tf_op jit(solution)/shard_map/ppermute | solution.py:29
  276.9 22.1 %collective-permute-done.8 = bf16[128,1024]{1,0:T(8,128)(2,1)S(1)} collective-permute-done((bf16[128,1024]{1,0:T(8,128)(2,1)S(1)}, bf16[128,1024]{1,0:T(8,128)(2,1)S(1)}, u32[]{:S(2)}, u32[]{:S(2)}) %collective-permute-start.8) | collective-permute-done | bytes 262176 | tf_op jit(solution)/shard_map/ppermute | solution.py:29
  (73 shorter events, 48.0 us)
Async XLA Ops:
  0.6 141.0 %copy-start = (bf16[1,1,1024,768]{3,2,1,0:T(8,128)(2,1)S(1)}, bf16[1,1,1024,768]{3,2,1,0:T(8,128)(2,1)}, u32[]{:S(2)}) copy-start(bf16[1,1,1024,768]{3,2,1,0:T(8,128)(2,1)} %param.16) | copy-start | bytes 4718596
  0.6 70.4 %copy-start.3 = (bf16[128,1024]{1,0:T(8,128)(2,1)S(1)}, bf16[128,1024]{1,0:T(8,128)(2,1)}, u32[]{:S(2)}) copy-start(bf16[128,1024]{1,0:T(8,128)(2,1)} %param.13) | copy-start | bytes 786436
  0.7 70.4 %copy-start.4 = (bf16[128,1024]{1,0:T(8,128)(2,1)S(1)}, bf16[128,1024]{1,0:T(8,128)(2,1)}, u32[]{:S(2)}) copy-start(bf16[128,1024]{1,0:T(8,128)(2,1)} %param.12) | copy-start | bytes 786436
  4.0 66.3 %collective-permute-start = (bf16[144,2048]{1,0:T(8,128)(2,1)S(1)}, bf16[144,2048]{1,0:T(8,128)(2,1)S(1)}, u32[]{:S(2)}, u32[]{:S(2)}) collective-permute-start(bf16[144,2048]{1,0:T(8,128)(2,1)S(1)} %pad_maximum_fusion.1), channel_id=1, source_target_pairs={{0,16},{1,17},{2,18},{3,19},{4,20},{5,21},{6,22},{7,23},{8,24},{9,... | collective-permute-start | bytes 1769480 | tf_op jit(solution)/shard_map/ppermute | solution.py:29
  75.1 42.8 %all-to-all-start = ((bf16[16,80,1024]{2,1,0:T(8,128)(2,1)}), bf16[16,80,1024]{2,1,0:T(8,128)(2,1)}, u32[]{:S(2)}, u32[]{:S(2)}) async-start(bf16[16,80,1024]{2,1,0:T(8,128)(2,1)} %bitcast.81), calls=%async_computation | async-start | bytes 5242880 | tf_op jit(solution)/shard_map/all_to_all | solution.py:39
  117.9 4.6 %copy-start.6 = (bf16[128,1024]{1,0:T(8,128)(2,1)S(1)}, bf16[128,1024]{1,0:T(8,128)(2,1)}, u32[]{:S(2)}) copy-start(bf16[128,1024]{1,0:T(8,128)(2,1)} %param.9) | copy-start | bytes 786436
  117.9 35.9 %all-to-all-start.1 = ((bf16[16,32,2048]{2,1,0:T(8,128)(2,1)}), bf16[16,32,2048]{2,1,0:T(8,128)(2,1)}, u32[]{:S(2)}, u32[]{:S(2)}) async-start(bf16[16,32,2048]{2,1,0:T(8,128)(2,1)} %bitcast.80), calls=%async_computation.1 | async-start | bytes 4194304 | tf_op jit(solution)/shard_map/all_to_all | solution.py:39
  122.5 25.0 %collective-permute-start.1 = (bf16[128,1024]{1,0:T(8,128)(2,1)S(1)}, bf16[128,1024]{1,0:T(8,128)(2,1)S(1)}, u32[]{:S(2)}, u32[]{:S(2)}) collective-permute-start(bf16[128,1024]{1,0:T(8,128)(2,1)S(1)} %copy-done.6), channel_id=1, source_target_pairs={{0,16},{1,17},{2,18},{3,19},{4,20},{5,21},{6,22},{7,23},{8,24},{9,... | collective-permute-start | bytes 786440 | tf_op jit(solution)/shard_map/ppermute | solution.py:29
  145.5 19.4 %collective-permute-start.3 = (bf16[800,768]{1,0:T(8,128)(2,1)}, bf16[800,768]{1,0:T(8,128)(2,1)}, u32[]{:S(2)}, u32[]{:S(2)}) collective-permute-start(bf16[800,768]{1,0:T(8,128)(2,1)} %fusion.24), channel_id=1, source_target_pairs={{0,32},{32,0},{1,33},{33,1},{2,34},{34,2},{3,35},{35,3},{4,36},{36... | collective-permute-start | bytes 3686408 | tf_op jit(solution)/shard_map/ppermute | solution.py:35
  151.4 24.0 %collective-permute-start.6 = (bf16[400,768]{1,0:T(8,128)(2,1)S(1)}, bf16[400,768]{1,0:T(8,128)(2,1)}, u32[]{:S(2)}, u32[]{:S(2)}) collective-permute-start(bf16[400,768]{1,0:T(8,128)(2,1)S(1)} %fusion.48), channel_id=1, source_target_pairs={{0,32},{32,0},{1,33},{33,1},{2,34},{34,2},{3,35},{35,3},{4,36},{36... | collective-permute-start | bytes 1843208 | tf_op jit(solution)/shard_map/ppermute | solution.py:35
  157.5 20.7 %collective-permute-start.4 = (bf16[512,768]{1,0:T(8,128)(2,1)}, bf16[512,768]{1,0:T(8,128)(2,1)}, u32[]{:S(2)}, u32[]{:S(2)}) collective-permute-start(bf16[512,768]{1,0:T(8,128)(2,1)} %fusion.45), channel_id=1, source_target_pairs={{0,32},{32,0},{1,33},{33,1},{2,34},{34,2},{3,35},{35,3},{4,36},{36... | collective-permute-start | bytes 2359304 | tf_op jit(solution)/shard_map/ppermute | solution.py:35
  162.5 15.7 %collective-permute-start.5 = (bf16[512,768]{1,0:T(8,128)(2,1)}, bf16[512,768]{1,0:T(8,128)(2,1)}, u32[]{:S(2)}, u32[]{:S(2)}) collective-permute-start(bf16[512,768]{1,0:T(8,128)(2,1)} %fusion.42), channel_id=1, source_target_pairs={{0,32},{32,0},{1,33},{33,1},{2,34},{34,2},{3,35},{35,3},{4,36},{36... | collective-permute-start | bytes 2359304 | tf_op jit(solution)/shard_map/ppermute | solution.py:35
  168.2 25.2 %all-to-all-start.2 = ((bf16[16,32,1024]{2,1,0:T(8,128)(2,1)}), bf16[16,32,1024]{2,1,0:T(8,128)(2,1)}, u32[]{:S(2)}, u32[]{:S(2)}) async-start(bf16[16,32,1024]{2,1,0:T(8,128)(2,1)} %bitcast.5), calls=%async_computation.2 | async-start | bytes 2097152 | tf_op jit(solution)/shard_map/all_to_all | solution.py:39
  193.4 28.7 %all-to-all-start.3 = ((bf16[16,56,1024]{2,1,0:T(8,128)(2,1)}), bf16[16,56,1024]{2,1,0:T(8,128)(2,1)S(1)}, u32[]{:S(2)}, u32[]{:S(2)}) async-start(bf16[16,56,1024]{2,1,0:T(8,128)(2,1)} %fusion.5), calls=%async_computation.3 | async-start | bytes 3670016 | tf_op jit(solution)/shard_map/all_to_all | solution.py:39
  197.1 5.2 %copy-start.2 = (f32[800,768]{1,0:T(8,128)S(1)}, f32[800,768]{1,0:T(8,128)}, u32[]{:S(2)}) copy-start(f32[800,768]{1,0:T(8,128)} %convert_add_fusion) | copy-start | bytes 7372804
  197.1 5.2 %copy-start.5 = (bf16[1,1,768,1024]{3,2,1,0:T(8,128)(2,1)S(1)}, bf16[1,1,768,1024]{3,2,1,0:T(8,128)(2,1)}, u32[]{:S(2)}) copy-start(bf16[1,1,768,1024]{3,2,1,0:T(8,128)(2,1)} %param.17) | copy-start | bytes 4718596
  200.4 6.1 %collective-permute-start.2 = (bf16[512,768]{1,0:T(8,128)(2,1)}, bf16[512,768]{1,0:T(8,128)(2,1)}, u32[]{:S(2)}, u32[]{:S(2)}) collective-permute-start(bf16[512,768]{1,0:T(8,128)(2,1)} %fusion.39), channel_id=1, source_target_pairs={{0,32},{32,0},{1,33},{33,1},{2,34},{34,2},{3,35},{35,3},{4,36},{36... | collective-permute-start | bytes 2359304 | tf_op jit(solution)/shard_map/ppermute | solution.py:35
  206.5 3.0 %copy-start.1 = (bf16[16,25,1024]{2,1,0:T(8,128)(2,1)S(1)}, bf16[16,25,1024]{2,1,0:T(8,128)(2,1)}, u32[]{:S(2)}) copy-start(bf16[16,25,1024]{2,1,0:T(8,128)(2,1)} %reshape.75) | copy-start | bytes 2457604
  222.2 28.4 %all-to-all-start.4 = ((bf16[16,56,1024]{2,1,0:T(8,128)(2,1)}), bf16[16,56,1024]{2,1,0:T(8,128)(2,1)}, u32[]{:S(2)}, u32[]{:S(2)}) async-start(bf16[16,56,1024]{2,1,0:T(8,128)(2,1)} %fusion.4), calls=%async_computation.4 | async-start | bytes 3670016 | tf_op jit(solution)/shard_map/all_to_all | solution.py:39
  227.4 33.0 %collective-permute-start.9 = (bf16[128,1024]{1,0:T(8,128)(2,1)S(1)}, bf16[128,1024]{1,0:T(8,128)(2,1)S(1)}, u32[]{:S(2)}, u32[]{:S(2)}) collective-permute-start(bf16[128,1024]{1,0:T(8,128)(2,1)S(1)} %get-tuple-element.37), channel_id=1, source_target_pairs={{0,448},{1,449},{2,450},{3,451},{4,452},{5,453},{6,454},{7,455},{8... | collective-permute-start | bytes 786440 | tf_op jit(solution)/shard_map/ppermute | solution.py:29
  229.4 46.7 %collective-permute-start.10 = (bf16[128,1024]{1,0:T(8,128)(2,1)S(1)}, bf16[128,1024]{1,0:T(8,128)(2,1)S(1)}, u32[]{:S(2)}, u32[]{:S(2)}) collective-permute-start(bf16[128,1024]{1,0:T(8,128)(2,1)S(1)} %get-tuple-element.38), channel_id=1, source_target_pairs={{0,464},{1,465},{2,466},{3,467},{4,468},{5,469},{6,470},{7,471},{8... | collective-permute-start | bytes 786440 | tf_op jit(solution)/shard_map/ppermute | solution.py:29
  252.8 24.1 %collective-permute-start.7 = (bf16[128,1024]{1,0:T(8,128)(2,1)S(1)}, bf16[128,1024]{1,0:T(8,128)(2,1)S(1)}, u32[]{:S(2)}, u32[]{:S(2)}) collective-permute-start(bf16[128,1024]{1,0:T(8,128)(2,1)S(1)} %get-tuple-element.39), channel_id=1, source_target_pairs={{0,64},{1,65},{2,66},{3,67},{4,68},{5,69},{6,70},{7,71},{8,72},{9,... | collective-permute-start | bytes 786440 | tf_op jit(solution)/shard_map/ppermute | solution.py:29
  254.7 44.3 %collective-permute-start.8 = (bf16[128,1024]{1,0:T(8,128)(2,1)S(1)}, bf16[128,1024]{1,0:T(8,128)(2,1)S(1)}, u32[]{:S(2)}, u32[]{:S(2)}) collective-permute-start(bf16[128,1024]{1,0:T(8,128)(2,1)S(1)} %get-tuple-element.40), channel_id=1, source_target_pairs={{0,80},{1,81},{2,82},{3,83},{4,84},{5,85},{6,86},{7,87},{8,88},{9,... | collective-permute-start | bytes 786440 | tf_op jit(solution)/shard_map/ppermute | solution.py:29

commit v3 on v2

--- a/solution.py
+++ b/solution.py
@@ -109,76 +109,60 @@
     bf = jnp.bfloat16
     contract = (((1,), (1,)), ((), ()))
 
-    note_f = note_of(routes_forward, gates_forward)
-    note_b = note_of(routes_backward, gates_backward)
-    notes = jnp.concatenate([note_b, note_f], axis=1)
-    both = jnp.concatenate([act_backward, grad_backward], axis=1)
-    notes_wide = jnp.pad(notes, ((0, 0), (0, 2 * cols - notes.shape[1])))
-    far_b = moved(jnp.concatenate([both, notes_wide], axis=0), 0, True)
-    far_f = moved(after(act_forward, far_b), 0, True)
+    eight = lambda n: (n + 7) // 8 * 8
+    rows_in, rows_out = eight(3 * CAP), eight(2 * CAP)
 
-    place_f, weight_f = places(note_f, top, first, experts)
-    place_b, weight_b = places(note_b, top, first, experts)
-    own_rows = jnp.concatenate([act_forward, act_backward, grad_backward], axis=0)
-    own_places = jnp.concatenate(
-        [place_f, offset(place_b, CAP), offset(place_b, 2 * CAP)], axis=1
+    notes = jnp.concatenate(
+        [note_of(routes_forward, gates_forward), note_of(routes_backward, gates_backward)], axis=1
     )
-    got_own = exchange(pack(own_places, (3 * CAP + 7) // 8 * 8, own_rows))
+    notes = jnp.pad(notes, ((0, 0), (0, cols - notes.shape[1])))
+    near = jnp.concatenate([act_forward, act_backward, grad_backward, notes], axis=0)
+    far = moved(near, 0, True)
 
-    far_place_b, far_weight_b = places(far_b[tok:, :tok], top, first, experts)
-    far_place_f, far_weight_f = places(far_b[tok:, tok : 2 * tok], top, first, experts)
-    padded = (CAP + 7) // 8 * 8
-    got_far_b = exchange(after(pack(far_place_b, padded, far_b[:tok]), got_own))
-    got_far_f = exchange(after(pack(far_place_f, padded, far_f), got_far_b))
+    def tables(block):
+        note = block[3 * tok :]
+        place_f, weight_f = places(note[:, :tok], top, first, experts)
+        place_b, weight_b = places(note[:, tok : 2 * tok], top, first, experts)
+        place_b1, place_b2 = offset(place_b, CAP), offset(place_b, 2 * CAP)
+        into = jnp.concatenate([place_f, place_b1, place_b2], axis=1)
+        back = jnp.concatenate([place_f, place_b1], axis=1)
+        return into, back, jnp.concatenate([weight_f, weight_b], axis=1)
 
     def added(part):
         part = part.astype(bf)
         return part.astype(jnp.float32) + other_core(part).astype(jnp.float32)
 
-    def forward(pre):
-        return dot32(jax.nn.silu(pre).astype(bf), weight_out).astype(bf)
+    def work(got):
+        rows = [got[:, i * CAP : (i + 1) * CAP].reshape(-1, cols) for i in range(3)]
+        pre_f = added(dot32(rows[0], weight_in))
+        pre_b = added(dot32(rows[1], weight_in))
+        back_h = added(dot32(rows[2], weight_out, contract))
+        out_f = dot32(jax.nn.silu(pre_f).astype(bf), weight_out).astype(bf)
+        sigma = jax.nn.sigmoid(pre_b)
+        slope = (back_h * sigma * (1.0 + pre_b * (1.0 - sigma))).astype(bf)
+        out_b = dot32(slope, weight_in, contract).astype(bf)
+        shape = (experts, CAP, cols)
+        joined = jnp.concatenate([out_f.reshape(shape), out_b.reshape(shape)], axis=1)
+        return jnp.pad(joined, ((0, 0), (0, rows_out - 2 * CAP), (0, 0)))
 
-    def backward(pre, back_h):
-        sigma = jax.nn.sigmoid(pre)
-        slope = (back_h * sigma * (1.0 + pre * (1.0 - sigma))).astype(bf)
-        return dot32(slope, weight_in, contract).astype(bf)
+    into, back, weight = tables(near)
+    got = exchange(pack(into, rows_in, near[: 3 * tok]))
+    far = after(far, got)
+    far_into, far_back, far_weight = tables(far)
+    far_got = exchange(pack(far_into, rows_in, far[: 3 * tok]))
+    out = work(got)
+    far_out = exchange(work(far_got))
+    far_sum = combine(far_back, far_weight, far_out)
+    far_f = moved(far_sum[:tok], 1, True)
+    far_b = moved(far_sum[tok:], -1, True)
+    near_sum = combine(back, weight, exchange(after(out, far_out)))
+    near_f = moved(near_sum[:tok], 1, False)
+    near_b = moved(near_sum[tok:], -1, False)
 
-    cut = experts * CAP
-    own_fa = jnp.concatenate([got_own[:, :CAP], got_own[:, CAP : 2 * CAP]], axis=0)
-    own_pre = added(dot32(own_fa.reshape(-1, cols), weight_in))
-    own_back = added(
-        dot32(got_own[:, 2 * CAP : 3 * CAP].reshape(-1, cols), weight_out, contract)
-    )
-    own_out_f = forward(own_pre[:cut]).reshape(experts, CAP, cols)
-    own_out_b = backward(own_pre[cut:], own_back).reshape(experts, CAP, cols)
+    def both(a, b):
+        return (a.astype(jnp.float32) + b.astype(jnp.float32)).astype(bf)
 
-    rows_b = got_far_b.reshape(-1, 2 * cols)
-    far_pre = added(dot32(rows_b[:, :cols], weight_in))
-    far_back = added(dot32(rows_b[:, cols:], weight_out, contract))
-    far_out_b = backward(far_pre, far_back).reshape(experts, padded, cols)
-    far_out_f = forward(added(dot32(got_far_f.reshape(-1, cols), weight_in))).reshape(
-        experts, padded, cols
-    )
-
-    def returned(far, own, *done):
-        joined = jnp.concatenate([far[:, :CAP], own], axis=1)
-        joined = jnp.pad(joined, ((0, 0), (0, (2 * CAP + 7) // 8 * 8 - 2 * CAP), (0, 0)))
-        return exchange(after(joined, *done))
-
-    back_b = returned(far_out_b, own_out_b, got_far_f)
-    back_f = returned(far_out_f, own_out_f, back_b)
-
-    def settle(back, far_place, far_weight, place, weight, by):
-        both_places = jnp.concatenate([far_place, offset(place, CAP)], axis=1)
-        total = combine(both_places, jnp.concatenate([far_weight, weight], axis=1), back)
-        far = moved(total[:tok], by, True)
-        near = moved(total[tok:], by, False)
-        return (near.astype(jnp.float32) + far.astype(jnp.float32)).astype(bf)
-
-    return (
-        settle(back_f, far_place_f, far_weight_f, place_f, weight_f, 1),
-        settle(back_b, far_place_b, far_weight_b, place_b, weight_b, -1),
-    )
+    return both(near_f, far_f), both(near_b, far_b)
 
 
 def solution(mesh):

time: 301 us -> 312 us (1.037)
  the two profiles are of different devices: /device:TPU:32 before, /device:TPU:1 now
where the time goes in v3:
time: 312 us; the launch traced here: 310 us
  starting transfers between devices  145 us (46%)
  waiting for transfers between devices  85.9 us (28%)
  matrix products  39.6 us (13%)
  local copies, waits for them, and re-layouts  27.2 us (9%)
  other arithmetic  10.9 us (3%)
    ppermute x5, starting transfers between devices, moved(): lax.ppermute(v, RING, pairs_of(shape, lambda s, h: ((s + by) % sections,...  101 us
    ppermute x5, waiting for transfers between devices, moved(): lax.ppermute(v, RING, pairs_of(shape, lambda s, h: ((s + by) % sections,...  61.1 us
    dot_general x14, matrix products, dot32(): return lax.dot_general(a, b, dims, preferred_element_type=jnp.float32)  39.1 us
    all_to_all x4, starting transfers between devices, exchange(): return lax.all_to_all(v, PLANE, split_axis=0, concat_axis=0, tiled=True)  25.1 us
    all_to_all x4, waiting for transfers between devices, exchange(): return lax.all_to_all(v, PLANE, split_axis=0, concat_axis=0, tiled=True)  24.8 us
    ppermute x6, starting transfers between devices, other_core(): return lax.ppermute(v, NODE, [(0, 1), (1, 0)])  19 us
    reshape x6, local copies, waits for them, and re-layouts, work(): rows = [got[:, i * CAP:(i + 1) * CAP].reshape(-1, cols) for i in range(3)]  12.4 us
    slice x2, local copies, waits for them, and re-layouts, work(): rows = [got[:, i * CAP:(i + 1) * CAP].reshape(-1, cols) for i in range(3)]  8.29 us
  transfers between devices with their start and end apart: 15, of which 5 were waited for; matrix products, arithmetic and copies ran while one was open for 18% of the time, Pallas kernels for 0%

profile of v3, /device:TPU:1, one launch (start us, length us, event | category | flops | bytes accessed | tf_op | source)
XLA Modules:
  0.0 310.1 jit_solution(1562611807384283753)
XLA Ops:
  3.7 4.1 %convolution_convert_fusion.1 = bf16[1280,1024]{1,0:T(8,128)(2,1)} fusion(pred[1280,384]{1,0:T(32,128)(4,1)S(1)} %bitcast_compare_fusion.1, bf16[128,1024]{1,0:T(8,128)(2,1)} %param.13, bf16[128,1024]{1,0:T(8,128)(2,1)} %param.12, bf16[128,1024]{1,0:T(8,128)(2,1)} %param.9), kind=kOutput, calls=%fused_computation.1 | convolution fusion | flops 1010302976 | bytes 3899392 | tf_op jit(solution)/shard_map/dot_general | solution.py:89
  7.8 7.8 %all-to-all-start = ((bf16[16,80,1024]{2,1,0:T(8,128)(2,1)}), bf16[16,80,1024]{2,1,0:T(8,128)(2,1)}, u32[]{:S(2)}, u32[]{:S(2)}) async-start(bf16[16,80,1024]{2,1,0:T(8,128)(2,1)} %bitcast.76), calls=%async_computation | async-start | bytes 5242880 | tf_op jit(solution)/shard_map/all_to_all | solution.py:39
  15.7 15.4 %collective-permute-start.3 = (bf16[400,1024]{1,0:T(8,128)(2,1)S(1)}, bf16[400,1024]{1,0:T(8,128)(2,1)S(1)}, u32[]{:S(2)}, u32[]{:S(2)}) collective-permute-start(bf16[400,1024]{1,0:T(8,128)(2,1)S(1)} %pad_maximum_fusion), channel_id=1, source_target_pairs={{0,16},{1,17},{2,18},{3,19},{4,20},{5,21},{6,22},{7,23},{8,24},{9,... | collective-permute-start | bytes 2457608 | tf_op jit(solution)/shard_map/ppermute | solution.py:29
  31.2 26.4 %collective-permute-done.3 = bf16[400,1024]{1,0:T(8,128)(2,1)S(1)} collective-permute-done((bf16[400,1024]{1,0:T(8,128)(2,1)S(1)}, bf16[400,1024]{1,0:T(8,128)(2,1)S(1)}, u32[]{:S(2)}, u32[]{:S(2)}) %collective-permute-start.3) | collective-permute-done | bytes 819232 | tf_op jit(solution)/shard_map/ppermute | solution.py:29
  58.4 3.0 convolution_convert_fusion
  61.4 6.3 %all-to-all-start.1 = ((bf16[16,80,1024]{2,1,0:T(8,128)(2,1)}), bf16[16,80,1024]{2,1,0:T(8,128)(2,1)}, u32[]{:S(2)}, u32[]{:S(2)}) async-start(bf16[16,80,1024]{2,1,0:T(8,128)(2,1)} %bitcast.77), calls=%async_computation.1 | async-start | bytes 5242880 | tf_op jit(solution)/shard_map/all_to_all | solution.py:39
  67.7 4.2 %fusion.108 = (bf16[16,25,1024]{2,1,0:T(8,128)(2,1)}, bf16[16,25,1024]{2,1,0:T(8,128)(2,1)S(1)}, bf16[16,25,1024]{2,1,0:T(8,128)(2,1)}) fusion(bf16[16,80,1024]{2,1,0:T(8,128)(2,1)} %all-to-all-done), kind=kLoop, calls=%fused_computation.142 | loop fusion | bytes 4915200 | tf_op jit(solution)/shard_map/slice | solution.py:136
  73.5 24.8 %all-to-all-done.1 = bf16[16,80,1024]{2,1,0:T(8,128)(2,1)} async-done(((bf16[16,80,1024]{2,1,0:T(8,128)(2,1)}), bf16[16,80,1024]{2,1,0:T(8,128)(2,1)}, u32[]{:S(2)}, u32[]{:S(2)}) %all-to-all-start.1) | async-done | bytes 2621472 | tf_op jit(solution)/shard_map/all_to_all | solution.py:39
  98.3 4.1 %fusion.109 = (bf16[16,25,1024]{2,1,0:T(8,128)(2,1)}, bf16[16,25,1024]{2,1,0:T(8,128)(2,1)}, bf16[16,25,1024]{2,1,0:T(8,128)(2,1)}) fusion(bf16[16,80,1024]{2,1,0:T(8,128)(2,1)} %all-to-all-done.1), kind=kLoop, calls=%fused_computation.143 | loop fusion | bytes 4915200 | tf_op jit(solution)/shard_map/slice | solution.py:136
  104.8 2.8 fusion.44
  107.6 8.0 %collective-permute-start.4 = (bf16[400,768]{1,0:T(8,128)(2,1)}, bf16[400,768]{1,0:T(8,128)(2,1)}, u32[]{:S(2)}, u32[]{:S(2)}) collective-permute-start(bf16[400,768]{1,0:T(8,128)(2,1)} %fusion.44), channel_id=1, source_target_pairs={{0,32},{32,0},{1,33},{33,1},{2,34},{34,2},{3,35},{35,3},{4,36},{36... | collective-permute-start | bytes 1843208 | tf_op jit(solution)/shard_map/ppermute | solution.py:35
  118.0 3.3 %fusion.53 = bf16[400,768]{1,0:T(8,128)(2,1)} fusion(bf16[400,1024]{1,0:T(8,128)(2,1)} %reshape.77, bf16[1,1,768,1024]{3,2,1,0:T(8,128)(2,1)} %param.17), kind=kOutput, calls=%fused_computation.42 | convolution fusion | flops 629452800 | bytes 3006464 | tf_op jit(solution)/shard_map/dot_general | solution.py:89
  125.7 2.9 fusion.47
  142.9 3.0 fusion.5
  145.9 4.0 %all-to-all-start.2 = ((bf16[16,56,1024]{2,1,0:T(8,128)(2,1)}), bf16[16,56,1024]{2,1,0:T(8,128)(2,1)S(1)}, u32[]{:S(2)}, u32[]{:S(2)}) async-start(bf16[16,56,1024]{2,1,0:T(8,128)(2,1)} %fusion.5), calls=%async_computation.2 | async-start | bytes 3670016 | tf_op jit(solution)/shard_map/all_to_all | solution.py:39
  162.6 3.7 %fusion.26 = bf16[400,1024]{1,0:T(8,128)(2,1)} fusion(bf16[1,1,1024,768]{3,2,1,0:T(8,128)(2,1)S(1)} %copy-done, bf16[400,768]{1,0:T(8,128)(2,1)} %collective-permute-done.2, bf16[400,768]{1,0:T(8,128)(2,1)} %fusion.41, bf16[400,768]{1,0:T(8,128)(2,1)} %collective-permute-done.1, bf16[400,768]{1,0:T(8,128)(2,1)} %fusion.50), kind=kOutput, calls=%fused_computation.31 | convolution fusion | flops 634163200 | bytes 4849664 | tf_op jit(solution)/shard_map/dot_general | solution.py:89
  168.7 3.6 %fusion.32 = bf16[400,1024]{1,0:T(8,128)(2,1)} fusion(bf16[1,1,768,1024]{3,2,1,0:T(8,128)(2,1)} %param.17, bf16[400,768]{1,0:T(8,128)(2,1)} %collective-permute-done, bf16[400,768]{1,0:T(8,128)(2,1)} %fusion.38), kind=kOutput, calls=%fused_computation.33 | convolution fusion | flops 632012800 | bytes 3620864 | tf_op jit(solution)/shard_map/dot_general | solution.py:89
  174.7 3.3 %fusion.4 = bf16[16,56,1024]{2,1,0:T(8,128)(2,1)} fusion(bf16[16,25,1024]{2,1,0:T(8,128)(2,1)} %reshape.73, bf16[16,25,1024]{2,1,0:T(8,128)(2,1)} %reshape.70), kind=kLoop, calls=%fused_computation.9 | loop fusion | flops 6422528 | bytes 3473408 | tf_op jit(solution)/shard_map/concatenate | solution.py:145
  178.0 7.0 %all-to-all-start.3 = ((bf16[16,56,1024]{2,1,0:T(8,128)(2,1)}), bf16[16,56,1024]{2,1,0:T(8,128)(2,1)}, u32[]{:S(2)}, u32[]{:S(2)}) async-start(bf16[16,56,1024]{2,1,0:T(8,128)(2,1)} %fusion.4), calls=%async_computation.3 | async-start | bytes 3670016 | tf_op jit(solution)/shard_map/all_to_all | solution.py:39
  185.8 42.9 %collective-permute-start.10 = (bf16[128,1024]{1,0:T(8,128)(2,1)S(1)}, bf16[128,1024]{1,0:T(8,128)(2,1)S(1)}, u32[]{:S(2)}, u32[]{:S(2)}) collective-permute-start(bf16[128,1024]{1,0:T(8,128)(2,1)S(1)} %get-tuple-element.34), channel_id=1, source_target_pairs={{0,464},{1,465},{2,466},{3,467},{4,468},{5,469},{6,470},{7,471},{8... | collective-permute-start | bytes 786440 | tf_op jit(solution)/shard_map/ppermute | solution.py:29
  231.0 20.1 %collective-permute-start.9 = (bf16[128,1024]{1,0:T(8,128)(2,1)S(1)}, bf16[128,1024]{1,0:T(8,128)(2,1)S(1)}, u32[]{:S(2)}, u32[]{:S(2)}) collective-permute-start(bf16[128,1024]{1,0:T(8,128)(2,1)S(1)} %get-tuple-element.32), channel_id=1, source_target_pairs={{0,448},{1,449},{2,450},{3,451},{4,452},{5,453},{6,454},{7,455},{8... | collective-permute-start | bytes 786440 | tf_op jit(solution)/shard_map/ppermute | solution.py:29
  251.1 19.5 %collective-permute-start.8 = (bf16[128,1024]{1,0:T(8,128)(2,1)S(1)}, bf16[128,1024]{1,0:T(8,128)(2,1)S(1)}, u32[]{:S(2)}, u32[]{:S(2)}) collective-permute-start(bf16[128,1024]{1,0:T(8,128)(2,1)S(1)} %get-tuple-element.35), channel_id=1, source_target_pairs={{0,80},{1,81},{2,82},{3,83},{4,84},{5,85},{6,86},{7,87},{8,88},{9,... | collective-permute-start | bytes 786440 | tf_op jit(solution)/shard_map/ppermute | solution.py:29
  270.6 3.4 %collective-permute-start.7 = (bf16[128,1024]{1,0:T(8,128)(2,1)S(1)}, bf16[128,1024]{1,0:T(8,128)(2,1)S(1)}, u32[]{:S(2)}, u32[]{:S(2)}) collective-permute-start(bf16[128,1024]{1,0:T(8,128)(2,1)S(1)} %get-tuple-element.33), channel_id=1, source_target_pairs={{0,64},{1,65},{2,66},{3,67},{4,68},{5,69},{6,70},{7,71},{8,72},{9,... | collective-permute-start | bytes 786440 | tf_op jit(solution)/shard_map/ppermute | solution.py:29
  278.2 31.1 %collective-permute-done.7 = bf16[128,1024]{1,0:T(8,128)(2,1)S(1)} collective-permute-done((bf16[128,1024]{1,0:T(8,128)(2,1)S(1)}, bf16[128,1024]{1,0:T(8,128)(2,1)S(1)}, u32[]{:S(2)}, u32[]{:S(2)}) %collective-permute-start.7) | collective-permute-done | bytes 262176 | tf_op jit(solution)/shard_map/ppermute | solution.py:29
  (76 shorter events, 54.3 us)
Async XLA Ops:
  0.6 104.1 %copy-start = (bf16[1,1,1024,768]{3,2,1,0:T(8,128)(2,1)S(1)}, bf16[1,1,1024,768]{3,2,1,0:T(8,128)(2,1)}, u32[]{:S(2)}) copy-start(bf16[1,1,1024,768]{3,2,1,0:T(8,128)(2,1)} %param.16) | copy-start | bytes 4718596
  7.8 7.8 %copy-start.4 = (bf16[128,6]{0,1:T(8,128)(2,1)S(1)}, bf16[128,6]{0,1:T(8,128)(2,1)}, u32[]{:S(2)}) copy-start(bf16[128,6]{0,1:T(8,128)(2,1)} %param.11) | copy-start | bytes 4612
  7.8 7.8 %copy-start.5 = (bf16[128,6]{0,1:T(8,128)(2,1)S(1)}, bf16[128,6]{0,1:T(8,128)(2,1)}, u32[]{:S(2)}) copy-start(bf16[128,6]{0,1:T(8,128)(2,1)} %param.15) | copy-start | bytes 4612
  7.8 7.9 %copy-start.1 = (bf16[128,1024]{1,0:T(8,128)(2,1)S(1)}, bf16[128,1024]{1,0:T(8,128)(2,1)}, u32[]{:S(2)}) copy-start(bf16[128,1024]{1,0:T(8,128)(2,1)} %param.13) | copy-start | bytes 786436
  7.8 7.9 %copy-start.2 = (bf16[128,1024]{1,0:T(8,128)(2,1)S(1)}, bf16[128,1024]{1,0:T(8,128)(2,1)}, u32[]{:S(2)}) copy-start(bf16[128,1024]{1,0:T(8,128)(2,1)} %param.12) | copy-start | bytes 786436
  7.8 7.9 %copy-start.3 = (bf16[128,1024]{1,0:T(8,128)(2,1)S(1)}, bf16[128,1024]{1,0:T(8,128)(2,1)}, u32[]{:S(2)}) copy-start(bf16[128,1024]{1,0:T(8,128)(2,1)} %param.9) | copy-start | bytes 786436
  7.8 49.8 %all-to-all-start = ((bf16[16,80,1024]{2,1,0:T(8,128)(2,1)}), bf16[16,80,1024]{2,1,0:T(8,128)(2,1)}, u32[]{:S(2)}, u32[]{:S(2)}) async-start(bf16[16,80,1024]{2,1,0:T(8,128)(2,1)} %bitcast.76), calls=%async_computation | async-start | bytes 5242880 | tf_op jit(solution)/shard_map/all_to_all | solution.py:39
  15.7 41.9 %collective-permute-start.3 = (bf16[400,1024]{1,0:T(8,128)(2,1)S(1)}, bf16[400,1024]{1,0:T(8,128)(2,1)S(1)}, u32[]{:S(2)}, u32[]{:S(2)}) collective-permute-start(bf16[400,1024]{1,0:T(8,128)(2,1)S(1)} %pad_maximum_fusion), channel_id=1, source_target_pairs={{0,16},{1,17},{2,18},{3,19},{4,20},{5,21},{6,22},{7,23},{8,24},{9,... | collective-permute-start | bytes 2457608 | tf_op jit(solution)/shard_map/ppermute | solution.py:29
  61.4 36.9 %all-to-all-start.1 = ((bf16[16,80,1024]{2,1,0:T(8,128)(2,1)}), bf16[16,80,1024]{2,1,0:T(8,128)(2,1)}, u32[]{:S(2)}, u32[]{:S(2)}) async-start(bf16[16,80,1024]{2,1,0:T(8,128)(2,1)} %bitcast.77), calls=%async_computation.1 | async-start | bytes 5242880 | tf_op jit(solution)/shard_map/all_to_all | solution.py:39
  107.6 28.4 %collective-permute-start.4 = (bf16[400,768]{1,0:T(8,128)(2,1)}, bf16[400,768]{1,0:T(8,128)(2,1)}, u32[]{:S(2)}, u32[]{:S(2)}) collective-permute-start(bf16[400,768]{1,0:T(8,128)(2,1)} %fusion.44), channel_id=1, source_target_pairs={{0,32},{32,0},{1,33},{33,1},{2,34},{34,2},{3,35},{35,3},{4,36},{36... | collective-permute-start | bytes 1843208 | tf_op jit(solution)/shard_map/ppermute | solution.py:35
  121.4 17.5 %collective-permute-start.5 = (bf16[400,768]{1,0:T(8,128)(2,1)}, bf16[400,768]{1,0:T(8,128)(2,1)}, u32[]{:S(2)}, u32[]{:S(2)}) collective-permute-start(bf16[400,768]{1,0:T(8,128)(2,1)} %fusion.53), channel_id=1, source_target_pairs={{0,32},{32,0},{1,33},{33,1},{2,34},{34,2},{3,35},{35,3},{4,36},{36... | collective-permute-start | bytes 1843208 | tf_op jit(solution)/shard_map/ppermute | solution.py:35
  125.7 5.3 %copy-start.6 = (bf16[1,1,768,1024]{3,2,1,0:T(8,128)(2,1)S(1)}, bf16[1,1,768,1024]{3,2,1,0:T(8,128)(2,1)}, u32[]{:S(2)}) copy-start(bf16[1,1,768,1024]{3,2,1,0:T(8,128)(2,1)} %param.17) | copy-start | bytes 4718596
  128.6 10.3 %collective-permute-start.6 = (bf16[400,768]{1,0:T(8,128)(2,1)}, bf16[400,768]{1,0:T(8,128)(2,1)}, u32[]{:S(2)}, u32[]{:S(2)}) collective-permute-start(bf16[400,768]{1,0:T(8,128)(2,1)} %fusion.47), channel_id=1, source_target_pairs={{0,32},{32,0},{1,33},{33,1},{2,34},{34,2},{3,35},{35,3},{4,36},{36... | collective-permute-start | bytes 1843208 | tf_op jit(solution)/shard_map/ppermute | solution.py:35
  132.7 29.9 %collective-permute-start.1 = (bf16[400,768]{1,0:T(8,128)(2,1)}, bf16[400,768]{1,0:T(8,128)(2,1)}, u32[]{:S(2)}, u32[]{:S(2)}) collective-permute-start(bf16[400,768]{1,0:T(8,128)(2,1)} %fusion.50), channel_id=1, source_target_pairs={{0,32},{32,0},{1,33},{33,1},{2,34},{34,2},{3,35},{35,3},{4,36},{36... | collective-permute-start | bytes 1843208 | tf_op jit(solution)/shard_map/ppermute | solution.py:35
  145.9 32.0 %all-to-all-start.2 = ((bf16[16,56,1024]{2,1,0:T(8,128)(2,1)}), bf16[16,56,1024]{2,1,0:T(8,128)(2,1)S(1)}, u32[]{:S(2)}, u32[]{:S(2)}) async-start(bf16[16,56,1024]{2,1,0:T(8,128)(2,1)} %fusion.5), calls=%async_computation.2 | async-start | bytes 3670016 | tf_op jit(solution)/shard_map/all_to_all | solution.py:39
  152.8 9.9 %collective-permute-start.2 = (bf16[400,768]{1,0:T(8,128)(2,1)}, bf16[400,768]{1,0:T(8,128)(2,1)}, u32[]{:S(2)}, u32[]{:S(2)}) collective-permute-start(bf16[400,768]{1,0:T(8,128)(2,1)} %fusion.41), channel_id=1, source_target_pairs={{0,32},{32,0},{1,33},{33,1},{2,34},{34,2},{3,35},{35,3},{4,36},{36... | collective-permute-start | bytes 1843208 | tf_op jit(solution)/shard_map/ppermute | solution.py:35
  160.7 8.0 %collective-permute-start = (bf16[400,768]{1,0:T(8,128)(2,1)}, bf16[400,768]{1,0:T(8,128)(2,1)}, u32[]{:S(2)}, u32[]{:S(2)}) collective-permute-start(bf16[400,768]{1,0:T(8,128)(2,1)} %fusion.38), channel_id=1, source_target_pairs={{0,32},{32,0},{1,33},{33,1},{2,34},{34,2},{3,35},{35,3},{4,36},{36... | collective-permute-start | bytes 1843208 | tf_op jit(solution)/shard_map/ppermute | solution.py:35
  178.0 50.7 %all-to-all-start.3 = ((bf16[16,56,1024]{2,1,0:T(8,128)(2,1)}), bf16[16,56,1024]{2,1,0:T(8,128)(2,1)}, u32[]{:S(2)}, u32[]{:S(2)}) async-start(bf16[16,56,1024]{2,1,0:T(8,128)(2,1)} %fusion.4), calls=%async_computation.3 | async-start | bytes 3670016 | tf_op jit(solution)/shard_map/all_to_all | solution.py:39
  185.8 89.0 %collective-permute-start.10 = (bf16[128,1024]{1,0:T(8,128)(2,1)S(1)}, bf16[128,1024]{1,0:T(8,128)(2,1)S(1)}, u32[]{:S(2)}, u32[]{:S(2)}) collective-permute-start(bf16[128,1024]{1,0:T(8,128)(2,1)S(1)} %get-tuple-element.34), channel_id=1, source_target_pairs={{0,464},{1,465},{2,466},{3,467},{4,468},{5,469},{6,470},{7,471},{8... | collective-permute-start | bytes 786440 | tf_op jit(solution)/shard_map/ppermute | solution.py:29
  231.0 46.4 %collective-permute-start.9 = (bf16[128,1024]{1,0:T(8,128)(2,1)S(1)}, bf16[128,1024]{1,0:T(8,128)(2,1)S(1)}, u32[]{:S(2)}, u32[]{:S(2)}) collective-permute-start(bf16[128,1024]{1,0:T(8,128)(2,1)S(1)} %get-tuple-element.32), channel_id=1, source_target_pairs={{0,448},{1,449},{2,450},{3,451},{4,452},{5,453},{6,454},{7,455},{8... | collective-permute-start | bytes 786440 | tf_op jit(solution)/shard_map/ppermute | solution.py:29
  251.1 27.1 %collective-permute-start.8 = (bf16[128,1024]{1,0:T(8,128)(2,1)S(1)}, bf16[128,1024]{1,0:T(8,128)(2,1)S(1)}, u32[]{:S(2)}, u32[]{:S(2)}) collective-permute-start(bf16[128,1024]{1,0:T(8,128)(2,1)S(1)} %get-tuple-element.35), channel_id=1, source_target_pairs={{0,80},{1,81},{2,82},{3,83},{4,84},{5,85},{6,86},{7,87},{8,88},{9,... | collective-permute-start | bytes 786440 | tf_op jit(solution)/shard_map/ppermute | solution.py:29
  270.6 38.8 %collective-permute-start.7 = (bf16[128,1024]{1,0:T(8,128)(2,1)S(1)}, bf16[128,1024]{1,0:T(8,128)(2,1)S(1)}, u32[]{:S(2)}, u32[]{:S(2)}) collective-permute-start(bf16[128,1024]{1,0:T(8,128)(2,1)S(1)} %get-tuple-element.33), channel_id=1, source_target_pairs={{0,64},{1,65},{2,66},{3,67},{4,68},{5,69},{6,70},{7,71},{8,72},{9,... | collective-permute-start | bytes 786440 | tf_op jit(solution)/shard_map/ppermute | solution.py:29

commit v4 on v1

v4 whole, which is shorter than its diff:
```python
import functools

import jax
import jax.numpy as jnp
from jax import lax
from jax.experimental import pallas as pl
from jax.experimental.pallas import tpu as pltpu
from jax.sharding import Mesh, PartitionSpec as P

SLOTS = 32
NODE = "node"
PLANE = ("x", "y")
RING = ("section", "zhi", "x", "y")
BF = jnp.bfloat16
F32 = jnp.float32
MATMUL = (((1,), (0,)), ((), ()))
TRANSPOSED = (((1,), (1,)), ((), ()))
OVER_ROWS = (((0,), (0,)), ((), ()))
WIDTH = 256


def pairs_of(shape, move):
    sections, halves, xs, ys = shape
    pairs = []
    for s in range(sections):
        for h in range(halves):
            for x in range(xs):
                for y in range(ys):
                    s2, h2 = move(s, h)
                    src = ((s * halves + h) * xs + x) * ys + y
                    dst = ((s2 * halves + h2) * xs + x) * ys + y
                    pairs.append((src, dst))
    return pairs


def moved(v, by, cross):
    shape = tuple(lax.axis_size(a) for a in RING)
    sections = shape[0]
    return lax.ppermute(
        v, RING, pairs_of(shape, lambda s, h: ((s + by) % sections, 1 - h if cross else h))
    )


def other_core(v):
    return lax.ppermute(v, NODE, [(0, 1), (1, 0)])


def exchange(v):
    return lax.all_to_all(v, PLANE, split_axis=0, concat_axis=0, tiled=True)


def after(value, *done):
    return lax.optimization_barrier((value,) + done)[0]


def dot32(a, b, dims=MATMUL):
    return lax.dot_general(a, b, dims, preferred_element_type=F32)


def run(kernel, outs, *args, scalars=0):
    where = [pl.BlockSpec(memory_space=pltpu.SMEM)] * scalars
    where += [pl.BlockSpec(memory_space=pltpu.VMEM)] * (len(args) - scalars)
    return pl.pallas_call(
        kernel,
        out_shape=outs,
        in_specs=where,
        out_specs=jax.tree.map(lambda _: pl.BlockSpec(memory_space=pltpu.VMEM), outs),
        compiler_params=pltpu.CompilerParams(vmem_limit_bytes=32 << 20),
        cost_estimate=pl.CostEstimate(flops=1000, bytes_accessed=1000, transcendentals=0),
    )(*args)


def shaped(*shape):
    return jax.ShapeDtypeStruct(shape, BF)


def note_of(routes, gates):
    note = jnp.concatenate([routes.astype(BF).T, gates.T], axis=0)
    return jnp.pad(note, ((0, 16 - note.shape[0]), (0, 0)))


def tables(note, first, top, experts):
    tokens = note.shape[1] // 2
    label = (lax.broadcasted_iota(jnp.int32, (experts, 2 * tokens), 0) + first).astype(F32)
    chosen = jnp.zeros((experts, 2 * tokens), F32)
    weight = jnp.zeros((experts, 2 * tokens), F32)
    for k in range(top):
        match = note[k : k + 1] == label
        chosen = chosen + jnp.where(match, 1.0, 0.0)
        weight = weight + jnp.where(match, note[top + k : top + k + 1], 0.0)
    i = lax.broadcasted_iota(jnp.int32, (tokens, tokens), 0)
    j = lax.broadcasted_iota(jnp.int32, (tokens, tokens), 1)
    earlier = jnp.where(i < j, 1.0, 0.0).astype(BF)
    slot = lax.broadcasted_iota(jnp.int32, (SLOTS, tokens), 0).astype(F32)
    result = []
    for half in range(2):
        span = slice(half * tokens, (half + 1) * tokens)
        rank = dot32(chosen[:, span].astype(BF), earlier)
        place = jnp.where(chosen[:, span] > 0.0, rank, -1.0)
        hit = [jnp.where(slot == place[e : e + 1], 1.0, 0.0) for e in range(experts)]
        mix = [hit[e] * weight[e : e + 1, span] for e in range(experts)]
        result.append(
            (jnp.concatenate(hit, axis=0).astype(BF), jnp.concatenate(mix, axis=0).astype(BF))
        )
    return result


def put(out_ref, at, hit, rows_ref, first=0):
    experts = out_ref.shape[0]
    tokens = hit.shape[1]
    for c in range(0, out_ref.shape[2], WIDTH):
        block = dot32(hit, rows_ref[first : first + tokens, c : c + WIDTH]).astype(BF)
        out_ref[:, at : at + SLOTS, c : c + WIDTH] = block.reshape(experts, SLOTS, WIDTH)


def pack_own(top, first_ref, f_ref, a_ref, g_ref, note_ref, out_ref, mix_f_ref, mix_b_ref):
    (hit_f, mix_f), (hit_b, mix_b) = tables(
        note_ref[...].astype(F32), first_ref[0], top, out_ref.shape[0]
    )
    mix_f_ref[...] = mix_f
    mix_b_ref[...] = mix_b
    put(out_ref, 0, hit_f, f_ref)
    put(out_ref, SLOTS, hit_b, a_ref)
    put(out_ref, 2 * SLOTS, hit_b, g_ref)


def pack_far(top, first_ref, far_ref, out_ref, hit_f_ref, mix_f_ref, mix_b_ref):
    tokens = hit_f_ref.shape[1]
    note = far_ref[2 * tokens :, : 2 * tokens].astype(F32)
    (hit_f, mix_f), (hit_b, mix_b) = tables(note, first_ref[0], top, out_ref.shape[0])
    hit_f_ref[...] = hit_f
    mix_f_ref[...] = mix_f
    mix_b_ref[...] = mix_b
    put(out_ref, 0, hit_b, far_ref)
    put(out_ref, SLOTS, hit_b, far_ref, tokens)


def pack_more(hit_ref, rows_ref, out_ref):
    put(out_ref, 0, hit_ref[...], rows_ref)


def parts(kinds, got_ref, w_in_ref, w_out_ref, out_ref):
    experts, _, cols = got_ref.shape
    hidden = w_in_ref.shape[1]
    rows = experts * SLOTS
    for i, kind in enumerate(kinds):
        x = got_ref[:, i * SLOTS : (i + 1) * SLOTS, :].reshape(rows, cols)
        for c in range(0, hidden, WIDTH):
            if kind == "g":
                part = dot32(x, w_out_ref[c : c + WIDTH, :], TRANSPOSED)
            else:
                part = dot32(x, w_in_ref[:, c : c + WIDTH])
            out_ref[i * rows : (i + 1) * rows, c : c + WIDTH] = part.astype(BF)


def results(kinds, mine_ref, theirs_ref, w_in_ref, w_out_ref, out_ref, hold_ref):
    experts, _, cols = out_ref.shape
    rows = experts * SLOTS
    hidden = w_in_ref.shape[1]

    def total(i, c):
        span = (slice(i * rows, (i + 1) * rows), slice(c, c + WIDTH))
        return mine_ref[span].astype(F32) + theirs_ref[span].astype(F32)

    i, at = 0, 0
    while i < len(kinds):
        forward = kinds[i] == "f"
        for c in range(0, hidden, WIDTH):
            pre = total(i, c)
            sigma = 1.0 / (1.0 + jnp.exp(-pre))
            if forward:
                value = pre * sigma
            else:
                value = total(i + 1, c) * sigma * (1.0 + pre * (1.0 - sigma))
            hold_ref[:, c : c + WIDTH] = value.astype(BF)
        for c in range(0, cols, WIDTH):
            if forward:
                block = dot32(hold_ref[...], w_out_ref[:, c : c + WIDTH])
            else:
                block = dot32(hold_ref[...], w_in_ref[c : c + WIDTH, :], TRANSPOSED)
            out_ref[:, at : at + SLOTS, c : c + WIDTH] = block.astype(BF).reshape(
                experts, SLOTS, WIDTH
            )
        i += 1 if forward else 2
        at += SLOTS


def sums(count, *refs):
    mixes, back_ref, outs = refs[:count], refs[count], refs[count + 1 :]
    experts, _, cols = back_ref.shape
    for i in range(count):
        mix = mixes[i][...]
        for c in range(0, cols, WIDTH):
            rows = back_ref[:, i * SLOTS : (i + 1) * SLOTS, c : c + WIDTH]
            rows = rows.reshape(experts * SLOTS, WIDTH)
            outs[i][:, c : c + WIDTH] = dot32(mix, rows, OVER_ROWS).astype(BF)


def local(
    act_forward,
    routes_forward,
    gates_forward,
    act_backward,
    grad_backward,
    routes_backward,
    gates_backward,
    w_in,
    w_out,
):
    weight_in = w_in[0, 0]
    weight_out = w_out[0, 0]
    tok, cols = act_forward.shape
    hidden = weight_in.shape[1]
    top = routes_forward.shape[1]
    experts = lax.axis_size("x") * lax.axis_size("y")
    rows = experts * SLOTS
    first = (lax.axis_index("zhi") * experts).astype(jnp.int32).reshape(1)
    table = shaped(rows, tok)

    note = jnp.concatenate(
        [note_of(routes_forward, gates_forward), note_of(routes_backward, gates_backward)], axis=1
    )
    wide = jnp.pad(note, ((0, 0), (0, cols - note.shape[1])))

    def work(got, kinds, many):
        mine = run(
            functools.partial(parts, kinds),
            shaped(len(kinds) * rows, hidden),
            got,
            weight_in,
            weight_out,
        )
        theirs = other_core(mine)
        return pl.pallas_call(
            functools.partial(results, kinds),
            out_shape=shaped(experts, many * SLOTS, cols),
            in_specs=[pl.BlockSpec(memory_space=pltpu.VMEM)] * 4,
            out_specs=pl.BlockSpec(memory_space=pltpu.VMEM),
            scratch_shapes=[pltpu.VMEM((rows, hidden), BF)],
            compiler_params=pltpu.CompilerParams(vmem_limit_bytes=32 << 20),
            cost_estimate=pl.CostEstimate(flops=1000, bytes_accessed=1000, transcendentals=0),
        )(mine, theirs, weight_in, weight_out)

    def combined(back, *mixes):
        return run(
            functools.partial(sums, len(mixes)), (shaped(tok, cols),) * len(mixes), *mixes, back
        )

    far_b = moved(jnp.concatenate([act_backward, grad_backward, wide], axis=0), 0, True)
    far_f = moved(after(act_forward, far_b), 0, True)

    sent, mix_f, mix_b = run(
        functools.partial(pack_own, top),
        (shaped(experts, 3 * SLOTS, cols), table, table),
        first,
        act_forward,
        act_backward,
        grad_backward,
        note,
        scalars=1,
    )
    got = exchange(sent)
    sent_b, far_hit_f, far_mix_f, far_mix_b = run(
        functools.partial(pack_far, top),
        (shaped(experts, 2 * SLOTS, cols), table, table, table),
        first,
        after(far_b, got),
        scalars=1,
    )
    got_b = exchange(sent_b)
    out = work(after(got, sent_b), "fag", 2)
    sent_f = run(pack_more, shaped(experts, SLOTS, cols), far_hit_f, after(far_f, out))
    got_f = exchange(after(sent_f, got_b))
    out_b = work(after(got_b, sent_f), "ag", 1)
    back_b = exchange(after(out_b, got_f))
    out_f = work(after(got_f, out_b), "f", 1)
    back_f = exchange(after(out_f, back_b))
    (far_sum_b,) = combined(back_b, far_mix_b)
    over_b = moved(far_sum_b, -1, True)
    (far_sum_f,) = combined(back_f, far_mix_f)
    over_f = moved(far_sum_f, 1, True)
    sum_f, sum_b = combined(exchange(after(out, far_sum_f)), mix_f, mix_b)
    near_f = moved(sum_f, 1, False)
    near_b = moved(sum_b, -1, False)

    def both(a, b):
        return (a.astype(F32) + b.astype(F32)).astype(BF)

    return both(near_f, over_f), both(near_b, over_b)


def solution(mesh):
    devices = mesh.devices
    sections, nodes, locals_ = devices.shape
    fine = Mesh(
        devices.reshape(sections, nodes, 2, 4, locals_ // 8), ("section", "node", "zhi", "x", "y")
    )
    where = ("zhi", "x", "y")
    tokens = P(("section",) + where, "node")
    picks = P(("section",) + where, None)
    in_specs = (
        tokens,
        picks,
        picks,
        tokens,
        tokens,
        picks,
        picks,
        P("section", where, "node", None),
        P("section", where, None, "node"),
    )
    return jax.shard_map(
        local, mesh=fine, in_specs=in_specs, out_specs=(tokens, tokens), check_vma=False
    )
```

time: 292 us -> 289 us (0.990)
  the two profiles are of different devices: /device:TPU:33 before, /device:TPU:97 now
where the time goes in v4:
time: 289 us; the launch traced here: 288 us
  waiting for transfers between devices  125 us (43%)
  starting transfers between devices  97.9 us (34%)
  Pallas kernels  27.9 us (10%)
  blocking collectives  18.5 us (6%)
  local copies, waits for them, and re-layouts  13.3 us (5%)
  other arithmetic  4.74 us (2%)
    ppermute x6, waiting for transfers between devices, moved(): lax.ppermute(v, RING, pairs_of(shape, lambda s, h: ((s + by) % sections,...  83.9 us
    ppermute x6, starting transfers between devices, moved(): lax.ppermute(v, RING, pairs_of(shape, lambda s, h: ((s + by) % sections,...  53.5 us
    all_to_all x5, waiting for transfers between devices, exchange(): return lax.all_to_all(v, PLANE, split_axis=0, concat_axis=0, tiled=True)  39 us
    all_to_all x5, starting transfers between devices, exchange(): return lax.all_to_all(v, PLANE, split_axis=0, concat_axis=0, tiled=True)  28.5 us
    all_to_all x1, blocking collectives, exchange(): return lax.all_to_all(v, PLANE, split_axis=0, concat_axis=0, tiled=True)  18.5 us
    pallas_call x9, Pallas kernels, run(): pl.pallas_call(kernel, out_shape=outs, in_specs=where, out_specs=jax.tree...  17.4 us
    ppermute x3, starting transfers between devices, other_core(): return lax.ppermute(v, NODE, [(0, 1), (1, 0)])  16 us
    unnamed x44, local copies, waits for them, and re-layouts  13.3 us
  transfers between devices with their start and end apart: 14, of which 7 were waited for; matrix products, arithmetic and copies ran while one was open for 1% of the time, Pallas kernels for 5%

profile of v4, /device:TPU:97, one launch (start us, length us, event | category | flops | bytes accessed | tf_op | source)
XLA Modules:
  0.0 288.0 jit_solution(1905930157638602549)
XLA Ops:
  9.1 6.9 %all-to-all-start = ((bf16[16,96,1024]{2,1,0:T(8,128)(2,1)}), bf16[16,96,1024]{2,1,0:T(8,128)(2,1)}, u32[]{:S(2)}, u32[]{:S(2)}) async-start(bf16[16,96,1024]{2,1,0:T(8,128)(2,1)} %copy-done.5), calls=%async_computation | async-start | bytes 6291456 | tf_op jit(solution)/shard_map/all_to_all | solution.py:49
  17.1 12.8 %collective-permute-start = (bf16[272,1024]{1,0:T(8,128)(2,1)S(1)}, bf16[272,1024]{1,0:T(8,128)(2,1)S(1)}, u32[]{:S(2)}, u32[]{:S(2)}) collective-permute-start(bf16[272,1024]{1,0:T(8,128)(2,1)S(1)} %fusion.1), channel_id=1, source_target_pairs={{0,16},{1,17},{2,18},{3,19},{4,20},{5,21},{6,22},{7,23},{8,24},{9,... | collective-permute-start | bytes 1671176 | tf_op jit(solution)/shard_map/ppermute | solution.py:39
  29.9 34.2 %collective-permute-done.far_ref = bf16[272,1024]{1,0:T(8,128)(2,1)S(1)} collective-permute-done((bf16[272,1024]{1,0:T(8,128)(2,1)S(1)}, bf16[272,1024]{1,0:T(8,128)(2,1)S(1)}, u32[]{:S(2)}, u32[]{:S(2)}) %collective-permute-start) | collective-permute-done | bytes 557088 | tf_op jit(solution)/shard_map/ppermute | solution.py:39
  70.1 5.9 %shard_map.106.mine_ref = bf16[1536,768]{1,0:T(8,128)(2,1)} custom-call(bf16[16,96,1024]{2,1,0:T(8,128)(2,1)} %all-to-all-done.got_ref, bf16[1024,768]{1,0:T(8,128)(2,1)S(1)} %bitcast.9, bf16[768,1024]{1,0:T(8,128)(2,1)S(1)} %bitcast.15), custom_call_target="tpu_custom_call" | custom-call | flops 1000 | bytes 1000 | tf_op jit(solution)/shard_map/pallas_call | solution.py:63
  76.0 9.6 %collective-permute-start.1 = (bf16[1536,768]{1,0:T(8,128)(2,1)}, bf16[1536,768]{1,0:T(8,128)(2,1)}, u32[]{:S(2)}, u32[]{:S(2)}) collective-permute-start(bf16[1536,768]{1,0:T(8,128)(2,1)} %shard_map.106.mine_ref), channel_id=1, source_target_pairs={{0,32},{32,0},{1,33},{33,1},{2,34},{34,2},{3,35},{35,3},{4,36},{36... | collective-permute-start | bytes 7077896 | tf_op jit(solution)/shard_map/ppermute | solution.py:45
  85.7 6.7 %all-to-all-start.1 = ((bf16[16,64,1024]{2,1,0:T(8,128)(2,1)}), bf16[16,64,1024]{2,1,0:T(8,128)(2,1)}, u32[]{:S(2)}, u32[]{:S(2)}) async-start(bf16[16,64,1024]{2,1,0:T(8,128)(2,1)} %copy-done.6), calls=%async_computation.1 | async-start | bytes 4194304 | tf_op jit(solution)/shard_map/all_to_all | solution.py:49
  92.4 19.0 %collective-permute-start.2 = (bf16[128,1024]{1,0:T(8,128)(2,1)S(1)}, bf16[128,1024]{1,0:T(8,128)(2,1)S(1)}, u32[]{:S(2)}, u32[]{:S(2)}) collective-permute-start(bf16[128,1024]{1,0:T(8,128)(2,1)S(1)} %copy-done.13), channel_id=1, source_target_pairs={{0,16},{1,17},{2,18},{3,19},{4,20},{5,21},{6,22},{7,23},{8,24},{9,... | collective-permute-start | bytes 786440 | tf_op jit(solution)/shard_map/ppermute | solution.py:39
  111.4 6.0 %shard_map.107 = bf16[16,64,1024]{2,1,0:T(8,128)(2,1)} custom-call(bf16[1536,768]{1,0:T(8,128)(2,1)} %shard_map.106.mine_ref, bf16[1536,768]{1,0:T(8,128)(2,1)} %collective-permute-done.1.theirs_ref, bf16[1024,768]{1,0:T(8,128)(2,1)S(1)} %bitcast.10, bf16[768,1024]{1,0:T(8,128)(2,1)S(1)} %bitcast.16), custom_call_target="tpu_custom_call" | custom-call | flops 1000 | bytes 1000 | tf_op jit(solution)/shard_map/pallas_call | solution.py:234
  117.4 5.9 %collective-permute-done.2.rows_ref = bf16[128,1024]{1,0:T(8,128)(2,1)S(1)} collective-permute-done((bf16[128,1024]{1,0:T(8,128)(2,1)S(1)}, bf16[128,1024]{1,0:T(8,128)(2,1)S(1)}, u32[]{:S(2)}, u32[]{:S(2)}) %collective-permute-start.2) | collective-permute-done | bytes 262176 | tf_op jit(solution)/shard_map/ppermute | solution.py:39
  124.7 4.6 %shard_map.109.mine_ref = bf16[1024,768]{1,0:T(8,128)(2,1)} custom-call(bf16[16,64,1024]{2,1,0:T(8,128)(2,1)} %all-to-all-done.1.got_ref, bf16[1024,768]{1,0:T(8,128)(2,1)S(1)} %bitcast.11, bf16[768,1024]{1,0:T(8,128)(2,1)S(1)} %bitcast.17), custom_call_target="tpu_custom_call" | custom-call | flops 1000 | bytes 1000 | tf_op jit(solution)/shard_map/pallas_call | solution.py:63
  129.4 2.5 collective-permute-start.3
  131.9 6.7 %all-to-all-start.2 = ((bf16[16,32,1024]{2,1,0:T(8,128)(2,1)}), bf16[16,32,1024]{2,1,0:T(8,128)(2,1)}, u32[]{:S(2)}, u32[]{:S(2)}) async-start(bf16[16,32,1024]{2,1,0:T(8,128)(2,1)} %copy-done.3), calls=%async_computation.2 | async-start | bytes 2097152 | tf_op jit(solution)/shard_map/all_to_all | solution.py:49
  138.5 3.3 %shard_map.110 = bf16[16,32,1024]{2,1,0:T(8,128)(2,1)S(1)} custom-call(bf16[1024,768]{1,0:T(8,128)(2,1)} %shard_map.109.mine_ref, bf16[1024,768]{1,0:T(8,128)(2,1)} %collective-permute-done.3.theirs_ref, bf16[1024,768]{1,0:T(8,128)(2,1)S(1)} %bitcast.12, bf16[768,1024]{1,0:T(8,128)(2,1)S(1)} %bitcast.18), custom_call_target="tpu_custom_call" | custom-call | flops 1000 | bytes 1000 | tf_op jit(solution)/shard_map/pallas_call | solution.py:234
  142.8 12.7 %all-to-all-done.2.got_ref = bf16[16,32,1024]{2,1,0:T(8,128)(2,1)} async-done(((bf16[16,32,1024]{2,1,0:T(8,128)(2,1)}), bf16[16,32,1024]{2,1,0:T(8,128)(2,1)}, u32[]{:S(2)}, u32[]{:S(2)}) %all-to-all-start.2) | async-done | bytes 1048608 | tf_op jit(solution)/shard_map/all_to_all | solution.py:49
  155.6 4.3 %all-to-all-start.3 = ((bf16[16,32,1024]{2,1,0:T(8,128)(2,1)}), bf16[16,32,1024]{2,1,0:T(8,128)(2,1)}, u32[]{:S(2)}, u32[]{:S(2)}) async-start(bf16[16,32,1024]{2,1,0:T(8,128)(2,1)} %copy-done.2), calls=%async_computation.3 | async-start | bytes 2097152 | tf_op jit(solution)/shard_map/all_to_all | solution.py:49
  159.9 2.2 shard_map.111.mine_ref
  162.1 3.9 %collective-permute-start.4 = (bf16[512,768]{1,0:T(8,128)(2,1)S(1)}, bf16[512,768]{1,0:T(8,128)(2,1)S(1)}, u32[]{:S(2)}, u32[]{:S(2)}) collective-permute-start(bf16[512,768]{1,0:T(8,128)(2,1)S(1)} %shard_map.111.mine_ref), channel_id=1, source_target_pairs={{0,32},{32,0},{1,33},{33,1},{2,34},{34,2},{3,35},{35,3},{4,36},{36... | collective-permute-start | bytes 2359304 | tf_op jit(solution)/shard_map/ppermute | solution.py:45
  169.8 5.2 %all-to-all-done.3.refs_1_ = bf16[16,32,1024]{2,1,0:T(8,128)(2,1)} async-done(((bf16[16,32,1024]{2,1,0:T(8,128)(2,1)}), bf16[16,32,1024]{2,1,0:T(8,128)(2,1)}, u32[]{:S(2)}, u32[]{:S(2)}) %all-to-all-start.3) | async-done | bytes 1048608 | tf_op jit(solution)/shard_map/all_to_all | solution.py:49
  175.0 18.5 %all_to_all.30.refs_1_ = bf16[16,32,1024]{2,1,0:T(8,128)(2,1)S(1)} all-to-all(bf16[16,32,1024]{2,1,0:T(8,128)(2,1)} %copy-done.4), channel_id=1, replica_groups=mesh['section'=8,'node'=2,'zhi'=2,'x'=4,'y'=4] {'x','y'}, dimensions={0} | all-to-all | bytes 2097152 | tf_op jit(solution)/shard_map/all_to_all | solution.py:49
  193.8 3.9 %all-to-all-start.5 = ((bf16[16,64,1024]{2,1,0:T(8,128)(2,1)}), bf16[16,64,1024]{2,1,0:T(8,128)(2,1)S(1)}, u32[]{:S(2)}, u32[]{:S(2)}) async-start(bf16[16,64,1024]{2,1,0:T(8,128)(2,1)} %shard_map.107), calls=%async_computation.5 | async-start | bytes 4194304 | tf_op jit(solution)/shard_map/all_to_all | solution.py:49
  199.3 2.3 collective-permute-start.8
  201.6 21.1 %all-to-all-done.5.refs_2_ = bf16[16,64,1024]{2,1,0:T(8,128)(2,1)S(1)} async-done(((bf16[16,64,1024]{2,1,0:T(8,128)(2,1)}), bf16[16,64,1024]{2,1,0:T(8,128)(2,1)S(1)}, u32[]{:S(2)}, u32[]{:S(2)}) %all-to-all-start.5) | async-done | bytes 2097184 | tf_op jit(solution)/shard_map/all_to_all | solution.py:49
  225.1 15.6 %collective-permute-start.6 = (bf16[128,1024]{1,0:T(8,128)(2,1)S(1)}, bf16[128,1024]{1,0:T(8,128)(2,1)S(1)}, u32[]{:S(2)}, u32[]{:S(2)}) collective-permute-start(bf16[128,1024]{1,0:T(8,128)(2,1)S(1)} %shard_map.113), channel_id=1, source_target_pairs={{0,80},{1,81},{2,82},{3,83},{4,84},{5,85},{6,86},{7,87},{8,88},{9,... | collective-permute-start | bytes 786440 | tf_op jit(solution)/shard_map/ppermute | solution.py:39
  243.4 43.8 %collective-permute-done.6 = bf16[128,1024]{1,0:T(8,128)(2,1)S(1)} collective-permute-done((bf16[128,1024]{1,0:T(8,128)(2,1)S(1)}, bf16[128,1024]{1,0:T(8,128)(2,1)S(1)}, u32[]{:S(2)}, u32[]{:S(2)}) %collective-permute-start.6) | collective-permute-done | bytes 262176 | tf_op jit(solution)/shard_map/ppermute | solution.py:39
  (68 shorter events, 29.4 us)
Async XLA Ops:
  6.7 1.7 copy-start.5
  9.1 6.9 %copy-start.8 = (bf16[128,1024]{1,0:T(8,128)(2,1)S(1)}, bf16[128,1024]{1,0:T(8,128)(2,1)}, u32[]{:S(2)}) copy-start(bf16[128,1024]{1,0:T(8,128)(2,1)} %g_ref.1) | copy-start | bytes 786436
  9.1 61.1 %copy-start.1 = (bf16[1,1,768,1024]{3,2,1,0:T(8,128)(2,1)S(1)}, bf16[1,1,768,1024]{3,2,1,0:T(8,128)(2,1)}, u32[]{:S(2)}) copy-start(bf16[1,1,768,1024]{3,2,1,0:T(8,128)(2,1)} %param.17) | copy-start | bytes 4718596
  9.1 55.8 %all-to-all-start = ((bf16[16,96,1024]{2,1,0:T(8,128)(2,1)}), bf16[16,96,1024]{2,1,0:T(8,128)(2,1)}, u32[]{:S(2)}, u32[]{:S(2)}) async-start(bf16[16,96,1024]{2,1,0:T(8,128)(2,1)} %copy-done.5), calls=%async_computation | async-start | bytes 6291456 | tf_op jit(solution)/shard_map/all_to_all | solution.py:49
  16.0 54.1 %copy-start = (bf16[1,1,1024,768]{3,2,1,0:T(8,128)(2,1)S(1)}, bf16[1,1,1024,768]{3,2,1,0:T(8,128)(2,1)}, u32[]{:S(2)}) copy-start(bf16[1,1,1024,768]{3,2,1,0:T(8,128)(2,1)} %param.16) | copy-start | bytes 4718596
  17.1 47.0 %collective-permute-start = (bf16[272,1024]{1,0:T(8,128)(2,1)S(1)}, bf16[272,1024]{1,0:T(8,128)(2,1)S(1)}, u32[]{:S(2)}, u32[]{:S(2)}) collective-permute-start(bf16[272,1024]{1,0:T(8,128)(2,1)S(1)} %fusion.1), channel_id=1, source_target_pairs={{0,16},{1,17},{2,18},{3,19},{4,20},{5,21},{6,22},{7,23},{8,24},{9,... | collective-permute-start | bytes 1671176 | tf_op jit(solution)/shard_map/ppermute | solution.py:39
  66.8 1.4 copy-start.6
  76.0 16.3 %copy-start.13 = (bf16[128,1024]{1,0:T(8,128)(2,1)S(1)}, bf16[128,1024]{1,0:T(8,128)(2,1)}, u32[]{:S(2)}) copy-start(bf16[128,1024]{1,0:T(8,128)(2,1)} %f_ref.1) | copy-start | bytes 786436
  76.0 35.3 %collective-permute-start.1 = (bf16[1536,768]{1,0:T(8,128)(2,1)}, bf16[1536,768]{1,0:T(8,128)(2,1)}, u32[]{:S(2)}, u32[]{:S(2)}) collective-permute-start(bf16[1536,768]{1,0:T(8,128)(2,1)} %shard_map.106.mine_ref), channel_id=1, source_target_pairs={{0,32},{32,0},{1,33},{33,1},{2,34},{34,2},{3,35},{35,3},{4,36},{36... | collective-permute-start | bytes 7077896 | tf_op jit(solution)/shard_map/ppermute | solution.py:45
  85.7 39.0 %all-to-all-start.1 = ((bf16[16,64,1024]{2,1,0:T(8,128)(2,1)}), bf16[16,64,1024]{2,1,0:T(8,128)(2,1)}, u32[]{:S(2)}, u32[]{:S(2)}) async-start(bf16[16,64,1024]{2,1,0:T(8,128)(2,1)} %copy-done.6), calls=%async_computation.1 | async-start | bytes 4194304 | tf_op jit(solution)/shard_map/all_to_all | solution.py:49
  92.4 30.9 %copy-start.21 = (bf16[512,128]{1,0:T(8,128)(2,1)S(1)}, bf16[512,128]{1,0:T(8,128)(2,1)}, u32[]{:S(2)}) copy-start(bf16[512,128]{1,0:T(8,128)(2,1)} %copy-done.20) | copy-start | bytes 393220
  92.4 30.9 %collective-permute-start.2 = (bf16[128,1024]{1,0:T(8,128)(2,1)S(1)}, bf16[128,1024]{1,0:T(8,128)(2,1)S(1)}, u32[]{:S(2)}, u32[]{:S(2)}) collective-permute-start(bf16[128,1024]{1,0:T(8,128)(2,1)S(1)} %copy-done.13), channel_id=1, source_target_pairs={{0,16},{1,17},{2,18},{3,19},{4,20},{5,21},{6,22},{7,23},{8,24},{9,... | collective-permute-start | bytes 786440 | tf_op jit(solution)/shard_map/ppermute | solution.py:39
  129.4 9.2 %collective-permute-start.3 = (bf16[1024,768]{1,0:T(8,128)(2,1)}, bf16[1024,768]{1,0:T(8,128)(2,1)}, u32[]{:S(2)}, u32[]{:S(2)}) collective-permute-start(bf16[1024,768]{1,0:T(8,128)(2,1)} %shard_map.109.mine_ref), channel_id=1, source_target_pairs={{0,32},{32,0},{1,33},{33,1},{2,34},{34,2},{3,35},{35,3},{4,36},{36... | collective-permute-start | bytes 4718600 | tf_op jit(solution)/shard_map/ppermute | solution.py:45
  131.9 23.7 %all-to-all-start.2 = ((bf16[16,32,1024]{2,1,0:T(8,128)(2,1)}), bf16[16,32,1024]{2,1,0:T(8,128)(2,1)}, u32[]{:S(2)}, u32[]{:S(2)}) async-start(bf16[16,32,1024]{2,1,0:T(8,128)(2,1)} %copy-done.3), calls=%async_computation.2 | async-start | bytes 2097152 | tf_op jit(solution)/shard_map/all_to_all | solution.py:49
  155.6 19.4 %all-to-all-start.3 = ((bf16[16,32,1024]{2,1,0:T(8,128)(2,1)}), bf16[16,32,1024]{2,1,0:T(8,128)(2,1)}, u32[]{:S(2)}, u32[]{:S(2)}) async-start(bf16[16,32,1024]{2,1,0:T(8,128)(2,1)} %copy-done.2), calls=%async_computation.3 | async-start | bytes 2097152 | tf_op jit(solution)/shard_map/all_to_all | solution.py:49
  162.1 5.6 %collective-permute-start.4 = (bf16[512,768]{1,0:T(8,128)(2,1)S(1)}, bf16[512,768]{1,0:T(8,128)(2,1)S(1)}, u32[]{:S(2)}, u32[]{:S(2)}) collective-permute-start(bf16[512,768]{1,0:T(8,128)(2,1)S(1)} %shard_map.111.mine_ref), channel_id=1, source_target_pairs={{0,32},{32,0},{1,33},{33,1},{2,34},{34,2},{3,35},{35,3},{4,36},{36... | collective-permute-start | bytes 2359304 | tf_op jit(solution)/shard_map/ppermute | solution.py:45
  169.8 23.7 %copy-start.19 = (bf16[512,128]{1,0:T(8,128)(2,1)S(1)}, bf16[512,128]{1,0:T(8,128)(2,1)}, u32[]{:S(2)}) copy-start(bf16[512,128]{1,0:T(8,128)(2,1)} %copy-done.18) | copy-start | bytes 393220
  193.8 3.9 %copy-start.17 = (bf16[512,128]{1,0:T(8,128)(2,1)S(1)}, bf16[512,128]{1,0:T(8,128)(2,1)}, u32[]{:S(2)}) copy-start(bf16[512,128]{1,0:T(8,128)(2,1)} %copy-done.16) | copy-start | bytes 393220
  193.8 28.9 %copy-start.15 = (bf16[512,128]{1,0:T(8,128)(2,1)S(1)}, bf16[512,128]{1,0:T(8,128)(2,1)}, u32[]{:S(2)}) copy-start(bf16[512,128]{1,0:T(8,128)(2,1)} %copy-done.14) | copy-start | bytes 393220
  193.8 28.9 %all-to-all-start.5 = ((bf16[16,64,1024]{2,1,0:T(8,128)(2,1)}), bf16[16,64,1024]{2,1,0:T(8,128)(2,1)S(1)}, u32[]{:S(2)}, u32[]{:S(2)}) async-start(bf16[16,64,1024]{2,1,0:T(8,128)(2,1)} %shard_map.107), calls=%async_computation.5 | async-start | bytes 4194304 | tf_op jit(solution)/shard_map/all_to_all | solution.py:49
  199.3 43.4 %collective-permute-start.8 = (bf16[128,1024]{1,0:T(8,128)(2,1)S(1)}, bf16[128,1024]{1,0:T(8,128)(2,1)S(1)}, u32[]{:S(2)}, u32[]{:S(2)}) collective-permute-start(bf16[128,1024]{1,0:T(8,128)(2,1)S(1)} %shard_map.115), channel_id=1, source_target_pairs={{0,464},{1,465},{2,466},{3,467},{4,468},{5,469},{6,470},{7,471},{8... | collective-permute-start | bytes 786440 | tf_op jit(solution)/shard_map/ppermute | solution.py:39
  223.2 19.5 %collective-permute-start.7 = (bf16[128,1024]{1,0:T(8,128)(2,1)S(1)}, bf16[128,1024]{1,0:T(8,128)(2,1)S(1)}, u32[]{:S(2)}, u32[]{:S(2)}) collective-permute-start(bf16[128,1024]{1,0:T(8,128)(2,1)S(1)} %get-tuple-element.38), channel_id=1, source_target_pairs={{0,448},{1,449},{2,450},{3,451},{4,452},{5,453},{6,454},{7,455},{8... | collective-permute-start | bytes 786440 | tf_op jit(solution)/shard_map/ppermute | solution.py:39
  225.1 62.2 %collective-permute-start.6 = (bf16[128,1024]{1,0:T(8,128)(2,1)S(1)}, bf16[128,1024]{1,0:T(8,128)(2,1)S(1)}, u32[]{:S(2)}, u32[]{:S(2)}) collective-permute-start(bf16[128,1024]{1,0:T(8,128)(2,1)S(1)} %shard_map.113), channel_id=1, source_target_pairs={{0,80},{1,81},{2,82},{3,83},{4,84},{5,85},{6,86},{7,87},{8,88},{9,... | collective-permute-start | bytes 786440 | tf_op jit(solution)/shard_map/ppermute | solution.py:39
  240.7 46.6 %collective-permute-start.5 = (bf16[128,1024]{1,0:T(8,128)(2,1)S(1)}, bf16[128,1024]{1,0:T(8,128)(2,1)S(1)}, u32[]{:S(2)}, u32[]{:S(2)}) collective-permute-start(bf16[128,1024]{1,0:T(8,128)(2,1)S(1)} %get-tuple-element.37), channel_id=1, source_target_pairs={{0,64},{1,65},{2,66},{3,67},{4,68},{5,69},{6,70},{7,71},{8,72},{9,... | collective-permute-start | bytes 786440 | tf_op jit(solution)/shard_map/ppermute | solution.py:39
  (12 other events, 10.3 us)

commit v5 on v4

--- a/solution.py
+++ b/solution.py
@@ -17,6 +17,7 @@
 TRANSPOSED = (((1,), (1,)), ((), ()))
 OVER_ROWS = (((0,), (0,)), ((), ()))
 WIDTH = 256
+LONG = 40_000_000_000
 
 
 def pairs_of(shape, move):
@@ -45,6 +46,11 @@
     return lax.ppermute(v, NODE, [(0, 1), (1, 0)])
 
 
+def in_pieces(v, count):
+    each = v.shape[0] // count
+    return jnp.concatenate([other_core(v[i * each : (i + 1) * each]) for i in range(count)], axis=0)
+
+
 def exchange(v):
     return lax.all_to_all(v, PLANE, split_axis=0, concat_axis=0, tiled=True)
 
@@ -57,7 +63,7 @@
     return lax.dot_general(a, b, dims, preferred_element_type=F32)
 
 
-def run(kernel, outs, *args, scalars=0):
+def run(kernel, outs, *args, scalars=0, scratch=(), flops=1000):
     where = [pl.BlockSpec(memory_space=pltpu.SMEM)] * scalars
     where += [pl.BlockSpec(memory_space=pltpu.VMEM)] * (len(args) - scalars)
     return pl.pallas_call(
@@ -65,8 +71,9 @@
         out_shape=outs,
         in_specs=where,
         out_specs=jax.tree.map(lambda _: pl.BlockSpec(memory_space=pltpu.VMEM), outs),
+        scratch_shapes=scratch,
         compiler_params=pltpu.CompilerParams(vmem_limit_bytes=32 << 20),
-        cost_estimate=pl.CostEstimate(flops=1000, bytes_accessed=1000, transcendentals=0),
+        cost_estimate=pl.CostEstimate(flops=flops, bytes_accessed=1000, transcendentals=0),
     )(*args)
 
 
@@ -74,9 +81,18 @@
     return jax.ShapeDtypeStruct(shape, BF)
 
 
-def note_of(routes, gates):
-    note = jnp.concatenate([routes.astype(BF).T, gates.T], axis=0)
-    return jnp.pad(note, ((0, 16 - note.shape[0]), (0, 0)))
+def gather_block(a_ref, g_ref, *refs):
+    notes, out_ref, hold_ref = refs[:4], refs[4], refs[5]
+    tokens = a_ref.shape[0]
+    top = notes[0].shape[0]
+    out_ref[:tokens, :] = a_ref[...]
+    out_ref[tokens : 2 * tokens, :] = g_ref[...]
+    hold_ref[...] = jnp.zeros(hold_ref.shape, F32)
+    for half in range(2):
+        span = slice(half * tokens, (half + 1) * tokens)
+        hold_ref[:top, span] = notes[2 * half][...].astype(F32)
+        hold_ref[8 : 8 + top, span] = notes[2 * half + 1][...].astype(F32)
+    out_ref[2 * tokens :, :] = hold_ref[...].astype(BF)
 
 
 def tables(note, first, top, experts):
@@ -87,7 +103,7 @@
     for k in range(top):
         match = note[k : k + 1] == label
         chosen = chosen + jnp.where(match, 1.0, 0.0)
-        weight = weight + jnp.where(match, note[top + k : top + k + 1], 0.0)
+        weight = weight + jnp.where(match, note[8 + k : 9 + k], 0.0)
     i = lax.broadcasted_iota(jnp.int32, (tokens, tokens), 0)
     j = lax.broadcasted_iota(jnp.int32, (tokens, tokens), 1)
     earlier = jnp.where(i < j, 1.0, 0.0).astype(BF)
@@ -113,26 +129,22 @@
         out_ref[:, at : at + SLOTS, c : c + WIDTH] = block.reshape(experts, SLOTS, WIDTH)
 
 
-def pack_own(top, first_ref, f_ref, a_ref, g_ref, note_ref, out_ref, mix_f_ref, mix_b_ref):
-    (hit_f, mix_f), (hit_b, mix_b) = tables(
-        note_ref[...].astype(F32), first_ref[0], top, out_ref.shape[0]
-    )
+def pack_first(top, near, *refs):
+    if near:
+        first_ref, block_ref, f_ref, out_ref, mix_f_ref, mix_b_ref = refs
+    else:
+        first_ref, block_ref, out_ref, mix_f_ref, mix_b_ref, hit_f_ref = refs
+    tokens = mix_f_ref.shape[1]
+    note = block_ref[2 * tokens :, : 2 * tokens].astype(F32)
+    (hit_f, mix_f), (hit_b, mix_b) = tables(note, first_ref[0], top, out_ref.shape[0])
     mix_f_ref[...] = mix_f
     mix_b_ref[...] = mix_b
-    put(out_ref, 0, hit_f, f_ref)
-    put(out_ref, SLOTS, hit_b, a_ref)
-    put(out_ref, 2 * SLOTS, hit_b, g_ref)
-
-
-def pack_far(top, first_ref, far_ref, out_ref, hit_f_ref, mix_f_ref, mix_b_ref):
-    tokens = hit_f_ref.shape[1]
-    note = far_ref[2 * tokens :, : 2 * tokens].astype(F32)
-    (hit_f, mix_f), (hit_b, mix_b) = tables(note, first_ref[0], top, out_ref.shape[0])
-    hit_f_ref[...] = hit_f
-    mix_f_ref[...] = mix_f
-    mix_b_ref[...] = mix_b
-    put(out_ref, 0, hit_b, far_ref)
-    put(out_ref, SLOTS, hit_b, far_ref, tokens)
+    put(out_ref, 0, hit_b, block_ref)
+    put(out_ref, SLOTS, hit_b, block_ref, tokens)
+    if near:
+        put(out_ref, 2 * SLOTS, hit_f, f_ref)
+    else:
+        hit_f_ref[...] = hit_f
 
 
 def pack_more(hit_ref, rows_ref, out_ref):
@@ -153,7 +165,8 @@
             out_ref[i * rows : (i + 1) * rows, c : c + WIDTH] = part.astype(BF)
 
 
-def results(kinds, mine_ref, theirs_ref, w_in_ref, w_out_ref, out_ref, hold_ref):
+def results(kinds, held, mine_ref, theirs_ref, w_in_ref, w_out_ref, *refs):
+    out_ref, hold_ref = refs[-2:]
     experts, _, cols = out_ref.shape
     rows = experts * SLOTS
     hidden = w_in_ref.shape[1]
@@ -163,6 +176,9 @@
         return mine_ref[span].astype(F32) + theirs_ref[span].astype(F32)
 
     i, at = 0, 0
+    if held:
+        at = refs[0].shape[1]
+        out_ref[:, :at, :] = refs[0][...]
     while i < len(kinds):
         forward = kinds[i] == "f"
         for c in range(0, hidden, WIDTH):
@@ -196,6 +212,16 @@
             outs[i][:, c : c + WIDTH] = dot32(mix, rows, OVER_ROWS).astype(BF)
 
 
+def hold(a_ref, b_ref, x_ref, y_ref):
+    x_ref[...] = a_ref[...]
+    y_ref[...] = b_ref[...]
+
+
+def add(a_ref, b_ref, c_ref, d_ref, x_ref, y_ref):
+    x_ref[...] = (a_ref[...].astype(F32) + c_ref[...].astype(F32)).astype(BF)
+    y_ref[...] = (b_ref[...].astype(F32) + d_ref[...].astype(F32)).astype(BF)
+
+
 def local(
     act_forward,
     routes_forward,
@@ -217,12 +243,7 @@
     first = (lax.axis_index("zhi") * experts).astype(jnp.int32).reshape(1)
     table = shaped(rows, tok)
 
-    note = jnp.concatenate(
-        [note_of(routes_forward, gates_forward), note_of(routes_backward, gates_backward)], axis=1
-    )
-    wide = jnp.pad(note, ((0, 0), (0, cols - note.shape[1])))
-
-    def work(got, kinds, many):
+    def work(got, kinds, *held):
         mine = run(
             functools.partial(parts, kinds),
             shaped(len(kinds) * rows, hidden),
@@ -230,63 +251,71 @@
             weight_in,
             weight_out,
         )
-        theirs = other_core(mine)
-        return pl.pallas_call(
-            functools.partial(results, kinds),
-            out_shape=shaped(experts, many * SLOTS, cols),
-            in_specs=[pl.BlockSpec(memory_space=pltpu.VMEM)] * 4,
-            out_specs=pl.BlockSpec(memory_space=pltpu.VMEM),
-            scratch_shapes=[pltpu.VMEM((rows, hidden), BF)],
-            compiler_params=pltpu.CompilerParams(vmem_limit_bytes=32 << 20),
-            cost_estimate=pl.CostEstimate(flops=1000, bytes_accessed=1000, transcendentals=0),
-        )(mine, theirs, weight_in, weight_out)
+        theirs = other_core(mine) if len(kinds) < 2 else in_pieces(mine, len(kinds))
+        many = kinds.count("f") + kinds.count("a") + len(held)
+        return run(
+            functools.partial(results, kinds, len(held)),
+            shaped(experts, many * SLOTS, cols),
+            mine,
+            theirs,
+            weight_in,
+            weight_out,
+            *held,
+            scratch=[pltpu.VMEM((rows, hidden), BF)],
+        )
 
     def combined(back, *mixes):
         return run(
             functools.partial(sums, len(mixes)), (shaped(tok, cols),) * len(mixes), *mixes, back
         )
 
-    far_b = moved(jnp.concatenate([act_backward, grad_backward, wide], axis=0), 0, True)
-    far_f = moved(after(act_forward, far_b), 0, True)
+    block = run(
+        gather_block,
+        shaped(2 * tok + 16, cols),
+        act_backward,
+        grad_backward,
+        routes_forward.T,
+        gates_forward.T,
+        routes_backward.T,
+        gates_backward.T,
+        scratch=[pltpu.VMEM((16, cols), F32)],
+    )
+    far_block = moved(block, 0, True)
+    far_rows = moved(after(act_forward, far_block), 0, True)
 
     sent, mix_f, mix_b = run(
-        functools.partial(pack_own, top),
+        functools.partial(pack_first, top, True),
         (shaped(experts, 3 * SLOTS, cols), table, table),
         first,
+        block,
         act_forward,
-        act_backward,
-        grad_backward,
-        note,
         scalars=1,
     )
     got = exchange(sent)
-    sent_b, far_hit_f, far_mix_f, far_mix_b = run(
-        functools.partial(pack_far, top),
+    sent_b, far_mix_f, far_mix_b, far_hit_f = run(
+        functools.partial(pack_first, top, False),
         (shaped(experts, 2 * SLOTS, cols), table, table, table),
         first,
-        after(far_b, got),
+        far_block,
         scalars=1,
-    )
-    got_b = exchange(sent_b)
-    out = work(after(got, sent_b), "fag", 2)
-    sent_f = run(pack_more, shaped(experts, SLOTS, cols), far_hit_f, after(far_f, out))
+        flops=LONG,
+    )
+    got_b = exchange(after(sent_b, got))
+    sent_f = run(pack_more, shaped(experts, SLOTS, cols), far_hit_f, far_rows, flops=LONG)
     got_f = exchange(after(sent_f, got_b))
-    out_b = work(after(got_b, sent_f), "ag", 1)
-    back_b = exchange(after(out_b, got_f))
-    out_f = work(after(got_f, out_b), "f", 1)
-    back_f = exchange(after(out_f, back_b))
-    (far_sum_b,) = combined(back_b, far_mix_b)
-    over_b = moved(far_sum_b, -1, True)
-    (far_sum_f,) = combined(back_f, far_mix_f)
-    over_f = moved(far_sum_f, 1, True)
-    sum_f, sum_b = combined(exchange(after(out, far_sum_f)), mix_f, mix_b)
-    near_f = moved(sum_f, 1, False)
-    near_b = moved(sum_b, -1, False)
-
-    def both(a, b):
-        return (a.astype(F32) + b.astype(F32)).astype(BF)
-
-    return both(near_f, over_f), both(near_b, over_b)
+    out_b = work(after(got_b, sent_f), "ag")
+    out_bf = work(after(got_f, out_b), "f", out_b)
+    far_out = exchange(out_bf)
+    out = work(after(got, out_bf), "agf")
+    far_sum_b, far_sum_f = combined(after(far_out, out), far_mix_b, far_mix_f)
+    over = (moved(far_sum_b, -1, True), moved(far_sum_f, 1, True))
+    back = exchange(after(out, far_sum_f))
+    sum_b, sum_f = combined(back, mix_b, mix_f)
+    near = (moved(sum_b, -1, False), moved(sum_f, 1, False))
+    pair = (shaped(tok, cols),) * 2
+    over = run(hold, pair, *over, flops=LONG)
+    input_grad, layer_out = run(add, pair, *near, *over)
+    return layer_out, input_grad
 
 
 def solution(mesh):

time: 289 us -> 255 us (0.88)
  the two profiles are of different devices: /device:TPU:97 before, /device:TPU:1 now
where the time goes in v5:
time: 255 us; the launch traced here: 254 us
  starting transfers between devices  112 us (44%)
  waiting for transfers between devices  99.2 us (39%)
  Pallas kernels  24.4 us (10%)
  local copies, waits for them, and re-layouts  17.5 us (7%)
    ppermute x6, starting transfers between devices, moved(): lax.ppermute(v, RING, pairs_of(shape, lambda s, h: ((s + by) % sections,...  63.4 us
    all_to_all x5, waiting for transfers between devices, exchange(): return lax.all_to_all(v, PLANE, split_axis=0, concat_axis=0, tiled=True)  59.2 us
    ppermute x6, waiting for transfers between devices, moved(): lax.ppermute(v, RING, pairs_of(shape, lambda s, h: ((s + by) % sections,...  34.2 us
    all_to_all x5, starting transfers between devices, exchange(): return lax.all_to_all(v, PLANE, split_axis=0, concat_axis=0, tiled=True)  29.5 us
    pallas_call x14, Pallas kernels, run(): pl.pallas_call(kernel, out_shape=outs, in_specs=where, out_specs=jax.tree...  24.4 us
    ppermute x6, starting transfers between devices, other_core(): return lax.ppermute(v, NODE, [(0, 1), (1, 0)])  18.6 us
    unnamed x52, local copies, waits for them, and re-layouts  17.3 us
    ppermute x6, waiting for transfers between devices, other_core(): return lax.ppermute(v, NODE, [(0, 1), (1, 0)])  5.83 us
  transfers between devices with their start and end apart: 17, of which 12 were waited for; matrix products, arithmetic and copies ran while one was open for 0% of the time, Pallas kernels for 7%

profile of v5, /device:TPU:1, one launch (start us, length us, event | category | flops | bytes accessed | tf_op | source)
XLA Modules:
  0.0 253.9 jit_solution(15545431673820473255)
XLA Ops:
  6.1 16.3 %collective-permute-start = (bf16[272,1024]{1,0:T(8,128)(2,1)}, bf16[272,1024]{1,0:T(8,128)(2,1)}, u32[]{:S(2)}, u32[]{:S(2)}) collective-permute-start(bf16[272,1024]{1,0:T(8,128)(2,1)} %shard_map.104.refs_1_), channel_id=1, source_target_pairs={{0,16},{1,17},{2,18},{3,19},{4,20},{5,21},{6,22},{7,23},{8,24},{9,... | collective-permute-start | bytes 1671176 | tf_op jit(solution)/shard_map/ppermute | solution.py:40
  27.8 6.9 %all-to-all-start = ((bf16[16,96,1024]{2,1,0:T(8,128)(2,1)}), bf16[16,96,1024]{2,1,0:T(8,128)(2,1)S(1)}, u32[]{:S(2)}, u32[]{:S(2)}) async-start(bf16[16,96,1024]{2,1,0:T(8,128)(2,1)} %copy-done.7), calls=%async_computation | async-start | bytes 6291456 | tf_op jit(solution)/shard_map/all_to_all | solution.py:55
  34.7 3.6 %collective-permute-done.refs_1_ = bf16[272,1024]{1,0:T(8,128)(2,1)} collective-permute-done((bf16[272,1024]{1,0:T(8,128)(2,1)}, bf16[272,1024]{1,0:T(8,128)(2,1)}, u32[]{:S(2)}, u32[]{:S(2)}) %collective-permute-start) | collective-permute-done | bytes 557088 | tf_op jit(solution)/shard_map/ppermute | solution.py:40
  38.4 12.9 %collective-permute-start.1 = (bf16[128,1024]{1,0:T(8,128)(2,1)S(1)}, bf16[128,1024]{1,0:T(8,128)(2,1)}, u32[]{:S(2)}, u32[]{:S(2)}) collective-permute-start(bf16[128,1024]{1,0:T(8,128)(2,1)S(1)} %copy-done.13), channel_id=1, source_target_pairs={{0,16},{1,17},{2,18},{3,19},{4,20},{5,21},{6,22},{7,23},{8,24},{9,... | collective-permute-start | bytes 786440 | tf_op jit(solution)/shard_map/ppermute | solution.py:40
  56.4 18.8 %all-to-all-done.got_ref = bf16[16,96,1024]{2,1,0:T(8,128)(2,1)S(1)} async-done(((bf16[16,96,1024]{2,1,0:T(8,128)(2,1)}), bf16[16,96,1024]{2,1,0:T(8,128)(2,1)S(1)}, u32[]{:S(2)}, u32[]{:S(2)}) %all-to-all-start) | async-done | bytes 3145760 | tf_op jit(solution)/shard_map/all_to_all | solution.py:55
  75.3 5.7 %all-to-all-start.1 = ((bf16[16,64,1024]{2,1,0:T(8,128)(2,1)}), bf16[16,64,1024]{2,1,0:T(8,128)(2,1)}, u32[]{:S(2)}, u32[]{:S(2)}) async-start(bf16[16,64,1024]{2,1,0:T(8,128)(2,1)} %copy-done.8), calls=%async_computation.1 | async-start | bytes 4194304 | tf_op jit(solution)/shard_map/all_to_all | solution.py:55
  86.9 19.4 %all-to-all-done.1.got_ref = bf16[16,64,1024]{2,1,0:T(8,128)(2,1)} async-done(((bf16[16,64,1024]{2,1,0:T(8,128)(2,1)}), bf16[16,64,1024]{2,1,0:T(8,128)(2,1)}, u32[]{:S(2)}, u32[]{:S(2)}) %all-to-all-start.1) | async-done | bytes 2097184 | tf_op jit(solution)/shard_map/all_to_all | solution.py:55
  106.2 6.7 %all-to-all-start.2 = ((bf16[16,32,1024]{2,1,0:T(8,128)(2,1)}), bf16[16,32,1024]{2,1,0:T(8,128)(2,1)}, u32[]{:S(2)}, u32[]{:S(2)}) async-start(bf16[16,32,1024]{2,1,0:T(8,128)(2,1)} %copy-done.9), calls=%async_computation.2 | async-start | bytes 2097152 | tf_op jit(solution)/shard_map/all_to_all | solution.py:55
  113.0 3.4 %shard_map.108.mine_ref = bf16[1024,768]{1,0:T(8,128)(2,1)S(1)} custom-call(bf16[16,64,1024]{2,1,0:T(8,128)(2,1)} %all-to-all-done.1.got_ref, bf16[1024,768]{1,0:T(8,128)(2,1)S(1)} %bitcast.7, bf16[768,1024]{1,0:T(8,128)(2,1)S(1)} %bitcast.13), custom_call_target="tpu_custom_call" | custom-call | flops 1000 | bytes 1000 | tf_op jit(solution)/shard_map/pallas_call | solution.py:69
  116.5 5.3 %collective-permute-start.3 = (bf16[512,768]{1,0:T(8,128)(2,1)S(1)}, bf16[512,768]{1,0:T(8,128)(2,1)S(1)}, u32[]{:S(2)}, u32[]{:S(2)}) collective-permute-start(bf16[512,768]{1,0:T(8,128)(2,1)S(1)} %get-tuple-element.52), channel_id=1, source_target_pairs={{0,32},{32,0},{1,33},{33,1},{2,34},{34,2},{3,35},{35,3},{4,36},{36... | collective-permute-start | bytes 2359304 | tf_op jit(solution)/shard_map/ppermute | solution.py:46
  130.8 4.6 %collective-permute-start.4 = (bf16[512,768]{1,0:T(8,128)(2,1)S(1)}, bf16[512,768]{1,0:T(8,128)(2,1)S(1)}, u32[]{:S(2)}, u32[]{:S(2)}) collective-permute-start(bf16[512,768]{1,0:T(8,128)(2,1)S(1)} %shard_map.110.mine_ref), channel_id=1, source_target_pairs={{0,32},{32,0},{1,33},{33,1},{2,34},{34,2},{3,35},{35,3},{4,36},{36... | collective-permute-start | bytes 2359304 | tf_op jit(solution)/shard_map/ppermute | solution.py:46
  139.8 4.7 %all-to-all-start.3 = ((bf16[16,64,1024]{2,1,0:T(8,128)(2,1)}), bf16[16,64,1024]{2,1,0:T(8,128)(2,1)}, u32[]{:S(2)}, u32[]{:S(2)}) async-start(bf16[16,64,1024]{2,1,0:T(8,128)(2,1)} %copy-done.4), calls=%async_computation.3 | async-start | bytes 4194304 | tf_op jit(solution)/shard_map/all_to_all | solution.py:55
  146.4 2.6 %shard_map.112.mine_ref = bf16[1536,768]{1,0:T(8,128)(2,1)S(1)} custom-call(bf16[16,96,1024]{2,1,0:T(8,128)(2,1)S(1)} %copy-done.3, bf16[1024,768]{1,0:T(8,128)(2,1)S(1)} %bitcast.11, bf16[768,1024]{1,0:T(8,128)(2,1)S(1)} %bitcast.17), custom_call_target="tpu_custom_call" | custom-call | flops 1000 | bytes 1000 | tf_op jit(solution)/shard_map/pallas_call | solution.py:69
  153.5 2.5 collective-permute-start.5
  157.9 3.7 %shard_map.113 = bf16[16,64,1024]{2,1,0:T(8,128)(2,1)} custom-call(bf16[1536,768]{1,0:T(8,128)(2,1)S(1)} %shard_map.112.mine_ref, bf16[1536,768]{1,0:T(8,128)(2,1)S(1)} %pad_maximum_fusion.theirs_ref, bf16[1024,768]{1,0:T(8,128)(2,1)S(1)} %bitcast.12, bf16[768,1024]{1,0:T(8,128)(2,1)S(1)} %bitcast.18), custom_call_target="tpu_custom_call" | custom-call | flops 1000 | bytes 1000 | tf_op jit(solution)/shard_map/pallas_call | solution.py:69
  161.6 12.1 %all-to-all-done.3.refs_2_ = bf16[16,64,1024]{2,1,0:T(8,128)(2,1)} async-done(((bf16[16,64,1024]{2,1,0:T(8,128)(2,1)}), bf16[16,64,1024]{2,1,0:T(8,128)(2,1)}, u32[]{:S(2)}, u32[]{:S(2)}) %all-to-all-start.3) | async-done | bytes 2097184 | tf_op jit(solution)/shard_map/all_to_all | solution.py:55
  175.8 5.6 %all-to-all-start.4 = ((bf16[16,64,1024]{2,1,0:T(8,128)(2,1)}), bf16[16,64,1024]{2,1,0:T(8,128)(2,1)S(1)}, u32[]{:S(2)}, u32[]{:S(2)}) async-start(bf16[16,64,1024]{2,1,0:T(8,128)(2,1)} %shard_map.113), calls=%async_computation.4 | async-start | bytes 4194304 | tf_op jit(solution)/shard_map/all_to_all | solution.py:55
  183.8 14.2 %collective-permute-start.11 = (bf16[128,1024]{1,0:T(8,128)(2,1)S(1)}, bf16[128,1024]{1,0:T(8,128)(2,1)S(1)}, u32[]{:S(2)}, u32[]{:S(2)}) collective-permute-start(bf16[128,1024]{1,0:T(8,128)(2,1)S(1)} %get-tuple-element.39), channel_id=1, source_target_pairs={{0,80},{1,81},{2,82},{3,83},{4,84},{5,85},{6,86},{7,87},{8,88},{9,... | collective-permute-start | bytes 786440 | tf_op jit(solution)/shard_map/ppermute | solution.py:40
  198.0 8.9 %all-to-all-done.4.refs_2_ = bf16[16,64,1024]{2,1,0:T(8,128)(2,1)S(1)} async-done(((bf16[16,64,1024]{2,1,0:T(8,128)(2,1)}), bf16[16,64,1024]{2,1,0:T(8,128)(2,1)S(1)}, u32[]{:S(2)}, u32[]{:S(2)}) %all-to-all-start.4) | async-done | bytes 2097184 | tf_op jit(solution)/shard_map/all_to_all | solution.py:55
  207.3 10.5 %collective-permute-start.8 = (bf16[128,1024]{1,0:T(8,128)(2,1)S(1)}, bf16[128,1024]{1,0:T(8,128)(2,1)S(1)}, u32[]{:S(2)}, u32[]{:S(2)}) collective-permute-start(bf16[128,1024]{1,0:T(8,128)(2,1)S(1)} %get-tuple-element.41), channel_id=1, source_target_pairs={{0,448},{1,449},{2,450},{3,451},{4,452},{5,453},{6,454},{7,455},{8... | collective-permute-start | bytes 786440 | tf_op jit(solution)/shard_map/ppermute | solution.py:40
  217.9 7.1 %collective-permute-start.9 = (bf16[128,1024]{1,0:T(8,128)(2,1)S(1)}, bf16[128,1024]{1,0:T(8,128)(2,1)S(1)}, u32[]{:S(2)}, u32[]{:S(2)}) collective-permute-start(bf16[128,1024]{1,0:T(8,128)(2,1)S(1)} %get-tuple-element.42), channel_id=1, source_target_pairs={{0,64},{1,65},{2,66},{3,67},{4,68},{5,69},{6,70},{7,71},{8,72},{9,... | collective-permute-start | bytes 786440 | tf_op jit(solution)/shard_map/ppermute | solution.py:40
  225.0 11.8 %collective-permute-done.11.b_ref = bf16[128,1024]{1,0:T(8,128)(2,1)S(1)} collective-permute-done((bf16[128,1024]{1,0:T(8,128)(2,1)S(1)}, bf16[128,1024]{1,0:T(8,128)(2,1)S(1)}, u32[]{:S(2)}, u32[]{:S(2)}) %collective-permute-start.11) | collective-permute-done | bytes 262176 | tf_op jit(solution)/shard_map/ppermute | solution.py:40
  236.8 2.9 %collective-permute-done.8.a_ref = bf16[128,1024]{1,0:T(8,128)(2,1)S(1)} collective-permute-done((bf16[128,1024]{1,0:T(8,128)(2,1)S(1)}, bf16[128,1024]{1,0:T(8,128)(2,1)S(1)}, u32[]{:S(2)}, u32[]{:S(2)}) %collective-permute-start.8) | collective-permute-done | bytes 262176 | tf_op jit(solution)/shard_map/ppermute | solution.py:40
  239.7 13.3 %collective-permute-done.9.b_ref = bf16[128,1024]{1,0:T(8,128)(2,1)S(1)} collective-permute-done((bf16[128,1024]{1,0:T(8,128)(2,1)S(1)}, bf16[128,1024]{1,0:T(8,128)(2,1)S(1)}, u32[]{:S(2)}, u32[]{:S(2)}) %collective-permute-start.9) | collective-permute-done | bytes 262176 | tf_op jit(solution)/shard_map/ppermute | solution.py:40
  (80 shorter events, 49.6 us)
Async XLA Ops:
  6.1 32.2 %collective-permute-start = (bf16[272,1024]{1,0:T(8,128)(2,1)}, bf16[272,1024]{1,0:T(8,128)(2,1)}, u32[]{:S(2)}, u32[]{:S(2)}) collective-permute-start(bf16[272,1024]{1,0:T(8,128)(2,1)} %shard_map.104.refs_1_), channel_id=1, source_target_pairs={{0,16},{1,17},{2,18},{3,19},{4,20},{5,21},{6,22},{7,23},{8,24},{9,... | collective-permute-start | bytes 1671176 | tf_op jit(solution)/shard_map/ppermute | solution.py:40
  27.8 10.5 %copy-start.13 = (bf16[128,1024]{1,0:T(8,128)(2,1)S(1)}, bf16[128,1024]{1,0:T(8,128)(2,1)}, u32[]{:S(2)}) copy-start(bf16[128,1024]{1,0:T(8,128)(2,1)} %refs_2_.1) | copy-start | bytes 786436
  27.8 47.5 %all-to-all-start = ((bf16[16,96,1024]{2,1,0:T(8,128)(2,1)}), bf16[16,96,1024]{2,1,0:T(8,128)(2,1)S(1)}, u32[]{:S(2)}, u32[]{:S(2)}) async-start(bf16[16,96,1024]{2,1,0:T(8,128)(2,1)} %copy-done.7), calls=%async_computation | async-start | bytes 6291456 | tf_op jit(solution)/shard_map/all_to_all | solution.py:55
  38.4 45.1 %collective-permute-start.1 = (bf16[128,1024]{1,0:T(8,128)(2,1)S(1)}, bf16[128,1024]{1,0:T(8,128)(2,1)}, u32[]{:S(2)}, u32[]{:S(2)}) collective-permute-start(bf16[128,1024]{1,0:T(8,128)(2,1)S(1)} %copy-done.13), channel_id=1, source_target_pairs={{0,16},{1,17},{2,18},{3,19},{4,20},{5,21},{6,22},{7,23},{8,24},{9,... | collective-permute-start | bytes 786440 | tf_op jit(solution)/shard_map/ppermute | solution.py:40
  75.3 30.9 %all-to-all-start.1 = ((bf16[16,64,1024]{2,1,0:T(8,128)(2,1)}), bf16[16,64,1024]{2,1,0:T(8,128)(2,1)}, u32[]{:S(2)}, u32[]{:S(2)}) async-start(bf16[16,64,1024]{2,1,0:T(8,128)(2,1)} %copy-done.8), calls=%async_computation.1 | async-start | bytes 4194304 | tf_op jit(solution)/shard_map/all_to_all | solution.py:55
  84.3 28.6 %copy-start.1 = (bf16[1,1,768,1024]{3,2,1,0:T(8,128)(2,1)S(1)}, bf16[1,1,768,1024]{3,2,1,0:T(8,128)(2,1)}, u32[]{:S(2)}) copy-start(bf16[1,1,768,1024]{3,2,1,0:T(8,128)(2,1)} %param.17) | copy-start | bytes 4718596
  86.8 26.1 %copy-start = (bf16[1,1,1024,768]{3,2,1,0:T(8,128)(2,1)S(1)}, bf16[1,1,1024,768]{3,2,1,0:T(8,128)(2,1)}, u32[]{:S(2)}) copy-start(bf16[1,1,1024,768]{3,2,1,0:T(8,128)(2,1)} %param.16) | copy-start | bytes 4718596
  106.2 22.3 %all-to-all-start.2 = ((bf16[16,32,1024]{2,1,0:T(8,128)(2,1)}), bf16[16,32,1024]{2,1,0:T(8,128)(2,1)}, u32[]{:S(2)}, u32[]{:S(2)}) async-start(bf16[16,32,1024]{2,1,0:T(8,128)(2,1)} %copy-done.9), calls=%async_computation.2 | async-start | bytes 2097152 | tf_op jit(solution)/shard_map/all_to_all | solution.py:55
  116.5 7.2 %collective-permute-start.3 = (bf16[512,768]{1,0:T(8,128)(2,1)S(1)}, bf16[512,768]{1,0:T(8,128)(2,1)S(1)}, u32[]{:S(2)}, u32[]{:S(2)}) collective-permute-start(bf16[512,768]{1,0:T(8,128)(2,1)S(1)} %get-tuple-element.52), channel_id=1, source_target_pairs={{0,32},{32,0},{1,33},{33,1},{2,34},{34,2},{3,35},{35,3},{4,36},{36... | collective-permute-start | bytes 2359304 | tf_op jit(solution)/shard_map/ppermute | solution.py:46
  121.8 4.2 %collective-permute-start.2 = (bf16[512,768]{1,0:T(8,128)(2,1)S(1)}, bf16[512,768]{1,0:T(8,128)(2,1)S(1)}, u32[]{:S(2)}, u32[]{:S(2)}) collective-permute-start(bf16[512,768]{1,0:T(8,128)(2,1)S(1)} %get-tuple-element.51), channel_id=1, source_target_pairs={{0,32},{32,0},{1,33},{33,1},{2,34},{34,2},{3,35},{35,3},{4,36},{36... | collective-permute-start | bytes 2359304 | tf_op jit(solution)/shard_map/ppermute | solution.py:46
  128.5 8.8 %copy-start.6 = (bf16[16,32,1024]{2,1,0:T(8,128)(2,1)S(1)}, bf16[16,32,1024]{2,1,0:T(8,128)(2,1)}, u32[]{:S(2)}) copy-start(bf16[16,32,1024]{2,1,0:T(8,128)(2,1)} %copy-done.5) | copy-start | bytes 3145732
  130.8 6.5 %collective-permute-start.4 = (bf16[512,768]{1,0:T(8,128)(2,1)S(1)}, bf16[512,768]{1,0:T(8,128)(2,1)S(1)}, u32[]{:S(2)}, u32[]{:S(2)}) collective-permute-start(bf16[512,768]{1,0:T(8,128)(2,1)S(1)} %shard_map.110.mine_ref), channel_id=1, source_target_pairs={{0,32},{32,0},{1,33},{33,1},{2,34},{34,2},{3,35},{35,3},{4,36},{36... | collective-permute-start | bytes 2359304 | tf_op jit(solution)/shard_map/ppermute | solution.py:46
  139.8 33.8 %all-to-all-start.3 = ((bf16[16,64,1024]{2,1,0:T(8,128)(2,1)}), bf16[16,64,1024]{2,1,0:T(8,128)(2,1)}, u32[]{:S(2)}, u32[]{:S(2)}) async-start(bf16[16,64,1024]{2,1,0:T(8,128)(2,1)} %copy-done.4), calls=%async_computation.3 | async-start | bytes 4194304 | tf_op jit(solution)/shard_map/all_to_all | solution.py:55
  149.2 6.9 %collective-permute-start.7 = (bf16[512,768]{1,0:T(8,128)(2,1)S(1)}, bf16[512,768]{1,0:T(8,128)(2,1)S(1)}, u32[]{:S(2)}, u32[]{:S(2)}) collective-permute-start(bf16[512,768]{1,0:T(8,128)(2,1)S(1)} %get-tuple-element.49), channel_id=1, source_target_pairs={{0,32},{32,0},{1,33},{33,1},{2,34},{34,2},{3,35},{35,3},{4,36},{36... | collective-permute-start | bytes 2359304 | tf_op jit(solution)/shard_map/ppermute | solution.py:46
  151.5 4.5 %collective-permute-start.6 = (bf16[512,768]{1,0:T(8,128)(2,1)S(1)}, bf16[512,768]{1,0:T(8,128)(2,1)S(1)}, u32[]{:S(2)}, u32[]{:S(2)}) collective-permute-start(bf16[512,768]{1,0:T(8,128)(2,1)S(1)} %get-tuple-element.50), channel_id=1, source_target_pairs={{0,32},{32,0},{1,33},{33,1},{2,34},{34,2},{3,35},{35,3},{4,36},{36... | collective-permute-start | bytes 2359304 | tf_op jit(solution)/shard_map/ppermute | solution.py:46
  153.5 4.2 %collective-permute-start.5 = (bf16[512,768]{1,0:T(8,128)(2,1)S(1)}, bf16[512,768]{1,0:T(8,128)(2,1)S(1)}, u32[]{:S(2)}, u32[]{:S(2)}) collective-permute-start(bf16[512,768]{1,0:T(8,128)(2,1)S(1)} %get-tuple-element.48), channel_id=1, source_target_pairs={{0,32},{32,0},{1,33},{33,1},{2,34},{34,2},{3,35},{35,3},{4,36},{36... | collective-permute-start | bytes 2359304 | tf_op jit(solution)/shard_map/ppermute | solution.py:46
  157.9 15.8 %copy-start.17 = (bf16[512,128]{1,0:T(8,128)(2,1)S(1)}, bf16[512,128]{1,0:T(8,128)(2,1)}, u32[]{:S(2)}) copy-start(bf16[512,128]{1,0:T(8,128)(2,1)} %copy-done.16) | copy-start | bytes 393220
  157.9 15.8 %copy-start.19 = (bf16[512,128]{1,0:T(8,128)(2,1)S(1)}, bf16[512,128]{1,0:T(8,128)(2,1)}, u32[]{:S(2)}) copy-start(bf16[512,128]{1,0:T(8,128)(2,1)} %copy-done.18) | copy-start | bytes 393220
  175.7 31.1 %copy-start.15 = (bf16[512,128]{1,0:T(8,128)(2,1)S(1)}, bf16[512,128]{1,0:T(8,128)(2,1)}, u32[]{:S(2)}) copy-start(bf16[512,128]{1,0:T(8,128)(2,1)} %copy-done.14) | copy-start | bytes 393220
  175.8 31.1 %all-to-all-start.4 = ((bf16[16,64,1024]{2,1,0:T(8,128)(2,1)}), bf16[16,64,1024]{2,1,0:T(8,128)(2,1)S(1)}, u32[]{:S(2)}, u32[]{:S(2)}) async-start(bf16[16,64,1024]{2,1,0:T(8,128)(2,1)} %shard_map.113), calls=%async_computation.4 | async-start | bytes 4194304 | tf_op jit(solution)/shard_map/all_to_all | solution.py:55
  181.3 43.6 %collective-permute-start.10 = (bf16[128,1024]{1,0:T(8,128)(2,1)S(1)}, bf16[128,1024]{1,0:T(8,128)(2,1)S(1)}, u32[]{:S(2)}, u32[]{:S(2)}) collective-permute-start(bf16[128,1024]{1,0:T(8,128)(2,1)S(1)} %get-tuple-element.43), channel_id=1, source_target_pairs={{0,464},{1,465},{2,466},{3,467},{4,468},{5,469},{6,470},{7,471},{8... | collective-permute-start | bytes 786440 | tf_op jit(solution)/shard_map/ppermute | solution.py:40
  183.8 52.9 %collective-permute-start.11 = (bf16[128,1024]{1,0:T(8,128)(2,1)S(1)}, bf16[128,1024]{1,0:T(8,128)(2,1)S(1)}, u32[]{:S(2)}, u32[]{:S(2)}) collective-permute-start(bf16[128,1024]{1,0:T(8,128)(2,1)S(1)} %get-tuple-element.39), channel_id=1, source_target_pairs={{0,80},{1,81},{2,82},{3,83},{4,84},{5,85},{6,86},{7,87},{8,88},{9,... | collective-permute-start | bytes 786440 | tf_op jit(solution)/shard_map/ppermute | solution.py:40
  207.3 32.4 %collective-permute-start.8 = (bf16[128,1024]{1,0:T(8,128)(2,1)S(1)}, bf16[128,1024]{1,0:T(8,128)(2,1)S(1)}, u32[]{:S(2)}, u32[]{:S(2)}) collective-permute-start(bf16[128,1024]{1,0:T(8,128)(2,1)S(1)} %get-tuple-element.41), channel_id=1, source_target_pairs={{0,448},{1,449},{2,450},{3,451},{4,452},{5,453},{6,454},{7,455},{8... | collective-permute-start | bytes 786440 | tf_op jit(solution)/shard_map/ppermute | solution.py:40
  217.9 35.2 %collective-permute-start.9 = (bf16[128,1024]{1,0:T(8,128)(2,1)S(1)}, bf16[128,1024]{1,0:T(8,128)(2,1)S(1)}, u32[]{:S(2)}, u32[]{:S(2)}) collective-permute-start(bf16[128,1024]{1,0:T(8,128)(2,1)S(1)} %get-tuple-element.42), channel_id=1, source_target_pairs={{0,64},{1,65},{2,66},{3,67},{4,68},{5,69},{6,70},{7,71},{8,72},{9,... | collective-permute-start | bytes 786440 | tf_op jit(solution)/shard_map/ppermute | solution.py:40
  (19 other events, 25.5 us)

commit v6 on v5

--- a/solution.py
+++ b/solution.py
@@ -46,11 +46,6 @@
     return lax.ppermute(v, NODE, [(0, 1), (1, 0)])
 
 
-def in_pieces(v, count):
-    each = v.shape[0] // count
-    return jnp.concatenate([other_core(v[i * each : (i + 1) * each]) for i in range(count)], axis=0)
-
-
 def exchange(v):
     return lax.all_to_all(v, PLANE, split_axis=0, concat_axis=0, tiled=True)
 
@@ -63,7 +58,7 @@
     return lax.dot_general(a, b, dims, preferred_element_type=F32)
 
 
-def run(kernel, outs, *args, scalars=0, scratch=(), flops=1000):
+def run(kernel, outs, *args, scalars=0, scratch=(), flops=1000, room=32 << 20):
     where = [pl.BlockSpec(memory_space=pltpu.SMEM)] * scalars
     where += [pl.BlockSpec(memory_space=pltpu.VMEM)] * (len(args) - scalars)
     return pl.pallas_call(
@@ -72,7 +67,7 @@
         in_specs=where,
         out_specs=jax.tree.map(lambda _: pl.BlockSpec(memory_space=pltpu.VMEM), outs),
         scratch_shapes=scratch,
-        compiler_params=pltpu.CompilerParams(vmem_limit_bytes=32 << 20),
+        compiler_params=pltpu.CompilerParams(vmem_limit_bytes=room),
         cost_estimate=pl.CostEstimate(flops=flops, bytes_accessed=1000, transcendentals=0),
     )(*args)
 
@@ -81,18 +76,17 @@
     return jax.ShapeDtypeStruct(shape, BF)
 
 
-def gather_block(a_ref, g_ref, *refs):
+def gather_block(f_ref, *refs):
     notes, out_ref, hold_ref = refs[:4], refs[4], refs[5]
-    tokens = a_ref.shape[0]
+    tokens = f_ref.shape[0]
     top = notes[0].shape[0]
-    out_ref[:tokens, :] = a_ref[...]
-    out_ref[tokens : 2 * tokens, :] = g_ref[...]
+    out_ref[:tokens, :] = f_ref[...]
     hold_ref[...] = jnp.zeros(hold_ref.shape, F32)
     for half in range(2):
         span = slice(half * tokens, (half + 1) * tokens)
         hold_ref[:top, span] = notes[2 * half][...].astype(F32)
         hold_ref[8 : 8 + top, span] = notes[2 * half + 1][...].astype(F32)
-    out_ref[2 * tokens :, :] = hold_ref[...].astype(BF)
+    out_ref[tokens:, :] = hold_ref[...].astype(BF)
 
 
 def tables(note, first, top, experts):
@@ -121,64 +115,68 @@
     return result
 
 
-def put(out_ref, at, hit, rows_ref, first=0):
+def put(out_ref, at, hit, rows_ref):
     experts = out_ref.shape[0]
     tokens = hit.shape[1]
     for c in range(0, out_ref.shape[2], WIDTH):
-        block = dot32(hit, rows_ref[first : first + tokens, c : c + WIDTH]).astype(BF)
+        block = dot32(hit, rows_ref[:tokens, c : c + WIDTH]).astype(BF)
         out_ref[:, at : at + SLOTS, c : c + WIDTH] = block.reshape(experts, SLOTS, WIDTH)
 
 
-def pack_first(top, near, *refs):
-    if near:
-        first_ref, block_ref, f_ref, out_ref, mix_f_ref, mix_b_ref = refs
-    else:
-        first_ref, block_ref, out_ref, mix_f_ref, mix_b_ref, hit_f_ref = refs
-    tokens = mix_f_ref.shape[1]
-    note = block_ref[2 * tokens :, : 2 * tokens].astype(F32)
-    (hit_f, mix_f), (hit_b, mix_b) = tables(note, first_ref[0], top, out_ref.shape[0])
+def block_tables(top, first_ref, block_ref, experts, tokens):
+    note = block_ref[tokens:, : 2 * tokens].astype(F32)
+    return tables(note, first_ref[0], top, experts)
+
+
+def pack_near(top, first_ref, block_ref, a_ref, g_ref, out_ref, mix_f_ref, mix_b_ref):
+    (hit_f, mix_f), (hit_b, mix_b) = block_tables(
+        top, first_ref, block_ref, out_ref.shape[0], a_ref.shape[0]
+    )
     mix_f_ref[...] = mix_f
     mix_b_ref[...] = mix_b
-    put(out_ref, 0, hit_b, block_ref)
-    put(out_ref, SLOTS, hit_b, block_ref, tokens)
-    if near:
-        put(out_ref, 2 * SLOTS, hit_f, f_ref)
-    else:
-        hit_f_ref[...] = hit_f
-
-
-def pack_more(hit_ref, rows_ref, out_ref):
-    put(out_ref, 0, hit_ref[...], rows_ref)
-
-
-def parts(kinds, got_ref, w_in_ref, w_out_ref, out_ref):
+    put(out_ref, 0, hit_b, a_ref)
+    put(out_ref, SLOTS, hit_b, g_ref)
+    put(out_ref, 2 * SLOTS, hit_f, block_ref)
+
+
+def pack_far_f(top, first_ref, block_ref, out_ref, mix_f_ref, mix_b_ref, hit_b_ref):
+    (hit_f, mix_f), (hit_b, mix_b) = block_tables(
+        top, first_ref, block_ref, out_ref.shape[0], mix_f_ref.shape[1]
+    )
+    mix_f_ref[...] = mix_f
+    mix_b_ref[...] = mix_b
+    hit_b_ref[...] = hit_b
+    put(out_ref, 0, hit_f, block_ref)
+
+
+def pack_far_b(hit_ref, a_ref, g_ref, out_ref):
+    put(out_ref, 0, hit_ref[...], a_ref)
+    put(out_ref, SLOTS, hit_ref[...], g_ref)
+
+
+def parts(kinds, got_ref, w_in_ref, w_out_ref, *outs):
     experts, _, cols = got_ref.shape
-    hidden = w_in_ref.shape[1]
-    rows = experts * SLOTS
     for i, kind in enumerate(kinds):
-        x = got_ref[:, i * SLOTS : (i + 1) * SLOTS, :].reshape(rows, cols)
-        for c in range(0, hidden, WIDTH):
+        x = got_ref[:, i * SLOTS : (i + 1) * SLOTS, :].reshape(experts * SLOTS, cols)
+        for c in range(0, w_in_ref.shape[1], WIDTH):
             if kind == "g":
                 part = dot32(x, w_out_ref[c : c + WIDTH, :], TRANSPOSED)
             else:
                 part = dot32(x, w_in_ref[:, c : c + WIDTH])
-            out_ref[i * rows : (i + 1) * rows, c : c + WIDTH] = part.astype(BF)
-
-
-def results(kinds, held, mine_ref, theirs_ref, w_in_ref, w_out_ref, *refs):
-    out_ref, hold_ref = refs[-2:]
+            outs[i][:, c : c + WIDTH] = part.astype(BF)
+
+
+def results(kinds, *refs):
+    mine, theirs = refs[: len(kinds)], refs[len(kinds) : 2 * len(kinds)]
+    w_in_ref, w_out_ref, out_ref, hold_ref = refs[2 * len(kinds) :]
     experts, _, cols = out_ref.shape
-    rows = experts * SLOTS
     hidden = w_in_ref.shape[1]
 
     def total(i, c):
-        span = (slice(i * rows, (i + 1) * rows), slice(c, c + WIDTH))
-        return mine_ref[span].astype(F32) + theirs_ref[span].astype(F32)
+        span = slice(c, c + WIDTH)
+        return mine[i][:, span].astype(F32) + theirs[i][:, span].astype(F32)
 
     i, at = 0, 0
-    if held:
-        at = refs[0].shape[1]
-        out_ref[:, :at, :] = refs[0][...]
     while i < len(kinds):
         forward = kinds[i] == "f"
         for c in range(0, hidden, WIDTH):
@@ -202,12 +200,13 @@
 
 
 def sums(count, *refs):
-    mixes, back_ref, outs = refs[:count], refs[count], refs[count + 1 :]
-    experts, _, cols = back_ref.shape
+    mixes, backs, outs = refs[:count], refs[count:-count], refs[-count:]
+    experts, _, cols = backs[0].shape
     for i in range(count):
         mix = mixes[i][...]
+        back_ref, at = (backs[i], 0) if len(backs) > 1 else (backs[0], i * SLOTS)
         for c in range(0, cols, WIDTH):
-            rows = back_ref[:, i * SLOTS : (i + 1) * SLOTS, c : c + WIDTH]
+            rows = back_ref[:, at : at + SLOTS, c : c + WIDTH]
             rows = rows.reshape(experts * SLOTS, WIDTH)
             outs[i][:, c : c + WIDTH] = dot32(mix, rows, OVER_ROWS).astype(BF)
 
@@ -243,74 +242,79 @@
     first = (lax.axis_index("zhi") * experts).astype(jnp.int32).reshape(1)
     table = shaped(rows, tok)
 
-    def work(got, kinds, *held):
+    def work(got, kinds):
         mine = run(
             functools.partial(parts, kinds),
-            shaped(len(kinds) * rows, hidden),
+            (shaped(rows, hidden),) * len(kinds),
             got,
             weight_in,
             weight_out,
         )
-        theirs = other_core(mine) if len(kinds) < 2 else in_pieces(mine, len(kinds))
-        many = kinds.count("f") + kinds.count("a") + len(held)
+        theirs = [other_core(part) for part in mine]
+        many = kinds.count("f") + kinds.count("a")
         return run(
-            functools.partial(results, kinds, len(held)),
+            functools.partial(results, kinds),
             shaped(experts, many * SLOTS, cols),
-            mine,
-            theirs,
+            *mine,
+            *theirs,
             weight_in,
             weight_out,
-            *held,
             scratch=[pltpu.VMEM((rows, hidden), BF)],
         )
 
     def combined(back, *mixes):
         return run(
-            functools.partial(sums, len(mixes)), (shaped(tok, cols),) * len(mixes), *mixes, back
+            functools.partial(sums, len(mixes)), (shaped(tok, cols),) * len(mixes), *mixes, *back
         )
 
     block = run(
         gather_block,
-        shaped(2 * tok + 16, cols),
-        act_backward,
-        grad_backward,
+        shaped(tok + 16, cols),
+        act_forward,
         routes_forward.T,
         gates_forward.T,
         routes_backward.T,
         gates_backward.T,
         scratch=[pltpu.VMEM((16, cols), F32)],
+        room=56 << 20,
     )
     far_block = moved(block, 0, True)
-    far_rows = moved(after(act_forward, far_block), 0, True)
+    far_a = moved(after(act_backward, far_block), 0, True)
+    far_g = moved(after(grad_backward, far_block), 0, True)
 
     sent, mix_f, mix_b = run(
-        functools.partial(pack_first, top, True),
+        functools.partial(pack_near, top),
         (shaped(experts, 3 * SLOTS, cols), table, table),
         first,
         block,
-        act_forward,
+        act_backward,
+        grad_backward,
         scalars=1,
+        room=56 << 20,
     )
     got = exchange(sent)
-    sent_b, far_mix_f, far_mix_b, far_hit_f = run(
-        functools.partial(pack_first, top, False),
-        (shaped(experts, 2 * SLOTS, cols), table, table, table),
+    sent_f, far_mix_f, far_mix_b, far_hit_b = run(
+        functools.partial(pack_far_f, top),
+        (shaped(experts, SLOTS, cols), table, table, table),
         first,
         far_block,
         scalars=1,
         flops=LONG,
     )
-    got_b = exchange(after(sent_b, got))
-    sent_f = run(pack_more, shaped(experts, SLOTS, cols), far_hit_f, far_rows, flops=LONG)
-    got_f = exchange(after(sent_f, got_b))
-    out_b = work(after(got_b, sent_f), "ag")
-    out_bf = work(after(got_f, out_b), "f", out_b)
-    far_out = exchange(out_bf)
-    out = work(after(got, out_bf), "agf")
-    far_sum_b, far_sum_f = combined(after(far_out, out), far_mix_b, far_mix_f)
+    got_f = exchange(after(sent_f, got))
+    sent_b = run(
+        pack_far_b, shaped(experts, 2 * SLOTS, cols), far_hit_b, far_a, far_g, flops=LONG
+    )
+    got_b = exchange(after(sent_b, got_f))
+    out = work(after(got, sent_b, got_f), "agf")
+    out_f = work(after(got_f, out), "f")
+    back_f = exchange(after(out_f, got_b))
+    out_b = work(after(got_b, out_f), "ag")
+    back_b = exchange(after(out_b, back_f))
+    far_sum_b, far_sum_f = combined((back_b, back_f), far_mix_b, far_mix_f)
     over = (moved(far_sum_b, -1, True), moved(far_sum_f, 1, True))
     back = exchange(after(out, far_sum_f))
-    sum_b, sum_f = combined(back, mix_b, mix_f)
+    sum_b, sum_f = combined((back,), mix_b, mix_f)
     near = (moved(sum_b, -1, False), moved(sum_f, 1, False))
     pair = (shaped(tok, cols),) * 2
     over = run(hold, pair, *over, flops=LONG)

time: 255 us -> 241 us (0.945)
  the two profiles are of different devices: /device:TPU:1 before, /device:TPU:18 now
where the time goes in v6:
time: 241 us; the launch traced here: 240 us
  starting transfers between devices  103 us (43%)
  waiting for transfers between devices  80.9 us (34%)
  Pallas kernels  25.3 us (10%)
  blocking collectives  20.1 us (8%)
  local copies, waits for them, and re-layouts  9.62 us (4%)
    ppermute x7, starting transfers between devices, moved(): lax.ppermute(v, RING, pairs_of(shape, lambda s, h: ((s + by) % sections,...  52.7 us
    all_to_all x5, waiting for transfers between devices, exchange(): return lax.all_to_all(v, PLANE, split_axis=0, concat_axis=0, tiled=True)  42 us
    all_to_all x5, starting transfers between devices, exchange(): return lax.all_to_all(v, PLANE, split_axis=0, concat_axis=0, tiled=True)  37.8 us
    ppermute x7, waiting for transfers between devices, moved(): lax.ppermute(v, RING, pairs_of(shape, lambda s, h: ((s + by) % sections,...  32.8 us
    pallas_call x14, Pallas kernels, run(): pl.pallas_call(kernel, out_shape=outs, in_specs=where, out_specs=jax.tree...  25.3 us
    all_to_all x1, blocking collectives, exchange(): return lax.all_to_all(v, PLANE, split_axis=0, concat_axis=0, tiled=True)  20.1 us
    ppermute x6, starting transfers between devices, other_core(): return lax.ppermute(v, NODE, [(0, 1), (1, 0)])  12.8 us
    unnamed x24, local copies, waits for them, and re-layouts  9.62 us
  transfers between devices with their start and end apart: 18, of which 10 were waited for; matrix products, arithmetic and copies ran while one was open for 0% of the time, Pallas kernels for 9%

profile of v6, /device:TPU:18, one launch (start us, length us, event | category | flops | bytes accessed | tf_op | source)
XLA Modules:
  0.0 240.2 jit_solution(16190976523535326277)
XLA Ops:
  2.4 15.7 %collective-permute-start = (bf16[144,1024]{1,0:T(8,128)(2,1)}, bf16[144,1024]{1,0:T(8,128)(2,1)S(1)}, u32[]{:S(2)}, u32[]{:S(2)}) collective-permute-start(bf16[144,1024]{1,0:T(8,128)(2,1)} %shard_map.104.block_ref), channel_id=1, source_target_pairs={{0,16},{1,17},{2,18},{3,19},{4,20},{5,21},{6,22},{7,23},{8,24},{9,... | collective-permute-start | bytes 884744 | tf_op jit(solution)/shard_map/ppermute | solution.py:40
  18.1 3.9 %shard_map.105 = (bf16[16,96,1024]{2,1,0:T(8,128)(2,1)}, bf16[512,128]{1,0:T(8,128)(2,1)}, bf16[512,128]{1,0:T(8,128)(2,1)}) custom-call(s32[1]{0:T(128)} %bitcast.first_ref, bf16[144,1024]{1,0:T(8,128)(2,1)} %shard_map.104.block_ref, bf16[128,1024]{1,0:T(8,128)(2,1)} %a_ref.1, bf16[128,1024]{1,0:T(8,128)(2,1)} %g_ref.1), custom_call_target="tpu_custom_call" | custom-call | flops 1000 | bytes 1000 | tf_op jit(solution)/shard_map/pallas_call | solution.py:64
  22.0 7.3 %all-to-all-start = ((bf16[16,96,1024]{2,1,0:T(8,128)(2,1)}), bf16[16,96,1024]{2,1,0:T(8,128)(2,1)S(1)}, u32[]{:S(2)}, u32[]{:S(2)}) async-start(bf16[16,96,1024]{2,1,0:T(8,128)(2,1)} %get-tuple-element.34), calls=%async_computation | async-start | bytes 6291456 | tf_op jit(solution)/shard_map/all_to_all | solution.py:50
  30.6 12.5 %collective-permute-start.1 = (bf16[128,1024]{1,0:T(8,128)(2,1)}, bf16[128,1024]{1,0:T(8,128)(2,1)}, u32[]{:S(2)}, u32[]{:S(2)}) collective-permute-start(bf16[128,1024]{1,0:T(8,128)(2,1)} %a_ref.1), channel_id=1, source_target_pairs={{0,16},{1,17},{2,18},{3,19},{4,20},{5,21},{6,22},{7,23},{8,24},{9,... | collective-permute-start | bytes 786440 | tf_op jit(solution)/shard_map/ppermute | solution.py:40
  47.7 20.7 %all-to-all-done.got_ref = bf16[16,96,1024]{2,1,0:T(8,128)(2,1)S(1)} async-done(((bf16[16,96,1024]{2,1,0:T(8,128)(2,1)}), bf16[16,96,1024]{2,1,0:T(8,128)(2,1)S(1)}, u32[]{:S(2)}, u32[]{:S(2)}) %all-to-all-start) | async-done | bytes 3145760 | tf_op jit(solution)/shard_map/all_to_all | solution.py:50
  70.0 8.9 %all-to-all-start.1 = ((bf16[16,32,1024]{2,1,0:T(8,128)(2,1)}), bf16[16,32,1024]{2,1,0:T(8,128)(2,1)}, u32[]{:S(2)}, u32[]{:S(2)}) async-start(bf16[16,32,1024]{2,1,0:T(8,128)(2,1)} %copy-done.7), calls=%async_computation.1 | async-start | bytes 2097152 | tf_op jit(solution)/shard_map/all_to_all | solution.py:50
  82.0 9.0 %all-to-all-done.1.got_ref = bf16[16,32,1024]{2,1,0:T(8,128)(2,1)} async-done(((bf16[16,32,1024]{2,1,0:T(8,128)(2,1)}), bf16[16,32,1024]{2,1,0:T(8,128)(2,1)}, u32[]{:S(2)}, u32[]{:S(2)}) %all-to-all-start.1) | async-done | bytes 1048608 | tf_op jit(solution)/shard_map/all_to_all | solution.py:50
  91.0 7.5 %all-to-all-start.2 = ((bf16[16,64,1024]{2,1,0:T(8,128)(2,1)}), bf16[16,64,1024]{2,1,0:T(8,128)(2,1)}, u32[]{:S(2)}, u32[]{:S(2)}) async-start(bf16[16,64,1024]{2,1,0:T(8,128)(2,1)} %copy-done.6), calls=%async_computation.2 | async-start | bytes 4194304 | tf_op jit(solution)/shard_map/all_to_all | solution.py:50
  100.3 2.6 %shard_map.108 = (bf16[512,768]{1,0:T(8,128)(2,1)S(1)}, bf16[512,768]{1,0:T(8,128)(2,1)S(1)}, bf16[512,768]{1,0:T(8,128)(2,1)S(1)}) custom-call(bf16[16,96,1024]{2,1,0:T(8,128)(2,1)S(1)} %copy-done.3, bf16[1024,768]{1,0:T(8,128)(2,1)S(1)} %bitcast.7, bf16[768,1024]{1,0:T(8,128)(2,1)S(1)} %bitcast.13), custom_call_target="tpu_custom_call" | custom-call | flops 1000 | bytes 1000 | tf_op jit(solution)/shard_map/pallas_call | solution.py:64
  104.9 2.4 %collective-permute-start.4 = (bf16[512,768]{1,0:T(8,128)(2,1)S(1)}, bf16[512,768]{1,0:T(8,128)(2,1)S(1)}, u32[]{:S(2)}, u32[]{:S(2)}) collective-permute-start(bf16[512,768]{1,0:T(8,128)(2,1)S(1)} %get-tuple-element.42.refs_1_), channel_id=1, source_target_pairs={{0,32},{32,0},{1,33},{33,1},{2,34},{34,2},{3,35},{35,3},{4,36},{36... | collective-permute-start | bytes 2359304 | tf_op jit(solution)/shard_map/ppermute | solution.py:46
  109.2 2.2 collective-permute-done.5.refs_5_
  111.5 3.7 %shard_map.109 = bf16[16,64,1024]{2,1,0:T(8,128)(2,1)} custom-call(bf16[512,768]{1,0:T(8,128)(2,1)S(1)} %get-tuple-element.41.refs_0_, bf16[512,768]{1,0:T(8,128)(2,1)S(1)} %get-tuple-element.42.refs_1_, bf16[512,768]{1,0:T(8,128)(2,1)S(1)} %get-tuple-element.43.refs_2_, bf16[512,768]{1,0:T(8,128)(2,1)S(1)} %collective-permute-done.3.refs_3_, ...), custom_call_target="tpu_custom_call" | custom-call | flops 1000 | bytes 1000 | tf_op jit(solution)/shard_map/pallas_call | solution.py:64
  123.7 7.3 %all-to-all-start.3 = ((bf16[16,32,1024]{2,1,0:T(8,128)(2,1)}), bf16[16,32,1024]{2,1,0:T(8,128)(2,1)}, u32[]{:S(2)}, u32[]{:S(2)}) async-start(bf16[16,32,1024]{2,1,0:T(8,128)(2,1)} %copy-done.5), calls=%async_computation.3 | async-start | bytes 2097152 | tf_op jit(solution)/shard_map/all_to_all | solution.py:50
  131.0 3.4 %shard_map.112 = (bf16[512,768]{1,0:T(8,128)(2,1)S(1)}, bf16[512,768]{1,0:T(8,128)(2,1)S(1)}) custom-call(bf16[16,64,1024]{2,1,0:T(8,128)(2,1)} %all-to-all-done.2.got_ref, bf16[1024,768]{1,0:T(8,128)(2,1)S(1)} %bitcast.11, bf16[768,1024]{1,0:T(8,128)(2,1)S(1)} %bitcast.17), custom_call_target="tpu_custom_call" | custom-call | flops 1000 | bytes 1000 | tf_op jit(solution)/shard_map/pallas_call | solution.py:64
  136.3 2.6 %collective-permute-start.8 = (bf16[512,768]{1,0:T(8,128)(2,1)S(1)}, bf16[512,768]{1,0:T(8,128)(2,1)S(1)}, u32[]{:S(2)}, u32[]{:S(2)}) collective-permute-start(bf16[512,768]{1,0:T(8,128)(2,1)S(1)} %get-tuple-element.50.refs_1_), channel_id=1, source_target_pairs={{0,32},{32,0},{1,33},{33,1},{2,34},{34,2},{3,35},{35,3},{4,36},{36... | collective-permute-start | bytes 2359304 | tf_op jit(solution)/shard_map/ppermute | solution.py:46
  143.0 2.4 all-to-all-done.3.refs_3_
  145.4 20.1 %all_to_all.30.refs_2_ = bf16[16,32,1024]{2,1,0:T(8,128)(2,1)S(1)} all-to-all(bf16[16,32,1024]{2,1,0:T(8,128)(2,1)} %copy-done.4), channel_id=1, replica_groups=mesh['section'=8,'node'=2,'zhi'=2,'x'=4,'y'=4] {'x','y'}, dimensions={0} | all-to-all | bytes 2097152 | tf_op jit(solution)/shard_map/all_to_all | solution.py:50
  167.2 6.9 %all-to-all-start.5 = ((bf16[16,64,1024]{2,1,0:T(8,128)(2,1)}), bf16[16,64,1024]{2,1,0:T(8,128)(2,1)S(1)}, u32[]{:S(2)}, u32[]{:S(2)}) async-start(bf16[16,64,1024]{2,1,0:T(8,128)(2,1)} %shard_map.109), calls=%async_computation.5 | async-start | bytes 4194304 | tf_op jit(solution)/shard_map/all_to_all | solution.py:50
  176.2 12.1 %collective-permute-start.12 = (bf16[128,1024]{1,0:T(8,128)(2,1)S(1)}, bf16[128,1024]{1,0:T(8,128)(2,1)S(1)}, u32[]{:S(2)}, u32[]{:S(2)}) collective-permute-start(bf16[128,1024]{1,0:T(8,128)(2,1)S(1)} %get-tuple-element.53), channel_id=1, source_target_pairs={{0,80},{1,81},{2,82},{3,83},{4,84},{5,85},{6,86},{7,87},{8,88},{9,... | collective-permute-start | bytes 786440 | tf_op jit(solution)/shard_map/ppermute | solution.py:40
  188.3 10.0 %all-to-all-done.5.refs_2_ = bf16[16,64,1024]{2,1,0:T(8,128)(2,1)S(1)} async-done(((bf16[16,64,1024]{2,1,0:T(8,128)(2,1)}), bf16[16,64,1024]{2,1,0:T(8,128)(2,1)S(1)}, u32[]{:S(2)}, u32[]{:S(2)}) %all-to-all-start.5) | async-done | bytes 2097184 | tf_op jit(solution)/shard_map/all_to_all | solution.py:50
  198.8 5.8 %collective-permute-start.9 = (bf16[128,1024]{1,0:T(8,128)(2,1)S(1)}, bf16[128,1024]{1,0:T(8,128)(2,1)S(1)}, u32[]{:S(2)}, u32[]{:S(2)}) collective-permute-start(bf16[128,1024]{1,0:T(8,128)(2,1)S(1)} %get-tuple-element.55), channel_id=1, source_target_pairs={{0,448},{1,449},{2,450},{3,451},{4,452},{5,453},{6,454},{7,455},{8... | collective-permute-start | bytes 786440 | tf_op jit(solution)/shard_map/ppermute | solution.py:40
  204.6 2.5 %collective-permute-start.10 = (bf16[128,1024]{1,0:T(8,128)(2,1)S(1)}, bf16[128,1024]{1,0:T(8,128)(2,1)S(1)}, u32[]{:S(2)}, u32[]{:S(2)}) collective-permute-start(bf16[128,1024]{1,0:T(8,128)(2,1)S(1)} %get-tuple-element.56), channel_id=1, source_target_pairs={{0,64},{1,65},{2,66},{3,67},{4,68},{5,69},{6,70},{7,71},{8,72},{9,... | collective-permute-start | bytes 786440 | tf_op jit(solution)/shard_map/ppermute | solution.py:40
  207.1 19.0 %collective-permute-done.12.b_ref = bf16[128,1024]{1,0:T(8,128)(2,1)S(1)} collective-permute-done((bf16[128,1024]{1,0:T(8,128)(2,1)S(1)}, bf16[128,1024]{1,0:T(8,128)(2,1)S(1)}, u32[]{:S(2)}, u32[]{:S(2)}) %collective-permute-start.12) | collective-permute-done | bytes 262176 | tf_op jit(solution)/shard_map/ppermute | solution.py:40
  226.1 13.2 %collective-permute-done.10.b_ref = bf16[128,1024]{1,0:T(8,128)(2,1)S(1)} collective-permute-done((bf16[128,1024]{1,0:T(8,128)(2,1)S(1)}, bf16[128,1024]{1,0:T(8,128)(2,1)S(1)}, u32[]{:S(2)}, u32[]{:S(2)}) %collective-permute-start.10) | collective-permute-done | bytes 262176 | tf_op jit(solution)/shard_map/ppermute | solution.py:40
  (51 shorter events, 37.8 us)
Async XLA Ops:
  2.4 27.5 %collective-permute-start = (bf16[144,1024]{1,0:T(8,128)(2,1)}, bf16[144,1024]{1,0:T(8,128)(2,1)S(1)}, u32[]{:S(2)}, u32[]{:S(2)}) collective-permute-start(bf16[144,1024]{1,0:T(8,128)(2,1)} %shard_map.104.block_ref), channel_id=1, source_target_pairs={{0,16},{1,17},{2,18},{3,19},{4,20},{5,21},{6,22},{7,23},{8,24},{9,... | collective-permute-start | bytes 884744 | tf_op jit(solution)/shard_map/ppermute | solution.py:40
  22.0 46.4 %all-to-all-start = ((bf16[16,96,1024]{2,1,0:T(8,128)(2,1)}), bf16[16,96,1024]{2,1,0:T(8,128)(2,1)S(1)}, u32[]{:S(2)}, u32[]{:S(2)}) async-start(bf16[16,96,1024]{2,1,0:T(8,128)(2,1)} %get-tuple-element.34), calls=%async_computation | async-start | bytes 6291456 | tf_op jit(solution)/shard_map/all_to_all | solution.py:50
  30.6 48.3 %collective-permute-start.1 = (bf16[128,1024]{1,0:T(8,128)(2,1)}, bf16[128,1024]{1,0:T(8,128)(2,1)}, u32[]{:S(2)}, u32[]{:S(2)}) collective-permute-start(bf16[128,1024]{1,0:T(8,128)(2,1)} %a_ref.1), channel_id=1, source_target_pairs={{0,16},{1,17},{2,18},{3,19},{4,20},{5,21},{6,22},{7,23},{8,24},{9,... | collective-permute-start | bytes 786440 | tf_op jit(solution)/shard_map/ppermute | solution.py:40
  43.1 35.8 %collective-permute-start.2 = (bf16[128,1024]{1,0:T(8,128)(2,1)}, bf16[128,1024]{1,0:T(8,128)(2,1)}, u32[]{:S(2)}, u32[]{:S(2)}) collective-permute-start(bf16[128,1024]{1,0:T(8,128)(2,1)} %g_ref.1), channel_id=1, source_target_pairs={{0,16},{1,17},{2,18},{3,19},{4,20},{5,21},{6,22},{7,23},{8,24},{9,... | collective-permute-start | bytes 786440 | tf_op jit(solution)/shard_map/ppermute | solution.py:40
  68.3 1.6 copy-start.2
  70.0 21.0 %all-to-all-start.1 = ((bf16[16,32,1024]{2,1,0:T(8,128)(2,1)}), bf16[16,32,1024]{2,1,0:T(8,128)(2,1)}, u32[]{:S(2)}, u32[]{:S(2)}) async-start(bf16[16,32,1024]{2,1,0:T(8,128)(2,1)} %copy-done.7), calls=%async_computation.1 | async-start | bytes 2097152 | tf_op jit(solution)/shard_map/all_to_all | solution.py:50
  82.0 16.4 %copy-start = (bf16[1,1,1024,768]{3,2,1,0:T(8,128)(2,1)S(1)}, bf16[1,1,1024,768]{3,2,1,0:T(8,128)(2,1)}, u32[]{:S(2)}) copy-start(bf16[1,1,1024,768]{3,2,1,0:T(8,128)(2,1)} %param.16) | copy-start | bytes 4718596
  82.0 16.4 %copy-start.1 = (bf16[1,1,768,1024]{3,2,1,0:T(8,128)(2,1)S(1)}, bf16[1,1,768,1024]{3,2,1,0:T(8,128)(2,1)}, u32[]{:S(2)}) copy-start(bf16[1,1,768,1024]{3,2,1,0:T(8,128)(2,1)} %param.17) | copy-start | bytes 4718596
  91.0 32.8 %all-to-all-start.2 = ((bf16[16,64,1024]{2,1,0:T(8,128)(2,1)}), bf16[16,64,1024]{2,1,0:T(8,128)(2,1)}, u32[]{:S(2)}, u32[]{:S(2)}) async-start(bf16[16,64,1024]{2,1,0:T(8,128)(2,1)} %copy-done.6), calls=%async_computation.2 | async-start | bytes 4194304 | tf_op jit(solution)/shard_map/all_to_all | solution.py:50
  98.4 1.9 copy-start.3
  102.9 6.3 %collective-permute-start.3 = (bf16[512,768]{1,0:T(8,128)(2,1)S(1)}, bf16[512,768]{1,0:T(8,128)(2,1)S(1)}, u32[]{:S(2)}, u32[]{:S(2)}) collective-permute-start(bf16[512,768]{1,0:T(8,128)(2,1)S(1)} %get-tuple-element.41.refs_0_), channel_id=1, source_target_pairs={{0,32},{32,0},{1,33},{33,1},{2,34},{34,2},{3,35},{35,3},{4,36},{36... | collective-permute-start | bytes 2359304 | tf_op jit(solution)/shard_map/ppermute | solution.py:46
  104.9 4.4 %collective-permute-start.4 = (bf16[512,768]{1,0:T(8,128)(2,1)S(1)}, bf16[512,768]{1,0:T(8,128)(2,1)S(1)}, u32[]{:S(2)}, u32[]{:S(2)}) collective-permute-start(bf16[512,768]{1,0:T(8,128)(2,1)S(1)} %get-tuple-element.42.refs_1_), channel_id=1, source_target_pairs={{0,32},{32,0},{1,33},{33,1},{2,34},{34,2},{3,35},{35,3},{4,36},{36... | collective-permute-start | bytes 2359304 | tf_op jit(solution)/shard_map/ppermute | solution.py:46
  107.3 4.2 %collective-permute-start.5 = (bf16[512,768]{1,0:T(8,128)(2,1)S(1)}, bf16[512,768]{1,0:T(8,128)(2,1)S(1)}, u32[]{:S(2)}, u32[]{:S(2)}) collective-permute-start(bf16[512,768]{1,0:T(8,128)(2,1)S(1)} %get-tuple-element.43.refs_2_), channel_id=1, source_target_pairs={{0,32},{32,0},{1,33},{33,1},{2,34},{34,2},{3,35},{35,3},{4,36},{36... | collective-permute-start | bytes 2359304 | tf_op jit(solution)/shard_map/ppermute | solution.py:46
  117.4 4.2 %collective-permute-start.6 = (bf16[512,768]{1,0:T(8,128)(2,1)S(1)}, bf16[512,768]{1,0:T(8,128)(2,1)S(1)}, u32[]{:S(2)}, u32[]{:S(2)}) collective-permute-start(bf16[512,768]{1,0:T(8,128)(2,1)S(1)} %shard_map.110.refs_0_), channel_id=1, source_target_pairs={{0,32},{32,0},{1,33},{33,1},{2,34},{34,2},{3,35},{35,3},{4,36},{36... | collective-permute-start | bytes 2359304 | tf_op jit(solution)/shard_map/ppermute | solution.py:46
  123.7 21.7 %all-to-all-start.3 = ((bf16[16,32,1024]{2,1,0:T(8,128)(2,1)}), bf16[16,32,1024]{2,1,0:T(8,128)(2,1)}, u32[]{:S(2)}, u32[]{:S(2)}) async-start(bf16[16,32,1024]{2,1,0:T(8,128)(2,1)} %copy-done.5), calls=%async_computation.3 | async-start | bytes 2097152 | tf_op jit(solution)/shard_map/all_to_all | solution.py:50
  134.4 4.5 %collective-permute-start.7 = (bf16[512,768]{1,0:T(8,128)(2,1)S(1)}, bf16[512,768]{1,0:T(8,128)(2,1)S(1)}, u32[]{:S(2)}, u32[]{:S(2)}) collective-permute-start(bf16[512,768]{1,0:T(8,128)(2,1)S(1)} %get-tuple-element.49.refs_0_), channel_id=1, source_target_pairs={{0,32},{32,0},{1,33},{33,1},{2,34},{34,2},{3,35},{35,3},{4,36},{36... | collective-permute-start | bytes 2359304 | tf_op jit(solution)/shard_map/ppermute | solution.py:46
  136.3 4.3 %collective-permute-start.8 = (bf16[512,768]{1,0:T(8,128)(2,1)S(1)}, bf16[512,768]{1,0:T(8,128)(2,1)S(1)}, u32[]{:S(2)}, u32[]{:S(2)}) collective-permute-start(bf16[512,768]{1,0:T(8,128)(2,1)S(1)} %get-tuple-element.50.refs_1_), channel_id=1, source_target_pairs={{0,32},{32,0},{1,33},{33,1},{2,34},{34,2},{3,35},{35,3},{4,36},{36... | collective-permute-start | bytes 2359304 | tf_op jit(solution)/shard_map/ppermute | solution.py:46
  167.2 31.1 %copy-start.8 = (bf16[512,128]{1,0:T(8,128)(2,1)S(1)}, bf16[512,128]{1,0:T(8,128)(2,1)}, u32[]{:S(2)}) copy-start(bf16[512,128]{1,0:T(8,128)(2,1)} %get-tuple-element.33.refs_1_) | copy-start | bytes 393220
  167.2 31.1 %copy-start.9 = (bf16[512,128]{1,0:T(8,128)(2,1)S(1)}, bf16[512,128]{1,0:T(8,128)(2,1)}, u32[]{:S(2)}) copy-start(bf16[512,128]{1,0:T(8,128)(2,1)} %get-tuple-element.32.refs_0_) | copy-start | bytes 393220
  167.2 31.1 %all-to-all-start.5 = ((bf16[16,64,1024]{2,1,0:T(8,128)(2,1)}), bf16[16,64,1024]{2,1,0:T(8,128)(2,1)S(1)}, u32[]{:S(2)}, u32[]{:S(2)}) async-start(bf16[16,64,1024]{2,1,0:T(8,128)(2,1)} %shard_map.109), calls=%async_computation.5 | async-start | bytes 4194304 | tf_op jit(solution)/shard_map/all_to_all | solution.py:50
  174.1 32.9 %collective-permute-start.11 = (bf16[128,1024]{1,0:T(8,128)(2,1)S(1)}, bf16[128,1024]{1,0:T(8,128)(2,1)S(1)}, u32[]{:S(2)}, u32[]{:S(2)}) collective-permute-start(bf16[128,1024]{1,0:T(8,128)(2,1)S(1)} %get-tuple-element.57), channel_id=1, source_target_pairs={{0,464},{1,465},{2,466},{3,467},{4,468},{5,469},{6,470},{7,471},{8... | collective-permute-start | bytes 786440 | tf_op jit(solution)/shard_map/ppermute | solution.py:40
  176.2 49.9 %collective-permute-start.12 = (bf16[128,1024]{1,0:T(8,128)(2,1)S(1)}, bf16[128,1024]{1,0:T(8,128)(2,1)S(1)}, u32[]{:S(2)}, u32[]{:S(2)}) collective-permute-start(bf16[128,1024]{1,0:T(8,128)(2,1)S(1)} %get-tuple-element.53), channel_id=1, source_target_pairs={{0,80},{1,81},{2,82},{3,83},{4,84},{5,85},{6,86},{7,87},{8,88},{9,... | collective-permute-start | bytes 786440 | tf_op jit(solution)/shard_map/ppermute | solution.py:40
  198.8 27.3 %collective-permute-start.9 = (bf16[128,1024]{1,0:T(8,128)(2,1)S(1)}, bf16[128,1024]{1,0:T(8,128)(2,1)S(1)}, u32[]{:S(2)}, u32[]{:S(2)}) collective-permute-start(bf16[128,1024]{1,0:T(8,128)(2,1)S(1)} %get-tuple-element.55), channel_id=1, source_target_pairs={{0,448},{1,449},{2,450},{3,451},{4,452},{5,453},{6,454},{7,455},{8... | collective-permute-start | bytes 786440 | tf_op jit(solution)/shard_map/ppermute | solution.py:40
  204.6 34.8 %collective-permute-start.10 = (bf16[128,1024]{1,0:T(8,128)(2,1)S(1)}, bf16[128,1024]{1,0:T(8,128)(2,1)S(1)}, u32[]{:S(2)}, u32[]{:S(2)}) collective-permute-start(bf16[128,1024]{1,0:T(8,128)(2,1)S(1)} %get-tuple-element.56), channel_id=1, source_target_pairs={{0,64},{1,65},{2,66},{3,67},{4,68},{5,69},{6,70},{7,71},{8,72},{9,... | collective-permute-start | bytes 786440 | tf_op jit(solution)/shard_map/ppermute | solution.py:40
  (6 other events, 6.1 us)

commit v7 on v6

--- a/solution.py
+++ b/solution.py
@@ -8,6 +8,8 @@
 from jax.sharding import Mesh, PartitionSpec as P
 
 SLOTS = 32
+HEAD = 24
+LANES = 128
 NODE = "node"
 PLANE = ("x", "y")
 RING = ("section", "zhi", "x", "y")
@@ -115,12 +117,46 @@
     return result
 
 
-def put(out_ref, at, hit, rows_ref):
-    experts = out_ref.shape[0]
+def flat(x):
+    blocks = x.shape[1] // LANES
+    pieces = [x[:HEAD, c * LANES : (c + 1) * LANES] for c in range(blocks)]
+    at = lax.broadcasted_iota(jnp.int32, (blocks, LANES), 0)
+    last = jnp.zeros((blocks, LANES), F32)
+    for c in range(blocks):
+        row = x[HEAD : HEAD + 1, c * LANES : (c + 1) * LANES]
+        last = jnp.where(at == c, jnp.broadcast_to(row, (blocks, LANES)), last)
+    return jnp.concatenate(pieces + [last], axis=0)
+
+
+def unflat(y):
+    blocks = y.shape[0] // (HEAD + 1)
+    tail = SLOTS - HEAD
+    columns = []
+    for c in range(blocks):
+        row = y[blocks * HEAD + c : blocks * HEAD + c + 1]
+        column = [y[c * HEAD : (c + 1) * HEAD], jnp.broadcast_to(row, (tail, LANES))]
+        columns.append(jnp.concatenate(column, axis=0))
+    return jnp.concatenate(columns, axis=1)
+
+
+def ship(out_ref, wides):
+    for e in range(out_ref.shape[0]):
+        rows = [flat(wide[e * SLOTS : (e + 1) * SLOTS, :]) for wide in wides]
+        out_ref[e] = jnp.concatenate(rows, axis=0).astype(BF)
+
+
+def unship(got_ref, wides):
+    each = got_ref.shape[1] // len(wides)
+    for e in range(got_ref.shape[0]):
+        rows = got_ref[e].astype(F32)
+        for i, wide in enumerate(wides):
+            wide[e * SLOTS : (e + 1) * SLOTS, :] = unflat(rows[i * each : (i + 1) * each]).astype(BF)
+
+
+def put(wide_ref, hit, rows_ref):
     tokens = hit.shape[1]
-    for c in range(0, out_ref.shape[2], WIDTH):
-        block = dot32(hit, rows_ref[:tokens, c : c + WIDTH]).astype(BF)
-        out_ref[:, at : at + SLOTS, c : c + WIDTH] = block.reshape(experts, SLOTS, WIDTH)
+    for c in range(0, wide_ref.shape[1], WIDTH):
+        wide_ref[:, c : c + WIDTH] = dot32(hit, rows_ref[:tokens, c : c + WIDTH])
 
 
 def block_tables(top, first_ref, block_ref, experts, tokens):
@@ -128,56 +164,66 @@
     return tables(note, first_ref[0], top, experts)
 
 
-def pack_near(top, first_ref, block_ref, a_ref, g_ref, out_ref, mix_f_ref, mix_b_ref):
+def pack_near(top, first_ref, block_ref, a_ref, g_ref, out_ref, mix_f_ref, mix_b_ref, *wides):
     (hit_f, mix_f), (hit_b, mix_b) = block_tables(
         top, first_ref, block_ref, out_ref.shape[0], a_ref.shape[0]
     )
     mix_f_ref[...] = mix_f
     mix_b_ref[...] = mix_b
-    put(out_ref, 0, hit_b, a_ref)
-    put(out_ref, SLOTS, hit_b, g_ref)
-    put(out_ref, 2 * SLOTS, hit_f, block_ref)
-
-
-def pack_far_f(top, first_ref, block_ref, out_ref, mix_f_ref, mix_b_ref, hit_b_ref):
+    put(wides[0], hit_b, a_ref)
+    put(wides[1], hit_b, g_ref)
+    put(wides[2], hit_f, block_ref)
+    ship(out_ref, wides)
+
+
+def pack_far_f(top, first_ref, block_ref, out_ref, mix_f_ref, mix_b_ref, hit_b_ref, *wides):
     (hit_f, mix_f), (hit_b, mix_b) = block_tables(
         top, first_ref, block_ref, out_ref.shape[0], mix_f_ref.shape[1]
     )
     mix_f_ref[...] = mix_f
     mix_b_ref[...] = mix_b
     hit_b_ref[...] = hit_b
-    put(out_ref, 0, hit_f, block_ref)
-
-
-def pack_far_b(hit_ref, a_ref, g_ref, out_ref):
-    put(out_ref, 0, hit_ref[...], a_ref)
-    put(out_ref, SLOTS, hit_ref[...], g_ref)
-
-
-def parts(kinds, got_ref, w_in_ref, w_out_ref, *outs):
-    experts, _, cols = got_ref.shape
-    for i, kind in enumerate(kinds):
-        x = got_ref[:, i * SLOTS : (i + 1) * SLOTS, :].reshape(experts * SLOTS, cols)
+    put(wides[0], hit_f, block_ref)
+    ship(out_ref, wides)
+
+
+def pack_far_b(hit_ref, a_ref, g_ref, out_ref, *wides):
+    put(wides[0], hit_ref[...], a_ref)
+    put(wides[1], hit_ref[...], g_ref)
+    ship(out_ref, wides)
+
+
+def parts(groups, *refs):
+    kinds = "".join(groups)
+    gots, refs = refs[: len(groups)], refs[len(groups) :]
+    w_in_ref, w_out_ref, *refs = refs
+    outs, wides = refs[: len(kinds)], refs[len(kinds) :]
+    at = 0
+    for got_ref, group in zip(gots, groups):
+        unship(got_ref, wides[at : at + len(group)])
+        at += len(group)
+    for kind, wide, out_ref in zip(kinds, wides, outs):
         for c in range(0, w_in_ref.shape[1], WIDTH):
             if kind == "g":
-                part = dot32(x, w_out_ref[c : c + WIDTH, :], TRANSPOSED)
+                part = dot32(wide[...], w_out_ref[c : c + WIDTH, :], TRANSPOSED)
             else:
-                part = dot32(x, w_in_ref[:, c : c + WIDTH])
-            outs[i][:, c : c + WIDTH] = part.astype(BF)
-
-
-def results(kinds, *refs):
+                part = dot32(wide[...], w_in_ref[:, c : c + WIDTH])
+            out_ref[:, c : c + WIDTH] = part.astype(BF)
+
+
+def results(groups, *refs):
+    kinds = "".join(groups)
     mine, theirs = refs[: len(kinds)], refs[len(kinds) : 2 * len(kinds)]
-    w_in_ref, w_out_ref, out_ref, hold_ref = refs[2 * len(kinds) :]
-    experts, _, cols = out_ref.shape
-    hidden = w_in_ref.shape[1]
+    w_in_ref, w_out_ref, *refs = refs[2 * len(kinds) :]
+    outs, hold_ref, wides = refs[: len(groups)], refs[len(groups)], refs[len(groups) + 1 :]
+    hidden, cols = w_in_ref.shape[1], w_in_ref.shape[0]
 
     def total(i, c):
         span = slice(c, c + WIDTH)
         return mine[i][:, span].astype(F32) + theirs[i][:, span].astype(F32)
 
-    i, at = 0, 0
-    while i < len(kinds):
+    i = 0
+    for wide in wides:
         forward = kinds[i] == "f"
         for c in range(0, hidden, WIDTH):
             pre = total(i, c)
@@ -192,23 +238,28 @@
                 block = dot32(hold_ref[...], w_out_ref[:, c : c + WIDTH])
             else:
                 block = dot32(hold_ref[...], w_in_ref[c : c + WIDTH, :], TRANSPOSED)
-            out_ref[:, at : at + SLOTS, c : c + WIDTH] = block.astype(BF).reshape(
-                experts, SLOTS, WIDTH
-            )
+            wide[:, c : c + WIDTH] = block
         i += 1 if forward else 2
-        at += SLOTS
+    at = 0
+    for out_ref, group in zip(outs, groups):
+        many = made(group)
+        ship(out_ref, wides[at : at + many])
+        at += many
+
+
+def made(group):
+    return group.count("f") + group.count("a")
 
 
 def sums(count, *refs):
-    mixes, backs, outs = refs[:count], refs[count:-count], refs[-count:]
-    experts, _, cols = backs[0].shape
-    for i in range(count):
-        mix = mixes[i][...]
-        back_ref, at = (backs[i], 0) if len(backs) > 1 else (backs[0], i * SLOTS)
-        for c in range(0, cols, WIDTH):
-            rows = back_ref[:, at : at + SLOTS, c : c + WIDTH]
-            rows = rows.reshape(experts * SLOTS, WIDTH)
-            outs[i][:, c : c + WIDTH] = dot32(mix, rows, OVER_ROWS).astype(BF)
+    mixes, wides = refs[:count], refs[-count:]
+    backs, outs = refs[count : -2 * count], refs[-2 * count : -count]
+    for i, back_ref in enumerate(backs):
+        unship(back_ref, [wides[i]] if len(backs) > 1 else wides)
+    for mix_ref, wide, out_ref in zip(mixes, wides, outs):
+        for c in range(0, out_ref.shape[1], WIDTH):
+            total = dot32(mix_ref[...], wide[:, c : c + WIDTH], OVER_ROWS)
+            out_ref[:, c : c + WIDTH] = total.astype(BF)
 
 
 def hold(a_ref, b_ref, x_ref, y_ref):
@@ -242,29 +293,40 @@
     first = (lax.axis_index("zhi") * experts).astype(jnp.int32).reshape(1)
     table = shaped(rows, tok)
 
-    def work(got, kinds):
+    def wide(count, dtype):
+        return [pltpu.VMEM((rows, cols), dtype)] * count
+
+    def sendable(kinds):
+        return shaped(experts, kinds * (HEAD + 1) * (cols // LANES), LANES)
+
+    def work(gots, *groups):
+        count = len("".join(groups))
         mine = run(
-            functools.partial(parts, kinds),
-            (shaped(rows, hidden),) * len(kinds),
-            got,
+            functools.partial(parts, groups),
+            (shaped(rows, hidden),) * count,
+            *gots,
             weight_in,
             weight_out,
+            scratch=wide(count, BF),
         )
         theirs = [other_core(part) for part in mine]
-        many = kinds.count("f") + kinds.count("a")
         return run(
-            functools.partial(results, kinds),
-            shaped(experts, many * SLOTS, cols),
+            functools.partial(results, groups),
+            tuple(sendable(made(group)) for group in groups),
             *mine,
             *theirs,
             weight_in,
             weight_out,
-            scratch=[pltpu.VMEM((rows, hidden), BF)],
+            scratch=[pltpu.VMEM((rows, hidden), BF)] + wide(made("".join(groups)), F32),
         )
 
     def combined(back, *mixes):
         return run(
-            functools.partial(sums, len(mixes)), (shaped(tok, cols),) * len(mixes), *mixes, *back
+            functools.partial(sums, len(mixes)),
+            (shaped(tok, cols),) * len(mixes),
+            *mixes,
+            *back,
+            scratch=wide(len(mixes), BF),
         )
 
     block = run(
@@ -284,32 +346,39 @@
 
     sent, mix_f, mix_b = run(
         functools.partial(pack_near, top),
-        (shaped(experts, 3 * SLOTS, cols), table, table),
+        (sendable(3), table, table),
         first,
         block,
         act_backward,
         grad_backward,
         scalars=1,
+        scratch=wide(3, F32),
         room=56 << 20,
     )
     got = exchange(sent)
     sent_f, far_mix_f, far_mix_b, far_hit_b = run(
         functools.partial(pack_far_f, top),
-        (shaped(experts, SLOTS, cols), table, table, table),
+        (sendable(1), table, table, table),
         first,
         far_block,
         scalars=1,
+        scratch=wide(1, F32),
         flops=LONG,
     )
     got_f = exchange(after(sent_f, got))
     sent_b = run(
-        pack_far_b, shaped(experts, 2 * SLOTS, cols), far_hit_b, far_a, far_g, flops=LONG
+        pack_far_b,
+        sendable(2),
+        far_hit_b,
+        far_a,
+        far_g,
+        scratch=wide(2, F32),
+        flops=LONG,
     )
     got_b = exchange(after(sent_b, got_f))
-    out = work(after(got, sent_b, got_f), "agf")
-    out_f = work(after(got_f, out), "f")
+    out, out_f = work((after(got, sent_b), got_f), "agf", "f")
     back_f = exchange(after(out_f, got_b))
-    out_b = work(after(got_b, out_f), "ag")
+    (out_b,) = work((after(got_b, out_f),), "ag")
     back_b = exchange(after(out_b, back_f))
     far_sum_b, far_sum_f = combined((back_b, back_f), far_mix_b, far_mix_f)
     over = (moved(far_sum_b, -1, True), moved(far_sum_f, 1, True))

time: 241 us -> 235 us (0.975)
  the two profiles are of different devices: /device:TPU:18 before, /device:TPU:99 now
where the time goes in v7:
time: 235 us; the launch traced here: 233 us
  starting transfers between devices  114 us (49%)
  waiting for transfers between devices  68.6 us (29%)
  Pallas kernels  27.1 us (12%)
  blocking collectives  16.6 us (7%)
  local copies, waits for them, and re-layouts  6.14 us (3%)
    ppermute x7, starting transfers between devices, moved(): lax.ppermute(v, RING, pairs_of(shape, lambda s, h: ((s + by) % sections,...  57.2 us
    ppermute x7, waiting for transfers between devices, moved(): lax.ppermute(v, RING, pairs_of(shape, lambda s, h: ((s + by) % sections,...  47.5 us
    all_to_all x5, starting transfers between devices, exchange(): return lax.all_to_all(v, PLANE, split_axis=0, concat_axis=0, tiled=True)  32.8 us
    pallas_call x12, Pallas kernels, run(): pl.pallas_call(kernel, out_shape=outs, in_specs=where, out_specs=jax.tree...  27.1 us
    ppermute x6, starting transfers between devices, other_core(): return lax.ppermute(v, NODE, [(0, 1), (1, 0)])  24 us
    all_to_all x5, waiting for transfers between devices, exchange(): return lax.all_to_all(v, PLANE, split_axis=0, concat_axis=0, tiled=True)  18.9 us
    all_to_all x1, blocking collectives, exchange(): return lax.all_to_all(v, PLANE, split_axis=0, concat_axis=0, tiled=True)  16.6 us
    unnamed x18, local copies, waits for them, and re-layouts  6.14 us
  transfers between devices with their start and end apart: 18, of which 9 were waited for; matrix products, arithmetic and copies ran while one was open for 0% of the time, Pallas kernels for 8%

profile of v7, /device:TPU:99, one launch (start us, length us, event | category | flops | bytes accessed | tf_op | source)
XLA Modules:
  0.0 233.4 jit_solution(3889984861515474600)
XLA Ops:
  2.4 12.7 %collective-permute-start = (bf16[144,1024]{1,0:T(8,128)(2,1)}, bf16[144,1024]{1,0:T(8,128)(2,1)S(1)}, u32[]{:S(2)}, u32[]{:S(2)}) collective-permute-start(bf16[144,1024]{1,0:T(8,128)(2,1)} %shard_map.104.block_ref), channel_id=1, source_target_pairs={{0,16},{1,17},{2,18},{3,19},{4,20},{5,21},{6,22},{7,23},{8,24},{9,... | collective-permute-start | bytes 884744 | tf_op jit(solution)/shard_map/ppermute | solution.py:42
  15.1 3.7 %shard_map.105 = (bf16[16,600,128]{2,1,0:T(8,128)(2,1)}, bf16[512,128]{1,0:T(8,128)(2,1)}, bf16[512,128]{1,0:T(8,128)(2,1)}) custom-call(s32[1]{0:T(128)} %bitcast.first_ref, bf16[144,1024]{1,0:T(8,128)(2,1)} %shard_map.104.block_ref, bf16[128,1024]{1,0:T(8,128)(2,1)} %a_ref.1, bf16[128,1024]{1,0:T(8,128)(2,1)} %g_ref.1), custom_call_target="tpu_custom_call" | custom-call | flops 1000 | bytes 1000 | tf_op jit(solution)/shard_map/pallas_call | solution.py:66
  18.8 6.9 %all-to-all-start = ((bf16[16,600,128]{2,1,0:T(8,128)(2,1)}), bf16[16,600,128]{2,1,0:T(8,128)(2,1)S(1)}, u32[]{:S(2)}, u32[]{:S(2)}) async-start(bf16[16,600,128]{2,1,0:T(8,128)(2,1)} %get-tuple-element.36), calls=%async_computation | async-start | bytes 4915200 | tf_op jit(solution)/shard_map/all_to_all | solution.py:52
  25.7 3.4 %collective-permute-done.block_ref = bf16[144,1024]{1,0:T(8,128)(2,1)S(1)} collective-permute-done((bf16[144,1024]{1,0:T(8,128)(2,1)}, bf16[144,1024]{1,0:T(8,128)(2,1)S(1)}, u32[]{:S(2)}, u32[]{:S(2)}) %collective-permute-start) | collective-permute-done | bytes 294944 | tf_op jit(solution)/shard_map/ppermute | solution.py:42
  29.2 11.9 %collective-permute-start.1 = (bf16[128,1024]{1,0:T(8,128)(2,1)}, bf16[128,1024]{1,0:T(8,128)(2,1)S(1)}, u32[]{:S(2)}, u32[]{:S(2)}) collective-permute-start(bf16[128,1024]{1,0:T(8,128)(2,1)} %a_ref.1), channel_id=1, source_target_pairs={{0,16},{1,17},{2,18},{3,19},{4,20},{5,21},{6,22},{7,23},{8,24},{9,... | collective-permute-start | bytes 786440 | tf_op jit(solution)/shard_map/ppermute | solution.py:42
  44.6 9.6 %all-to-all-done.refs_0_ = bf16[16,600,128]{2,1,0:T(8,128)(2,1)S(1)} async-done(((bf16[16,600,128]{2,1,0:T(8,128)(2,1)}), bf16[16,600,128]{2,1,0:T(8,128)(2,1)S(1)}, u32[]{:S(2)}, u32[]{:S(2)}) %all-to-all-start) | async-done | bytes 2457632 | tf_op jit(solution)/shard_map/all_to_all | solution.py:52
  55.7 7.1 %all-to-all-start.1 = ((bf16[16,200,128]{2,1,0:T(8,128)(2,1)}), bf16[16,200,128]{2,1,0:T(8,128)(2,1)}, u32[]{:S(2)}, u32[]{:S(2)}) async-start(bf16[16,200,128]{2,1,0:T(8,128)(2,1)} %get-tuple-element.42), calls=%async_computation.1 | async-start | bytes 1638400 | tf_op jit(solution)/shard_map/all_to_all | solution.py:52
  62.8 4.5 %collective-permute-done.2.g_ref = bf16[128,1024]{1,0:T(8,128)(2,1)} collective-permute-done((bf16[128,1024]{1,0:T(8,128)(2,1)}, bf16[128,1024]{1,0:T(8,128)(2,1)}, u32[]{:S(2)}, u32[]{:S(2)}) %collective-permute-start.2) | collective-permute-done | bytes 262176 | tf_op jit(solution)/shard_map/ppermute | solution.py:42
  71.5 6.5 %all-to-all-start.2 = ((bf16[16,400,128]{2,1,0:T(8,128)(2,1)}), bf16[16,400,128]{2,1,0:T(8,128)(2,1)}, u32[]{:S(2)}, u32[]{:S(2)}) async-start(bf16[16,400,128]{2,1,0:T(8,128)(2,1)} %copy-done.5), calls=%async_computation.2 | async-start | bytes 3276800 | tf_op jit(solution)/shard_map/all_to_all | solution.py:52
  79.7 4.6 %shard_map.108 = (bf16[512,768]{1,0:T(8,128)(2,1)S(1)}, bf16[512,768]{1,0:T(8,128)(2,1)S(1)}, bf16[512,768]{1,0:T(8,128)(2,1)S(1)}, bf16[512,768]{1,0:T(8,128)(2,1)S(1)}) custom-call(bf16[16,600,128]{2,1,0:T(8,128)(2,1)S(1)} %copy-done.3, bf16[16,200,128]{2,1,0:T(8,128)(2,1)} %all-to-all-done.1.refs_1_, bf16[1024,768]{1,0:T(8,128)(2,1)S(1)} %bitcast.7, ...), custom_call_target="tpu_custom_call" | custom-call | flops 1000 | bytes 1000 | tf_op jit(solution)/shard_map/pallas_call | solution.py:66
  84.3 13.5 %collective-permute-start.3 = (bf16[512,768]{1,0:T(8,128)(2,1)S(1)}, bf16[512,768]{1,0:T(8,128)(2,1)S(1)}, u32[]{:S(2)}, u32[]{:S(2)}) collective-permute-start(bf16[512,768]{1,0:T(8,128)(2,1)S(1)} %get-tuple-element.43.refs_0_), channel_id=1, source_target_pairs={{0,32},{32,0},{1,33},{33,1},{2,34},{34,2},{3,35},{35,3},{4,36},{36... | collective-permute-start | bytes 2359304 | tf_op jit(solution)/shard_map/ppermute | solution.py:48
  99.7 2.4 %collective-permute-start.5 = (bf16[512,768]{1,0:T(8,128)(2,1)S(1)}, bf16[512,768]{1,0:T(8,128)(2,1)S(1)}, u32[]{:S(2)}, u32[]{:S(2)}) collective-permute-start(bf16[512,768]{1,0:T(8,128)(2,1)S(1)} %get-tuple-element.45.refs_2_), channel_id=1, source_target_pairs={{0,32},{32,0},{1,33},{33,1},{2,34},{34,2},{3,35},{35,3},{4,36},{36... | collective-permute-start | bytes 2359304 | tf_op jit(solution)/shard_map/ppermute | solution.py:48
  106.3 3.5 %shard_map.109 = (bf16[16,400,128]{2,1,0:T(8,128)(2,1)}, bf16[16,200,128]{2,1,0:T(8,128)(2,1)S(1)}) custom-call(bf16[512,768]{1,0:T(8,128)(2,1)S(1)} %get-tuple-element.43.refs_0_, bf16[512,768]{1,0:T(8,128)(2,1)S(1)} %get-tuple-element.44.refs_1_, bf16[512,768]{1,0:T(8,128)(2,1)S(1)} %get-tuple-element.45.refs_2_, ...), custom_call_target="tpu_custom_call" | custom-call | flops 1000 | bytes 1000 | tf_op jit(solution)/shard_map/pallas_call | solution.py:66
  110.7 4.2 %shard_map.110 = (bf16[512,768]{1,0:T(8,128)(2,1)}, bf16[512,768]{1,0:T(8,128)(2,1)}) custom-call(bf16[16,400,128]{2,1,0:T(8,128)(2,1)} %all-to-all-done.2.refs_0_, bf16[1024,768]{1,0:T(8,128)(2,1)S(1)} %bitcast.9, bf16[768,1024]{1,0:T(8,128)(2,1)S(1)} %bitcast.13), custom_call_target="tpu_custom_call" | custom-call | flops 1000 | bytes 1000 | tf_op jit(solution)/shard_map/pallas_call | solution.py:66
  116.9 2.3 collective-permute-start.8
  119.2 6.7 %all-to-all-start.3 = ((bf16[16,200,128]{2,1,0:T(8,128)(2,1)}), bf16[16,200,128]{2,1,0:T(8,128)(2,1)}, u32[]{:S(2)}, u32[]{:S(2)}) async-start(bf16[16,200,128]{2,1,0:T(8,128)(2,1)} %copy-done.6), calls=%async_computation.3 | async-start | bytes 1638400 | tf_op jit(solution)/shard_map/all_to_all | solution.py:52
  125.9 3.3 %shard_map.111 = bf16[16,200,128]{2,1,0:T(8,128)(2,1)S(1)} custom-call(bf16[512,768]{1,0:T(8,128)(2,1)} %get-tuple-element.53.refs_0_, bf16[512,768]{1,0:T(8,128)(2,1)} %get-tuple-element.54.refs_1_, bf16[512,768]{1,0:T(8,128)(2,1)} %collective-permute-done.7.refs_2_, bf16[512,768]{1,0:T(8,128)(2,1)} %collective-permute-done.8.refs_3_, ...), custom_call_target="tpu_custom_call" | custom-call | flops 1000 | bytes 1000 | tf_op jit(solution)/shard_map/pallas_call | solution.py:66
  130.1 7.7 %all-to-all-done.3.refs_3_ = bf16[16,200,128]{2,1,0:T(8,128)(2,1)} async-done(((bf16[16,200,128]{2,1,0:T(8,128)(2,1)}), bf16[16,200,128]{2,1,0:T(8,128)(2,1)}, u32[]{:S(2)}, u32[]{:S(2)}) %all-to-all-start.3) | async-done | bytes 819232 | tf_op jit(solution)/shard_map/all_to_all | solution.py:52
  137.8 16.6 %all_to_all.30.refs_2_ = bf16[16,200,128]{2,1,0:T(8,128)(2,1)S(1)} all-to-all(bf16[16,200,128]{2,1,0:T(8,128)(2,1)} %copy-done.4), channel_id=1, replica_groups=mesh['section'=8,'node'=2,'zhi'=2,'x'=4,'y'=4] {'x','y'}, dimensions={0} | all-to-all | bytes 1638400 | tf_op jit(solution)/shard_map/all_to_all | solution.py:52
  156.1 5.6 %all-to-all-start.5 = ((bf16[16,400,128]{2,1,0:T(8,128)(2,1)}), bf16[16,400,128]{2,1,0:T(8,128)(2,1)S(1)}, u32[]{:S(2)}, u32[]{:S(2)}) async-start(bf16[16,400,128]{2,1,0:T(8,128)(2,1)} %get-tuple-element.58), calls=%async_computation.5 | async-start | bytes 3276800 | tf_op jit(solution)/shard_map/all_to_all | solution.py:52
  161.7 16.5 %collective-permute-start.11 = (bf16[128,1024]{1,0:T(8,128)(2,1)S(1)}, bf16[128,1024]{1,0:T(8,128)(2,1)S(1)}, u32[]{:S(2)}, u32[]{:S(2)}) collective-permute-start(bf16[128,1024]{1,0:T(8,128)(2,1)S(1)} %get-tuple-element.61), channel_id=1, source_target_pairs={{0,464},{1,465},{2,466},{3,467},{4,468},{5,469},{6,470},{7,471},{8... | collective-permute-start | bytes 786440 | tf_op jit(solution)/shard_map/ppermute | solution.py:42
  180.9 4.2 %collective-permute-start.9 = (bf16[128,1024]{1,0:T(8,128)(2,1)S(1)}, bf16[128,1024]{1,0:T(8,128)(2,1)S(1)}, u32[]{:S(2)}, u32[]{:S(2)}) collective-permute-start(bf16[128,1024]{1,0:T(8,128)(2,1)S(1)} %get-tuple-element.59), channel_id=1, source_target_pairs={{0,448},{1,449},{2,450},{3,451},{4,452},{5,453},{6,454},{7,455},{8... | collective-permute-start | bytes 786440 | tf_op jit(solution)/shard_map/ppermute | solution.py:42
  185.1 7.9 %collective-permute-start.10 = (bf16[128,1024]{1,0:T(8,128)(2,1)S(1)}, bf16[128,1024]{1,0:T(8,128)(2,1)S(1)}, u32[]{:S(2)}, u32[]{:S(2)}) collective-permute-start(bf16[128,1024]{1,0:T(8,128)(2,1)S(1)} %get-tuple-element.60), channel_id=1, source_target_pairs={{0,64},{1,65},{2,66},{3,67},{4,68},{5,69},{6,70},{7,71},{8,72},{9,... | collective-permute-start | bytes 786440 | tf_op jit(solution)/shard_map/ppermute | solution.py:42
  193.5 39.0 %collective-permute-done.9.a_ref = bf16[128,1024]{1,0:T(8,128)(2,1)S(1)} collective-permute-done((bf16[128,1024]{1,0:T(8,128)(2,1)S(1)}, bf16[128,1024]{1,0:T(8,128)(2,1)S(1)}, u32[]{:S(2)}, u32[]{:S(2)}) %collective-permute-start.9) | collective-permute-done | bytes 262176 | tf_op jit(solution)/shard_map/ppermute | solution.py:42
  (43 shorter events, 28.2 us)
Async XLA Ops:
  2.4 26.8 %collective-permute-start = (bf16[144,1024]{1,0:T(8,128)(2,1)}, bf16[144,1024]{1,0:T(8,128)(2,1)S(1)}, u32[]{:S(2)}, u32[]{:S(2)}) collective-permute-start(bf16[144,1024]{1,0:T(8,128)(2,1)} %shard_map.104.block_ref), channel_id=1, source_target_pairs={{0,16},{1,17},{2,18},{3,19},{4,20},{5,21},{6,22},{7,23},{8,24},{9,... | collective-permute-start | bytes 884744 | tf_op jit(solution)/shard_map/ppermute | solution.py:42
  18.8 35.4 %all-to-all-start = ((bf16[16,600,128]{2,1,0:T(8,128)(2,1)}), bf16[16,600,128]{2,1,0:T(8,128)(2,1)S(1)}, u32[]{:S(2)}, u32[]{:S(2)}) async-start(bf16[16,600,128]{2,1,0:T(8,128)(2,1)} %get-tuple-element.36), calls=%async_computation | async-start | bytes 4915200 | tf_op jit(solution)/shard_map/all_to_all | solution.py:52
  29.2 33.6 %collective-permute-start.1 = (bf16[128,1024]{1,0:T(8,128)(2,1)}, bf16[128,1024]{1,0:T(8,128)(2,1)S(1)}, u32[]{:S(2)}, u32[]{:S(2)}) collective-permute-start(bf16[128,1024]{1,0:T(8,128)(2,1)} %a_ref.1), channel_id=1, source_target_pairs={{0,16},{1,17},{2,18},{3,19},{4,20},{5,21},{6,22},{7,23},{8,24},{9,... | collective-permute-start | bytes 786440 | tf_op jit(solution)/shard_map/ppermute | solution.py:42
  41.1 26.3 %collective-permute-start.2 = (bf16[128,1024]{1,0:T(8,128)(2,1)}, bf16[128,1024]{1,0:T(8,128)(2,1)}, u32[]{:S(2)}, u32[]{:S(2)}) collective-permute-start(bf16[128,1024]{1,0:T(8,128)(2,1)} %g_ref.1), channel_id=1, source_target_pairs={{0,16},{1,17},{2,18},{3,19},{4,20},{5,21},{6,22},{7,23},{8,24},{9,... | collective-permute-start | bytes 786440 | tf_op jit(solution)/shard_map/ppermute | solution.py:42
  54.2 1.5 copy-start.2
  55.7 15.8 %all-to-all-start.1 = ((bf16[16,200,128]{2,1,0:T(8,128)(2,1)}), bf16[16,200,128]{2,1,0:T(8,128)(2,1)}, u32[]{:S(2)}, u32[]{:S(2)}) async-start(bf16[16,200,128]{2,1,0:T(8,128)(2,1)} %get-tuple-element.42), calls=%async_computation.1 | async-start | bytes 1638400 | tf_op jit(solution)/shard_map/all_to_all | solution.py:52
  70.2 7.8 %copy-start = (bf16[1,1,1024,768]{3,2,1,0:T(8,128)(2,1)S(1)}, bf16[1,1,1024,768]{3,2,1,0:T(8,128)(2,1)}, u32[]{:S(2)}) copy-start(bf16[1,1,1024,768]{3,2,1,0:T(8,128)(2,1)} %param.16) | copy-start | bytes 4718596
  70.2 7.8 %copy-start.1 = (bf16[1,1,768,1024]{3,2,1,0:T(8,128)(2,1)S(1)}, bf16[1,1,768,1024]{3,2,1,0:T(8,128)(2,1)}, u32[]{:S(2)}) copy-start(bf16[1,1,768,1024]{3,2,1,0:T(8,128)(2,1)} %param.17) | copy-start | bytes 4718596
  71.5 39.2 %all-to-all-start.2 = ((bf16[16,400,128]{2,1,0:T(8,128)(2,1)}), bf16[16,400,128]{2,1,0:T(8,128)(2,1)}, u32[]{:S(2)}, u32[]{:S(2)}) async-start(bf16[16,400,128]{2,1,0:T(8,128)(2,1)} %copy-done.5), calls=%async_computation.2 | async-start | bytes 3276800 | tf_op jit(solution)/shard_map/all_to_all | solution.py:52
  78.0 1.7 copy-start.3
  84.3 19.7 %collective-permute-start.3 = (bf16[512,768]{1,0:T(8,128)(2,1)S(1)}, bf16[512,768]{1,0:T(8,128)(2,1)S(1)}, u32[]{:S(2)}, u32[]{:S(2)}) collective-permute-start(bf16[512,768]{1,0:T(8,128)(2,1)S(1)} %get-tuple-element.43.refs_0_), channel_id=1, source_target_pairs={{0,32},{32,0},{1,33},{33,1},{2,34},{34,2},{3,35},{35,3},{4,36},{36... | collective-permute-start | bytes 2359304 | tf_op jit(solution)/shard_map/ppermute | solution.py:48
  97.8 6.3 %collective-permute-start.4 = (bf16[512,768]{1,0:T(8,128)(2,1)S(1)}, bf16[512,768]{1,0:T(8,128)(2,1)S(1)}, u32[]{:S(2)}, u32[]{:S(2)}) collective-permute-start(bf16[512,768]{1,0:T(8,128)(2,1)S(1)} %get-tuple-element.44.refs_1_), channel_id=1, source_target_pairs={{0,32},{32,0},{1,33},{33,1},{2,34},{34,2},{3,35},{35,3},{4,36},{36... | collective-permute-start | bytes 2359304 | tf_op jit(solution)/shard_map/ppermute | solution.py:48
  99.7 4.4 %collective-permute-start.5 = (bf16[512,768]{1,0:T(8,128)(2,1)S(1)}, bf16[512,768]{1,0:T(8,128)(2,1)S(1)}, u32[]{:S(2)}, u32[]{:S(2)}) collective-permute-start(bf16[512,768]{1,0:T(8,128)(2,1)S(1)} %get-tuple-element.45.refs_2_), channel_id=1, source_target_pairs={{0,32},{32,0},{1,33},{33,1},{2,34},{34,2},{3,35},{35,3},{4,36},{36... | collective-permute-start | bytes 2359304 | tf_op jit(solution)/shard_map/ppermute | solution.py:48
  102.1 4.2 %collective-permute-start.6 = (bf16[512,768]{1,0:T(8,128)(2,1)S(1)}, bf16[512,768]{1,0:T(8,128)(2,1)S(1)}, u32[]{:S(2)}, u32[]{:S(2)}) collective-permute-start(bf16[512,768]{1,0:T(8,128)(2,1)S(1)} %get-tuple-element.46.refs_3_), channel_id=1, source_target_pairs={{0,32},{32,0},{1,33},{33,1},{2,34},{34,2},{3,35},{35,3},{4,36},{36... | collective-permute-start | bytes 2359304 | tf_op jit(solution)/shard_map/ppermute | solution.py:48
  114.9 11.0 %collective-permute-start.7 = (bf16[512,768]{1,0:T(8,128)(2,1)}, bf16[512,768]{1,0:T(8,128)(2,1)}, u32[]{:S(2)}, u32[]{:S(2)}) collective-permute-start(bf16[512,768]{1,0:T(8,128)(2,1)} %get-tuple-element.53.refs_0_), channel_id=1, source_target_pairs={{0,32},{32,0},{1,33},{33,1},{2,34},{34,2},{3,35},{35,3},{4,36},{36... | collective-permute-start | bytes 2359304 | tf_op jit(solution)/shard_map/ppermute | solution.py:48
  116.9 9.0 %collective-permute-start.8 = (bf16[512,768]{1,0:T(8,128)(2,1)}, bf16[512,768]{1,0:T(8,128)(2,1)}, u32[]{:S(2)}, u32[]{:S(2)}) collective-permute-start(bf16[512,768]{1,0:T(8,128)(2,1)} %get-tuple-element.54.refs_1_), channel_id=1, source_target_pairs={{0,32},{32,0},{1,33},{33,1},{2,34},{34,2},{3,35},{35,3},{4,36},{36... | collective-permute-start | bytes 2359304 | tf_op jit(solution)/shard_map/ppermute | solution.py:48
  119.2 18.6 %all-to-all-start.3 = ((bf16[16,200,128]{2,1,0:T(8,128)(2,1)}), bf16[16,200,128]{2,1,0:T(8,128)(2,1)}, u32[]{:S(2)}, u32[]{:S(2)}) async-start(bf16[16,200,128]{2,1,0:T(8,128)(2,1)} %copy-done.6), calls=%async_computation.3 | async-start | bytes 1638400 | tf_op jit(solution)/shard_map/all_to_all | solution.py:52
  156.1 24.3 %copy-start.7 = (bf16[512,128]{1,0:T(8,128)(2,1)S(1)}, bf16[512,128]{1,0:T(8,128)(2,1)}, u32[]{:S(2)}) copy-start(bf16[512,128]{1,0:T(8,128)(2,1)} %get-tuple-element.35.refs_1_) | copy-start | bytes 393220
  156.1 24.3 %copy-start.8 = (bf16[512,128]{1,0:T(8,128)(2,1)S(1)}, bf16[512,128]{1,0:T(8,128)(2,1)}, u32[]{:S(2)}) copy-start(bf16[512,128]{1,0:T(8,128)(2,1)} %get-tuple-element.34.refs_0_) | copy-start | bytes 393220
  156.1 24.3 %all-to-all-start.5 = ((bf16[16,400,128]{2,1,0:T(8,128)(2,1)}), bf16[16,400,128]{2,1,0:T(8,128)(2,1)S(1)}, u32[]{:S(2)}, u32[]{:S(2)}) async-start(bf16[16,400,128]{2,1,0:T(8,128)(2,1)} %get-tuple-element.58), calls=%async_computation.5 | async-start | bytes 3276800 | tf_op jit(solution)/shard_map/all_to_all | solution.py:52
  161.7 31.3 %collective-permute-start.11 = (bf16[128,1024]{1,0:T(8,128)(2,1)S(1)}, bf16[128,1024]{1,0:T(8,128)(2,1)S(1)}, u32[]{:S(2)}, u32[]{:S(2)}) collective-permute-start(bf16[128,1024]{1,0:T(8,128)(2,1)S(1)} %get-tuple-element.61), channel_id=1, source_target_pairs={{0,464},{1,465},{2,466},{3,467},{4,468},{5,469},{6,470},{7,471},{8... | collective-permute-start | bytes 786440 | tf_op jit(solution)/shard_map/ppermute | solution.py:42
  178.2 15.2 %collective-permute-start.12 = (bf16[128,1024]{1,0:T(8,128)(2,1)S(1)}, bf16[128,1024]{1,0:T(8,128)(2,1)S(1)}, u32[]{:S(2)}, u32[]{:S(2)}) collective-permute-start(bf16[128,1024]{1,0:T(8,128)(2,1)S(1)} %get-tuple-element.57), channel_id=1, source_target_pairs={{0,80},{1,81},{2,82},{3,83},{4,84},{5,85},{6,86},{7,87},{8,88},{9,... | collective-permute-start | bytes 786440 | tf_op jit(solution)/shard_map/ppermute | solution.py:42
  180.9 51.6 %collective-permute-start.9 = (bf16[128,1024]{1,0:T(8,128)(2,1)S(1)}, bf16[128,1024]{1,0:T(8,128)(2,1)S(1)}, u32[]{:S(2)}, u32[]{:S(2)}) collective-permute-start(bf16[128,1024]{1,0:T(8,128)(2,1)S(1)} %get-tuple-element.59), channel_id=1, source_target_pairs={{0,448},{1,449},{2,450},{3,451},{4,452},{5,453},{6,454},{7,455},{8... | collective-permute-start | bytes 786440 | tf_op jit(solution)/shard_map/ppermute | solution.py:42
  185.1 47.4 %collective-permute-start.10 = (bf16[128,1024]{1,0:T(8,128)(2,1)S(1)}, bf16[128,1024]{1,0:T(8,128)(2,1)S(1)}, u32[]{:S(2)}, u32[]{:S(2)}) collective-permute-start(bf16[128,1024]{1,0:T(8,128)(2,1)S(1)} %get-tuple-element.60), channel_id=1, source_target_pairs={{0,64},{1,65},{2,66},{3,67},{4,68},{5,69},{6,70},{7,71},{8,72},{9,... | collective-permute-start | bytes 786440 | tf_op jit(solution)/shard_map/ppermute | solution.py:42
  (3 other events, 3.0 us)

commit v8 on v7

--- a/solution.py
+++ b/solution.py
@@ -78,17 +78,18 @@
     return jax.ShapeDtypeStruct(shape, BF)
 
 
-def gather_block(f_ref, *refs):
+def gather_block(a_ref, g_ref, *refs):
     notes, out_ref, hold_ref = refs[:4], refs[4], refs[5]
-    tokens = f_ref.shape[0]
+    tokens = a_ref.shape[0]
     top = notes[0].shape[0]
-    out_ref[:tokens, :] = f_ref[...]
+    out_ref[:tokens, :] = a_ref[...]
+    out_ref[tokens : 2 * tokens, :] = g_ref[...]
     hold_ref[...] = jnp.zeros(hold_ref.shape, F32)
     for half in range(2):
         span = slice(half * tokens, (half + 1) * tokens)
         hold_ref[:top, span] = notes[2 * half][...].astype(F32)
         hold_ref[8 : 8 + top, span] = notes[2 * half + 1][...].astype(F32)
-    out_ref[tokens:, :] = hold_ref[...].astype(BF)
+    out_ref[2 * tokens :, :] = hold_ref[...].astype(BF)
 
 
 def tables(note, first, top, experts):
@@ -153,43 +154,45 @@
             wide[e * SLOTS : (e + 1) * SLOTS, :] = unflat(rows[i * each : (i + 1) * each]).astype(BF)
 
 
-def put(wide_ref, hit, rows_ref):
-    tokens = hit.shape[1]
+def put(wide_ref, hit, rows_ref, first=0):
+    rows = slice(first, first + hit.shape[1])
     for c in range(0, wide_ref.shape[1], WIDTH):
-        wide_ref[:, c : c + WIDTH] = dot32(hit, rows_ref[:tokens, c : c + WIDTH])
+        wide_ref[:, c : c + WIDTH] = dot32(hit, rows_ref[rows, c : c + WIDTH])
 
 
 def block_tables(top, first_ref, block_ref, experts, tokens):
-    note = block_ref[tokens:, : 2 * tokens].astype(F32)
+    note = block_ref[2 * tokens :, : 2 * tokens].astype(F32)
     return tables(note, first_ref[0], top, experts)
 
 
-def pack_near(top, first_ref, block_ref, a_ref, g_ref, out_ref, mix_f_ref, mix_b_ref, *wides):
+def pack_near(top, first_ref, block_ref, f_ref, out_ref, mix_f_ref, mix_b_ref, *wides):
+    tokens = f_ref.shape[0]
     (hit_f, mix_f), (hit_b, mix_b) = block_tables(
-        top, first_ref, block_ref, out_ref.shape[0], a_ref.shape[0]
+        top, first_ref, block_ref, out_ref.shape[0], tokens
     )
     mix_f_ref[...] = mix_f
     mix_b_ref[...] = mix_b
-    put(wides[0], hit_b, a_ref)
-    put(wides[1], hit_b, g_ref)
-    put(wides[2], hit_f, block_ref)
+    put(wides[0], hit_b, block_ref)
+    put(wides[1], hit_b, block_ref, tokens)
+    put(wides[2], hit_f, f_ref)
     ship(out_ref, wides)
 
 
-def pack_far_f(top, first_ref, block_ref, out_ref, mix_f_ref, mix_b_ref, hit_b_ref, *wides):
+def pack_far_b(top, first_ref, block_ref, out_ref, mix_f_ref, mix_b_ref, hit_f_ref, *wides):
+    tokens = mix_f_ref.shape[1]
     (hit_f, mix_f), (hit_b, mix_b) = block_tables(
-        top, first_ref, block_ref, out_ref.shape[0], mix_f_ref.shape[1]
+        top, first_ref, block_ref, out_ref.shape[0], tokens
     )
     mix_f_ref[...] = mix_f
     mix_b_ref[...] = mix_b
-    hit_b_ref[...] = hit_b
-    put(wides[0], hit_f, block_ref)
+    hit_f_ref[...] = hit_f
+    put(wides[0], hit_b, block_ref)
+    put(wides[1], hit_b, block_ref, tokens)
     ship(out_ref, wides)
 
 
-def pack_far_b(hit_ref, a_ref, g_ref, out_ref, *wides):
-    put(wides[0], hit_ref[...], a_ref)
-    put(wides[1], hit_ref[...], g_ref)
+def pack_far_f(hit_ref, f_ref, out_ref, *wides):
+    put(wides[0], hit_ref[...], f_ref)
     ship(out_ref, wides)
 
 
@@ -331,8 +334,9 @@
 
     block = run(
         gather_block,
-        shaped(tok + 16, cols),
-        act_forward,
+        shaped(2 * tok + 16, cols),
+        act_backward,
+        grad_backward,
         routes_forward.T,
         gates_forward.T,
         routes_backward.T,
@@ -341,45 +345,37 @@
         room=56 << 20,
     )
     far_block = moved(block, 0, True)
-    far_a = moved(after(act_backward, far_block), 0, True)
-    far_g = moved(after(grad_backward, far_block), 0, True)
+    far_rows = moved(after(act_forward, far_block), 0, True)
 
     sent, mix_f, mix_b = run(
         functools.partial(pack_near, top),
         (sendable(3), table, table),
         first,
         block,
-        act_backward,
-        grad_backward,
+        act_forward,
         scalars=1,
         scratch=wide(3, F32),
         room=56 << 20,
     )
     got = exchange(sent)
-    sent_f, far_mix_f, far_mix_b, far_hit_b = run(
-        functools.partial(pack_far_f, top),
-        (sendable(1), table, table, table),
+    sent_b, far_mix_f, far_mix_b, far_hit_f = run(
+        functools.partial(pack_far_b, top),
+        (sendable(2), table, table, table),
         first,
         far_block,
         scalars=1,
-        scratch=wide(1, F32),
-        flops=LONG,
-    )
-    got_f = exchange(after(sent_f, got))
-    sent_b = run(
-        pack_far_b,
-        sendable(2),
-        far_hit_b,
-        far_a,
-        far_g,
         scratch=wide(2, F32),
         flops=LONG,
     )
-    got_b = exchange(after(sent_b, got_f))
-    out, out_f = work((after(got, sent_b), got_f), "agf", "f")
-    back_f = exchange(after(out_f, got_b))
-    (out_b,) = work((after(got_b, out_f),), "ag")
-    back_b = exchange(after(out_b, back_f))
+    got_b = exchange(after(sent_b, got))
+    sent_f = run(pack_far_f, sendable(1), far_hit_f, far_rows, scratch=wide(1, F32), flops=LONG)
+    got_f = exchange(after(sent_f, got_b))
+    (out_b,) = work((after(got_b, sent_f),), "ag")
+    back_b = exchange(after(out_b, got_f))
+    (out_f,) = work((after(got_f, out_b),), "f")
+    back_f = exchange(after(out_f, back_b))
+    (out,) = work((after(got, out_f),), "agf")
+    back_f = after(back_f, out)
     far_sum_b, far_sum_f = combined((back_b, back_f), far_mix_b, far_mix_f)
     over = (moved(far_sum_b, -1, True), moved(far_sum_f, 1, True))
     back = exchange(after(out, far_sum_f))

time: 235 us -> 250 us (1.064)
  the two profiles are of different devices: /device:TPU:99 before, /device:TPU:1 now
where the time goes in v8:
time: 250 us; the launch traced here: 249 us
  starting transfers between devices  128 us (51%)
  waiting for transfers between devices  80.9 us (32%)
  Pallas kernels  33.7 us (13%)
  local copies, waits for them, and re-layouts  5.35 us (2%)
    ppermute x6, starting transfers between devices, moved(): lax.ppermute(v, RING, pairs_of(shape, lambda s, h: ((s + by) % sections,...  77.2 us
    ppermute x6, waiting for transfers between devices, moved(): lax.ppermute(v, RING, pairs_of(shape, lambda s, h: ((s + by) % sections,...  48.5 us
    pallas_call x14, Pallas kernels, run(): pl.pallas_call(kernel, out_shape=outs, in_specs=where, out_specs=jax.tree...  33.7 us
    all_to_all x6, waiting for transfers between devices, exchange(): return lax.all_to_all(v, PLANE, split_axis=0, concat_axis=0, tiled=True)  32.4 us
    all_to_all x6, starting transfers between devices, exchange(): return lax.all_to_all(v, PLANE, split_axis=0, concat_axis=0, tiled=True)  30.1 us
    ppermute x6, starting transfers between devices, other_core(): return lax.ppermute(v, NODE, [(0, 1), (1, 0)])  20.7 us
    unnamed x20, local copies, waits for them, and re-layouts  5.35 us
  transfers between devices with their start and end apart: 18, of which 11 were waited for; matrix products, arithmetic and copies ran while one was open for 0% of the time, Pallas kernels for 9%

profile of v8, /device:TPU:1, one launch (start us, length us, event | category | flops | bytes accessed | tf_op | source)
XLA Modules:
  0.0 248.9 jit_solution(9874200971934636107)
XLA Ops:
  2.5 16.3 %collective-permute-start = (bf16[272,1024]{1,0:T(8,128)(2,1)}, bf16[272,1024]{1,0:T(8,128)(2,1)S(1)}, u32[]{:S(2)}, u32[]{:S(2)}) collective-permute-start(bf16[272,1024]{1,0:T(8,128)(2,1)} %shard_map.104.block_ref), channel_id=1, source_target_pairs={{0,16},{1,17},{2,18},{3,19},{4,20},{5,21},{6,22},{7,23},{8,24},{9,... | collective-permute-start | bytes 1671176 | tf_op jit(solution)/shard_map/ppermute | solution.py:42
  22.5 6.7 %all-to-all-start = ((bf16[16,600,128]{2,1,0:T(8,128)(2,1)}), bf16[16,600,128]{2,1,0:T(8,128)(2,1)S(1)}, u32[]{:S(2)}, u32[]{:S(2)}) async-start(bf16[16,600,128]{2,1,0:T(8,128)(2,1)} %get-tuple-element.34), calls=%async_computation | async-start | bytes 4915200 | tf_op jit(solution)/shard_map/all_to_all | solution.py:52
  29.3 5.5 %collective-permute-done.block_ref = bf16[272,1024]{1,0:T(8,128)(2,1)S(1)} collective-permute-done((bf16[272,1024]{1,0:T(8,128)(2,1)}, bf16[272,1024]{1,0:T(8,128)(2,1)S(1)}, u32[]{:S(2)}, u32[]{:S(2)}) %collective-permute-start) | collective-permute-done | bytes 557088 | tf_op jit(solution)/shard_map/ppermute | solution.py:42
  34.7 12.8 %collective-permute-start.1 = (bf16[128,1024]{1,0:T(8,128)(2,1)}, bf16[128,1024]{1,0:T(8,128)(2,1)}, u32[]{:S(2)}, u32[]{:S(2)}) collective-permute-start(bf16[128,1024]{1,0:T(8,128)(2,1)} %f_ref.1), channel_id=1, source_target_pairs={{0,16},{1,17},{2,18},{3,19},{4,20},{5,21},{6,22},{7,23},{8,24},{9,... | collective-permute-start | bytes 786440 | tf_op jit(solution)/shard_map/ppermute | solution.py:42
  49.6 11.1 %all-to-all-done.refs_0_ = bf16[16,600,128]{2,1,0:T(8,128)(2,1)S(1)} async-done(((bf16[16,600,128]{2,1,0:T(8,128)(2,1)}), bf16[16,600,128]{2,1,0:T(8,128)(2,1)S(1)}, u32[]{:S(2)}, u32[]{:S(2)}) %all-to-all-start) | async-done | bytes 2457632 | tf_op jit(solution)/shard_map/all_to_all | solution.py:52
  62.1 4.4 %all-to-all-start.1 = ((bf16[16,400,128]{2,1,0:T(8,128)(2,1)}), bf16[16,400,128]{2,1,0:T(8,128)(2,1)}, u32[]{:S(2)}, u32[]{:S(2)}) async-start(bf16[16,400,128]{2,1,0:T(8,128)(2,1)} %copy-done.6), calls=%async_computation.1 | async-start | bytes 3276800 | tf_op jit(solution)/shard_map/all_to_all | solution.py:52
  66.5 13.3 %collective-permute-done.1.f_ref = bf16[128,1024]{1,0:T(8,128)(2,1)} collective-permute-done((bf16[128,1024]{1,0:T(8,128)(2,1)}, bf16[128,1024]{1,0:T(8,128)(2,1)}, u32[]{:S(2)}, u32[]{:S(2)}) %collective-permute-start.1) | collective-permute-done | bytes 262176 | tf_op jit(solution)/shard_map/ppermute | solution.py:42
  82.2 3.9 %all-to-all-done.1.refs_0_ = bf16[16,400,128]{2,1,0:T(8,128)(2,1)} async-done(((bf16[16,400,128]{2,1,0:T(8,128)(2,1)}), bf16[16,400,128]{2,1,0:T(8,128)(2,1)}, u32[]{:S(2)}, u32[]{:S(2)}) %all-to-all-start.1) | async-done | bytes 1638432 | tf_op jit(solution)/shard_map/all_to_all | solution.py:52
  86.2 4.1 %shard_map.108 = (bf16[512,768]{1,0:T(8,128)(2,1)}, bf16[512,768]{1,0:T(8,128)(2,1)}) custom-call(bf16[16,400,128]{2,1,0:T(8,128)(2,1)} %all-to-all-done.1.refs_0_, bf16[1024,768]{1,0:T(8,128)(2,1)S(1)} %bitcast.7, bf16[768,1024]{1,0:T(8,128)(2,1)S(1)} %bitcast.13), custom_call_target="tpu_custom_call" | custom-call | flops 1000 | bytes 1000 | tf_op jit(solution)/shard_map/pallas_call | solution.py:66
  90.3 7.8 %collective-permute-start.2 = (bf16[512,768]{1,0:T(8,128)(2,1)}, bf16[512,768]{1,0:T(8,128)(2,1)}, u32[]{:S(2)}, u32[]{:S(2)}) collective-permute-start(bf16[512,768]{1,0:T(8,128)(2,1)} %get-tuple-element.41.refs_0_), channel_id=1, source_target_pairs={{0,32},{32,0},{1,33},{33,1},{2,34},{34,2},{3,35},{35,3},{4,36},{36... | collective-permute-start | bytes 2359304 | tf_op jit(solution)/shard_map/ppermute | solution.py:48
  100.0 4.3 %all-to-all-start.2 = ((bf16[16,200,128]{2,1,0:T(8,128)(2,1)}), bf16[16,200,128]{2,1,0:T(8,128)(2,1)}, u32[]{:S(2)}, u32[]{:S(2)}) async-start(bf16[16,200,128]{2,1,0:T(8,128)(2,1)} %copy-done.7), calls=%async_computation.2 | async-start | bytes 1638400 | tf_op jit(solution)/shard_map/all_to_all | solution.py:52
  108.5 8.9 %all-to-all-done.2.refs_0_ = bf16[16,200,128]{2,1,0:T(8,128)(2,1)} async-done(((bf16[16,200,128]{2,1,0:T(8,128)(2,1)}), bf16[16,200,128]{2,1,0:T(8,128)(2,1)}, u32[]{:S(2)}, u32[]{:S(2)}) %all-to-all-start.2) | async-done | bytes 819232 | tf_op jit(solution)/shard_map/all_to_all | solution.py:52
  120.4 4.8 %collective-permute-start.4 = (bf16[512,768]{1,0:T(8,128)(2,1)}, bf16[512,768]{1,0:T(8,128)(2,1)}, u32[]{:S(2)}, u32[]{:S(2)}) collective-permute-start(bf16[512,768]{1,0:T(8,128)(2,1)} %shard_map.110.refs_0_), channel_id=1, source_target_pairs={{0,32},{32,0},{1,33},{33,1},{2,34},{34,2},{3,35},{35,3},{4,36},{36... | collective-permute-start | bytes 2359304 | tf_op jit(solution)/shard_map/ppermute | solution.py:48
  125.2 4.3 %all-to-all-start.3 = ((bf16[16,200,128]{2,1,0:T(8,128)(2,1)}), bf16[16,200,128]{2,1,0:T(8,128)(2,1)}, u32[]{:S(2)}, u32[]{:S(2)}) async-start(bf16[16,200,128]{2,1,0:T(8,128)(2,1)} %copy-done.4), calls=%async_computation.3 | async-start | bytes 1638400 | tf_op jit(solution)/shard_map/all_to_all | solution.py:52
  144.4 5.4 %all-to-all-start.4 = ((bf16[16,200,128]{2,1,0:T(8,128)(2,1)}), bf16[16,200,128]{2,1,0:T(8,128)(2,1)}, u32[]{:S(2)}, u32[]{:S(2)}) async-start(bf16[16,200,128]{2,1,0:T(8,128)(2,1)} %copy-done.5), calls=%async_computation.4 | async-start | bytes 1638400 | tf_op jit(solution)/shard_map/all_to_all | solution.py:52
  149.9 5.8 %shard_map.113 = bf16[16,400,128]{2,1,0:T(8,128)(2,1)} custom-call(bf16[512,768]{1,0:T(8,128)(2,1)} %get-tuple-element.45.refs_0_, bf16[512,768]{1,0:T(8,128)(2,1)} %get-tuple-element.46.refs_1_, bf16[512,768]{1,0:T(8,128)(2,1)} %get-tuple-element.47.refs_2_, bf16[512,768]{1,0:T(8,128)(2,1)} %collective-permute-done.5.refs_3_, ...), custom_call_target="tpu_custom_call" | custom-call | flops 1000 | bytes 1000 | tf_op jit(solution)/shard_map/pallas_call | solution.py:66
  155.7 7.1 %all-to-all-done.4.refs_3_ = bf16[16,200,128]{2,1,0:T(8,128)(2,1)} async-done(((bf16[16,200,128]{2,1,0:T(8,128)(2,1)}), bf16[16,200,128]{2,1,0:T(8,128)(2,1)}, u32[]{:S(2)}, u32[]{:S(2)}) %all-to-all-start.4) | async-done | bytes 819232 | tf_op jit(solution)/shard_map/all_to_all | solution.py:52
  164.7 4.9 %all-to-all-start.5 = ((bf16[16,400,128]{2,1,0:T(8,128)(2,1)}), bf16[16,400,128]{2,1,0:T(8,128)(2,1)S(1)}, u32[]{:S(2)}, u32[]{:S(2)}) async-start(bf16[16,400,128]{2,1,0:T(8,128)(2,1)} %shard_map.113), calls=%async_computation.5 | async-start | bytes 3276800 | tf_op jit(solution)/shard_map/all_to_all | solution.py:52
  169.6 11.9 %collective-permute-start.10 = (bf16[128,1024]{1,0:T(8,128)(2,1)S(1)}, bf16[128,1024]{1,0:T(8,128)(2,1)S(1)}, u32[]{:S(2)}, u32[]{:S(2)}) collective-permute-start(bf16[128,1024]{1,0:T(8,128)(2,1)S(1)} %get-tuple-element.57), channel_id=1, source_target_pairs={{0,464},{1,465},{2,466},{3,467},{4,468},{5,469},{6,470},{7,471},{8... | collective-permute-start | bytes 786440 | tf_op jit(solution)/shard_map/ppermute | solution.py:42
  181.5 13.8 %collective-permute-start.11 = (bf16[128,1024]{1,0:T(8,128)(2,1)S(1)}, bf16[128,1024]{1,0:T(8,128)(2,1)S(1)}, u32[]{:S(2)}, u32[]{:S(2)}) collective-permute-start(bf16[128,1024]{1,0:T(8,128)(2,1)S(1)} %get-tuple-element.53), channel_id=1, source_target_pairs={{0,80},{1,81},{2,82},{3,83},{4,84},{5,85},{6,86},{7,87},{8,88},{9,... | collective-permute-start | bytes 786440 | tf_op jit(solution)/shard_map/ppermute | solution.py:42
  195.8 14.9 %collective-permute-start.8 = (bf16[128,1024]{1,0:T(8,128)(2,1)S(1)}, bf16[128,1024]{1,0:T(8,128)(2,1)S(1)}, u32[]{:S(2)}, u32[]{:S(2)}) collective-permute-start(bf16[128,1024]{1,0:T(8,128)(2,1)S(1)} %get-tuple-element.55), channel_id=1, source_target_pairs={{0,448},{1,449},{2,450},{3,451},{4,452},{5,453},{6,454},{7,455},{8... | collective-permute-start | bytes 786440 | tf_op jit(solution)/shard_map/ppermute | solution.py:42
  210.8 7.5 %collective-permute-start.9 = (bf16[128,1024]{1,0:T(8,128)(2,1)S(1)}, bf16[128,1024]{1,0:T(8,128)(2,1)S(1)}, u32[]{:S(2)}, u32[]{:S(2)}) collective-permute-start(bf16[128,1024]{1,0:T(8,128)(2,1)S(1)} %get-tuple-element.56), channel_id=1, source_target_pairs={{0,64},{1,65},{2,66},{3,67},{4,68},{5,69},{6,70},{7,71},{8,72},{9,... | collective-permute-start | bytes 786440 | tf_op jit(solution)/shard_map/ppermute | solution.py:42
  218.3 15.4 %collective-permute-done.10.a_ref = bf16[128,1024]{1,0:T(8,128)(2,1)S(1)} collective-permute-done((bf16[128,1024]{1,0:T(8,128)(2,1)S(1)}, bf16[128,1024]{1,0:T(8,128)(2,1)S(1)}, u32[]{:S(2)}, u32[]{:S(2)}) %collective-permute-start.10) | collective-permute-done | bytes 262176 | tf_op jit(solution)/shard_map/ppermute | solution.py:42
  237.0 11.0 %collective-permute-done.9.b_ref = bf16[128,1024]{1,0:T(8,128)(2,1)S(1)} collective-permute-done((bf16[128,1024]{1,0:T(8,128)(2,1)S(1)}, bf16[128,1024]{1,0:T(8,128)(2,1)S(1)}, u32[]{:S(2)}, u32[]{:S(2)}) %collective-permute-start.9) | collective-permute-done | bytes 262176 | tf_op jit(solution)/shard_map/ppermute | solution.py:42
  (46 shorter events, 42.0 us)
Async XLA Ops:
  2.5 32.2 %collective-permute-start = (bf16[272,1024]{1,0:T(8,128)(2,1)}, bf16[272,1024]{1,0:T(8,128)(2,1)S(1)}, u32[]{:S(2)}, u32[]{:S(2)}) collective-permute-start(bf16[272,1024]{1,0:T(8,128)(2,1)} %shard_map.104.block_ref), channel_id=1, source_target_pairs={{0,16},{1,17},{2,18},{3,19},{4,20},{5,21},{6,22},{7,23},{8,24},{9,... | collective-permute-start | bytes 1671176 | tf_op jit(solution)/shard_map/ppermute | solution.py:42
  22.5 38.2 %all-to-all-start = ((bf16[16,600,128]{2,1,0:T(8,128)(2,1)}), bf16[16,600,128]{2,1,0:T(8,128)(2,1)S(1)}, u32[]{:S(2)}, u32[]{:S(2)}) async-start(bf16[16,600,128]{2,1,0:T(8,128)(2,1)} %get-tuple-element.34), calls=%async_computation | async-start | bytes 4915200 | tf_op jit(solution)/shard_map/all_to_all | solution.py:52
  34.7 45.1 %collective-permute-start.1 = (bf16[128,1024]{1,0:T(8,128)(2,1)}, bf16[128,1024]{1,0:T(8,128)(2,1)}, u32[]{:S(2)}, u32[]{:S(2)}) collective-permute-start(bf16[128,1024]{1,0:T(8,128)(2,1)} %f_ref.1), channel_id=1, source_target_pairs={{0,16},{1,17},{2,18},{3,19},{4,20},{5,21},{6,22},{7,23},{8,24},{9,... | collective-permute-start | bytes 786440 | tf_op jit(solution)/shard_map/ppermute | solution.py:42
  60.7 1.5 copy-start.2
  62.1 24.0 %all-to-all-start.1 = ((bf16[16,400,128]{2,1,0:T(8,128)(2,1)}), bf16[16,400,128]{2,1,0:T(8,128)(2,1)}, u32[]{:S(2)}, u32[]{:S(2)}) async-start(bf16[16,400,128]{2,1,0:T(8,128)(2,1)} %copy-done.6), calls=%async_computation.1 | async-start | bytes 3276800 | tf_op jit(solution)/shard_map/all_to_all | solution.py:52
  79.8 6.4 %copy-start = (bf16[1,1,1024,768]{3,2,1,0:T(8,128)(2,1)S(1)}, bf16[1,1,1024,768]{3,2,1,0:T(8,128)(2,1)}, u32[]{:S(2)}) copy-start(bf16[1,1,1024,768]{3,2,1,0:T(8,128)(2,1)} %param.16) | copy-start | bytes 4718596
  79.8 6.4 %copy-start.1 = (bf16[1,1,768,1024]{3,2,1,0:T(8,128)(2,1)S(1)}, bf16[1,1,768,1024]{3,2,1,0:T(8,128)(2,1)}, u32[]{:S(2)}) copy-start(bf16[1,1,768,1024]{3,2,1,0:T(8,128)(2,1)} %param.17) | copy-start | bytes 4718596
  90.3 14.0 %collective-permute-start.2 = (bf16[512,768]{1,0:T(8,128)(2,1)}, bf16[512,768]{1,0:T(8,128)(2,1)}, u32[]{:S(2)}, u32[]{:S(2)}) collective-permute-start(bf16[512,768]{1,0:T(8,128)(2,1)} %get-tuple-element.41.refs_0_), channel_id=1, source_target_pairs={{0,32},{32,0},{1,33},{33,1},{2,34},{34,2},{3,35},{35,3},{4,36},{36... | collective-permute-start | bytes 2359304 | tf_op jit(solution)/shard_map/ppermute | solution.py:48
  98.0 6.3 %collective-permute-start.3 = (bf16[512,768]{1,0:T(8,128)(2,1)}, bf16[512,768]{1,0:T(8,128)(2,1)}, u32[]{:S(2)}, u32[]{:S(2)}) collective-permute-start(bf16[512,768]{1,0:T(8,128)(2,1)} %get-tuple-element.42.refs_1_), channel_id=1, source_target_pairs={{0,32},{32,0},{1,33},{33,1},{2,34},{34,2},{3,35},{35,3},{4,36},{36... | collective-permute-start | bytes 2359304 | tf_op jit(solution)/shard_map/ppermute | solution.py:48
  100.0 17.4 %all-to-all-start.2 = ((bf16[16,200,128]{2,1,0:T(8,128)(2,1)}), bf16[16,200,128]{2,1,0:T(8,128)(2,1)}, u32[]{:S(2)}, u32[]{:S(2)}) async-start(bf16[16,200,128]{2,1,0:T(8,128)(2,1)} %copy-done.7), calls=%async_computation.2 | async-start | bytes 1638400 | tf_op jit(solution)/shard_map/all_to_all | solution.py:52
  120.4 9.1 %collective-permute-start.4 = (bf16[512,768]{1,0:T(8,128)(2,1)}, bf16[512,768]{1,0:T(8,128)(2,1)}, u32[]{:S(2)}, u32[]{:S(2)}) collective-permute-start(bf16[512,768]{1,0:T(8,128)(2,1)} %shard_map.110.refs_0_), channel_id=1, source_target_pairs={{0,32},{32,0},{1,33},{33,1},{2,34},{34,2},{3,35},{35,3},{4,36},{36... | collective-permute-start | bytes 2359304 | tf_op jit(solution)/shard_map/ppermute | solution.py:48
  125.2 19.2 %all-to-all-start.3 = ((bf16[16,200,128]{2,1,0:T(8,128)(2,1)}), bf16[16,200,128]{2,1,0:T(8,128)(2,1)}, u32[]{:S(2)}, u32[]{:S(2)}) async-start(bf16[16,200,128]{2,1,0:T(8,128)(2,1)} %copy-done.4), calls=%async_computation.3 | async-start | bytes 1638400 | tf_op jit(solution)/shard_map/all_to_all | solution.py:52
  129.5 3.5 %copy-start.3 = (bf16[16,600,128]{2,1,0:T(8,128)(2,1)S(1)}, bf16[16,600,128]{2,1,0:T(8,128)(2,1)}, u32[]{:S(2)}) copy-start(bf16[16,600,128]{2,1,0:T(8,128)(2,1)} %copy-done.2) | copy-start | bytes 7372804
  136.7 13.2 %collective-permute-start.5 = (bf16[512,768]{1,0:T(8,128)(2,1)}, bf16[512,768]{1,0:T(8,128)(2,1)}, u32[]{:S(2)}, u32[]{:S(2)}) collective-permute-start(bf16[512,768]{1,0:T(8,128)(2,1)} %get-tuple-element.45.refs_0_), channel_id=1, source_target_pairs={{0,32},{32,0},{1,33},{33,1},{2,34},{34,2},{3,35},{35,3},{4,36},{36... | collective-permute-start | bytes 2359304 | tf_op jit(solution)/shard_map/ppermute | solution.py:48
  138.6 11.3 %collective-permute-start.6 = (bf16[512,768]{1,0:T(8,128)(2,1)}, bf16[512,768]{1,0:T(8,128)(2,1)}, u32[]{:S(2)}, u32[]{:S(2)}) collective-permute-start(bf16[512,768]{1,0:T(8,128)(2,1)} %get-tuple-element.46.refs_1_), channel_id=1, source_target_pairs={{0,32},{32,0},{1,33},{33,1},{2,34},{34,2},{3,35},{35,3},{4,36},{36... | collective-permute-start | bytes 2359304 | tf_op jit(solution)/shard_map/ppermute | solution.py:48
  141.0 8.9 %collective-permute-start.7 = (bf16[512,768]{1,0:T(8,128)(2,1)}, bf16[512,768]{1,0:T(8,128)(2,1)}, u32[]{:S(2)}, u32[]{:S(2)}) collective-permute-start(bf16[512,768]{1,0:T(8,128)(2,1)} %get-tuple-element.47.refs_2_), channel_id=1, source_target_pairs={{0,32},{32,0},{1,33},{33,1},{2,34},{34,2},{3,35},{35,3},{4,36},{36... | collective-permute-start | bytes 2359304 | tf_op jit(solution)/shard_map/ppermute | solution.py:48
  144.4 18.4 %all-to-all-start.4 = ((bf16[16,200,128]{2,1,0:T(8,128)(2,1)}), bf16[16,200,128]{2,1,0:T(8,128)(2,1)}, u32[]{:S(2)}, u32[]{:S(2)}) async-start(bf16[16,200,128]{2,1,0:T(8,128)(2,1)} %copy-done.5), calls=%async_computation.4 | async-start | bytes 1638400 | tf_op jit(solution)/shard_map/all_to_all | solution.py:52
  164.7 30.7 %copy-start.8 = (bf16[512,128]{1,0:T(8,128)(2,1)S(1)}, bf16[512,128]{1,0:T(8,128)(2,1)}, u32[]{:S(2)}) copy-start(bf16[512,128]{1,0:T(8,128)(2,1)} %get-tuple-element.33.refs_1_) | copy-start | bytes 393220
  164.7 30.7 %copy-start.9 = (bf16[512,128]{1,0:T(8,128)(2,1)S(1)}, bf16[512,128]{1,0:T(8,128)(2,1)}, u32[]{:S(2)}) copy-start(bf16[512,128]{1,0:T(8,128)(2,1)} %get-tuple-element.32.refs_0_) | copy-start | bytes 393220
  164.7 30.6 %all-to-all-start.5 = ((bf16[16,400,128]{2,1,0:T(8,128)(2,1)}), bf16[16,400,128]{2,1,0:T(8,128)(2,1)S(1)}, u32[]{:S(2)}, u32[]{:S(2)}) async-start(bf16[16,400,128]{2,1,0:T(8,128)(2,1)} %shard_map.113), calls=%async_computation.5 | async-start | bytes 3276800 | tf_op jit(solution)/shard_map/all_to_all | solution.py:52
  169.6 64.1 %collective-permute-start.10 = (bf16[128,1024]{1,0:T(8,128)(2,1)S(1)}, bf16[128,1024]{1,0:T(8,128)(2,1)S(1)}, u32[]{:S(2)}, u32[]{:S(2)}) collective-permute-start(bf16[128,1024]{1,0:T(8,128)(2,1)S(1)} %get-tuple-element.57), channel_id=1, source_target_pairs={{0,464},{1,465},{2,466},{3,467},{4,468},{5,469},{6,470},{7,471},{8... | collective-permute-start | bytes 786440 | tf_op jit(solution)/shard_map/ppermute | solution.py:42
  181.5 52.6 %collective-permute-start.11 = (bf16[128,1024]{1,0:T(8,128)(2,1)S(1)}, bf16[128,1024]{1,0:T(8,128)(2,1)S(1)}, u32[]{:S(2)}, u32[]{:S(2)}) collective-permute-start(bf16[128,1024]{1,0:T(8,128)(2,1)S(1)} %get-tuple-element.53), channel_id=1, source_target_pairs={{0,80},{1,81},{2,82},{3,83},{4,84},{5,85},{6,86},{7,87},{8,88},{9,... | collective-permute-start | bytes 786440 | tf_op jit(solution)/shard_map/ppermute | solution.py:42
  195.8 41.2 %collective-permute-start.8 = (bf16[128,1024]{1,0:T(8,128)(2,1)S(1)}, bf16[128,1024]{1,0:T(8,128)(2,1)S(1)}, u32[]{:S(2)}, u32[]{:S(2)}) collective-permute-start(bf16[128,1024]{1,0:T(8,128)(2,1)S(1)} %get-tuple-element.55), channel_id=1, source_target_pairs={{0,448},{1,449},{2,450},{3,451},{4,452},{5,453},{6,454},{7,455},{8... | collective-permute-start | bytes 786440 | tf_op jit(solution)/shard_map/ppermute | solution.py:42
  210.8 37.3 %collective-permute-start.9 = (bf16[128,1024]{1,0:T(8,128)(2,1)S(1)}, bf16[128,1024]{1,0:T(8,128)(2,1)S(1)}, u32[]{:S(2)}, u32[]{:S(2)}) collective-permute-start(bf16[128,1024]{1,0:T(8,128)(2,1)S(1)} %get-tuple-element.56), channel_id=1, source_target_pairs={{0,64},{1,65},{2,66},{3,67},{4,68},{5,69},{6,70},{7,71},{8,72},{9,... | collective-permute-start | bytes 786440 | tf_op jit(solution)/shard_map/ppermute | solution.py:42
  (4 other events, 3.9 us)

commit v9 on v7

--- a/solution.py
+++ b/solution.py
@@ -139,9 +139,10 @@
     return jnp.concatenate(columns, axis=1)
 
 
-def ship(out_ref, wides):
+def ship(out_ref, wides, added=()):
     for e in range(out_ref.shape[0]):
         rows = [flat(wide[e * SLOTS : (e + 1) * SLOTS, :]) for wide in wides]
+        rows += [ref[e].astype(F32) for ref in added]
         out_ref[e] = jnp.concatenate(rows, axis=0).astype(BF)
 
 
@@ -211,10 +212,11 @@
             out_ref[:, c : c + WIDTH] = part.astype(BF)
 
 
-def results(groups, *refs):
+def results(groups, more, *refs):
     kinds = "".join(groups)
     mine, theirs = refs[: len(kinds)], refs[len(kinds) : 2 * len(kinds)]
     w_in_ref, w_out_ref, *refs = refs[2 * len(kinds) :]
+    added, refs = refs[:more], refs[more:]
     outs, hold_ref, wides = refs[: len(groups)], refs[len(groups)], refs[len(groups) + 1 :]
     hidden, cols = w_in_ref.shape[1], w_in_ref.shape[0]
 
@@ -243,7 +245,7 @@
     at = 0
     for out_ref, group in zip(outs, groups):
         many = made(group)
-        ship(out_ref, wides[at : at + many])
+        ship(out_ref, wides[at : at + many], added)
         at += many
 
 
@@ -299,7 +301,7 @@
     def sendable(kinds):
         return shaped(experts, kinds * (HEAD + 1) * (cols // LANES), LANES)
 
-    def work(gots, *groups):
+    def work(gots, *groups, added=()):
         count = len("".join(groups))
         mine = run(
             functools.partial(parts, groups),
@@ -311,12 +313,13 @@
         )
         theirs = [other_core(part) for part in mine]
         return run(
-            functools.partial(results, groups),
-            tuple(sendable(made(group)) for group in groups),
+            functools.partial(results, groups, len(added)),
+            tuple(sendable(made(group) + len(added)) for group in groups),
             *mine,
             *theirs,
             weight_in,
             weight_out,
+            *added,
             scratch=[pltpu.VMEM((rows, hidden), BF)] + wide(made("".join(groups)), F32),
         )
 
@@ -377,10 +380,8 @@
     )
     got_b = exchange(after(sent_b, got_f))
     out, out_f = work((after(got, sent_b), got_f), "agf", "f")
-    back_f = exchange(after(out_f, got_b))
-    (out_b,) = work((after(got_b, out_f),), "ag")
-    back_b = exchange(after(out_b, back_f))
-    far_sum_b, far_sum_f = combined((back_b, back_f), far_mix_b, far_mix_f)
+    (out_bf,) = work((after(got_b, out_f),), "ag", added=(out_f,))
+    far_sum_b, far_sum_f = combined((exchange(out_bf),), far_mix_b, far_mix_f)
     over = (moved(far_sum_b, -1, True), moved(far_sum_f, 1, True))
     back = exchange(after(out, far_sum_f))
     sum_b, sum_f = combined((back,), mix_b, mix_f)

time: 235 us -> 228 us (0.970)
  the two profiles are of different devices: /device:TPU:99 before, /device:TPU:1 now
where the time goes in v9:
time: 228 us; the launch traced here: 227 us
  starting transfers between devices  109 us (48%)
  waiting for transfers between devices  58.8 us (26%)
  blocking collectives  29.3 us (13%)
  Pallas kernels  23.3 us (10%)
  local copies, waits for them, and re-layouts  5.25 us (2%)
    ppermute x7, starting transfers between devices, moved(): lax.ppermute(v, RING, pairs_of(shape, lambda s, h: ((s + by) % sections,...  71.9 us
    ppermute x7, waiting for transfers between devices, moved(): lax.ppermute(v, RING, pairs_of(shape, lambda s, h: ((s + by) % sections,...  31.2 us
    all_to_all x1, blocking collectives, exchange(): return lax.all_to_all(v, PLANE, split_axis=0, concat_axis=0, tiled=True)  29.3 us
    all_to_all x4, waiting for transfers between devices, exchange(): return lax.all_to_all(v, PLANE, split_axis=0, concat_axis=0, tiled=True)  23.7 us
    pallas_call x12, Pallas kernels, run(): pl.pallas_call(kernel, out_shape=outs, in_specs=where, out_specs=jax.tree...  23.3 us
    all_to_all x4, starting transfers between devices, exchange(): return lax.all_to_all(v, PLANE, split_axis=0, concat_axis=0, tiled=True)  19.3 us
    ppermute x6, starting transfers between devices, other_core(): return lax.ppermute(v, NODE, [(0, 1), (1, 0)])  17.9 us
    unnamed x18, local copies, waits for them, and re-layouts  5.25 us
  transfers between devices with their start and end apart: 17, of which 6 were waited for; matrix products, arithmetic and copies ran while one was open for 0% of the time, Pallas kernels for 7%

profile of v9, /device:TPU:1, one launch (start us, length us, event | category | flops | bytes accessed | tf_op | source)
XLA Modules:
  0.0 226.8 jit_solution(4954731178332952206)
XLA Ops:
  2.4 16.3 %collective-permute-start = (bf16[144,1024]{1,0:T(8,128)(2,1)}, bf16[144,1024]{1,0:T(8,128)(2,1)S(1)}, u32[]{:S(2)}, u32[]{:S(2)}) collective-permute-start(bf16[144,1024]{1,0:T(8,128)(2,1)} %shard_map.104.block_ref), channel_id=1, source_target_pairs={{0,16},{1,17},{2,18},{3,19},{4,20},{5,21},{6,22},{7,23},{8,24},{9,... | collective-permute-start | bytes 884744 | tf_op jit(solution)/shard_map/ppermute | solution.py:42
  18.7 3.7 %shard_map.105 = (bf16[16,600,128]{2,1,0:T(8,128)(2,1)}, bf16[512,128]{1,0:T(8,128)(2,1)}, bf16[512,128]{1,0:T(8,128)(2,1)}) custom-call(s32[1]{0:T(128)} %bitcast.first_ref, bf16[144,1024]{1,0:T(8,128)(2,1)} %shard_map.104.block_ref, bf16[128,1024]{1,0:T(8,128)(2,1)} %a_ref.1, bf16[128,1024]{1,0:T(8,128)(2,1)} %g_ref.1), custom_call_target="tpu_custom_call" | custom-call | flops 1000 | bytes 1000 | tf_op jit(solution)/shard_map/pallas_call | solution.py:66
  22.3 6.7 %all-to-all-start = ((bf16[16,600,128]{2,1,0:T(8,128)(2,1)}), bf16[16,600,128]{2,1,0:T(8,128)(2,1)S(1)}, u32[]{:S(2)}, u32[]{:S(2)}) async-start(bf16[16,600,128]{2,1,0:T(8,128)(2,1)} %get-tuple-element.34), calls=%async_computation | async-start | bytes 4915200 | tf_op jit(solution)/shard_map/all_to_all | solution.py:52
  29.1 8.3 %collective-permute-start.1 = (bf16[128,1024]{1,0:T(8,128)(2,1)}, bf16[128,1024]{1,0:T(8,128)(2,1)S(1)}, u32[]{:S(2)}, u32[]{:S(2)}) collective-permute-start(bf16[128,1024]{1,0:T(8,128)(2,1)} %a_ref.1), channel_id=1, source_target_pairs={{0,16},{1,17},{2,18},{3,19},{4,20},{5,21},{6,22},{7,23},{8,24},{9,... | collective-permute-start | bytes 786440 | tf_op jit(solution)/shard_map/ppermute | solution.py:42
  37.4 5.7 %collective-permute-start.2 = (bf16[128,1024]{1,0:T(8,128)(2,1)}, bf16[128,1024]{1,0:T(8,128)(2,1)}, u32[]{:S(2)}, u32[]{:S(2)}) collective-permute-start(bf16[128,1024]{1,0:T(8,128)(2,1)} %g_ref.1), channel_id=1, source_target_pairs={{0,16},{1,17},{2,18},{3,19},{4,20},{5,21},{6,22},{7,23},{8,24},{9,... | collective-permute-start | bytes 786440 | tf_op jit(solution)/shard_map/ppermute | solution.py:42
  44.6 15.9 %all-to-all-done.refs_0_ = bf16[16,600,128]{2,1,0:T(8,128)(2,1)S(1)} async-done(((bf16[16,600,128]{2,1,0:T(8,128)(2,1)}), bf16[16,600,128]{2,1,0:T(8,128)(2,1)S(1)}, u32[]{:S(2)}, u32[]{:S(2)}) %all-to-all-start) | async-done | bytes 2457632 | tf_op jit(solution)/shard_map/all_to_all | solution.py:52
  62.0 4.3 %all-to-all-start.1 = ((bf16[16,200,128]{2,1,0:T(8,128)(2,1)}), bf16[16,200,128]{2,1,0:T(8,128)(2,1)}, u32[]{:S(2)}, u32[]{:S(2)}) async-start(bf16[16,200,128]{2,1,0:T(8,128)(2,1)} %get-tuple-element.40), calls=%async_computation.1 | async-start | bytes 1638400 | tf_op jit(solution)/shard_map/all_to_all | solution.py:52
  69.1 7.8 %all-to-all-done.1.refs_1_ = bf16[16,200,128]{2,1,0:T(8,128)(2,1)} async-done(((bf16[16,200,128]{2,1,0:T(8,128)(2,1)}), bf16[16,200,128]{2,1,0:T(8,128)(2,1)}, u32[]{:S(2)}, u32[]{:S(2)}) %all-to-all-start.1) | async-done | bytes 819232 | tf_op jit(solution)/shard_map/all_to_all | solution.py:52
  76.9 4.4 %all-to-all-start.2 = ((bf16[16,400,128]{2,1,0:T(8,128)(2,1)}), bf16[16,400,128]{2,1,0:T(8,128)(2,1)}, u32[]{:S(2)}, u32[]{:S(2)}) async-start(bf16[16,400,128]{2,1,0:T(8,128)(2,1)} %copy-done.4), calls=%async_computation.2 | async-start | bytes 3276800 | tf_op jit(solution)/shard_map/all_to_all | solution.py:52
  83.0 4.6 %shard_map.108 = (bf16[512,768]{1,0:T(8,128)(2,1)S(1)}, bf16[512,768]{1,0:T(8,128)(2,1)S(1)}, bf16[512,768]{1,0:T(8,128)(2,1)S(1)}, bf16[512,768]{1,0:T(8,128)(2,1)S(1)}) custom-call(bf16[16,600,128]{2,1,0:T(8,128)(2,1)S(1)} %copy-done.3, bf16[16,200,128]{2,1,0:T(8,128)(2,1)} %all-to-all-done.1.refs_1_, bf16[1024,768]{1,0:T(8,128)(2,1)S(1)} %bitcast.7, ...), custom_call_target="tpu_custom_call" | custom-call | flops 1000 | bytes 1000 | tf_op jit(solution)/shard_map/pallas_call | solution.py:66
  87.6 7.2 %collective-permute-start.3 = (bf16[512,768]{1,0:T(8,128)(2,1)S(1)}, bf16[512,768]{1,0:T(8,128)(2,1)S(1)}, u32[]{:S(2)}, u32[]{:S(2)}) collective-permute-start(bf16[512,768]{1,0:T(8,128)(2,1)S(1)} %get-tuple-element.41.refs_0_), channel_id=1, source_target_pairs={{0,32},{32,0},{1,33},{33,1},{2,34},{34,2},{3,35},{35,3},{4,36},{36... | collective-permute-start | bytes 2359304 | tf_op jit(solution)/shard_map/ppermute | solution.py:48
  96.7 2.4 %collective-permute-start.5 = (bf16[512,768]{1,0:T(8,128)(2,1)S(1)}, bf16[512,768]{1,0:T(8,128)(2,1)S(1)}, u32[]{:S(2)}, u32[]{:S(2)}) collective-permute-start(bf16[512,768]{1,0:T(8,128)(2,1)S(1)} %get-tuple-element.43.refs_2_), channel_id=1, source_target_pairs={{0,32},{32,0},{1,33},{33,1},{2,34},{34,2},{3,35},{35,3},{4,36},{36... | collective-permute-start | bytes 2359304 | tf_op jit(solution)/shard_map/ppermute | solution.py:48
  101.1 2.2 collective-permute-done.6.refs_7_
  103.3 3.5 %shard_map.109 = (bf16[16,400,128]{2,1,0:T(8,128)(2,1)}, bf16[16,200,128]{2,1,0:T(8,128)(2,1)S(1)}) custom-call(bf16[512,768]{1,0:T(8,128)(2,1)S(1)} %get-tuple-element.41.refs_0_, bf16[512,768]{1,0:T(8,128)(2,1)S(1)} %get-tuple-element.42.refs_1_, bf16[512,768]{1,0:T(8,128)(2,1)S(1)} %get-tuple-element.43.refs_2_, ...), custom_call_target="tpu_custom_call" | custom-call | flops 1000 | bytes 1000 | tf_op jit(solution)/shard_map/pallas_call | solution.py:66
  107.8 3.3 %shard_map.110 = (bf16[512,768]{1,0:T(8,128)(2,1)S(1)}, bf16[512,768]{1,0:T(8,128)(2,1)S(1)}) custom-call(bf16[16,400,128]{2,1,0:T(8,128)(2,1)} %all-to-all-done.2.refs_0_, bf16[1024,768]{1,0:T(8,128)(2,1)S(1)} %bitcast.9, bf16[768,1024]{1,0:T(8,128)(2,1)S(1)} %bitcast.13), custom_call_target="tpu_custom_call" | custom-call | flops 1000 | bytes 1000 | tf_op jit(solution)/shard_map/pallas_call | solution.py:66
  113.1 2.5 %collective-permute-start.8 = (bf16[512,768]{1,0:T(8,128)(2,1)S(1)}, bf16[512,768]{1,0:T(8,128)(2,1)S(1)}, u32[]{:S(2)}, u32[]{:S(2)}) collective-permute-start(bf16[512,768]{1,0:T(8,128)(2,1)S(1)} %get-tuple-element.52.refs_1_), channel_id=1, source_target_pairs={{0,32},{32,0},{1,33},{33,1},{2,34},{34,2},{3,35},{35,3},{4,36},{36... | collective-permute-start | bytes 2359304 | tf_op jit(solution)/shard_map/ppermute | solution.py:48
  118.8 29.3 %all_to_all.25.refs_2_ = bf16[16,400,128]{2,1,0:T(8,128)(2,1)S(1)} all-to-all(bf16[16,400,128]{2,1,0:T(8,128)(2,1)S(1)} %shard_map.111), channel_id=1, replica_groups=mesh['section'=8,'node'=2,'zhi'=2,'x'=4,'y'=4] {'x','y'}, dimensions={0} | all-to-all | bytes 3276800 | tf_op jit(solution)/shard_map/all_to_all | solution.py:52
  148.6 3.9 %all-to-all-start.4 = ((bf16[16,400,128]{2,1,0:T(8,128)(2,1)}), bf16[16,400,128]{2,1,0:T(8,128)(2,1)S(1)}, u32[]{:S(2)}, u32[]{:S(2)}) async-start(bf16[16,400,128]{2,1,0:T(8,128)(2,1)} %get-tuple-element.54), calls=%async_computation.4 | async-start | bytes 3276800 | tf_op jit(solution)/shard_map/all_to_all | solution.py:52
  152.5 5.6 %collective-permute-start.11 = (bf16[128,1024]{1,0:T(8,128)(2,1)S(1)}, bf16[128,1024]{1,0:T(8,128)(2,1)S(1)}, u32[]{:S(2)}, u32[]{:S(2)}) collective-permute-start(bf16[128,1024]{1,0:T(8,128)(2,1)S(1)} %get-tuple-element.57), channel_id=1, source_target_pairs={{0,464},{1,465},{2,466},{3,467},{4,468},{5,469},{6,470},{7,471},{8... | collective-permute-start | bytes 786440 | tf_op jit(solution)/shard_map/ppermute | solution.py:42
  158.1 20.8 %collective-permute-start.12 = (bf16[128,1024]{1,0:T(8,128)(2,1)S(1)}, bf16[128,1024]{1,0:T(8,128)(2,1)S(1)}, u32[]{:S(2)}, u32[]{:S(2)}) collective-permute-start(bf16[128,1024]{1,0:T(8,128)(2,1)S(1)} %get-tuple-element.53), channel_id=1, source_target_pairs={{0,80},{1,81},{2,82},{3,83},{4,84},{5,85},{6,86},{7,87},{8,88},{9,... | collective-permute-start | bytes 786440 | tf_op jit(solution)/shard_map/ppermute | solution.py:42
  179.5 9.7 %collective-permute-start.9 = (bf16[128,1024]{1,0:T(8,128)(2,1)S(1)}, bf16[128,1024]{1,0:T(8,128)(2,1)S(1)}, u32[]{:S(2)}, u32[]{:S(2)}) collective-permute-start(bf16[128,1024]{1,0:T(8,128)(2,1)S(1)} %get-tuple-element.55), channel_id=1, source_target_pairs={{0,448},{1,449},{2,450},{3,451},{4,452},{5,453},{6,454},{7,455},{8... | collective-permute-start | bytes 786440 | tf_op jit(solution)/shard_map/ppermute | solution.py:42
  189.1 5.6 %collective-permute-start.10 = (bf16[128,1024]{1,0:T(8,128)(2,1)S(1)}, bf16[128,1024]{1,0:T(8,128)(2,1)S(1)}, u32[]{:S(2)}, u32[]{:S(2)}) collective-permute-start(bf16[128,1024]{1,0:T(8,128)(2,1)S(1)} %get-tuple-element.56), channel_id=1, source_target_pairs={{0,64},{1,65},{2,66},{3,67},{4,68},{5,69},{6,70},{7,71},{8,72},{9,... | collective-permute-start | bytes 786440 | tf_op jit(solution)/shard_map/ppermute | solution.py:42
  194.7 20.0 %collective-permute-done.12.b_ref = bf16[128,1024]{1,0:T(8,128)(2,1)S(1)} collective-permute-done((bf16[128,1024]{1,0:T(8,128)(2,1)S(1)}, bf16[128,1024]{1,0:T(8,128)(2,1)S(1)}, u32[]{:S(2)}, u32[]{:S(2)}) %collective-permute-start.12) | collective-permute-done | bytes 262176 | tf_op jit(solution)/shard_map/ppermute | solution.py:42
  214.8 11.2 %collective-permute-done.10.b_ref = bf16[128,1024]{1,0:T(8,128)(2,1)S(1)} collective-permute-done((bf16[128,1024]{1,0:T(8,128)(2,1)S(1)}, bf16[128,1024]{1,0:T(8,128)(2,1)S(1)}, u32[]{:S(2)}, u32[]{:S(2)}) %collective-permute-start.10) | collective-permute-done | bytes 262176 | tf_op jit(solution)/shard_map/ppermute | solution.py:42
  (41 shorter events, 21.0 us)
Async XLA Ops:
  2.4 26.7 %collective-permute-start = (bf16[144,1024]{1,0:T(8,128)(2,1)}, bf16[144,1024]{1,0:T(8,128)(2,1)S(1)}, u32[]{:S(2)}, u32[]{:S(2)}) collective-permute-start(bf16[144,1024]{1,0:T(8,128)(2,1)} %shard_map.104.block_ref), channel_id=1, source_target_pairs={{0,16},{1,17},{2,18},{3,19},{4,20},{5,21},{6,22},{7,23},{8,24},{9,... | collective-permute-start | bytes 884744 | tf_op jit(solution)/shard_map/ppermute | solution.py:42
  22.3 38.2 %all-to-all-start = ((bf16[16,600,128]{2,1,0:T(8,128)(2,1)}), bf16[16,600,128]{2,1,0:T(8,128)(2,1)S(1)}, u32[]{:S(2)}, u32[]{:S(2)}) async-start(bf16[16,600,128]{2,1,0:T(8,128)(2,1)} %get-tuple-element.34), calls=%async_computation | async-start | bytes 4915200 | tf_op jit(solution)/shard_map/all_to_all | solution.py:52
  29.1 37.2 %collective-permute-start.1 = (bf16[128,1024]{1,0:T(8,128)(2,1)}, bf16[128,1024]{1,0:T(8,128)(2,1)S(1)}, u32[]{:S(2)}, u32[]{:S(2)}) collective-permute-start(bf16[128,1024]{1,0:T(8,128)(2,1)} %a_ref.1), channel_id=1, source_target_pairs={{0,16},{1,17},{2,18},{3,19},{4,20},{5,21},{6,22},{7,23},{8,24},{9,... | collective-permute-start | bytes 786440 | tf_op jit(solution)/shard_map/ppermute | solution.py:42
  37.4 28.9 %collective-permute-start.2 = (bf16[128,1024]{1,0:T(8,128)(2,1)}, bf16[128,1024]{1,0:T(8,128)(2,1)}, u32[]{:S(2)}, u32[]{:S(2)}) collective-permute-start(bf16[128,1024]{1,0:T(8,128)(2,1)} %g_ref.1), channel_id=1, source_target_pairs={{0,16},{1,17},{2,18},{3,19},{4,20},{5,21},{6,22},{7,23},{8,24},{9,... | collective-permute-start | bytes 786440 | tf_op jit(solution)/shard_map/ppermute | solution.py:42
  60.5 1.5 copy-start.2
  62.0 14.9 %all-to-all-start.1 = ((bf16[16,200,128]{2,1,0:T(8,128)(2,1)}), bf16[16,200,128]{2,1,0:T(8,128)(2,1)}, u32[]{:S(2)}, u32[]{:S(2)}) async-start(bf16[16,200,128]{2,1,0:T(8,128)(2,1)} %get-tuple-element.40), calls=%async_computation.1 | async-start | bytes 1638400 | tf_op jit(solution)/shard_map/all_to_all | solution.py:52
  69.1 12.2 %copy-start = (bf16[1,1,1024,768]{3,2,1,0:T(8,128)(2,1)S(1)}, bf16[1,1,1024,768]{3,2,1,0:T(8,128)(2,1)}, u32[]{:S(2)}) copy-start(bf16[1,1,1024,768]{3,2,1,0:T(8,128)(2,1)} %param.16) | copy-start | bytes 4718596
  69.1 12.2 %copy-start.1 = (bf16[1,1,768,1024]{3,2,1,0:T(8,128)(2,1)S(1)}, bf16[1,1,768,1024]{3,2,1,0:T(8,128)(2,1)}, u32[]{:S(2)}) copy-start(bf16[1,1,768,1024]{3,2,1,0:T(8,128)(2,1)} %param.17) | copy-start | bytes 4718596
  76.9 30.9 %all-to-all-start.2 = ((bf16[16,400,128]{2,1,0:T(8,128)(2,1)}), bf16[16,400,128]{2,1,0:T(8,128)(2,1)}, u32[]{:S(2)}, u32[]{:S(2)}) async-start(bf16[16,400,128]{2,1,0:T(8,128)(2,1)} %copy-done.4), calls=%async_computation.2 | async-start | bytes 3276800 | tf_op jit(solution)/shard_map/all_to_all | solution.py:52
  81.4 1.7 copy-start.3
  87.6 13.5 %collective-permute-start.3 = (bf16[512,768]{1,0:T(8,128)(2,1)S(1)}, bf16[512,768]{1,0:T(8,128)(2,1)S(1)}, u32[]{:S(2)}, u32[]{:S(2)}) collective-permute-start(bf16[512,768]{1,0:T(8,128)(2,1)S(1)} %get-tuple-element.41.refs_0_), channel_id=1, source_target_pairs={{0,32},{32,0},{1,33},{33,1},{2,34},{34,2},{3,35},{35,3},{4,36},{36... | collective-permute-start | bytes 2359304 | tf_op jit(solution)/shard_map/ppermute | solution.py:48
  94.8 6.3 %collective-permute-start.4 = (bf16[512,768]{1,0:T(8,128)(2,1)S(1)}, bf16[512,768]{1,0:T(8,128)(2,1)S(1)}, u32[]{:S(2)}, u32[]{:S(2)}) collective-permute-start(bf16[512,768]{1,0:T(8,128)(2,1)S(1)} %get-tuple-element.42.refs_1_), channel_id=1, source_target_pairs={{0,32},{32,0},{1,33},{33,1},{2,34},{34,2},{3,35},{35,3},{4,36},{36... | collective-permute-start | bytes 2359304 | tf_op jit(solution)/shard_map/ppermute | solution.py:48
  96.7 4.4 %collective-permute-start.5 = (bf16[512,768]{1,0:T(8,128)(2,1)S(1)}, bf16[512,768]{1,0:T(8,128)(2,1)S(1)}, u32[]{:S(2)}, u32[]{:S(2)}) collective-permute-start(bf16[512,768]{1,0:T(8,128)(2,1)S(1)} %get-tuple-element.43.refs_2_), channel_id=1, source_target_pairs={{0,32},{32,0},{1,33},{33,1},{2,34},{34,2},{3,35},{35,3},{4,36},{36... | collective-permute-start | bytes 2359304 | tf_op jit(solution)/shard_map/ppermute | solution.py:48
  99.2 4.2 %collective-permute-start.6 = (bf16[512,768]{1,0:T(8,128)(2,1)S(1)}, bf16[512,768]{1,0:T(8,128)(2,1)S(1)}, u32[]{:S(2)}, u32[]{:S(2)}) collective-permute-start(bf16[512,768]{1,0:T(8,128)(2,1)S(1)} %get-tuple-element.44.refs_3_), channel_id=1, source_target_pairs={{0,32},{32,0},{1,33},{33,1},{2,34},{34,2},{3,35},{35,3},{4,36},{36... | collective-permute-start | bytes 2359304 | tf_op jit(solution)/shard_map/ppermute | solution.py:48
  107.8 9.5 %copy-start.6 = (bf16[16,200,128]{2,1,0:T(8,128)(2,1)S(1)}, bf16[16,200,128]{2,1,0:T(8,128)(2,1)}, u32[]{:S(2)}) copy-start(bf16[16,200,128]{2,1,0:T(8,128)(2,1)} %copy-done.5) | copy-start | bytes 2457604
  111.1 4.5 %collective-permute-start.7 = (bf16[512,768]{1,0:T(8,128)(2,1)S(1)}, bf16[512,768]{1,0:T(8,128)(2,1)S(1)}, u32[]{:S(2)}, u32[]{:S(2)}) collective-permute-start(bf16[512,768]{1,0:T(8,128)(2,1)S(1)} %get-tuple-element.51.refs_0_), channel_id=1, source_target_pairs={{0,32},{32,0},{1,33},{33,1},{2,34},{34,2},{3,35},{35,3},{4,36},{36... | collective-permute-start | bytes 2359304 | tf_op jit(solution)/shard_map/ppermute | solution.py:48
  113.1 4.2 %collective-permute-start.8 = (bf16[512,768]{1,0:T(8,128)(2,1)S(1)}, bf16[512,768]{1,0:T(8,128)(2,1)S(1)}, u32[]{:S(2)}, u32[]{:S(2)}) collective-permute-start(bf16[512,768]{1,0:T(8,128)(2,1)S(1)} %get-tuple-element.52.refs_1_), channel_id=1, source_target_pairs={{0,32},{32,0},{1,33},{33,1},{2,34},{34,2},{3,35},{35,3},{4,36},{36... | collective-permute-start | bytes 2359304 | tf_op jit(solution)/shard_map/ppermute | solution.py:48
  148.6 30.3 %copy-start.7 = (bf16[512,128]{1,0:T(8,128)(2,1)S(1)}, bf16[512,128]{1,0:T(8,128)(2,1)}, u32[]{:S(2)}) copy-start(bf16[512,128]{1,0:T(8,128)(2,1)} %get-tuple-element.33.refs_1_) | copy-start | bytes 393220
  148.6 30.3 %copy-start.8 = (bf16[512,128]{1,0:T(8,128)(2,1)S(1)}, bf16[512,128]{1,0:T(8,128)(2,1)}, u32[]{:S(2)}) copy-start(bf16[512,128]{1,0:T(8,128)(2,1)} %get-tuple-element.32.refs_0_) | copy-start | bytes 393220
  148.6 30.3 %all-to-all-start.4 = ((bf16[16,400,128]{2,1,0:T(8,128)(2,1)}), bf16[16,400,128]{2,1,0:T(8,128)(2,1)S(1)}, u32[]{:S(2)}, u32[]{:S(2)}) async-start(bf16[16,400,128]{2,1,0:T(8,128)(2,1)} %get-tuple-element.54), calls=%async_computation.4 | async-start | bytes 3276800 | tf_op jit(solution)/shard_map/all_to_all | solution.py:52
  152.5 42.2 %collective-permute-start.11 = (bf16[128,1024]{1,0:T(8,128)(2,1)S(1)}, bf16[128,1024]{1,0:T(8,128)(2,1)S(1)}, u32[]{:S(2)}, u32[]{:S(2)}) collective-permute-start(bf16[128,1024]{1,0:T(8,128)(2,1)S(1)} %get-tuple-element.57), channel_id=1, source_target_pairs={{0,464},{1,465},{2,466},{3,467},{4,468},{5,469},{6,470},{7,471},{8... | collective-permute-start | bytes 786440 | tf_op jit(solution)/shard_map/ppermute | solution.py:42
  158.1 56.6 %collective-permute-start.12 = (bf16[128,1024]{1,0:T(8,128)(2,1)S(1)}, bf16[128,1024]{1,0:T(8,128)(2,1)S(1)}, u32[]{:S(2)}, u32[]{:S(2)}) collective-permute-start(bf16[128,1024]{1,0:T(8,128)(2,1)S(1)} %get-tuple-element.53), channel_id=1, source_target_pairs={{0,80},{1,81},{2,82},{3,83},{4,84},{5,85},{6,86},{7,87},{8,88},{9,... | collective-permute-start | bytes 786440 | tf_op jit(solution)/shard_map/ppermute | solution.py:42
  179.5 35.3 %collective-permute-start.9 = (bf16[128,1024]{1,0:T(8,128)(2,1)S(1)}, bf16[128,1024]{1,0:T(8,128)(2,1)S(1)}, u32[]{:S(2)}, u32[]{:S(2)}) collective-permute-start(bf16[128,1024]{1,0:T(8,128)(2,1)S(1)} %get-tuple-element.55), channel_id=1, source_target_pairs={{0,448},{1,449},{2,450},{3,451},{4,452},{5,453},{6,454},{7,455},{8... | collective-permute-start | bytes 786440 | tf_op jit(solution)/shard_map/ppermute | solution.py:42
  189.1 36.8 %collective-permute-start.10 = (bf16[128,1024]{1,0:T(8,128)(2,1)S(1)}, bf16[128,1024]{1,0:T(8,128)(2,1)S(1)}, u32[]{:S(2)}, u32[]{:S(2)}) collective-permute-start(bf16[128,1024]{1,0:T(8,128)(2,1)S(1)} %get-tuple-element.56), channel_id=1, source_target_pairs={{0,64},{1,65},{2,66},{3,67},{4,68},{5,69},{6,70},{7,71},{8,72},{9,... | collective-permute-start | bytes 786440 | tf_op jit(solution)/shard_map/ppermute | solution.py:42
  (2 other events, 2.1 us)

commit v10 on v9

--- a/solution.py
+++ b/solution.py
@@ -78,11 +78,13 @@
     return jax.ShapeDtypeStruct(shape, BF)
 
 
-def gather_block(f_ref, *refs):
-    notes, out_ref, hold_ref = refs[:4], refs[4], refs[5]
+def gather_block(f_ref, a_ref, g_ref, *refs):
+    notes, out_ref, pair_ref, hold_ref = refs[:4], refs[4], refs[5], refs[6]
     tokens = f_ref.shape[0]
     top = notes[0].shape[0]
     out_ref[:tokens, :] = f_ref[...]
+    pair_ref[:tokens, :] = a_ref[...]
+    pair_ref[tokens:, :] = g_ref[...]
     hold_ref[...] = jnp.zeros(hold_ref.shape, F32)
     for half in range(2):
         span = slice(half * tokens, (half + 1) * tokens)
@@ -154,10 +156,10 @@
             wide[e * SLOTS : (e + 1) * SLOTS, :] = unflat(rows[i * each : (i + 1) * each]).astype(BF)
 
 
-def put(wide_ref, hit, rows_ref):
-    tokens = hit.shape[1]
+def put(wide_ref, hit, rows_ref, first=0):
+    rows = slice(first, first + hit.shape[1])
     for c in range(0, wide_ref.shape[1], WIDTH):
-        wide_ref[:, c : c + WIDTH] = dot32(hit, rows_ref[:tokens, c : c + WIDTH])
+        wide_ref[:, c : c + WIDTH] = dot32(hit, rows_ref[rows, c : c + WIDTH])
 
 
 def block_tables(top, first_ref, block_ref, experts, tokens):
@@ -165,14 +167,15 @@
     return tables(note, first_ref[0], top, experts)
 
 
-def pack_near(top, first_ref, block_ref, a_ref, g_ref, out_ref, mix_f_ref, mix_b_ref, *wides):
+def pack_near(top, first_ref, block_ref, pair_ref, out_ref, mix_f_ref, mix_b_ref, *wides):
+    tokens = mix_f_ref.shape[1]
     (hit_f, mix_f), (hit_b, mix_b) = block_tables(
-        top, first_ref, block_ref, out_ref.shape[0], a_ref.shape[0]
+        top, first_ref, block_ref, out_ref.shape[0], tokens
     )
     mix_f_ref[...] = mix_f
     mix_b_ref[...] = mix_b
-    put(wides[0], hit_b, a_ref)
-    put(wides[1], hit_b, g_ref)
+    put(wides[0], hit_b, pair_ref)
+    put(wides[1], hit_b, pair_ref, tokens)
     put(wides[2], hit_f, block_ref)
     ship(out_ref, wides)
 
@@ -188,9 +191,9 @@
     ship(out_ref, wides)
 
 
-def pack_far_b(hit_ref, a_ref, g_ref, out_ref, *wides):
-    put(wides[0], hit_ref[...], a_ref)
-    put(wides[1], hit_ref[...], g_ref)
+def pack_far_b(hit_ref, pair_ref, out_ref, *wides):
+    put(wides[0], hit_ref[...], pair_ref)
+    put(wides[1], hit_ref[...], pair_ref, hit_ref.shape[1])
     ship(out_ref, wides)
 
 
@@ -253,25 +256,24 @@
     return group.count("f") + group.count("a")
 
 
-def sums(count, *refs):
-    mixes, wides = refs[:count], refs[-count:]
-    backs, outs = refs[count : -2 * count], refs[-2 * count : -count]
-    for i, back_ref in enumerate(backs):
-        unship(back_ref, [wides[i]] if len(backs) > 1 else wides)
-    for mix_ref, wide, out_ref in zip(mixes, wides, outs):
-        for c in range(0, out_ref.shape[1], WIDTH):
-            total = dot32(mix_ref[...], wide[:, c : c + WIDTH], OVER_ROWS)
-            out_ref[:, c : c + WIDTH] = total.astype(BF)
-
-
-def hold(a_ref, b_ref, x_ref, y_ref):
-    x_ref[...] = a_ref[...]
-    y_ref[...] = b_ref[...]
-
-
-def add(a_ref, b_ref, c_ref, d_ref, x_ref, y_ref):
-    x_ref[...] = (a_ref[...].astype(F32) + c_ref[...].astype(F32)).astype(BF)
-    y_ref[...] = (b_ref[...].astype(F32) + d_ref[...].astype(F32)).astype(BF)
+def sums(count, last, *refs):
+    mixes, back_ref, wides = refs[:count], refs[count], refs[-count:]
+    unship(back_ref, wides)
+    tokens = mixes[0].shape[1]
+    for i, (mix_ref, wide) in enumerate(zip(mixes, wides)):
+        rows = slice(i * tokens, (i + 1) * tokens)
+        for c in range(0, wide.shape[1], WIDTH):
+            cols = slice(c, c + WIDTH)
+            total = dot32(mix_ref[...], wide[:, cols], OVER_ROWS)
+            if last:
+                over_ref, out_ref = refs[count + 1], refs[count + 2 + i]
+                out_ref[:, cols] = (total + over_ref[rows, cols].astype(F32)).astype(BF)
+            else:
+                refs[count + 1][rows, cols] = total.astype(BF)
+
+
+def hold(from_ref, to_ref):
+    to_ref[...] = from_ref[...]
 
 
 def local(
@@ -323,19 +325,12 @@
             scratch=[pltpu.VMEM((rows, hidden), BF)] + wide(made("".join(groups)), F32),
         )
 
-    def combined(back, *mixes):
-        return run(
-            functools.partial(sums, len(mixes)),
-            (shaped(tok, cols),) * len(mixes),
-            *mixes,
-            *back,
-            scratch=wide(len(mixes), BF),
-        )
-
-    block = run(
+    block, pair = run(
         gather_block,
-        shaped(tok + 16, cols),
+        (shaped(tok + 16, cols), shaped(2 * tok, cols)),
         act_forward,
+        act_backward,
+        grad_backward,
         routes_forward.T,
         gates_forward.T,
         routes_backward.T,
@@ -344,16 +339,14 @@
         room=56 << 20,
     )
     far_block = moved(block, 0, True)
-    far_a = moved(after(act_backward, far_block), 0, True)
-    far_g = moved(after(grad_backward, far_block), 0, True)
+    far_pair = moved(pair, 0, True)
 
     sent, mix_f, mix_b = run(
         functools.partial(pack_near, top),
         (sendable(3), table, table),
         first,
         block,
-        act_backward,
-        grad_backward,
+        pair,
         scalars=1,
         scratch=wide(3, F32),
         room=56 << 20,
@@ -373,23 +366,32 @@
         pack_far_b,
         sendable(2),
         far_hit_b,
-        far_a,
-        far_g,
+        far_pair,
         scratch=wide(2, F32),
         flops=LONG,
     )
     got_b = exchange(after(sent_b, got_f))
     out, out_f = work((after(got, sent_b), got_f), "agf", "f")
     (out_bf,) = work((after(got_b, out_f),), "ag", added=(out_f,))
-    far_sum_b, far_sum_f = combined((exchange(out_bf),), far_mix_b, far_mix_f)
-    over = (moved(far_sum_b, -1, True), moved(far_sum_f, 1, True))
-    back = exchange(after(out, far_sum_f))
-    sum_b, sum_f = combined((back,), mix_b, mix_f)
-    near = (moved(sum_b, -1, False), moved(sum_f, 1, False))
-    pair = (shaped(tok, cols),) * 2
-    over = run(hold, pair, *over, flops=LONG)
-    input_grad, layer_out = run(add, pair, *near, *over)
-    return layer_out, input_grad
+    far_sum = run(
+        functools.partial(sums, 2, False),
+        shaped(2 * tok, cols),
+        far_mix_b,
+        far_mix_f,
+        exchange(out_bf),
+        scratch=wide(2, BF),
+    )
+    over = run(hold, shaped(2 * tok, cols), moved(far_sum, 0, True), flops=LONG)
+    sum_b, sum_f = run(
+        functools.partial(sums, 2, True),
+        (shaped(tok, cols),) * 2,
+        mix_b,
+        mix_f,
+        exchange(after(out, far_sum)),
+        over,
+        scratch=wide(2, BF),
+    )
+    return moved(sum_f, 1, False), moved(sum_b, -1, False)
 
 
 def solution(mesh):

time: 228 us -> 229 us (level)
  waiting for transfers between devices: 58.8 us -> 70.6 us
  starting transfers between devices: 109 us -> 97.3 us
  local copies, waits for them, and re-layouts: 5.25 us -> 8.31 us
    all_to_all x4, waiting for transfers between devices: 23.7 us -> 49.1 us  [exchange(): return lax.all_to_all(v, PLANE, split_axis=0, concat_axis=0, tiled=True)]
    ppermute x7 -> x5, waiting for transfers between devices: 31.2 us -> 17.6 us  [moved(): lax.ppermute(v, RING, pairs_of(shape, lambda s, h: ((s + by) % sections,...]
    ppermute x7 -> x5, starting transfers between devices: 71.9 us -> 60.2 us  [moved(): lax.ppermute(v, RING, pairs_of(shape, lambda s, h: ((s + by) % sections,...]
    unnamed x18 -> x24, local copies, waits for them, and re-layouts: 5.25 us -> 8.31 us
    pallas_call x12 -> x11, Pallas kernels: 23.3 us -> 21.9 us  [run(): pl.pallas_call(kernel, out_shape=outs, in_specs=where, out_specs=jax.tree...]
  transfers between devices with their start and end apart: 17 -> 15, of which waited for: 6 -> 8; matrix products, arithmetic and copies ran while one was open for 0% -> 0% of each run, Pallas kernels for 7% -> 6%
where the time goes in v10:
time: 229 us; the launch traced here: 228 us
  starting transfers between devices  97.3 us (42%)
  waiting for transfers between devices  70.6 us (31%)
  blocking collectives  29.4 us (13%)
  Pallas kernels  21.9 us (10%)
  local copies, waits for them, and re-layouts  8.31 us (4%)
    ppermute x5, starting transfers between devices, moved(): lax.ppermute(v, RING, pairs_of(shape, lambda s, h: ((s + by) % sections,...  60.2 us
    all_to_all x4, waiting for transfers between devices, exchange(): return lax.all_to_all(v, PLANE, split_axis=0, concat_axis=0, tiled=True)  49.1 us
    all_to_all x1, blocking collectives, exchange(): return lax.all_to_all(v, PLANE, split_axis=0, concat_axis=0, tiled=True)  29.4 us
    pallas_call x11, Pallas kernels, run(): pl.pallas_call(kernel, out_shape=outs, in_specs=where, out_specs=jax.tree...  21.9 us
    all_to_all x4, starting transfers between devices, exchange(): return lax.all_to_all(v, PLANE, split_axis=0, concat_axis=0, tiled=True)  19.2 us
    ppermute x6, starting transfers between devices, other_core(): return lax.ppermute(v, NODE, [(0, 1), (1, 0)])  17.9 us
    ppermute x5, waiting for transfers between devices, moved(): lax.ppermute(v, RING, pairs_of(shape, lambda s, h: ((s + by) % sections,...  17.6 us
    unnamed x24, local copies, waits for them, and re-layouts  8.31 us
  transfers between devices with their start and end apart: 15, of which 8 were waited for; matrix products, arithmetic and copies ran while one was open for 0% of the time, Pallas kernels for 6%

profile of v10, /device:TPU:1, one launch (start us, length us, event | category | flops | bytes accessed | tf_op | source)
XLA Modules:
  0.0 228.4 jit_solution(3061336408350874327)
XLA Ops:
  0.6 2.1 shard_map.104
  2.8 16.3 %collective-permute-start = (bf16[144,1024]{1,0:T(8,128)(2,1)}, bf16[144,1024]{1,0:T(8,128)(2,1)S(1)}, u32[]{:S(2)}, u32[]{:S(2)}) collective-permute-start(bf16[144,1024]{1,0:T(8,128)(2,1)} %get-tuple-element.26.block_ref), channel_id=1, source_target_pairs={{0,16},{1,17},{2,18},{3,19},{4,20},{5,21},{6,22},{7,23},{8,24},{9,... | collective-permute-start | bytes 884744 | tf_op jit(solution)/shard_map/ppermute | solution.py:42
  21.0 3.7 %shard_map.105 = (bf16[16,600,128]{2,1,0:T(8,128)(2,1)}, bf16[512,128]{1,0:T(8,128)(2,1)}, bf16[512,128]{1,0:T(8,128)(2,1)}) custom-call(s32[1]{0:T(128)} %bitcast.first_ref, bf16[144,1024]{1,0:T(8,128)(2,1)} %get-tuple-element.26.block_ref, bf16[256,1024]{1,0:T(8,128)(2,1)} %get-tuple-element.27.pair_ref), custom_call_target="tpu_custom_call" | custom-call | flops 1000 | bytes 1000 | tf_op jit(solution)/shard_map/pallas_call | solution.py:66
  24.7 6.7 %all-to-all-start = ((bf16[16,600,128]{2,1,0:T(8,128)(2,1)}), bf16[16,600,128]{2,1,0:T(8,128)(2,1)S(1)}, u32[]{:S(2)}, u32[]{:S(2)}) async-start(bf16[16,600,128]{2,1,0:T(8,128)(2,1)} %get-tuple-element.30), calls=%async_computation | async-start | bytes 4915200 | tf_op jit(solution)/shard_map/all_to_all | solution.py:52
  34.6 28.2 %all-to-all-done.refs_0_ = bf16[16,600,128]{2,1,0:T(8,128)(2,1)S(1)} async-done(((bf16[16,600,128]{2,1,0:T(8,128)(2,1)}), bf16[16,600,128]{2,1,0:T(8,128)(2,1)S(1)}, u32[]{:S(2)}, u32[]{:S(2)}) %all-to-all-start) | async-done | bytes 2457632 | tf_op jit(solution)/shard_map/all_to_all | solution.py:52
  64.3 4.3 %all-to-all-start.1 = ((bf16[16,200,128]{2,1,0:T(8,128)(2,1)}), bf16[16,200,128]{2,1,0:T(8,128)(2,1)}, u32[]{:S(2)}, u32[]{:S(2)}) async-start(bf16[16,200,128]{2,1,0:T(8,128)(2,1)} %get-tuple-element.34), calls=%async_computation.1 | async-start | bytes 1638400 | tf_op jit(solution)/shard_map/all_to_all | solution.py:52
  70.4 8.8 %all-to-all-done.1.refs_1_ = bf16[16,200,128]{2,1,0:T(8,128)(2,1)} async-done(((bf16[16,200,128]{2,1,0:T(8,128)(2,1)}), bf16[16,200,128]{2,1,0:T(8,128)(2,1)}, u32[]{:S(2)}, u32[]{:S(2)}) %all-to-all-start.1) | async-done | bytes 819232 | tf_op jit(solution)/shard_map/all_to_all | solution.py:52
  79.2 4.4 %all-to-all-start.2 = ((bf16[16,400,128]{2,1,0:T(8,128)(2,1)}), bf16[16,400,128]{2,1,0:T(8,128)(2,1)}, u32[]{:S(2)}, u32[]{:S(2)}) async-start(bf16[16,400,128]{2,1,0:T(8,128)(2,1)} %copy-done.4), calls=%async_computation.2 | async-start | bytes 3276800 | tf_op jit(solution)/shard_map/all_to_all | solution.py:52
  85.3 4.6 %shard_map.108 = (bf16[512,768]{1,0:T(8,128)(2,1)S(1)}, bf16[512,768]{1,0:T(8,128)(2,1)S(1)}, bf16[512,768]{1,0:T(8,128)(2,1)S(1)}, bf16[512,768]{1,0:T(8,128)(2,1)S(1)}) custom-call(bf16[16,600,128]{2,1,0:T(8,128)(2,1)S(1)} %copy-done.3, bf16[16,200,128]{2,1,0:T(8,128)(2,1)} %all-to-all-done.1.refs_1_, bf16[1024,768]{1,0:T(8,128)(2,1)S(1)} %bitcast.7, ...), custom_call_target="tpu_custom_call" | custom-call | flops 1000 | bytes 1000 | tf_op jit(solution)/shard_map/pallas_call | solution.py:66
  89.9 7.2 %collective-permute-start.2 = (bf16[512,768]{1,0:T(8,128)(2,1)S(1)}, bf16[512,768]{1,0:T(8,128)(2,1)S(1)}, u32[]{:S(2)}, u32[]{:S(2)}) collective-permute-start(bf16[512,768]{1,0:T(8,128)(2,1)S(1)} %get-tuple-element.35.refs_0_), channel_id=1, source_target_pairs={{0,32},{32,0},{1,33},{33,1},{2,34},{34,2},{3,35},{35,3},{4,36},{36... | collective-permute-start | bytes 2359304 | tf_op jit(solution)/shard_map/ppermute | solution.py:48
  99.0 2.4 %collective-permute-start.4 = (bf16[512,768]{1,0:T(8,128)(2,1)S(1)}, bf16[512,768]{1,0:T(8,128)(2,1)S(1)}, u32[]{:S(2)}, u32[]{:S(2)}) collective-permute-start(bf16[512,768]{1,0:T(8,128)(2,1)S(1)} %get-tuple-element.37.refs_2_), channel_id=1, source_target_pairs={{0,32},{32,0},{1,33},{33,1},{2,34},{34,2},{3,35},{35,3},{4,36},{36... | collective-permute-start | bytes 2359304 | tf_op jit(solution)/shard_map/ppermute | solution.py:48
  103.4 2.2 collective-permute-done.5.refs_7_
  105.6 3.5 %shard_map.109 = (bf16[16,400,128]{2,1,0:T(8,128)(2,1)}, bf16[16,200,128]{2,1,0:T(8,128)(2,1)S(1)}) custom-call(bf16[512,768]{1,0:T(8,128)(2,1)S(1)} %get-tuple-element.35.refs_0_, bf16[512,768]{1,0:T(8,128)(2,1)S(1)} %get-tuple-element.36.refs_1_, bf16[512,768]{1,0:T(8,128)(2,1)S(1)} %get-tuple-element.37.refs_2_, ...), custom_call_target="tpu_custom_call" | custom-call | flops 1000 | bytes 1000 | tf_op jit(solution)/shard_map/pallas_call | solution.py:66
  110.1 3.3 %shard_map.110 = (bf16[512,768]{1,0:T(8,128)(2,1)S(1)}, bf16[512,768]{1,0:T(8,128)(2,1)S(1)}) custom-call(bf16[16,400,128]{2,1,0:T(8,128)(2,1)} %all-to-all-done.2.refs_0_, bf16[1024,768]{1,0:T(8,128)(2,1)S(1)} %bitcast.9, bf16[768,1024]{1,0:T(8,128)(2,1)S(1)} %bitcast.13), custom_call_target="tpu_custom_call" | custom-call | flops 1000 | bytes 1000 | tf_op jit(solution)/shard_map/pallas_call | solution.py:66
  113.4 2.0 collective-permute-start.6
  115.4 2.5 %collective-permute-start.7 = (bf16[512,768]{1,0:T(8,128)(2,1)S(1)}, bf16[512,768]{1,0:T(8,128)(2,1)S(1)}, u32[]{:S(2)}, u32[]{:S(2)}) collective-permute-start(bf16[512,768]{1,0:T(8,128)(2,1)S(1)} %get-tuple-element.46.refs_1_), channel_id=1, source_target_pairs={{0,32},{32,0},{1,33},{33,1},{2,34},{34,2},{3,35},{35,3},{4,36},{36... | collective-permute-start | bytes 2359304 | tf_op jit(solution)/shard_map/ppermute | solution.py:48
  121.1 29.4 %all_to_all.25.refs_2_ = bf16[16,400,128]{2,1,0:T(8,128)(2,1)S(1)} all-to-all(bf16[16,400,128]{2,1,0:T(8,128)(2,1)S(1)} %shard_map.111), channel_id=1, replica_groups=mesh['section'=8,'node'=2,'zhi'=2,'x'=4,'y'=4] {'x','y'}, dimensions={0} | all-to-all | bytes 3276800 | tf_op jit(solution)/shard_map/all_to_all | solution.py:52
  150.9 11.9 %collective-permute-start.8 = (bf16[256,1024]{1,0:T(8,128)(2,1)S(1)}, bf16[256,1024]{1,0:T(8,128)(2,1)S(1)}, u32[]{:S(2)}, u32[]{:S(2)}) collective-permute-start(bf16[256,1024]{1,0:T(8,128)(2,1)S(1)} %shard_map.112), channel_id=1, source_target_pairs={{0,16},{1,17},{2,18},{3,19},{4,20},{5,21},{6,22},{7,23},{8,24},{9,... | collective-permute-start | bytes 1572872 | tf_op jit(solution)/shard_map/ppermute | solution.py:42
  162.8 3.7 %all-to-all-start.4 = ((bf16[16,400,128]{2,1,0:T(8,128)(2,1)}), bf16[16,400,128]{2,1,0:T(8,128)(2,1)S(1)}, u32[]{:S(2)}, u32[]{:S(2)}) async-start(bf16[16,400,128]{2,1,0:T(8,128)(2,1)} %get-tuple-element.47), calls=%async_computation.4 | async-start | bytes 3276800 | tf_op jit(solution)/shard_map/all_to_all | solution.py:52
  166.6 9.0 %collective-permute-done.8.from_ref = bf16[256,1024]{1,0:T(8,128)(2,1)S(1)} collective-permute-done((bf16[256,1024]{1,0:T(8,128)(2,1)S(1)}, bf16[256,1024]{1,0:T(8,128)(2,1)S(1)}, u32[]{:S(2)}, u32[]{:S(2)}) %collective-permute-start.8) | collective-permute-done | bytes 524320 | tf_op jit(solution)/shard_map/ppermute | solution.py:42
  175.6 12.1 %all-to-all-done.4.refs_2_ = bf16[16,400,128]{2,1,0:T(8,128)(2,1)S(1)} async-done(((bf16[16,400,128]{2,1,0:T(8,128)(2,1)}), bf16[16,400,128]{2,1,0:T(8,128)(2,1)S(1)}, u32[]{:S(2)}, u32[]{:S(2)}) %all-to-all-start.4) | async-done | bytes 1638432 | tf_op jit(solution)/shard_map/all_to_all | solution.py:52
  188.2 28.2 %collective-permute-start.9 = (bf16[128,1024]{1,0:T(8,128)(2,1)S(1)}, bf16[128,1024]{1,0:T(8,128)(2,1)S(1)}, u32[]{:S(2)}, u32[]{:S(2)}) collective-permute-start(bf16[128,1024]{1,0:T(8,128)(2,1)S(1)} %get-tuple-element.48), channel_id=1, source_target_pairs={{0,64},{1,65},{2,66},{3,67},{4,68},{5,69},{6,70},{7,71},{8,72},{9,... | collective-permute-start | bytes 786440 | tf_op jit(solution)/shard_map/ppermute | solution.py:42
  218.3 3.1 %collective-permute-done.9 = bf16[128,1024]{1,0:T(8,128)(2,1)S(1)} collective-permute-done((bf16[128,1024]{1,0:T(8,128)(2,1)S(1)}, bf16[128,1024]{1,0:T(8,128)(2,1)S(1)}, u32[]{:S(2)}, u32[]{:S(2)}) %collective-permute-start.9) | collective-permute-done | bytes 262176 | tf_op jit(solution)/shard_map/ppermute | solution.py:42
  221.4 5.6 %collective-permute-done.10 = bf16[128,1024]{1,0:T(8,128)(2,1)S(1)} collective-permute-done((bf16[128,1024]{1,0:T(8,128)(2,1)S(1)}, bf16[128,1024]{1,0:T(8,128)(2,1)S(1)}, u32[]{:S(2)}, u32[]{:S(2)}) %collective-permute-start.10) | collective-permute-done | bytes 262176 | tf_op jit(solution)/shard_map/ppermute | solution.py:42
  (42 shorter events, 22.3 us)
Async XLA Ops:
  2.8 28.7 %collective-permute-start = (bf16[144,1024]{1,0:T(8,128)(2,1)}, bf16[144,1024]{1,0:T(8,128)(2,1)S(1)}, u32[]{:S(2)}, u32[]{:S(2)}) collective-permute-start(bf16[144,1024]{1,0:T(8,128)(2,1)} %get-tuple-element.26.block_ref), channel_id=1, source_target_pairs={{0,16},{1,17},{2,18},{3,19},{4,20},{5,21},{6,22},{7,23},{8,24},{9,... | collective-permute-start | bytes 884744 | tf_op jit(solution)/shard_map/ppermute | solution.py:42
  19.0 49.5 %collective-permute-start.1 = (bf16[256,1024]{1,0:T(8,128)(2,1)}, bf16[256,1024]{1,0:T(8,128)(2,1)S(1)}, u32[]{:S(2)}, u32[]{:S(2)}) collective-permute-start(bf16[256,1024]{1,0:T(8,128)(2,1)} %get-tuple-element.27.pair_ref), channel_id=1, source_target_pairs={{0,16},{1,17},{2,18},{3,19},{4,20},{5,21},{6,22},{7,23},{8,24},{9,... | collective-permute-start | bytes 1572872 | tf_op jit(solution)/shard_map/ppermute | solution.py:42
  24.7 38.2 %all-to-all-start = ((bf16[16,600,128]{2,1,0:T(8,128)(2,1)}), bf16[16,600,128]{2,1,0:T(8,128)(2,1)S(1)}, u32[]{:S(2)}, u32[]{:S(2)}) async-start(bf16[16,600,128]{2,1,0:T(8,128)(2,1)} %get-tuple-element.30), calls=%async_computation | async-start | bytes 4915200 | tf_op jit(solution)/shard_map/all_to_all | solution.py:52
  32.2 1.0 copy-start.10
  62.8 1.4 copy-start.2
  64.3 14.9 %all-to-all-start.1 = ((bf16[16,200,128]{2,1,0:T(8,128)(2,1)}), bf16[16,200,128]{2,1,0:T(8,128)(2,1)}, u32[]{:S(2)}, u32[]{:S(2)}) async-start(bf16[16,200,128]{2,1,0:T(8,128)(2,1)} %get-tuple-element.34), calls=%async_computation.1 | async-start | bytes 1638400 | tf_op jit(solution)/shard_map/all_to_all | solution.py:52
  69.3 1.2 copy-start.4
  70.4 13.2 %copy-start = (bf16[1,1,1024,768]{3,2,1,0:T(8,128)(2,1)S(1)}, bf16[1,1,1024,768]{3,2,1,0:T(8,128)(2,1)}, u32[]{:S(2)}) copy-start(bf16[1,1,1024,768]{3,2,1,0:T(8,128)(2,1)} %param.16) | copy-start | bytes 4718596
  70.4 13.2 %copy-start.1 = (bf16[1,1,768,1024]{3,2,1,0:T(8,128)(2,1)S(1)}, bf16[1,1,768,1024]{3,2,1,0:T(8,128)(2,1)}, u32[]{:S(2)}) copy-start(bf16[1,1,768,1024]{3,2,1,0:T(8,128)(2,1)} %param.17) | copy-start | bytes 4718596
  79.2 30.9 %all-to-all-start.2 = ((bf16[16,400,128]{2,1,0:T(8,128)(2,1)}), bf16[16,400,128]{2,1,0:T(8,128)(2,1)}, u32[]{:S(2)}, u32[]{:S(2)}) async-start(bf16[16,400,128]{2,1,0:T(8,128)(2,1)} %copy-done.4), calls=%async_computation.2 | async-start | bytes 3276800 | tf_op jit(solution)/shard_map/all_to_all | solution.py:52
  83.6 1.7 copy-start.3
  89.9 13.5 %collective-permute-start.2 = (bf16[512,768]{1,0:T(8,128)(2,1)S(1)}, bf16[512,768]{1,0:T(8,128)(2,1)S(1)}, u32[]{:S(2)}, u32[]{:S(2)}) collective-permute-start(bf16[512,768]{1,0:T(8,128)(2,1)S(1)} %get-tuple-element.35.refs_0_), channel_id=1, source_target_pairs={{0,32},{32,0},{1,33},{33,1},{2,34},{34,2},{3,35},{35,3},{4,36},{36... | collective-permute-start | bytes 2359304 | tf_op jit(solution)/shard_map/ppermute | solution.py:48
  97.1 6.3 %collective-permute-start.3 = (bf16[512,768]{1,0:T(8,128)(2,1)S(1)}, bf16[512,768]{1,0:T(8,128)(2,1)S(1)}, u32[]{:S(2)}, u32[]{:S(2)}) collective-permute-start(bf16[512,768]{1,0:T(8,128)(2,1)S(1)} %get-tuple-element.36.refs_1_), channel_id=1, source_target_pairs={{0,32},{32,0},{1,33},{33,1},{2,34},{34,2},{3,35},{35,3},{4,36},{36... | collective-permute-start | bytes 2359304 | tf_op jit(solution)/shard_map/ppermute | solution.py:48
  99.0 4.4 %collective-permute-start.4 = (bf16[512,768]{1,0:T(8,128)(2,1)S(1)}, bf16[512,768]{1,0:T(8,128)(2,1)S(1)}, u32[]{:S(2)}, u32[]{:S(2)}) collective-permute-start(bf16[512,768]{1,0:T(8,128)(2,1)S(1)} %get-tuple-element.37.refs_2_), channel_id=1, source_target_pairs={{0,32},{32,0},{1,33},{33,1},{2,34},{34,2},{3,35},{35,3},{4,36},{36... | collective-permute-start | bytes 2359304 | tf_op jit(solution)/shard_map/ppermute | solution.py:48
  101.4 4.2 %collective-permute-start.5 = (bf16[512,768]{1,0:T(8,128)(2,1)S(1)}, bf16[512,768]{1,0:T(8,128)(2,1)S(1)}, u32[]{:S(2)}, u32[]{:S(2)}) collective-permute-start(bf16[512,768]{1,0:T(8,128)(2,1)S(1)} %get-tuple-element.38.refs_3_), channel_id=1, source_target_pairs={{0,32},{32,0},{1,33},{33,1},{2,34},{34,2},{3,35},{35,3},{4,36},{36... | collective-permute-start | bytes 2359304 | tf_op jit(solution)/shard_map/ppermute | solution.py:48
  110.1 9.5 %copy-start.6 = (bf16[16,200,128]{2,1,0:T(8,128)(2,1)S(1)}, bf16[16,200,128]{2,1,0:T(8,128)(2,1)}, u32[]{:S(2)}) copy-start(bf16[16,200,128]{2,1,0:T(8,128)(2,1)} %copy-done.5) | copy-start | bytes 2457604
  113.4 4.5 %collective-permute-start.6 = (bf16[512,768]{1,0:T(8,128)(2,1)S(1)}, bf16[512,768]{1,0:T(8,128)(2,1)S(1)}, u32[]{:S(2)}, u32[]{:S(2)}) collective-permute-start(bf16[512,768]{1,0:T(8,128)(2,1)S(1)} %get-tuple-element.45.refs_0_), channel_id=1, source_target_pairs={{0,32},{32,0},{1,33},{33,1},{2,34},{34,2},{3,35},{35,3},{4,36},{36... | collective-permute-start | bytes 2359304 | tf_op jit(solution)/shard_map/ppermute | solution.py:48
  115.4 4.2 %collective-permute-start.7 = (bf16[512,768]{1,0:T(8,128)(2,1)S(1)}, bf16[512,768]{1,0:T(8,128)(2,1)S(1)}, u32[]{:S(2)}, u32[]{:S(2)}) collective-permute-start(bf16[512,768]{1,0:T(8,128)(2,1)S(1)} %get-tuple-element.46.refs_1_), channel_id=1, source_target_pairs={{0,32},{32,0},{1,33},{33,1},{2,34},{34,2},{3,35},{35,3},{4,36},{36... | collective-permute-start | bytes 2359304 | tf_op jit(solution)/shard_map/ppermute | solution.py:48
  150.9 24.6 %collective-permute-start.8 = (bf16[256,1024]{1,0:T(8,128)(2,1)S(1)}, bf16[256,1024]{1,0:T(8,128)(2,1)S(1)}, u32[]{:S(2)}, u32[]{:S(2)}) collective-permute-start(bf16[256,1024]{1,0:T(8,128)(2,1)S(1)} %shard_map.112), channel_id=1, source_target_pairs={{0,16},{1,17},{2,18},{3,19},{4,20},{5,21},{6,22},{7,23},{8,24},{9,... | collective-permute-start | bytes 1572872 | tf_op jit(solution)/shard_map/ppermute | solution.py:42
  162.8 24.9 %all-to-all-start.4 = ((bf16[16,400,128]{2,1,0:T(8,128)(2,1)}), bf16[16,400,128]{2,1,0:T(8,128)(2,1)S(1)}, u32[]{:S(2)}, u32[]{:S(2)}) async-start(bf16[16,400,128]{2,1,0:T(8,128)(2,1)} %get-tuple-element.47), calls=%async_computation.4 | async-start | bytes 3276800 | tf_op jit(solution)/shard_map/all_to_all | solution.py:52
  166.6 21.1 %copy-start.7 = (bf16[512,128]{1,0:T(8,128)(2,1)S(1)}, bf16[512,128]{1,0:T(8,128)(2,1)}, u32[]{:S(2)}) copy-start(bf16[512,128]{1,0:T(8,128)(2,1)} %get-tuple-element.29.refs_1_) | copy-start | bytes 393220
  166.6 21.1 %copy-start.8 = (bf16[512,128]{1,0:T(8,128)(2,1)S(1)}, bf16[512,128]{1,0:T(8,128)(2,1)}, u32[]{:S(2)}) copy-start(bf16[512,128]{1,0:T(8,128)(2,1)} %get-tuple-element.28.refs_0_) | copy-start | bytes 393220
  188.2 33.2 %collective-permute-start.9 = (bf16[128,1024]{1,0:T(8,128)(2,1)S(1)}, bf16[128,1024]{1,0:T(8,128)(2,1)S(1)}, u32[]{:S(2)}, u32[]{:S(2)}) collective-permute-start(bf16[128,1024]{1,0:T(8,128)(2,1)S(1)} %get-tuple-element.48), channel_id=1, source_target_pairs={{0,64},{1,65},{2,66},{3,67},{4,68},{5,69},{6,70},{7,71},{8,72},{9,... | collective-permute-start | bytes 786440 | tf_op jit(solution)/shard_map/ppermute | solution.py:42
  216.4 10.6 %collective-permute-start.10 = (bf16[128,1024]{1,0:T(8,128)(2,1)S(1)}, bf16[128,1024]{1,0:T(8,128)(2,1)S(1)}, u32[]{:S(2)}, u32[]{:S(2)}) collective-permute-start(bf16[128,1024]{1,0:T(8,128)(2,1)S(1)} %get-tuple-element.49), channel_id=1, source_target_pairs={{0,448},{1,449},{2,450},{3,451},{4,452},{5,453},{6,454},{7,455},{8... | collective-permute-start | bytes 786440 | tf_op jit(solution)/shard_map/ppermute | solution.py:42
  (2 other events, 1.6 us)

commit v11 on v10

--- a/solution.py
+++ b/solution.py
@@ -141,10 +141,9 @@
     return jnp.concatenate(columns, axis=1)
 
 
-def ship(out_ref, wides, added=()):
+def ship(out_ref, wides):
     for e in range(out_ref.shape[0]):
         rows = [flat(wide[e * SLOTS : (e + 1) * SLOTS, :]) for wide in wides]
-        rows += [ref[e].astype(F32) for ref in added]
         out_ref[e] = jnp.concatenate(rows, axis=0).astype(BF)
 
 
@@ -215,11 +214,10 @@
             out_ref[:, c : c + WIDTH] = part.astype(BF)
 
 
-def results(groups, more, *refs):
+def results(groups, *refs):
     kinds = "".join(groups)
     mine, theirs = refs[: len(kinds)], refs[len(kinds) : 2 * len(kinds)]
     w_in_ref, w_out_ref, *refs = refs[2 * len(kinds) :]
-    added, refs = refs[:more], refs[more:]
     outs, hold_ref, wides = refs[: len(groups)], refs[len(groups)], refs[len(groups) + 1 :]
     hidden, cols = w_in_ref.shape[1], w_in_ref.shape[0]
 
@@ -248,7 +246,7 @@
     at = 0
     for out_ref, group in zip(outs, groups):
         many = made(group)
-        ship(out_ref, wides[at : at + many], added)
+        ship(out_ref, wides[at : at + many])
         at += many
 
 
@@ -257,19 +255,16 @@
 
 
 def sums(count, last, *refs):
-    mixes, back_ref, wides = refs[:count], refs[count], refs[-count:]
+    mixes, back_ref, overs = refs[:count], refs[count], refs[count + 1 : count + 1 + last]
+    outs, wides = refs[-2 * count : -count], refs[-count:]
     unship(back_ref, wides)
-    tokens = mixes[0].shape[1]
-    for i, (mix_ref, wide) in enumerate(zip(mixes, wides)):
-        rows = slice(i * tokens, (i + 1) * tokens)
+    for i, (mix_ref, wide, out_ref) in enumerate(zip(mixes, wides, outs)):
         for c in range(0, wide.shape[1], WIDTH):
             cols = slice(c, c + WIDTH)
             total = dot32(mix_ref[...], wide[:, cols], OVER_ROWS)
             if last:
-                over_ref, out_ref = refs[count + 1], refs[count + 2 + i]
-                out_ref[:, cols] = (total + over_ref[rows, cols].astype(F32)).astype(BF)
-            else:
-                refs[count + 1][rows, cols] = total.astype(BF)
+                total = total + overs[i][:, cols].astype(F32)
+            out_ref[:, cols] = total.astype(BF)
 
 
 def hold(from_ref, to_ref):
@@ -303,7 +298,7 @@
     def sendable(kinds):
         return shaped(experts, kinds * (HEAD + 1) * (cols // LANES), LANES)
 
-    def work(gots, *groups, added=()):
+    def work(gots, *groups):
         count = len("".join(groups))
         mine = run(
             functools.partial(parts, groups),
@@ -315,14 +310,23 @@
         )
         theirs = [other_core(part) for part in mine]
         return run(
-            functools.partial(results, groups, len(added)),
-            tuple(sendable(made(group) + len(added)) for group in groups),
+            functools.partial(results, groups),
+            tuple(sendable(made(group)) for group in groups),
             *mine,
             *theirs,
             weight_in,
             weight_out,
-            *added,
             scratch=[pltpu.VMEM((rows, hidden), BF)] + wide(made("".join(groups)), F32),
+        )
+
+    def combined(back, mixes, overs=()):
+        return run(
+            functools.partial(sums, len(mixes), len(overs)),
+            (shaped(tok, cols),) * len(mixes),
+            *mixes,
+            back,
+            *overs,
+            scratch=wide(len(mixes), BF),
         )
 
     block, pair = run(
@@ -372,25 +376,15 @@
     )
     got_b = exchange(after(sent_b, got_f))
     out, out_f = work((after(got, sent_b), got_f), "agf", "f")
-    (out_bf,) = work((after(got_b, out_f),), "ag", added=(out_f,))
-    far_sum = run(
-        functools.partial(sums, 2, False),
-        shaped(2 * tok, cols),
-        far_mix_b,
-        far_mix_f,
-        exchange(out_bf),
-        scratch=wide(2, BF),
-    )
-    over = run(hold, shaped(2 * tok, cols), moved(far_sum, 0, True), flops=LONG)
-    sum_b, sum_f = run(
-        functools.partial(sums, 2, True),
-        (shaped(tok, cols),) * 2,
-        mix_b,
-        mix_f,
-        exchange(after(out, far_sum)),
-        over,
-        scratch=wide(2, BF),
-    )
+    back_f = exchange(after(out_f, got_b))
+    (out_b,) = work((after(got_b, out_f),), "ag")
+    back_b = exchange(after(out_b, back_f))
+    over_f = moved(combined(back_f, (far_mix_f,))[0], 0, True)
+    over_f = run(hold, shaped(tok, cols), over_f, flops=LONG)
+    far_sum_b = combined(back_b, (far_mix_b,))[0]
+    over_b = moved(far_sum_b, 0, True)
+    back = exchange(after(out, far_sum_b))
+    sum_b, sum_f = combined(back, (mix_b, mix_f), (over_b, over_f))
     return moved(sum_f, 1, False), moved(sum_b, -1, False)
 
 

time: 229 us -> 225 us (0.983)
  the two profiles are of different devices: /device:TPU:1 before, /device:TPU:488 now
where the time goes in v11:
time: 225 us; the launch traced here: 223 us
  waiting for transfers between devices  97.1 us (43%)
  starting transfers between devices  90.1 us (40%)
  Pallas kernels  25.7 us (11%)
  local copies, waits for them, and re-layouts  9.6 us (4%)
    all_to_all x6, waiting for transfers between devices, exchange(): return lax.all_to_all(v, PLANE, split_axis=0, concat_axis=0, tiled=True)  50 us
    ppermute x6, waiting for transfers between devices, moved(): lax.ppermute(v, RING, pairs_of(shape, lambda s, h: ((s + by) % sections,...  45.3 us
    ppermute x6, starting transfers between devices, moved(): lax.ppermute(v, RING, pairs_of(shape, lambda s, h: ((s + by) % sections,...  39.3 us
    all_to_all x6, starting transfers between devices, exchange(): return lax.all_to_all(v, PLANE, split_axis=0, concat_axis=0, tiled=True)  37.9 us
    pallas_call x12, Pallas kernels, run(): pl.pallas_call(kernel, out_shape=outs, in_specs=where, out_specs=jax.tree...  25.7 us
    ppermute x6, starting transfers between devices, other_core(): return lax.ppermute(v, NODE, [(0, 1), (1, 0)])  13 us
    unnamed x24, local copies, waits for them, and re-layouts  9.6 us
  transfers between devices with their start and end apart: 18, of which 12 were waited for; matrix products, arithmetic and copies ran while one was open for 0% of the time, Pallas kernels for 8%

profile of v11, /device:TPU:488, one launch (start us, length us, event | category | flops | bytes accessed | tf_op | source)
XLA Modules:
  0.0 223.5 jit_solution(17547033139059852164)
XLA Ops:
  2.8 6.3 %collective-permute-start = (bf16[144,1024]{1,0:T(8,128)(2,1)}, bf16[144,1024]{1,0:T(8,128)(2,1)S(1)}, u32[]{:S(2)}, u32[]{:S(2)}) collective-permute-start(bf16[144,1024]{1,0:T(8,128)(2,1)} %get-tuple-element.28.block_ref), channel_id=1, source_target_pairs={{0,16},{1,17},{2,18},{3,19},{4,20},{5,21},{6,22},{7,23},{8,24},{9,... | collective-permute-start | bytes 884744 | tf_op jit(solution)/shard_map/ppermute | solution.py:42
  9.1 8.2 %collective-permute-start.1 = (bf16[256,1024]{1,0:T(8,128)(2,1)}, bf16[256,1024]{1,0:T(8,128)(2,1)}, u32[]{:S(2)}, u32[]{:S(2)}) collective-permute-start(bf16[256,1024]{1,0:T(8,128)(2,1)} %get-tuple-element.29.pair_ref), channel_id=1, source_target_pairs={{0,16},{1,17},{2,18},{3,19},{4,20},{5,21},{6,22},{7,23},{8,24},{9,... | collective-permute-start | bytes 1572872 | tf_op jit(solution)/shard_map/ppermute | solution.py:42
  17.3 3.7 %shard_map.105 = (bf16[16,600,128]{2,1,0:T(8,128)(2,1)}, bf16[512,128]{1,0:T(8,128)(2,1)}, bf16[512,128]{1,0:T(8,128)(2,1)}) custom-call(s32[1]{0:T(128)} %bitcast.first_ref, bf16[144,1024]{1,0:T(8,128)(2,1)} %get-tuple-element.28.block_ref, bf16[256,1024]{1,0:T(8,128)(2,1)} %get-tuple-element.29.pair_ref), custom_call_target="tpu_custom_call" | custom-call | flops 1000 | bytes 1000 | tf_op jit(solution)/shard_map/pallas_call | solution.py:66
  21.0 7.4 %all-to-all-start = ((bf16[16,600,128]{2,1,0:T(8,128)(2,1)}), bf16[16,600,128]{2,1,0:T(8,128)(2,1)S(1)}, u32[]{:S(2)}, u32[]{:S(2)}) async-start(bf16[16,600,128]{2,1,0:T(8,128)(2,1)} %get-tuple-element.32), calls=%async_computation | async-start | bytes 4915200 | tf_op jit(solution)/shard_map/all_to_all | solution.py:52
  28.4 5.8 %collective-permute-done.block_ref = bf16[144,1024]{1,0:T(8,128)(2,1)S(1)} collective-permute-done((bf16[144,1024]{1,0:T(8,128)(2,1)}, bf16[144,1024]{1,0:T(8,128)(2,1)S(1)}, u32[]{:S(2)}, u32[]{:S(2)}) %collective-permute-start) | collective-permute-done | bytes 294944 | tf_op jit(solution)/shard_map/ppermute | solution.py:42
  35.7 25.2 %all-to-all-done.refs_0_ = bf16[16,600,128]{2,1,0:T(8,128)(2,1)S(1)} async-done(((bf16[16,600,128]{2,1,0:T(8,128)(2,1)}), bf16[16,600,128]{2,1,0:T(8,128)(2,1)S(1)}, u32[]{:S(2)}, u32[]{:S(2)}) %all-to-all-start) | async-done | bytes 2457632 | tf_op jit(solution)/shard_map/all_to_all | solution.py:52
  62.4 5.5 %all-to-all-start.1 = ((bf16[16,200,128]{2,1,0:T(8,128)(2,1)}), bf16[16,200,128]{2,1,0:T(8,128)(2,1)}, u32[]{:S(2)}, u32[]{:S(2)}) async-start(bf16[16,200,128]{2,1,0:T(8,128)(2,1)} %copy-done.8), calls=%async_computation.1 | async-start | bytes 1638400 | tf_op jit(solution)/shard_map/all_to_all | solution.py:52
  67.8 7.5 %collective-permute-done.1.pair_ref = bf16[256,1024]{1,0:T(8,128)(2,1)} collective-permute-done((bf16[256,1024]{1,0:T(8,128)(2,1)}, bf16[256,1024]{1,0:T(8,128)(2,1)}, u32[]{:S(2)}, u32[]{:S(2)}) %collective-permute-start.1) | collective-permute-done | bytes 524320 | tf_op jit(solution)/shard_map/ppermute | solution.py:42
  78.4 7.5 %all-to-all-start.2 = ((bf16[16,400,128]{2,1,0:T(8,128)(2,1)}), bf16[16,400,128]{2,1,0:T(8,128)(2,1)}, u32[]{:S(2)}, u32[]{:S(2)}) async-start(bf16[16,400,128]{2,1,0:T(8,128)(2,1)} %copy-done.6), calls=%async_computation.2 | async-start | bytes 3276800 | tf_op jit(solution)/shard_map/all_to_all | solution.py:52
  87.6 4.6 %shard_map.108 = (bf16[512,768]{1,0:T(8,128)(2,1)S(1)}, bf16[512,768]{1,0:T(8,128)(2,1)S(1)}, bf16[512,768]{1,0:T(8,128)(2,1)S(1)}, bf16[512,768]{1,0:T(8,128)(2,1)S(1)}) custom-call(bf16[16,600,128]{2,1,0:T(8,128)(2,1)S(1)} %copy-done.3, bf16[16,200,128]{2,1,0:T(8,128)(2,1)} %all-to-all-done.1.refs_1_, bf16[1024,768]{1,0:T(8,128)(2,1)S(1)} %bitcast.7, ...), custom_call_target="tpu_custom_call" | custom-call | flops 1000 | bytes 1000 | tf_op jit(solution)/shard_map/pallas_call | solution.py:66
  109.2 4.1 %shard_map.110 = (bf16[512,768]{1,0:T(8,128)(2,1)}, bf16[512,768]{1,0:T(8,128)(2,1)}) custom-call(bf16[16,400,128]{2,1,0:T(8,128)(2,1)} %all-to-all-done.2.refs_0_, bf16[1024,768]{1,0:T(8,128)(2,1)S(1)} %bitcast.9, bf16[768,1024]{1,0:T(8,128)(2,1)S(1)} %bitcast.13), custom_call_target="tpu_custom_call" | custom-call | flops 1000 | bytes 1000 | tf_op jit(solution)/shard_map/pallas_call | solution.py:66
  117.6 6.3 %all-to-all-start.3 = ((bf16[16,200,128]{2,1,0:T(8,128)(2,1)}), bf16[16,200,128]{2,1,0:T(8,128)(2,1)}, u32[]{:S(2)}, u32[]{:S(2)}) async-start(bf16[16,200,128]{2,1,0:T(8,128)(2,1)} %copy-done.7), calls=%async_computation.3 | async-start | bytes 1638400 | tf_op jit(solution)/shard_map/all_to_all | solution.py:52
  128.1 10.1 %all-to-all-done.3.refs_1_ = bf16[16,200,128]{2,1,0:T(8,128)(2,1)} async-done(((bf16[16,200,128]{2,1,0:T(8,128)(2,1)}), bf16[16,200,128]{2,1,0:T(8,128)(2,1)}, u32[]{:S(2)}, u32[]{:S(2)}) %all-to-all-start.3) | async-done | bytes 819232 | tf_op jit(solution)/shard_map/all_to_all | solution.py:52
  138.1 4.9 %all-to-all-start.4 = ((bf16[16,200,128]{2,1,0:T(8,128)(2,1)}), bf16[16,200,128]{2,1,0:T(8,128)(2,1)S(1)}, u32[]{:S(2)}, u32[]{:S(2)}) async-start(bf16[16,200,128]{2,1,0:T(8,128)(2,1)} %copy-done.4), calls=%async_computation.4 | async-start | bytes 1638400 | tf_op jit(solution)/shard_map/all_to_all | solution.py:52
  144.6 4.5 %collective-permute-start.9 = (bf16[128,1024]{1,0:T(8,128)(2,1)S(1)}, bf16[128,1024]{1,0:T(8,128)(2,1)S(1)}, u32[]{:S(2)}, u32[]{:S(2)}) collective-permute-start(bf16[128,1024]{1,0:T(8,128)(2,1)S(1)} %shard_map.113), channel_id=1, source_target_pairs={{0,16},{1,17},{2,18},{3,19},{4,20},{5,21},{6,22},{7,23},{8,24},{9,... | collective-permute-start | bytes 786440 | tf_op jit(solution)/shard_map/ppermute | solution.py:42
  149.1 6.5 %all-to-all-done.4.refs_1_ = bf16[16,200,128]{2,1,0:T(8,128)(2,1)S(1)} async-done(((bf16[16,200,128]{2,1,0:T(8,128)(2,1)}), bf16[16,200,128]{2,1,0:T(8,128)(2,1)S(1)}, u32[]{:S(2)}, u32[]{:S(2)}) %all-to-all-start.4) | async-done | bytes 819232 | tf_op jit(solution)/shard_map/all_to_all | solution.py:52
  155.9 4.5 %collective-permute-start.8 = (bf16[128,1024]{1,0:T(8,128)(2,1)S(1)}, bf16[128,1024]{1,0:T(8,128)(2,1)S(1)}, u32[]{:S(2)}, u32[]{:S(2)}) collective-permute-start(bf16[128,1024]{1,0:T(8,128)(2,1)S(1)} %shard_map.112), channel_id=1, source_target_pairs={{0,16},{1,17},{2,18},{3,19},{4,20},{5,21},{6,22},{7,23},{8,24},{9,... | collective-permute-start | bytes 786440 | tf_op jit(solution)/shard_map/ppermute | solution.py:42
  160.5 6.3 %all-to-all-start.5 = ((bf16[16,400,128]{2,1,0:T(8,128)(2,1)}), bf16[16,400,128]{2,1,0:T(8,128)(2,1)S(1)}, u32[]{:S(2)}, u32[]{:S(2)}) async-start(bf16[16,400,128]{2,1,0:T(8,128)(2,1)} %copy-done.5), calls=%async_computation.5 | async-start | bytes 3276800 | tf_op jit(solution)/shard_map/all_to_all | solution.py:52
  166.8 13.8 %collective-permute-done.8.refs_3_ = bf16[128,1024]{1,0:T(8,128)(2,1)S(1)} collective-permute-done((bf16[128,1024]{1,0:T(8,128)(2,1)S(1)}, bf16[128,1024]{1,0:T(8,128)(2,1)S(1)}, u32[]{:S(2)}, u32[]{:S(2)}) %collective-permute-start.8) | collective-permute-done | bytes 262176 | tf_op jit(solution)/shard_map/ppermute | solution.py:42
  180.6 7.0 %all-to-all-done.5.refs_2_ = bf16[16,400,128]{2,1,0:T(8,128)(2,1)S(1)} async-done(((bf16[16,400,128]{2,1,0:T(8,128)(2,1)}), bf16[16,400,128]{2,1,0:T(8,128)(2,1)S(1)}, u32[]{:S(2)}, u32[]{:S(2)}) %all-to-all-start.5) | async-done | bytes 1638432 | tf_op jit(solution)/shard_map/all_to_all | solution.py:52
  188.1 5.0 %collective-permute-start.10 = (bf16[128,1024]{1,0:T(8,128)(2,1)S(1)}, bf16[128,1024]{1,0:T(8,128)(2,1)S(1)}, u32[]{:S(2)}, u32[]{:S(2)}) collective-permute-start(bf16[128,1024]{1,0:T(8,128)(2,1)S(1)} %get-tuple-element.52), channel_id=1, source_target_pairs={{0,64},{1,65},{2,66},{3,67},{4,68},{5,69},{6,70},{7,71},{8,72},{9,... | collective-permute-start | bytes 786440 | tf_op jit(solution)/shard_map/ppermute | solution.py:42
  193.1 10.8 %collective-permute-start.11 = (bf16[128,1024]{1,0:T(8,128)(2,1)S(1)}, bf16[128,1024]{1,0:T(8,128)(2,1)S(1)}, u32[]{:S(2)}, u32[]{:S(2)}) collective-permute-start(bf16[128,1024]{1,0:T(8,128)(2,1)S(1)} %get-tuple-element.53), channel_id=1, source_target_pairs={{0,448},{1,449},{2,450},{3,451},{4,452},{5,453},{6,454},{7,455},{8... | collective-permute-start | bytes 786440 | tf_op jit(solution)/shard_map/ppermute | solution.py:42
  203.8 4.3 %collective-permute-done.10 = bf16[128,1024]{1,0:T(8,128)(2,1)S(1)} collective-permute-done((bf16[128,1024]{1,0:T(8,128)(2,1)S(1)}, bf16[128,1024]{1,0:T(8,128)(2,1)S(1)}, u32[]{:S(2)}, u32[]{:S(2)}) %collective-permute-start.10) | collective-permute-done | bytes 262176 | tf_op jit(solution)/shard_map/ppermute | solution.py:42
  208.2 13.9 %collective-permute-done.11 = bf16[128,1024]{1,0:T(8,128)(2,1)S(1)} collective-permute-done((bf16[128,1024]{1,0:T(8,128)(2,1)S(1)}, bf16[128,1024]{1,0:T(8,128)(2,1)S(1)}, u32[]{:S(2)}, u32[]{:S(2)}) %collective-permute-start.11) | collective-permute-done | bytes 262176 | tf_op jit(solution)/shard_map/ppermute | solution.py:42
  (48 shorter events, 38.9 us)
Async XLA Ops:
  2.8 31.5 %collective-permute-start = (bf16[144,1024]{1,0:T(8,128)(2,1)}, bf16[144,1024]{1,0:T(8,128)(2,1)S(1)}, u32[]{:S(2)}, u32[]{:S(2)}) collective-permute-start(bf16[144,1024]{1,0:T(8,128)(2,1)} %get-tuple-element.28.block_ref), channel_id=1, source_target_pairs={{0,16},{1,17},{2,18},{3,19},{4,20},{5,21},{6,22},{7,23},{8,24},{9,... | collective-permute-start | bytes 884744 | tf_op jit(solution)/shard_map/ppermute | solution.py:42
  9.1 66.2 %collective-permute-start.1 = (bf16[256,1024]{1,0:T(8,128)(2,1)}, bf16[256,1024]{1,0:T(8,128)(2,1)}, u32[]{:S(2)}, u32[]{:S(2)}) collective-permute-start(bf16[256,1024]{1,0:T(8,128)(2,1)} %get-tuple-element.29.pair_ref), channel_id=1, source_target_pairs={{0,16},{1,17},{2,18},{3,19},{4,20},{5,21},{6,22},{7,23},{8,24},{9,... | collective-permute-start | bytes 1572872 | tf_op jit(solution)/shard_map/ppermute | solution.py:42
  21.0 39.9 %all-to-all-start = ((bf16[16,600,128]{2,1,0:T(8,128)(2,1)}), bf16[16,600,128]{2,1,0:T(8,128)(2,1)S(1)}, u32[]{:S(2)}, u32[]{:S(2)}) async-start(bf16[16,600,128]{2,1,0:T(8,128)(2,1)} %get-tuple-element.32), calls=%async_computation | async-start | bytes 4915200 | tf_op jit(solution)/shard_map/all_to_all | solution.py:52
  60.9 1.5 copy-start.2
  62.4 16.0 %all-to-all-start.1 = ((bf16[16,200,128]{2,1,0:T(8,128)(2,1)}), bf16[16,200,128]{2,1,0:T(8,128)(2,1)}, u32[]{:S(2)}, u32[]{:S(2)}) async-start(bf16[16,200,128]{2,1,0:T(8,128)(2,1)} %copy-done.8), calls=%async_computation.1 | async-start | bytes 1638400 | tf_op jit(solution)/shard_map/all_to_all | solution.py:52
  78.3 7.7 %copy-start = (bf16[1,1,1024,768]{3,2,1,0:T(8,128)(2,1)S(1)}, bf16[1,1,1024,768]{3,2,1,0:T(8,128)(2,1)}, u32[]{:S(2)}) copy-start(bf16[1,1,1024,768]{3,2,1,0:T(8,128)(2,1)} %param.16) | copy-start | bytes 4718596
  78.3 7.7 %copy-start.1 = (bf16[1,1,768,1024]{3,2,1,0:T(8,128)(2,1)S(1)}, bf16[1,1,768,1024]{3,2,1,0:T(8,128)(2,1)}, u32[]{:S(2)}) copy-start(bf16[1,1,768,1024]{3,2,1,0:T(8,128)(2,1)} %param.17) | copy-start | bytes 4718596
  78.4 30.7 %all-to-all-start.2 = ((bf16[16,400,128]{2,1,0:T(8,128)(2,1)}), bf16[16,400,128]{2,1,0:T(8,128)(2,1)}, u32[]{:S(2)}, u32[]{:S(2)}) async-start(bf16[16,400,128]{2,1,0:T(8,128)(2,1)} %copy-done.6), calls=%async_computation.2 | async-start | bytes 3276800 | tf_op jit(solution)/shard_map/all_to_all | solution.py:52
  85.9 1.7 copy-start.3
  92.2 8.7 %collective-permute-start.2 = (bf16[512,768]{1,0:T(8,128)(2,1)S(1)}, bf16[512,768]{1,0:T(8,128)(2,1)S(1)}, u32[]{:S(2)}, u32[]{:S(2)}) collective-permute-start(bf16[512,768]{1,0:T(8,128)(2,1)S(1)} %get-tuple-element.37.refs_0_), channel_id=1, source_target_pairs={{0,32},{32,0},{1,33},{33,1},{2,34},{34,2},{3,35},{35,3},{4,36},{36... | collective-permute-start | bytes 2359304 | tf_op jit(solution)/shard_map/ppermute | solution.py:48
  94.1 6.8 %collective-permute-start.3 = (bf16[512,768]{1,0:T(8,128)(2,1)S(1)}, bf16[512,768]{1,0:T(8,128)(2,1)S(1)}, u32[]{:S(2)}, u32[]{:S(2)}) collective-permute-start(bf16[512,768]{1,0:T(8,128)(2,1)S(1)} %get-tuple-element.38.refs_1_), channel_id=1, source_target_pairs={{0,32},{32,0},{1,33},{33,1},{2,34},{34,2},{3,35},{35,3},{4,36},{36... | collective-permute-start | bytes 2359304 | tf_op jit(solution)/shard_map/ppermute | solution.py:48
  96.5 4.4 %collective-permute-start.4 = (bf16[512,768]{1,0:T(8,128)(2,1)S(1)}, bf16[512,768]{1,0:T(8,128)(2,1)S(1)}, u32[]{:S(2)}, u32[]{:S(2)}) collective-permute-start(bf16[512,768]{1,0:T(8,128)(2,1)S(1)} %get-tuple-element.39.refs_2_), channel_id=1, source_target_pairs={{0,32},{32,0},{1,33},{33,1},{2,34},{34,2},{3,35},{35,3},{4,36},{36... | collective-permute-start | bytes 2359304 | tf_op jit(solution)/shard_map/ppermute | solution.py:48
  98.5 4.3 %collective-permute-start.5 = (bf16[512,768]{1,0:T(8,128)(2,1)S(1)}, bf16[512,768]{1,0:T(8,128)(2,1)S(1)}, u32[]{:S(2)}, u32[]{:S(2)}) collective-permute-start(bf16[512,768]{1,0:T(8,128)(2,1)S(1)} %get-tuple-element.40.refs_3_), channel_id=1, source_target_pairs={{0,32},{32,0},{1,33},{33,1},{2,34},{34,2},{3,35},{35,3},{4,36},{36... | collective-permute-start | bytes 2359304 | tf_op jit(solution)/shard_map/ppermute | solution.py:48
  113.3 10.6 %collective-permute-start.6 = (bf16[512,768]{1,0:T(8,128)(2,1)}, bf16[512,768]{1,0:T(8,128)(2,1)}, u32[]{:S(2)}, u32[]{:S(2)}) collective-permute-start(bf16[512,768]{1,0:T(8,128)(2,1)} %get-tuple-element.46.refs_0_), channel_id=1, source_target_pairs={{0,32},{32,0},{1,33},{33,1},{2,34},{34,2},{3,35},{35,3},{4,36},{36... | collective-permute-start | bytes 2359304 | tf_op jit(solution)/shard_map/ppermute | solution.py:48
  115.2 8.7 %collective-permute-start.7 = (bf16[512,768]{1,0:T(8,128)(2,1)}, bf16[512,768]{1,0:T(8,128)(2,1)}, u32[]{:S(2)}, u32[]{:S(2)}) collective-permute-start(bf16[512,768]{1,0:T(8,128)(2,1)} %get-tuple-element.47.refs_1_), channel_id=1, source_target_pairs={{0,32},{32,0},{1,33},{33,1},{2,34},{34,2},{3,35},{35,3},{4,36},{36... | collective-permute-start | bytes 2359304 | tf_op jit(solution)/shard_map/ppermute | solution.py:48
  117.6 20.5 %all-to-all-start.3 = ((bf16[16,200,128]{2,1,0:T(8,128)(2,1)}), bf16[16,200,128]{2,1,0:T(8,128)(2,1)}, u32[]{:S(2)}, u32[]{:S(2)}) async-start(bf16[16,200,128]{2,1,0:T(8,128)(2,1)} %copy-done.7), calls=%async_computation.3 | async-start | bytes 1638400 | tf_op jit(solution)/shard_map/all_to_all | solution.py:52
  138.1 17.4 %all-to-all-start.4 = ((bf16[16,200,128]{2,1,0:T(8,128)(2,1)}), bf16[16,200,128]{2,1,0:T(8,128)(2,1)S(1)}, u32[]{:S(2)}, u32[]{:S(2)}) async-start(bf16[16,200,128]{2,1,0:T(8,128)(2,1)} %copy-done.4), calls=%async_computation.4 | async-start | bytes 1638400 | tf_op jit(solution)/shard_map/all_to_all | solution.py:52
  144.6 22.2 %collective-permute-start.9 = (bf16[128,1024]{1,0:T(8,128)(2,1)S(1)}, bf16[128,1024]{1,0:T(8,128)(2,1)S(1)}, u32[]{:S(2)}, u32[]{:S(2)}) collective-permute-start(bf16[128,1024]{1,0:T(8,128)(2,1)S(1)} %shard_map.113), channel_id=1, source_target_pairs={{0,16},{1,17},{2,18},{3,19},{4,20},{5,21},{6,22},{7,23},{8,24},{9,... | collective-permute-start | bytes 786440 | tf_op jit(solution)/shard_map/ppermute | solution.py:42
  155.9 24.6 %collective-permute-start.8 = (bf16[128,1024]{1,0:T(8,128)(2,1)S(1)}, bf16[128,1024]{1,0:T(8,128)(2,1)S(1)}, u32[]{:S(2)}, u32[]{:S(2)}) collective-permute-start(bf16[128,1024]{1,0:T(8,128)(2,1)S(1)} %shard_map.112), channel_id=1, source_target_pairs={{0,16},{1,17},{2,18},{3,19},{4,20},{5,21},{6,22},{7,23},{8,24},{9,... | collective-permute-start | bytes 786440 | tf_op jit(solution)/shard_map/ppermute | solution.py:42
  160.5 27.1 %all-to-all-start.5 = ((bf16[16,400,128]{2,1,0:T(8,128)(2,1)}), bf16[16,400,128]{2,1,0:T(8,128)(2,1)S(1)}, u32[]{:S(2)}, u32[]{:S(2)}) async-start(bf16[16,400,128]{2,1,0:T(8,128)(2,1)} %copy-done.5), calls=%async_computation.5 | async-start | bytes 3276800 | tf_op jit(solution)/shard_map/all_to_all | solution.py:52
  166.8 20.8 %copy-start.9 = (bf16[512,128]{1,0:T(8,128)(2,1)S(1)}, bf16[512,128]{1,0:T(8,128)(2,1)}, u32[]{:S(2)}) copy-start(bf16[512,128]{1,0:T(8,128)(2,1)} %get-tuple-element.31.refs_1_) | copy-start | bytes 393220
  166.8 20.8 %copy-start.10 = (bf16[512,128]{1,0:T(8,128)(2,1)S(1)}, bf16[512,128]{1,0:T(8,128)(2,1)}, u32[]{:S(2)}) copy-start(bf16[512,128]{1,0:T(8,128)(2,1)} %get-tuple-element.30.refs_0_) | copy-start | bytes 393220
  188.1 20.1 %collective-permute-start.10 = (bf16[128,1024]{1,0:T(8,128)(2,1)S(1)}, bf16[128,1024]{1,0:T(8,128)(2,1)S(1)}, u32[]{:S(2)}, u32[]{:S(2)}) collective-permute-start(bf16[128,1024]{1,0:T(8,128)(2,1)S(1)} %get-tuple-element.52), channel_id=1, source_target_pairs={{0,64},{1,65},{2,66},{3,67},{4,68},{5,69},{6,70},{7,71},{8,72},{9,... | collective-permute-start | bytes 786440 | tf_op jit(solution)/shard_map/ppermute | solution.py:42
  193.1 29.0 %collective-permute-start.11 = (bf16[128,1024]{1,0:T(8,128)(2,1)S(1)}, bf16[128,1024]{1,0:T(8,128)(2,1)S(1)}, u32[]{:S(2)}, u32[]{:S(2)}) collective-permute-start(bf16[128,1024]{1,0:T(8,128)(2,1)S(1)} %get-tuple-element.53), channel_id=1, source_target_pairs={{0,448},{1,449},{2,450},{3,451},{4,452},{5,453},{6,454},{7,455},{8... | collective-permute-start | bytes 786440 | tf_op jit(solution)/shard_map/ppermute | solution.py:42
  (5 other events, 5.1 us)

commit v12 on v11

--- a/solution.py
+++ b/solution.py
@@ -196,34 +196,42 @@
     ship(out_ref, wides)
 
 
-def parts(groups, *refs):
+def parts(groups, pieces, *refs):
     kinds = "".join(groups)
     gots, refs = refs[: len(groups)], refs[len(groups) :]
     w_in_ref, w_out_ref, *refs = refs
-    outs, wides = refs[: len(kinds)], refs[len(kinds) :]
+    outs, wides = refs[: len(kinds) * pieces], refs[len(kinds) * pieces :]
     at = 0
     for got_ref, group in zip(gots, groups):
         unship(got_ref, wides[at : at + len(group)])
         at += len(group)
-    for kind, wide, out_ref in zip(kinds, wides, outs):
+    for i, (kind, wide) in enumerate(zip(kinds, wides)):
+        each = wide.shape[0] // pieces
         for c in range(0, w_in_ref.shape[1], WIDTH):
             if kind == "g":
                 part = dot32(wide[...], w_out_ref[c : c + WIDTH, :], TRANSPOSED)
             else:
                 part = dot32(wide[...], w_in_ref[:, c : c + WIDTH])
-            out_ref[:, c : c + WIDTH] = part.astype(BF)
-
-
-def results(groups, *refs):
+            for j in range(pieces):
+                block = part[j * each : (j + 1) * each].astype(BF)
+                outs[i * pieces + j][:, c : c + WIDTH] = block
+
+
+def results(groups, pieces, *refs):
     kinds = "".join(groups)
-    mine, theirs = refs[: len(kinds)], refs[len(kinds) : 2 * len(kinds)]
-    w_in_ref, w_out_ref, *refs = refs[2 * len(kinds) :]
+    count = len(kinds) * pieces
+    mine, theirs = refs[:count], refs[count : 2 * count]
+    w_in_ref, w_out_ref, *refs = refs[2 * count :]
     outs, hold_ref, wides = refs[: len(groups)], refs[len(groups)], refs[len(groups) + 1 :]
     hidden, cols = w_in_ref.shape[1], w_in_ref.shape[0]
 
     def total(i, c):
         span = slice(c, c + WIDTH)
-        return mine[i][:, span].astype(F32) + theirs[i][:, span].astype(F32)
+        blocks = [
+            mine[j][:, span].astype(F32) + theirs[j][:, span].astype(F32)
+            for j in range(i * pieces, (i + 1) * pieces)
+        ]
+        return jnp.concatenate(blocks, axis=0)
 
     i = 0
     for wide in wides:
@@ -298,11 +306,11 @@
     def sendable(kinds):
         return shaped(experts, kinds * (HEAD + 1) * (cols // LANES), LANES)
 
-    def work(gots, *groups):
+    def work(gots, *groups, pieces=1):
         count = len("".join(groups))
         mine = run(
-            functools.partial(parts, groups),
-            (shaped(rows, hidden),) * count,
+            functools.partial(parts, groups, pieces),
+            (shaped(rows // pieces, hidden),) * (count * pieces),
             *gots,
             weight_in,
             weight_out,
@@ -310,7 +318,7 @@
         )
         theirs = [other_core(part) for part in mine]
         return run(
-            functools.partial(results, groups),
+            functools.partial(results, groups, pieces),
             tuple(sendable(made(group)) for group in groups),
             *mine,
             *theirs,
@@ -377,7 +385,7 @@
     got_b = exchange(after(sent_b, got_f))
     out, out_f = work((after(got, sent_b), got_f), "agf", "f")
     back_f = exchange(after(out_f, got_b))
-    (out_b,) = work((after(got_b, out_f),), "ag")
+    (out_b,) = work((after(got_b, out_f),), "ag", pieces=2)
     back_b = exchange(after(out_b, back_f))
     over_f = moved(combined(back_f, (far_mix_f,))[0], 0, True)
     over_f = run(hold, shaped(tok, cols), over_f, flops=LONG)

time: 225 us -> 220 us (0.978)
  the two profiles are of different devices: /device:TPU:488 before, /device:TPU:8 now
where the time goes in v12:
time: 220 us; the launch traced here: 219 us
  starting transfers between devices  116 us (53%)
  waiting for transfers between devices  70.3 us (32%)
  Pallas kernels  23 us (10%)
  local copies, waits for them, and re-layouts  9.18 us (4%)
    ppermute x6, starting transfers between devices, moved(): lax.ppermute(v, RING, pairs_of(shape, lambda s, h: ((s + by) % sections,...  60.3 us
    all_to_all x6, waiting for transfers between devices, exchange(): return lax.all_to_all(v, PLANE, split_axis=0, concat_axis=0, tiled=True)  52.5 us
    all_to_all x6, starting transfers between devices, exchange(): return lax.all_to_all(v, PLANE, split_axis=0, concat_axis=0, tiled=True)  38 us
    pallas_call x12, Pallas kernels, run(): pl.pallas_call(kernel, out_shape=outs, in_specs=where, out_specs=jax.tree...  23 us
    ppermute x8, starting transfers between devices, other_core(): return lax.ppermute(v, NODE, [(0, 1), (1, 0)])  17.5 us
    ppermute x6, waiting for transfers between devices, moved(): lax.ppermute(v, RING, pairs_of(shape, lambda s, h: ((s + by) % sections,...  14.8 us
    unnamed x24, local copies, waits for them, and re-layouts  9.18 us
  transfers between devices with their start and end apart: 20, of which 10 were waited for; matrix products, arithmetic and copies ran while one was open for 0% of the time, Pallas kernels for 9%

profile of v12, /device:TPU:8, one launch (start us, length us, event | category | flops | bytes accessed | tf_op | source)
XLA Modules:
  0.0 219.3 jit_solution(3929497618436042167)
XLA Ops:
  2.7 15.7 %collective-permute-start = (bf16[144,1024]{1,0:T(8,128)(2,1)}, bf16[144,1024]{1,0:T(8,128)(2,1)S(1)}, u32[]{:S(2)}, u32[]{:S(2)}) collective-permute-start(bf16[144,1024]{1,0:T(8,128)(2,1)} %get-tuple-element.30.block_ref), channel_id=1, source_target_pairs={{0,16},{1,17},{2,18},{3,19},{4,20},{5,21},{6,22},{7,23},{8,24},{9,... | collective-permute-start | bytes 884744 | tf_op jit(solution)/shard_map/ppermute | solution.py:42
  20.4 3.7 %shard_map.105 = (bf16[16,600,128]{2,1,0:T(8,128)(2,1)}, bf16[512,128]{1,0:T(8,128)(2,1)}, bf16[512,128]{1,0:T(8,128)(2,1)}) custom-call(s32[1]{0:T(128)} %bitcast.first_ref, bf16[144,1024]{1,0:T(8,128)(2,1)} %get-tuple-element.30.block_ref, bf16[256,1024]{1,0:T(8,128)(2,1)} %get-tuple-element.31.pair_ref), custom_call_target="tpu_custom_call" | custom-call | flops 1000 | bytes 1000 | tf_op jit(solution)/shard_map/pallas_call | solution.py:66
  24.1 7.4 %all-to-all-start = ((bf16[16,600,128]{2,1,0:T(8,128)(2,1)}), bf16[16,600,128]{2,1,0:T(8,128)(2,1)S(1)}, u32[]{:S(2)}, u32[]{:S(2)}) async-start(bf16[16,600,128]{2,1,0:T(8,128)(2,1)} %get-tuple-element.34), calls=%async_computation | async-start | bytes 4915200 | tf_op jit(solution)/shard_map/all_to_all | solution.py:52
  35.1 29.4 %all-to-all-done.refs_0_ = bf16[16,600,128]{2,1,0:T(8,128)(2,1)S(1)} async-done(((bf16[16,600,128]{2,1,0:T(8,128)(2,1)}), bf16[16,600,128]{2,1,0:T(8,128)(2,1)S(1)}, u32[]{:S(2)}, u32[]{:S(2)}) %all-to-all-start) | async-done | bytes 2457632 | tf_op jit(solution)/shard_map/all_to_all | solution.py:52
  66.0 5.5 %all-to-all-start.1 = ((bf16[16,200,128]{2,1,0:T(8,128)(2,1)}), bf16[16,200,128]{2,1,0:T(8,128)(2,1)}, u32[]{:S(2)}, u32[]{:S(2)}) async-start(bf16[16,200,128]{2,1,0:T(8,128)(2,1)} %get-tuple-element.38), calls=%async_computation.1 | async-start | bytes 1638400 | tf_op jit(solution)/shard_map/all_to_all | solution.py:52
  73.3 8.6 %all-to-all-done.1.refs_1_ = bf16[16,200,128]{2,1,0:T(8,128)(2,1)} async-done(((bf16[16,200,128]{2,1,0:T(8,128)(2,1)}), bf16[16,200,128]{2,1,0:T(8,128)(2,1)}, u32[]{:S(2)}, u32[]{:S(2)}) %all-to-all-start.1) | async-done | bytes 819232 | tf_op jit(solution)/shard_map/all_to_all | solution.py:52
  81.9 5.6 %all-to-all-start.2 = ((bf16[16,400,128]{2,1,0:T(8,128)(2,1)}), bf16[16,400,128]{2,1,0:T(8,128)(2,1)}, u32[]{:S(2)}, u32[]{:S(2)}) async-start(bf16[16,400,128]{2,1,0:T(8,128)(2,1)} %copy-done.5), calls=%async_computation.2 | async-start | bytes 3276800 | tf_op jit(solution)/shard_map/all_to_all | solution.py:52
  89.2 4.6 %shard_map.108 = (bf16[512,768]{1,0:T(8,128)(2,1)S(1)}, bf16[512,768]{1,0:T(8,128)(2,1)S(1)}, bf16[512,768]{1,0:T(8,128)(2,1)S(1)}, bf16[512,768]{1,0:T(8,128)(2,1)S(1)}) custom-call(bf16[16,600,128]{2,1,0:T(8,128)(2,1)S(1)} %copy-done.3, bf16[16,200,128]{2,1,0:T(8,128)(2,1)} %all-to-all-done.1.refs_1_, bf16[1024,768]{1,0:T(8,128)(2,1)S(1)} %bitcast.7, ...), custom_call_target="tpu_custom_call" | custom-call | flops 1000 | bytes 1000 | tf_op jit(solution)/shard_map/pallas_call | solution.py:66
  95.7 2.4 %collective-permute-start.3 = (bf16[512,768]{1,0:T(8,128)(2,1)S(1)}, bf16[512,768]{1,0:T(8,128)(2,1)S(1)}, u32[]{:S(2)}, u32[]{:S(2)}) collective-permute-start(bf16[512,768]{1,0:T(8,128)(2,1)S(1)} %get-tuple-element.40.refs_1_), channel_id=1, source_target_pairs={{0,32},{32,0},{1,33},{33,1},{2,34},{34,2},{3,35},{35,3},{4,36},{36... | collective-permute-start | bytes 2359304 | tf_op jit(solution)/shard_map/ppermute | solution.py:48
  100.1 2.4 %collective-permute-start.5 = (bf16[512,768]{1,0:T(8,128)(2,1)S(1)}, bf16[512,768]{1,0:T(8,128)(2,1)S(1)}, u32[]{:S(2)}, u32[]{:S(2)}) collective-permute-start(bf16[512,768]{1,0:T(8,128)(2,1)S(1)} %get-tuple-element.42.refs_3_), channel_id=1, source_target_pairs={{0,32},{32,0},{1,33},{33,1},{2,34},{34,2},{3,35},{35,3},{4,36},{36... | collective-permute-start | bytes 2359304 | tf_op jit(solution)/shard_map/ppermute | solution.py:48
  104.4 3.5 %shard_map.109 = (bf16[16,400,128]{2,1,0:T(8,128)(2,1)}, bf16[16,200,128]{2,1,0:T(8,128)(2,1)S(1)}) custom-call(bf16[512,768]{1,0:T(8,128)(2,1)S(1)} %get-tuple-element.39.refs_0_, bf16[512,768]{1,0:T(8,128)(2,1)S(1)} %get-tuple-element.40.refs_1_, bf16[512,768]{1,0:T(8,128)(2,1)S(1)} %get-tuple-element.41.refs_2_, ...), custom_call_target="tpu_custom_call" | custom-call | flops 1000 | bytes 1000 | tf_op jit(solution)/shard_map/pallas_call | solution.py:66
  108.8 7.3 %all-to-all-start.3 = ((bf16[16,200,128]{2,1,0:T(8,128)(2,1)}), bf16[16,200,128]{2,1,0:T(8,128)(2,1)}, u32[]{:S(2)}, u32[]{:S(2)}) async-start(bf16[16,200,128]{2,1,0:T(8,128)(2,1)} %copy-done.6), calls=%async_computation.3 | async-start | bytes 1638400 | tf_op jit(solution)/shard_map/all_to_all | solution.py:52
  116.1 3.2 %shard_map.110 = (bf16[256,768]{1,0:T(8,128)(2,1)S(1)}, bf16[256,768]{1,0:T(8,128)(2,1)S(1)}, bf16[256,768]{1,0:T(8,128)(2,1)S(1)}, bf16[256,768]{1,0:T(8,128)(2,1)S(1)}) custom-call(bf16[16,400,128]{2,1,0:T(8,128)(2,1)} %all-to-all-done.2.refs_0_, bf16[1024,768]{1,0:T(8,128)(2,1)S(1)} %bitcast.9, bf16[768,1024]{1,0:T(8,128)(2,1)S(1)} %bitcast.13), custom_call_target="tpu_custom_call" | custom-call | flops 1000 | bytes 1000 | tf_op jit(solution)/shard_map/pallas_call | solution.py:66
  121.3 2.4 %collective-permute-start.7 = (bf16[256,768]{1,0:T(8,128)(2,1)S(1)}, bf16[256,768]{1,0:T(8,128)(2,1)S(1)}, u32[]{:S(2)}, u32[]{:S(2)}) collective-permute-start(bf16[256,768]{1,0:T(8,128)(2,1)S(1)} %get-tuple-element.49.refs_1_), channel_id=1, source_target_pairs={{0,32},{32,0},{1,33},{33,1},{2,34},{34,2},{3,35},{35,3},{4,36},{36... | collective-permute-start | bytes 1179656 | tf_op jit(solution)/shard_map/ppermute | solution.py:48
  125.6 2.6 %collective-permute-start.9 = (bf16[256,768]{1,0:T(8,128)(2,1)S(1)}, bf16[256,768]{1,0:T(8,128)(2,1)S(1)}, u32[]{:S(2)}, u32[]{:S(2)}) collective-permute-start(bf16[256,768]{1,0:T(8,128)(2,1)S(1)} %get-tuple-element.51.refs_3_), channel_id=1, source_target_pairs={{0,32},{32,0},{1,33},{33,1},{2,34},{34,2},{3,35},{35,3},{4,36},{36... | collective-permute-start | bytes 1179656 | tf_op jit(solution)/shard_map/ppermute | solution.py:48
  131.7 7.3 %all-to-all-start.4 = ((bf16[16,200,128]{2,1,0:T(8,128)(2,1)}), bf16[16,200,128]{2,1,0:T(8,128)(2,1)S(1)}, u32[]{:S(2)}, u32[]{:S(2)}) async-start(bf16[16,200,128]{2,1,0:T(8,128)(2,1)} %copy-done.4), calls=%async_computation.4 | async-start | bytes 1638400 | tf_op jit(solution)/shard_map/all_to_all | solution.py:52
  140.5 12.2 %collective-permute-start.11 = (bf16[128,1024]{1,0:T(8,128)(2,1)S(1)}, bf16[128,1024]{1,0:T(8,128)(2,1)S(1)}, u32[]{:S(2)}, u32[]{:S(2)}) collective-permute-start(bf16[128,1024]{1,0:T(8,128)(2,1)S(1)} %shard_map.113), channel_id=1, source_target_pairs={{0,16},{1,17},{2,18},{3,19},{4,20},{5,21},{6,22},{7,23},{8,24},{9,... | collective-permute-start | bytes 786440 | tf_op jit(solution)/shard_map/ppermute | solution.py:42
  153.5 12.2 %collective-permute-start.10 = (bf16[128,1024]{1,0:T(8,128)(2,1)S(1)}, bf16[128,1024]{1,0:T(8,128)(2,1)S(1)}, u32[]{:S(2)}, u32[]{:S(2)}) collective-permute-start(bf16[128,1024]{1,0:T(8,128)(2,1)S(1)} %shard_map.112), channel_id=1, source_target_pairs={{0,16},{1,17},{2,18},{3,19},{4,20},{5,21},{6,22},{7,23},{8,24},{9,... | collective-permute-start | bytes 786440 | tf_op jit(solution)/shard_map/ppermute | solution.py:42
  165.7 5.0 %all-to-all-start.5 = ((bf16[16,400,128]{2,1,0:T(8,128)(2,1)}), bf16[16,400,128]{2,1,0:T(8,128)(2,1)S(1)}, u32[]{:S(2)}, u32[]{:S(2)}) async-start(bf16[16,400,128]{2,1,0:T(8,128)(2,1)} %get-tuple-element.54), calls=%async_computation.5 | async-start | bytes 3276800 | tf_op jit(solution)/shard_map/all_to_all | solution.py:52
  170.7 8.0 %collective-permute-done.10.refs_3_ = bf16[128,1024]{1,0:T(8,128)(2,1)S(1)} collective-permute-done((bf16[128,1024]{1,0:T(8,128)(2,1)S(1)}, bf16[128,1024]{1,0:T(8,128)(2,1)S(1)}, u32[]{:S(2)}, u32[]{:S(2)}) %collective-permute-start.10) | collective-permute-done | bytes 262176 | tf_op jit(solution)/shard_map/ppermute | solution.py:42
  178.7 13.9 %all-to-all-done.5.refs_2_ = bf16[16,400,128]{2,1,0:T(8,128)(2,1)S(1)} async-done(((bf16[16,400,128]{2,1,0:T(8,128)(2,1)}), bf16[16,400,128]{2,1,0:T(8,128)(2,1)S(1)}, u32[]{:S(2)}, u32[]{:S(2)}) %all-to-all-start.5) | async-done | bytes 1638432 | tf_op jit(solution)/shard_map/all_to_all | solution.py:52
  193.2 16.4 %collective-permute-start.12 = (bf16[128,1024]{1,0:T(8,128)(2,1)S(1)}, bf16[128,1024]{1,0:T(8,128)(2,1)S(1)}, u32[]{:S(2)}, u32[]{:S(2)}) collective-permute-start(bf16[128,1024]{1,0:T(8,128)(2,1)S(1)} %get-tuple-element.56), channel_id=1, source_target_pairs={{0,64},{1,65},{2,66},{3,67},{4,68},{5,69},{6,70},{7,71},{8,72},{9,... | collective-permute-start | bytes 786440 | tf_op jit(solution)/shard_map/ppermute | solution.py:42
  211.5 2.9 %collective-permute-done.12 = bf16[128,1024]{1,0:T(8,128)(2,1)S(1)} collective-permute-done((bf16[128,1024]{1,0:T(8,128)(2,1)S(1)}, bf16[128,1024]{1,0:T(8,128)(2,1)S(1)}, u32[]{:S(2)}, u32[]{:S(2)}) %collective-permute-start.12) | collective-permute-done | bytes 262176 | tf_op jit(solution)/shard_map/ppermute | solution.py:42
  214.4 3.5 %collective-permute-done.13 = bf16[128,1024]{1,0:T(8,128)(2,1)S(1)} collective-permute-done((bf16[128,1024]{1,0:T(8,128)(2,1)S(1)}, bf16[128,1024]{1,0:T(8,128)(2,1)S(1)}, u32[]{:S(2)}, u32[]{:S(2)}) %collective-permute-start.13) | collective-permute-done | bytes 262176 | tf_op jit(solution)/shard_map/ppermute | solution.py:42
  (52 shorter events, 32.7 us)
Async XLA Ops:
  2.7 29.2 %collective-permute-start = (bf16[144,1024]{1,0:T(8,128)(2,1)}, bf16[144,1024]{1,0:T(8,128)(2,1)S(1)}, u32[]{:S(2)}, u32[]{:S(2)}) collective-permute-start(bf16[144,1024]{1,0:T(8,128)(2,1)} %get-tuple-element.30.block_ref), channel_id=1, source_target_pairs={{0,16},{1,17},{2,18},{3,19},{4,20},{5,21},{6,22},{7,23},{8,24},{9,... | collective-permute-start | bytes 884744 | tf_op jit(solution)/shard_map/ppermute | solution.py:42
  18.4 53.0 %collective-permute-start.1 = (bf16[256,1024]{1,0:T(8,128)(2,1)}, bf16[256,1024]{1,0:T(8,128)(2,1)S(1)}, u32[]{:S(2)}, u32[]{:S(2)}) collective-permute-start(bf16[256,1024]{1,0:T(8,128)(2,1)} %get-tuple-element.31.pair_ref), channel_id=1, source_target_pairs={{0,16},{1,17},{2,18},{3,19},{4,20},{5,21},{6,22},{7,23},{8,24},{9,... | collective-permute-start | bytes 1572872 | tf_op jit(solution)/shard_map/ppermute | solution.py:42
  24.1 40.4 %all-to-all-start = ((bf16[16,600,128]{2,1,0:T(8,128)(2,1)}), bf16[16,600,128]{2,1,0:T(8,128)(2,1)S(1)}, u32[]{:S(2)}, u32[]{:S(2)}) async-start(bf16[16,600,128]{2,1,0:T(8,128)(2,1)} %get-tuple-element.34), calls=%async_computation | async-start | bytes 4915200 | tf_op jit(solution)/shard_map/all_to_all | solution.py:52
  66.0 16.0 %all-to-all-start.1 = ((bf16[16,200,128]{2,1,0:T(8,128)(2,1)}), bf16[16,200,128]{2,1,0:T(8,128)(2,1)}, u32[]{:S(2)}, u32[]{:S(2)}) async-start(bf16[16,200,128]{2,1,0:T(8,128)(2,1)} %get-tuple-element.38), calls=%async_computation.1 | async-start | bytes 1638400 | tf_op jit(solution)/shard_map/all_to_all | solution.py:52
  73.3 14.2 %copy-start = (bf16[1,1,1024,768]{3,2,1,0:T(8,128)(2,1)S(1)}, bf16[1,1,1024,768]{3,2,1,0:T(8,128)(2,1)}, u32[]{:S(2)}) copy-start(bf16[1,1,1024,768]{3,2,1,0:T(8,128)(2,1)} %param.16) | copy-start | bytes 4718596
  73.3 14.2 %copy-start.1 = (bf16[1,1,768,1024]{3,2,1,0:T(8,128)(2,1)S(1)}, bf16[1,1,768,1024]{3,2,1,0:T(8,128)(2,1)}, u32[]{:S(2)}) copy-start(bf16[1,1,768,1024]{3,2,1,0:T(8,128)(2,1)} %param.17) | copy-start | bytes 4718596
  81.9 26.9 %all-to-all-start.2 = ((bf16[16,400,128]{2,1,0:T(8,128)(2,1)}), bf16[16,400,128]{2,1,0:T(8,128)(2,1)}, u32[]{:S(2)}, u32[]{:S(2)}) async-start(bf16[16,400,128]{2,1,0:T(8,128)(2,1)} %copy-done.5), calls=%async_computation.2 | async-start | bytes 3276800 | tf_op jit(solution)/shard_map/all_to_all | solution.py:52
  93.8 8.7 %collective-permute-start.2 = (bf16[512,768]{1,0:T(8,128)(2,1)S(1)}, bf16[512,768]{1,0:T(8,128)(2,1)S(1)}, u32[]{:S(2)}, u32[]{:S(2)}) collective-permute-start(bf16[512,768]{1,0:T(8,128)(2,1)S(1)} %get-tuple-element.39.refs_0_), channel_id=1, source_target_pairs={{0,32},{32,0},{1,33},{33,1},{2,34},{34,2},{3,35},{35,3},{4,36},{36... | collective-permute-start | bytes 2359304 | tf_op jit(solution)/shard_map/ppermute | solution.py:48
  95.7 6.8 %collective-permute-start.3 = (bf16[512,768]{1,0:T(8,128)(2,1)S(1)}, bf16[512,768]{1,0:T(8,128)(2,1)S(1)}, u32[]{:S(2)}, u32[]{:S(2)}) collective-permute-start(bf16[512,768]{1,0:T(8,128)(2,1)S(1)} %get-tuple-element.40.refs_1_), channel_id=1, source_target_pairs={{0,32},{32,0},{1,33},{33,1},{2,34},{34,2},{3,35},{35,3},{4,36},{36... | collective-permute-start | bytes 2359304 | tf_op jit(solution)/shard_map/ppermute | solution.py:48
  98.2 4.4 %collective-permute-start.4 = (bf16[512,768]{1,0:T(8,128)(2,1)S(1)}, bf16[512,768]{1,0:T(8,128)(2,1)S(1)}, u32[]{:S(2)}, u32[]{:S(2)}) collective-permute-start(bf16[512,768]{1,0:T(8,128)(2,1)S(1)} %get-tuple-element.41.refs_2_), channel_id=1, source_target_pairs={{0,32},{32,0},{1,33},{33,1},{2,34},{34,2},{3,35},{35,3},{4,36},{36... | collective-permute-start | bytes 2359304 | tf_op jit(solution)/shard_map/ppermute | solution.py:48
  100.1 4.3 %collective-permute-start.5 = (bf16[512,768]{1,0:T(8,128)(2,1)S(1)}, bf16[512,768]{1,0:T(8,128)(2,1)S(1)}, u32[]{:S(2)}, u32[]{:S(2)}) collective-permute-start(bf16[512,768]{1,0:T(8,128)(2,1)S(1)} %get-tuple-element.42.refs_3_), channel_id=1, source_target_pairs={{0,32},{32,0},{1,33},{33,1},{2,34},{34,2},{3,35},{35,3},{4,36},{36... | collective-permute-start | bytes 2359304 | tf_op jit(solution)/shard_map/ppermute | solution.py:48
  108.8 22.9 %all-to-all-start.3 = ((bf16[16,200,128]{2,1,0:T(8,128)(2,1)}), bf16[16,200,128]{2,1,0:T(8,128)(2,1)}, u32[]{:S(2)}, u32[]{:S(2)}) async-start(bf16[16,200,128]{2,1,0:T(8,128)(2,1)} %copy-done.6), calls=%async_computation.3 | async-start | bytes 1638400 | tf_op jit(solution)/shard_map/all_to_all | solution.py:52
  119.4 8.9 %collective-permute-start.6 = (bf16[256,768]{1,0:T(8,128)(2,1)S(1)}, bf16[256,768]{1,0:T(8,128)(2,1)S(1)}, u32[]{:S(2)}, u32[]{:S(2)}) collective-permute-start(bf16[256,768]{1,0:T(8,128)(2,1)S(1)} %get-tuple-element.48.refs_0_), channel_id=1, source_target_pairs={{0,32},{32,0},{1,33},{33,1},{2,34},{34,2},{3,35},{35,3},{4,36},{36... | collective-permute-start | bytes 1179656 | tf_op jit(solution)/shard_map/ppermute | solution.py:48
  121.3 7.0 %collective-permute-start.7 = (bf16[256,768]{1,0:T(8,128)(2,1)S(1)}, bf16[256,768]{1,0:T(8,128)(2,1)S(1)}, u32[]{:S(2)}, u32[]{:S(2)}) collective-permute-start(bf16[256,768]{1,0:T(8,128)(2,1)S(1)} %get-tuple-element.49.refs_1_), channel_id=1, source_target_pairs={{0,32},{32,0},{1,33},{33,1},{2,34},{34,2},{3,35},{35,3},{4,36},{36... | collective-permute-start | bytes 1179656 | tf_op jit(solution)/shard_map/ppermute | solution.py:48
  123.7 4.5 %collective-permute-start.8 = (bf16[256,768]{1,0:T(8,128)(2,1)S(1)}, bf16[256,768]{1,0:T(8,128)(2,1)S(1)}, u32[]{:S(2)}, u32[]{:S(2)}) collective-permute-start(bf16[256,768]{1,0:T(8,128)(2,1)S(1)} %get-tuple-element.50.refs_2_), channel_id=1, source_target_pairs={{0,32},{32,0},{1,33},{33,1},{2,34},{34,2},{3,35},{35,3},{4,36},{36... | collective-permute-start | bytes 1179656 | tf_op jit(solution)/shard_map/ppermute | solution.py:48
  125.6 3.7 %collective-permute-start.9 = (bf16[256,768]{1,0:T(8,128)(2,1)S(1)}, bf16[256,768]{1,0:T(8,128)(2,1)S(1)}, u32[]{:S(2)}, u32[]{:S(2)}) collective-permute-start(bf16[256,768]{1,0:T(8,128)(2,1)S(1)} %get-tuple-element.51.refs_3_), channel_id=1, source_target_pairs={{0,32},{32,0},{1,33},{33,1},{2,34},{34,2},{3,35},{35,3},{4,36},{36... | collective-permute-start | bytes 1179656 | tf_op jit(solution)/shard_map/ppermute | solution.py:48
  131.7 21.4 %all-to-all-start.4 = ((bf16[16,200,128]{2,1,0:T(8,128)(2,1)}), bf16[16,200,128]{2,1,0:T(8,128)(2,1)S(1)}, u32[]{:S(2)}, u32[]{:S(2)}) async-start(bf16[16,200,128]{2,1,0:T(8,128)(2,1)} %copy-done.4), calls=%async_computation.4 | async-start | bytes 1638400 | tf_op jit(solution)/shard_map/all_to_all | solution.py:52
  140.5 30.2 %collective-permute-start.11 = (bf16[128,1024]{1,0:T(8,128)(2,1)S(1)}, bf16[128,1024]{1,0:T(8,128)(2,1)S(1)}, u32[]{:S(2)}, u32[]{:S(2)}) collective-permute-start(bf16[128,1024]{1,0:T(8,128)(2,1)S(1)} %shard_map.113), channel_id=1, source_target_pairs={{0,16},{1,17},{2,18},{3,19},{4,20},{5,21},{6,22},{7,23},{8,24},{9,... | collective-permute-start | bytes 786440 | tf_op jit(solution)/shard_map/ppermute | solution.py:42
  153.5 25.2 %collective-permute-start.10 = (bf16[128,1024]{1,0:T(8,128)(2,1)S(1)}, bf16[128,1024]{1,0:T(8,128)(2,1)S(1)}, u32[]{:S(2)}, u32[]{:S(2)}) collective-permute-start(bf16[128,1024]{1,0:T(8,128)(2,1)S(1)} %shard_map.112), channel_id=1, source_target_pairs={{0,16},{1,17},{2,18},{3,19},{4,20},{5,21},{6,22},{7,23},{8,24},{9,... | collective-permute-start | bytes 786440 | tf_op jit(solution)/shard_map/ppermute | solution.py:42
  165.7 27.0 %all-to-all-start.5 = ((bf16[16,400,128]{2,1,0:T(8,128)(2,1)}), bf16[16,400,128]{2,1,0:T(8,128)(2,1)S(1)}, u32[]{:S(2)}, u32[]{:S(2)}) async-start(bf16[16,400,128]{2,1,0:T(8,128)(2,1)} %get-tuple-element.54), calls=%async_computation.5 | async-start | bytes 3276800 | tf_op jit(solution)/shard_map/all_to_all | solution.py:52
  170.7 22.0 %copy-start.7 = (bf16[512,128]{1,0:T(8,128)(2,1)S(1)}, bf16[512,128]{1,0:T(8,128)(2,1)}, u32[]{:S(2)}) copy-start(bf16[512,128]{1,0:T(8,128)(2,1)} %get-tuple-element.33.refs_1_) | copy-start | bytes 393220
  170.7 22.0 %copy-start.8 = (bf16[512,128]{1,0:T(8,128)(2,1)S(1)}, bf16[512,128]{1,0:T(8,128)(2,1)}, u32[]{:S(2)}) copy-start(bf16[512,128]{1,0:T(8,128)(2,1)} %get-tuple-element.32.refs_0_) | copy-start | bytes 393220
  193.2 21.2 %collective-permute-start.12 = (bf16[128,1024]{1,0:T(8,128)(2,1)S(1)}, bf16[128,1024]{1,0:T(8,128)(2,1)S(1)}, u32[]{:S(2)}, u32[]{:S(2)}) collective-permute-start(bf16[128,1024]{1,0:T(8,128)(2,1)S(1)} %get-tuple-element.56), channel_id=1, source_target_pairs={{0,64},{1,65},{2,66},{3,67},{4,68},{5,69},{6,70},{7,71},{8,72},{9,... | collective-permute-start | bytes 786440 | tf_op jit(solution)/shard_map/ppermute | solution.py:42
  209.6 8.3 %collective-permute-start.13 = (bf16[128,1024]{1,0:T(8,128)(2,1)S(1)}, bf16[128,1024]{1,0:T(8,128)(2,1)S(1)}, u32[]{:S(2)}, u32[]{:S(2)}) collective-permute-start(bf16[128,1024]{1,0:T(8,128)(2,1)S(1)} %get-tuple-element.57), channel_id=1, source_target_pairs={{0,448},{1,449},{2,450},{3,451},{4,452},{5,453},{6,454},{7,455},{8... | collective-permute-start | bytes 786440 | tf_op jit(solution)/shard_map/ppermute | solution.py:42
  (7 other events, 7.8 us)

commit v13 on v12

--- a/solution.py
+++ b/solution.py
@@ -381,6 +381,7 @@
         far_pair,
         scratch=wide(2, F32),
         flops=LONG,
+        room=56 << 20,
     )
     got_b = exchange(after(sent_b, got_f))
     out, out_f = work((after(got, sent_b), got_f), "agf", "f")

time: 220 us -> 222 us (level)
  the two profiles are of different devices: /device:TPU:8 before, /device:TPU:66 now
where the time goes in v13:
time: 222 us; the launch traced here: 221 us
  starting transfers between devices  118 us (53%)
  waiting for transfers between devices  68.9 us (31%)
  Pallas kernels  25.4 us (11%)
  local copies, waits for them, and re-layouts  7.83 us (4%)
    ppermute x6, starting transfers between devices, moved(): lax.ppermute(v, RING, pairs_of(shape, lambda s, h: ((s + by) % sections,...  58.3 us
    ppermute x6, waiting for transfers between devices, moved(): lax.ppermute(v, RING, pairs_of(shape, lambda s, h: ((s + by) % sections,...  52.6 us
    all_to_all x6, starting transfers between devices, exchange(): return lax.all_to_all(v, PLANE, split_axis=0, concat_axis=0, tiled=True)  42.2 us
    pallas_call x12, Pallas kernels, run(): pl.pallas_call(kernel, out_shape=outs, in_specs=where, out_specs=jax.tree...  25.4 us
    ppermute x8, starting transfers between devices, other_core(): return lax.ppermute(v, NODE, [(0, 1), (1, 0)])  17.5 us
    all_to_all x6, waiting for transfers between devices, exchange(): return lax.all_to_all(v, PLANE, split_axis=0, concat_axis=0, tiled=True)  13.3 us
    unnamed x22, local copies, waits for them, and re-layouts  7.83 us
  transfers between devices with their start and end apart: 20, of which 9 were waited for; matrix products, arithmetic and copies ran while one was open for 0% of the time, Pallas kernels for 10%

profile of v13, /device:TPU:66, one launch (start us, length us, event | category | flops | bytes accessed | tf_op | source)
XLA Modules:
  0.0 221.1 jit_solution(15060404221012640843)
XLA Ops:
  2.8 13.9 %collective-permute-start = (bf16[144,1024]{1,0:T(8,128)(2,1)}, bf16[144,1024]{1,0:T(8,128)(2,1)S(1)}, u32[]{:S(2)}, u32[]{:S(2)}) collective-permute-start(bf16[144,1024]{1,0:T(8,128)(2,1)} %get-tuple-element.30.block_ref), channel_id=1, source_target_pairs={{0,16},{1,17},{2,18},{3,19},{4,20},{5,21},{6,22},{7,23},{8,24},{9,... | collective-permute-start | bytes 884744 | tf_op jit(solution)/shard_map/ppermute | solution.py:42
  18.6 3.7 %shard_map.105 = (bf16[16,600,128]{2,1,0:T(8,128)(2,1)}, bf16[512,128]{1,0:T(8,128)(2,1)}, bf16[512,128]{1,0:T(8,128)(2,1)}) custom-call(s32[1]{0:T(128)} %bitcast.first_ref, bf16[144,1024]{1,0:T(8,128)(2,1)} %get-tuple-element.30.block_ref, bf16[256,1024]{1,0:T(8,128)(2,1)} %get-tuple-element.31.pair_ref), custom_call_target="tpu_custom_call" | custom-call | flops 1000 | bytes 1000 | tf_op jit(solution)/shard_map/pallas_call | solution.py:66
  22.3 7.5 %all-to-all-start = ((bf16[16,600,128]{2,1,0:T(8,128)(2,1)}), bf16[16,600,128]{2,1,0:T(8,128)(2,1)S(1)}, u32[]{:S(2)}, u32[]{:S(2)}) async-start(bf16[16,600,128]{2,1,0:T(8,128)(2,1)} %get-tuple-element.34), calls=%async_computation | async-start | bytes 4915200 | tf_op jit(solution)/shard_map/all_to_all | solution.py:52
  29.8 20.6 %collective-permute-done.block_ref = bf16[144,1024]{1,0:T(8,128)(2,1)S(1)} collective-permute-done((bf16[144,1024]{1,0:T(8,128)(2,1)}, bf16[144,1024]{1,0:T(8,128)(2,1)S(1)}, u32[]{:S(2)}, u32[]{:S(2)}) %collective-permute-start) | collective-permute-done | bytes 294944 | tf_op jit(solution)/shard_map/ppermute | solution.py:42
  52.5 8.3 %all-to-all-done.refs_0_ = bf16[16,600,128]{2,1,0:T(8,128)(2,1)S(1)} async-done(((bf16[16,600,128]{2,1,0:T(8,128)(2,1)}), bf16[16,600,128]{2,1,0:T(8,128)(2,1)S(1)}, u32[]{:S(2)}, u32[]{:S(2)}) %all-to-all-start) | async-done | bytes 2457632 | tf_op jit(solution)/shard_map/all_to_all | solution.py:52
  62.3 7.5 %all-to-all-start.1 = ((bf16[16,200,128]{2,1,0:T(8,128)(2,1)}), bf16[16,200,128]{2,1,0:T(8,128)(2,1)}, u32[]{:S(2)}, u32[]{:S(2)}) async-start(bf16[16,200,128]{2,1,0:T(8,128)(2,1)} %get-tuple-element.38), calls=%async_computation.1 | async-start | bytes 1638400 | tf_op jit(solution)/shard_map/all_to_all | solution.py:52
  71.4 3.0 %shard_map.107 = bf16[16,400,128]{2,1,0:T(8,128)(2,1)} custom-call(bf16[512,128]{1,0:T(8,128)(2,1)} %copy-done.8, bf16[256,1024]{1,0:T(8,128)(2,1)} %copy-done.9), custom_call_target="tpu_custom_call" | custom-call | flops 40000000000 | bytes 1000 | tf_op jit(solution)/shard_map/pallas_call | solution.py:66
  74.4 5.0 %all-to-all-done.1.refs_1_ = bf16[16,200,128]{2,1,0:T(8,128)(2,1)} async-done(((bf16[16,200,128]{2,1,0:T(8,128)(2,1)}), bf16[16,200,128]{2,1,0:T(8,128)(2,1)}, u32[]{:S(2)}, u32[]{:S(2)}) %all-to-all-start.1) | async-done | bytes 819232 | tf_op jit(solution)/shard_map/all_to_all | solution.py:52
  79.4 6.6 %all-to-all-start.2 = ((bf16[16,400,128]{2,1,0:T(8,128)(2,1)}), bf16[16,400,128]{2,1,0:T(8,128)(2,1)}, u32[]{:S(2)}, u32[]{:S(2)}) async-start(bf16[16,400,128]{2,1,0:T(8,128)(2,1)} %shard_map.107), calls=%async_computation.2 | async-start | bytes 3276800 | tf_op jit(solution)/shard_map/all_to_all | solution.py:52
  87.6 4.6 %shard_map.108 = (bf16[512,768]{1,0:T(8,128)(2,1)S(1)}, bf16[512,768]{1,0:T(8,128)(2,1)S(1)}, bf16[512,768]{1,0:T(8,128)(2,1)S(1)}, bf16[512,768]{1,0:T(8,128)(2,1)S(1)}) custom-call(bf16[16,600,128]{2,1,0:T(8,128)(2,1)S(1)} %copy-done.3, bf16[16,200,128]{2,1,0:T(8,128)(2,1)} %all-to-all-done.1.refs_1_, bf16[1024,768]{1,0:T(8,128)(2,1)S(1)} %bitcast.7, ...), custom_call_target="tpu_custom_call" | custom-call | flops 1000 | bytes 1000 | tf_op jit(solution)/shard_map/pallas_call | solution.py:66
  94.1 2.4 %collective-permute-start.3 = (bf16[512,768]{1,0:T(8,128)(2,1)S(1)}, bf16[512,768]{1,0:T(8,128)(2,1)S(1)}, u32[]{:S(2)}, u32[]{:S(2)}) collective-permute-start(bf16[512,768]{1,0:T(8,128)(2,1)S(1)} %get-tuple-element.40.refs_1_), channel_id=1, source_target_pairs={{0,32},{32,0},{1,33},{33,1},{2,34},{34,2},{3,35},{35,3},{4,36},{36... | collective-permute-start | bytes 2359304 | tf_op jit(solution)/shard_map/ppermute | solution.py:48
  102.8 3.5 %shard_map.109 = (bf16[16,400,128]{2,1,0:T(8,128)(2,1)}, bf16[16,200,128]{2,1,0:T(8,128)(2,1)S(1)}) custom-call(bf16[512,768]{1,0:T(8,128)(2,1)S(1)} %get-tuple-element.39.refs_0_, bf16[512,768]{1,0:T(8,128)(2,1)S(1)} %get-tuple-element.40.refs_1_, bf16[512,768]{1,0:T(8,128)(2,1)S(1)} %get-tuple-element.41.refs_2_, ...), custom_call_target="tpu_custom_call" | custom-call | flops 1000 | bytes 1000 | tf_op jit(solution)/shard_map/pallas_call | solution.py:66
  107.2 7.3 %all-to-all-start.3 = ((bf16[16,200,128]{2,1,0:T(8,128)(2,1)}), bf16[16,200,128]{2,1,0:T(8,128)(2,1)}, u32[]{:S(2)}, u32[]{:S(2)}) async-start(bf16[16,200,128]{2,1,0:T(8,128)(2,1)} %copy-done.5), calls=%async_computation.3 | async-start | bytes 1638400 | tf_op jit(solution)/shard_map/all_to_all | solution.py:52
  114.5 3.2 %shard_map.110 = (bf16[256,768]{1,0:T(8,128)(2,1)S(1)}, bf16[256,768]{1,0:T(8,128)(2,1)S(1)}, bf16[256,768]{1,0:T(8,128)(2,1)S(1)}, bf16[256,768]{1,0:T(8,128)(2,1)S(1)}) custom-call(bf16[16,400,128]{2,1,0:T(8,128)(2,1)} %all-to-all-done.2.refs_0_, bf16[1024,768]{1,0:T(8,128)(2,1)S(1)} %bitcast.9, bf16[768,1024]{1,0:T(8,128)(2,1)S(1)} %bitcast.13), custom_call_target="tpu_custom_call" | custom-call | flops 1000 | bytes 1000 | tf_op jit(solution)/shard_map/pallas_call | solution.py:66
  119.7 2.4 %collective-permute-start.7 = (bf16[256,768]{1,0:T(8,128)(2,1)S(1)}, bf16[256,768]{1,0:T(8,128)(2,1)S(1)}, u32[]{:S(2)}, u32[]{:S(2)}) collective-permute-start(bf16[256,768]{1,0:T(8,128)(2,1)S(1)} %get-tuple-element.49.refs_1_), channel_id=1, source_target_pairs={{0,32},{32,0},{1,33},{33,1},{2,34},{34,2},{3,35},{35,3},{4,36},{36... | collective-permute-start | bytes 1179656 | tf_op jit(solution)/shard_map/ppermute | solution.py:48
  124.0 2.6 %collective-permute-start.9 = (bf16[256,768]{1,0:T(8,128)(2,1)S(1)}, bf16[256,768]{1,0:T(8,128)(2,1)S(1)}, u32[]{:S(2)}, u32[]{:S(2)}) collective-permute-start(bf16[256,768]{1,0:T(8,128)(2,1)S(1)} %get-tuple-element.51.refs_3_), channel_id=1, source_target_pairs={{0,32},{32,0},{1,33},{33,1},{2,34},{34,2},{3,35},{35,3},{4,36},{36... | collective-permute-start | bytes 1179656 | tf_op jit(solution)/shard_map/ppermute | solution.py:48
  130.1 7.2 %all-to-all-start.4 = ((bf16[16,200,128]{2,1,0:T(8,128)(2,1)}), bf16[16,200,128]{2,1,0:T(8,128)(2,1)S(1)}, u32[]{:S(2)}, u32[]{:S(2)}) async-start(bf16[16,200,128]{2,1,0:T(8,128)(2,1)} %copy-done.4), calls=%async_computation.4 | async-start | bytes 1638400 | tf_op jit(solution)/shard_map/all_to_all | solution.py:52
  138.9 25.2 %collective-permute-start.11 = (bf16[128,1024]{1,0:T(8,128)(2,1)S(1)}, bf16[128,1024]{1,0:T(8,128)(2,1)S(1)}, u32[]{:S(2)}, u32[]{:S(2)}) collective-permute-start(bf16[128,1024]{1,0:T(8,128)(2,1)S(1)} %shard_map.113), channel_id=1, source_target_pairs={{0,16},{1,17},{2,18},{3,19},{4,20},{5,21},{6,22},{7,23},{8,24},{9,... | collective-permute-start | bytes 786440 | tf_op jit(solution)/shard_map/ppermute | solution.py:42
  164.4 11.5 %collective-permute-start.10 = (bf16[128,1024]{1,0:T(8,128)(2,1)S(1)}, bf16[128,1024]{1,0:T(8,128)(2,1)S(1)}, u32[]{:S(2)}, u32[]{:S(2)}) collective-permute-start(bf16[128,1024]{1,0:T(8,128)(2,1)S(1)} %shard_map.112), channel_id=1, source_target_pairs={{0,16},{1,17},{2,18},{3,19},{4,20},{5,21},{6,22},{7,23},{8,24},{9,... | collective-permute-start | bytes 786440 | tf_op jit(solution)/shard_map/ppermute | solution.py:42
  175.9 6.2 %all-to-all-start.5 = ((bf16[16,400,128]{2,1,0:T(8,128)(2,1)}), bf16[16,400,128]{2,1,0:T(8,128)(2,1)S(1)}, u32[]{:S(2)}, u32[]{:S(2)}) async-start(bf16[16,400,128]{2,1,0:T(8,128)(2,1)} %get-tuple-element.54), calls=%async_computation.5 | async-start | bytes 3276800 | tf_op jit(solution)/shard_map/all_to_all | solution.py:52
  182.1 6.0 %collective-permute-done.11.from_ref = bf16[128,1024]{1,0:T(8,128)(2,1)S(1)} collective-permute-done((bf16[128,1024]{1,0:T(8,128)(2,1)S(1)}, bf16[128,1024]{1,0:T(8,128)(2,1)S(1)}, u32[]{:S(2)}, u32[]{:S(2)}) %collective-permute-start.11) | collective-permute-done | bytes 262176 | tf_op jit(solution)/shard_map/ppermute | solution.py:42
  188.1 15.9 %collective-permute-done.10.refs_3_ = bf16[128,1024]{1,0:T(8,128)(2,1)S(1)} collective-permute-done((bf16[128,1024]{1,0:T(8,128)(2,1)S(1)}, bf16[128,1024]{1,0:T(8,128)(2,1)S(1)}, u32[]{:S(2)}, u32[]{:S(2)}) %collective-permute-start.10) | collective-permute-done | bytes 262176 | tf_op jit(solution)/shard_map/ppermute | solution.py:42
  206.4 3.9 %collective-permute-start.13 = (bf16[128,1024]{1,0:T(8,128)(2,1)S(1)}, bf16[128,1024]{1,0:T(8,128)(2,1)S(1)}, u32[]{:S(2)}, u32[]{:S(2)}) collective-permute-start(bf16[128,1024]{1,0:T(8,128)(2,1)S(1)} %get-tuple-element.57), channel_id=1, source_target_pairs={{0,448},{1,449},{2,450},{3,451},{4,452},{5,453},{6,454},{7,455},{8... | collective-permute-start | bytes 786440 | tf_op jit(solution)/shard_map/ppermute | solution.py:42
  210.3 9.4 %collective-permute-done.12 = bf16[128,1024]{1,0:T(8,128)(2,1)S(1)} collective-permute-done((bf16[128,1024]{1,0:T(8,128)(2,1)S(1)}, bf16[128,1024]{1,0:T(8,128)(2,1)S(1)}, u32[]{:S(2)}, u32[]{:S(2)}) %collective-permute-start.12) | collective-permute-done | bytes 262176 | tf_op jit(solution)/shard_map/ppermute | solution.py:42
  (50 shorter events, 32.9 us)
Async XLA Ops:
  2.8 47.6 %collective-permute-start = (bf16[144,1024]{1,0:T(8,128)(2,1)}, bf16[144,1024]{1,0:T(8,128)(2,1)S(1)}, u32[]{:S(2)}, u32[]{:S(2)}) collective-permute-start(bf16[144,1024]{1,0:T(8,128)(2,1)} %get-tuple-element.30.block_ref), channel_id=1, source_target_pairs={{0,16},{1,17},{2,18},{3,19},{4,20},{5,21},{6,22},{7,23},{8,24},{9,... | collective-permute-start | bytes 884744 | tf_op jit(solution)/shard_map/ppermute | solution.py:42
  16.7 53.9 %collective-permute-start.1 = (bf16[256,1024]{1,0:T(8,128)(2,1)}, bf16[256,1024]{1,0:T(8,128)(2,1)S(1)}, u32[]{:S(2)}, u32[]{:S(2)}) collective-permute-start(bf16[256,1024]{1,0:T(8,128)(2,1)} %get-tuple-element.31.pair_ref), channel_id=1, source_target_pairs={{0,16},{1,17},{2,18},{3,19},{4,20},{5,21},{6,22},{7,23},{8,24},{9,... | collective-permute-start | bytes 1572872 | tf_op jit(solution)/shard_map/ppermute | solution.py:42
  22.3 38.5 %all-to-all-start = ((bf16[16,600,128]{2,1,0:T(8,128)(2,1)}), bf16[16,600,128]{2,1,0:T(8,128)(2,1)S(1)}, u32[]{:S(2)}, u32[]{:S(2)}) async-start(bf16[16,600,128]{2,1,0:T(8,128)(2,1)} %get-tuple-element.34), calls=%async_computation | async-start | bytes 4915200 | tf_op jit(solution)/shard_map/all_to_all | solution.py:52
  62.3 17.1 %all-to-all-start.1 = ((bf16[16,200,128]{2,1,0:T(8,128)(2,1)}), bf16[16,200,128]{2,1,0:T(8,128)(2,1)}, u32[]{:S(2)}, u32[]{:S(2)}) async-start(bf16[16,200,128]{2,1,0:T(8,128)(2,1)} %get-tuple-element.38), calls=%async_computation.1 | async-start | bytes 1638400 | tf_op jit(solution)/shard_map/all_to_all | solution.py:52
  74.4 11.5 %copy-start = (bf16[1,1,1024,768]{3,2,1,0:T(8,128)(2,1)S(1)}, bf16[1,1,1024,768]{3,2,1,0:T(8,128)(2,1)}, u32[]{:S(2)}) copy-start(bf16[1,1,1024,768]{3,2,1,0:T(8,128)(2,1)} %param.16) | copy-start | bytes 4718596
  74.4 11.5 %copy-start.1 = (bf16[1,1,768,1024]{3,2,1,0:T(8,128)(2,1)S(1)}, bf16[1,1,768,1024]{3,2,1,0:T(8,128)(2,1)}, u32[]{:S(2)}) copy-start(bf16[1,1,768,1024]{3,2,1,0:T(8,128)(2,1)} %param.17) | copy-start | bytes 4718596
  79.4 27.9 %all-to-all-start.2 = ((bf16[16,400,128]{2,1,0:T(8,128)(2,1)}), bf16[16,400,128]{2,1,0:T(8,128)(2,1)}, u32[]{:S(2)}, u32[]{:S(2)}) async-start(bf16[16,400,128]{2,1,0:T(8,128)(2,1)} %shard_map.107), calls=%async_computation.2 | async-start | bytes 3276800 | tf_op jit(solution)/shard_map/all_to_all | solution.py:52
  92.2 8.7 %collective-permute-start.2 = (bf16[512,768]{1,0:T(8,128)(2,1)S(1)}, bf16[512,768]{1,0:T(8,128)(2,1)S(1)}, u32[]{:S(2)}, u32[]{:S(2)}) collective-permute-start(bf16[512,768]{1,0:T(8,128)(2,1)S(1)} %get-tuple-element.39.refs_0_), channel_id=1, source_target_pairs={{0,32},{32,0},{1,33},{33,1},{2,34},{34,2},{3,35},{35,3},{4,36},{36... | collective-permute-start | bytes 2359304 | tf_op jit(solution)/shard_map/ppermute | solution.py:48
  94.1 6.8 %collective-permute-start.3 = (bf16[512,768]{1,0:T(8,128)(2,1)S(1)}, bf16[512,768]{1,0:T(8,128)(2,1)S(1)}, u32[]{:S(2)}, u32[]{:S(2)}) collective-permute-start(bf16[512,768]{1,0:T(8,128)(2,1)S(1)} %get-tuple-element.40.refs_1_), channel_id=1, source_target_pairs={{0,32},{32,0},{1,33},{33,1},{2,34},{34,2},{3,35},{35,3},{4,36},{36... | collective-permute-start | bytes 2359304 | tf_op jit(solution)/shard_map/ppermute | solution.py:48
  96.5 4.4 %collective-permute-start.4 = (bf16[512,768]{1,0:T(8,128)(2,1)S(1)}, bf16[512,768]{1,0:T(8,128)(2,1)S(1)}, u32[]{:S(2)}, u32[]{:S(2)}) collective-permute-start(bf16[512,768]{1,0:T(8,128)(2,1)S(1)} %get-tuple-element.41.refs_2_), channel_id=1, source_target_pairs={{0,32},{32,0},{1,33},{33,1},{2,34},{34,2},{3,35},{35,3},{4,36},{36... | collective-permute-start | bytes 2359304 | tf_op jit(solution)/shard_map/ppermute | solution.py:48
  98.5 4.3 %collective-permute-start.5 = (bf16[512,768]{1,0:T(8,128)(2,1)S(1)}, bf16[512,768]{1,0:T(8,128)(2,1)S(1)}, u32[]{:S(2)}, u32[]{:S(2)}) collective-permute-start(bf16[512,768]{1,0:T(8,128)(2,1)S(1)} %get-tuple-element.42.refs_3_), channel_id=1, source_target_pairs={{0,32},{32,0},{1,33},{33,1},{2,34},{34,2},{3,35},{35,3},{4,36},{36... | collective-permute-start | bytes 2359304 | tf_op jit(solution)/shard_map/ppermute | solution.py:48
  107.2 22.9 %all-to-all-start.3 = ((bf16[16,200,128]{2,1,0:T(8,128)(2,1)}), bf16[16,200,128]{2,1,0:T(8,128)(2,1)}, u32[]{:S(2)}, u32[]{:S(2)}) async-start(bf16[16,200,128]{2,1,0:T(8,128)(2,1)} %copy-done.5), calls=%async_computation.3 | async-start | bytes 1638400 | tf_op jit(solution)/shard_map/all_to_all | solution.py:52
  117.7 8.9 %collective-permute-start.6 = (bf16[256,768]{1,0:T(8,128)(2,1)S(1)}, bf16[256,768]{1,0:T(8,128)(2,1)S(1)}, u32[]{:S(2)}, u32[]{:S(2)}) collective-permute-start(bf16[256,768]{1,0:T(8,128)(2,1)S(1)} %get-tuple-element.48.refs_0_), channel_id=1, source_target_pairs={{0,32},{32,0},{1,33},{33,1},{2,34},{34,2},{3,35},{35,3},{4,36},{36... | collective-permute-start | bytes 1179656 | tf_op jit(solution)/shard_map/ppermute | solution.py:48
  119.7 7.0 %collective-permute-start.7 = (bf16[256,768]{1,0:T(8,128)(2,1)S(1)}, bf16[256,768]{1,0:T(8,128)(2,1)S(1)}, u32[]{:S(2)}, u32[]{:S(2)}) collective-permute-start(bf16[256,768]{1,0:T(8,128)(2,1)S(1)} %get-tuple-element.49.refs_1_), channel_id=1, source_target_pairs={{0,32},{32,0},{1,33},{33,1},{2,34},{34,2},{3,35},{35,3},{4,36},{36... | collective-permute-start | bytes 1179656 | tf_op jit(solution)/shard_map/ppermute | solution.py:48
  122.1 4.5 %collective-permute-start.8 = (bf16[256,768]{1,0:T(8,128)(2,1)S(1)}, bf16[256,768]{1,0:T(8,128)(2,1)S(1)}, u32[]{:S(2)}, u32[]{:S(2)}) collective-permute-start(bf16[256,768]{1,0:T(8,128)(2,1)S(1)} %get-tuple-element.50.refs_2_), channel_id=1, source_target_pairs={{0,32},{32,0},{1,33},{33,1},{2,34},{34,2},{3,35},{35,3},{4,36},{36... | collective-permute-start | bytes 1179656 | tf_op jit(solution)/shard_map/ppermute | solution.py:48
  124.0 3.7 %collective-permute-start.9 = (bf16[256,768]{1,0:T(8,128)(2,1)S(1)}, bf16[256,768]{1,0:T(8,128)(2,1)S(1)}, u32[]{:S(2)}, u32[]{:S(2)}) collective-permute-start(bf16[256,768]{1,0:T(8,128)(2,1)S(1)} %get-tuple-element.51.refs_3_), channel_id=1, source_target_pairs={{0,32},{32,0},{1,33},{33,1},{2,34},{34,2},{3,35},{35,3},{4,36},{36... | collective-permute-start | bytes 1179656 | tf_op jit(solution)/shard_map/ppermute | solution.py:48
  130.1 33.9 %all-to-all-start.4 = ((bf16[16,200,128]{2,1,0:T(8,128)(2,1)}), bf16[16,200,128]{2,1,0:T(8,128)(2,1)S(1)}, u32[]{:S(2)}, u32[]{:S(2)}) async-start(bf16[16,200,128]{2,1,0:T(8,128)(2,1)} %copy-done.4), calls=%async_computation.4 | async-start | bytes 1638400 | tf_op jit(solution)/shard_map/all_to_all | solution.py:52
  138.9 49.2 %collective-permute-start.11 = (bf16[128,1024]{1,0:T(8,128)(2,1)S(1)}, bf16[128,1024]{1,0:T(8,128)(2,1)S(1)}, u32[]{:S(2)}, u32[]{:S(2)}) collective-permute-start(bf16[128,1024]{1,0:T(8,128)(2,1)S(1)} %shard_map.113), channel_id=1, source_target_pairs={{0,16},{1,17},{2,18},{3,19},{4,20},{5,21},{6,22},{7,23},{8,24},{9,... | collective-permute-start | bytes 786440 | tf_op jit(solution)/shard_map/ppermute | solution.py:42
  164.4 39.5 %collective-permute-start.10 = (bf16[128,1024]{1,0:T(8,128)(2,1)S(1)}, bf16[128,1024]{1,0:T(8,128)(2,1)S(1)}, u32[]{:S(2)}, u32[]{:S(2)}) collective-permute-start(bf16[128,1024]{1,0:T(8,128)(2,1)S(1)} %shard_map.112), channel_id=1, source_target_pairs={{0,16},{1,17},{2,18},{3,19},{4,20},{5,21},{6,22},{7,23},{8,24},{9,... | collective-permute-start | bytes 786440 | tf_op jit(solution)/shard_map/ppermute | solution.py:42
  175.9 28.0 %all-to-all-start.5 = ((bf16[16,400,128]{2,1,0:T(8,128)(2,1)}), bf16[16,400,128]{2,1,0:T(8,128)(2,1)S(1)}, u32[]{:S(2)}, u32[]{:S(2)}) async-start(bf16[16,400,128]{2,1,0:T(8,128)(2,1)} %get-tuple-element.54), calls=%async_computation.5 | async-start | bytes 3276800 | tf_op jit(solution)/shard_map/all_to_all | solution.py:52
  182.1 21.9 %copy-start.6 = (bf16[512,128]{1,0:T(8,128)(2,1)S(1)}, bf16[512,128]{1,0:T(8,128)(2,1)}, u32[]{:S(2)}) copy-start(bf16[512,128]{1,0:T(8,128)(2,1)} %get-tuple-element.33.refs_1_) | copy-start | bytes 393220
  182.1 21.9 %copy-start.7 = (bf16[512,128]{1,0:T(8,128)(2,1)S(1)}, bf16[512,128]{1,0:T(8,128)(2,1)}, u32[]{:S(2)}) copy-start(bf16[512,128]{1,0:T(8,128)(2,1)} %get-tuple-element.32.refs_0_) | copy-start | bytes 393220
  204.5 15.2 %collective-permute-start.12 = (bf16[128,1024]{1,0:T(8,128)(2,1)S(1)}, bf16[128,1024]{1,0:T(8,128)(2,1)S(1)}, u32[]{:S(2)}, u32[]{:S(2)}) collective-permute-start(bf16[128,1024]{1,0:T(8,128)(2,1)S(1)} %get-tuple-element.56), channel_id=1, source_target_pairs={{0,64},{1,65},{2,66},{3,67},{4,68},{5,69},{6,70},{7,71},{8,72},{9,... | collective-permute-start | bytes 786440 | tf_op jit(solution)/shard_map/ppermute | solution.py:42
  206.4 13.3 %collective-permute-start.13 = (bf16[128,1024]{1,0:T(8,128)(2,1)S(1)}, bf16[128,1024]{1,0:T(8,128)(2,1)S(1)}, u32[]{:S(2)}, u32[]{:S(2)}) collective-permute-start(bf16[128,1024]{1,0:T(8,128)(2,1)S(1)} %get-tuple-element.57), channel_id=1, source_target_pairs={{0,448},{1,449},{2,450},{3,451},{4,452},{5,453},{6,454},{7,455},{8... | collective-permute-start | bytes 786440 | tf_op jit(solution)/shard_map/ppermute | solution.py:42
  (6 other events, 6.4 us)
